TPU v7x, 128 devices: a whole 4x4x4 slice. The times are simulated.
128 devices in a mesh: azim: 32 (over z, x_hi, y), rad: 4 (over x_lo, core).
Axes of the slice: x: 4 (x_hi: 2, x_lo: 2; x = x_hi * 2 + x_lo), y: 4, z: 4, core: 2. Of those that a mesh axis runs over, the one named last changes fastest.
Arguments:
- perturbation_in: float32 [512, 512, 256], P('azim', 'rad'), may hold values from -6 to 6
- coefficients: float32 [4, 29, 512, 512], P(None, None, 'azim', 'rad'), may hold values from -0.4 to 0.4
- wall_cells: int32 [131072], P(('azim', 'rad')), may hold values from 0 to 2047
- wall_count: int32 [128], P(('azim', 'rad')), may hold values from 1 to 1024, as said below
- mode_row: int32 [131072], P(('azim', 'rad')), may hold values from 0 to 4095
- mode_table: bfloat16 [4096, 512], replicated, may hold values from -0.03125 to 0.03125
Outputs:
- perturbation: float32 [512, 512, 256], P('azim', 'rad')
- markov: float32 [512, 256], P(('azim', 'rad'))
Inputs may be any that keep to these rules, and one draw needn't show every extreme that they name: wall_count[t] counts the live slots of tile t; tiles in the azimuthal sectors nearest the 4 blades hold far more wall cells than the others, and some tile holds exactly 1024.
All inputs are finite; a program needn't handle non-finite values.
Results may differ from a plain program's by a relative error of at most 0.0004.
Values sent between devices are 32-bit elements; how exact they have to be, the bound alone decides.
No kernel may reach another device: no remote copies, remote signals or barrier semaphores. Data moves between devices by JAX's collectives and lax.ppermute only.
A program may use at most 320 MiB of HBM per device.

v0:
```python
import jax
import jax.numpy as jnp
from jax import lax
from jax.sharding import PartitionSpec as P

STEPS = 2


def with_halo(block, sides, width, periodic):
    for axis, dim in sides:
        count = lax.axis_size(axis)
        forward = [(i, i + 1) for i in range(count - 1)]
        if periodic:
            forward.append((count - 1, 0))
        backward = [(target, source) for source, target in forward]
        low = lax.ppermute(
            lax.slice_in_dim(block, block.shape[dim] - width, None, axis=dim), axis, forward
        )
        high = lax.ppermute(lax.slice_in_dim(block, 0, width, axis=dim), axis, backward)
        block = jnp.concatenate([low, block, high], axis=dim)
    return block


def flux(extended, coef, center):
    height = center.shape[0]
    width = center.shape[1]
    nvar = coef.shape[0]
    columns = center.shape[2] // nvar
    lanes = jnp.transpose(coef, (2, 3, 0, 1))
    total = jnp.zeros((height, width, nvar * columns), jnp.float32)
    for i in range(5):
        for j in range(5):
            weight = jnp.repeat(lanes[:, :, :, 5 * i + j], columns, axis=2)
            total = total + weight * extended[i : i + height, j : j + width]
    for source in range(nvar):
        weight = jnp.repeat(lanes[:, :, :, 25 + source], columns, axis=2)
        block = jnp.tile(center[:, :, source * columns : (source + 1) * columns], (1, 1, nvar))
        total = total + weight * block
    return total


def body(perturbation_in, coefficients, wall_cells, wall_count, mode_row, mode_table):
    state = perturbation_in

    def rimmed(field):
        cycle = with_halo(field, (("azim", 0),), 2, True)
        return with_halo(cycle, (("rad", 1),), 2, False)

    for step in range(STEPS):
        first = state + flux(rimmed(state), coefficients, state)
        state = 0.5 * (state + first + flux(rimmed(first), coefficients, first))
    flat = state.reshape(-1, state.shape[2])
    rows = jnp.take(flat, wall_cells, axis=0)
    slots = wall_cells.shape[0]
    live = (jnp.arange(slots, dtype=jnp.int32) < wall_count[0]).astype(jnp.float32)
    weights = jnp.take(mode_table, mode_row, axis=0).astype(jnp.float32) * live[:, None]
    term = lax.dot_general(weights, rows, (((0,), (0,)), ((), ())), precision=lax.Precision.HIGHEST)
    totals = lax.psum(term, ("azim", "rad"))
    share = term.shape[0] // lax.axis_size(("azim", "rad"))
    markov = lax.dynamic_slice_in_dim(totals, lax.axis_index(("azim", "rad")) * share, share, 0)
    return (state, markov)


def solution(mesh):
    return jax.shard_map(
        body,
        mesh=mesh,
        in_specs=(
            P("azim", "rad", None),
            P(None, None, "azim", "rad"),
            P(("azim", "rad")),
            P(("azim", "rad")),
            P(("azim", "rad")),
            P(),
        ),
        out_specs=(P("azim", "rad", None), P(("azim", "rad"), None)),
        check_vma=False,
    )
```

profile of v0, /device:TPU:1, one launch (start us, length us, event | category | flops | bytes accessed | tf_op | source)
XLA Modules:
  0.0 521.1 jit_solution(11757235638766196649)
XLA Ops:
  7.2 1.9 copy.124
  10.0 2.1 collective-permute-start
  12.2 7.4 %collective-permute-start.1 = (f32[2,128,256]{1,2,0:T(8,128)}, f32[2,128,256]{1,2,0:T(8,128)}, u32[]{:S(2)}, u32[]{:S(2)}) collective-permute-start(f32[2,128,256]{1,2,0:T(8,128)} %get-tuple-element.41), channel_id=1, source_target_pairs={{4,0},{8,4},{12,8},{16,12},{20,16},{24,20},{28,24},{32,28},{36,32}... | collective-permute-start | bytes 786440 | tf_op jit(solution)/shard_map/ppermute | solution.py:19
  19.5 4.5 fusion.140
  24.9 2.4 copy.116
  27.3 2.4 copy.118
  30.5 2.4 copy.120
  34.6 4.0 broadcast_multiply_fusion.14
  38.6 2.7 broadcast_multiply_fusion.12
  43.5 3.2 fusion.132
  46.7 2.5 copy.84
  49.3 3.2 collective-permute-start.2
  52.5 2.5 copy.90
  55.0 2.2 collective-permute-start.3
  58.2 7.8 %gather_fusion = bf16[1024,512]{1,0:T(8,128)(2,1)} fusion(bf16[4096,512]{1,0:T(8,128)(2,1)} %param.11, s32[1024]{0:T(1024)S(1)} %fusion.125), kind=kCustom, calls=%fused_computation | custom fusion | bytes 2101248 | tf_op jit(solution)/shard_map/jit(_take)/gather | solution.py:56
  66.1 2.3 copy.85
  68.3 2.3 copy.91
  70.6 7.1 %maximum_maximum_fusion = (f32[20,130,256]{1,2,0:T(8,128)}, f32[20,130,256]{1,2,0:T(8,128)}) fusion(f32[2,128,256]{1,2,0:T(8,128)} %collective-permute-done.1, f32[16,128,256]{1,2,0:T(8,128)S(1)} %copy.124, f32[2,128,256]{1,2,0:T(8,128)S(1)} %collective-permute-done, f32[20,2,256]{1,2,0:T(8,128)} %copy.85, f32[20,2,256]{1,2,0:T(8,128)} %copy.91), kind=kLoop, calls=%fused_computation.2 | loop fusion | flops 3993600 | bytes 8028160 | tf_op jit(solution)/shard_map/concatenate | solution.py:20
  77.9 33.4 %fusion.113 = f32[16,128,256]{1,2,0:T(8,128)} fusion(f32[16,128,256]{1,2,0:T(8,128)S(1)} %copy.124, f32[16,128,4,64]{1,3,2,0:T(8,128)} %get-tuple-element.75, f32[16,128,4,64]{1,3,2,0:T(8,128)} %get-tuple-element.76, f32[16,128,4,64]{1,3,2,0:T(8,128)} %get-tuple-element.77, f32[16,128,4,64]{1,3,2,0:T(8,128)} %get-tuple-element.78, ...), kind=kLoop, calls=%fused_computation.261 | loop fusion | flops 30408704 | bytes 55869440 | tf_op jit(solution)/shard_map/add | solution.py:50
  112.4 1.7 fusion.138
  114.2 7.2 %collective-permute-start.5 = (f32[2,128,256]{1,2,0:T(8,128)S(1)}, f32[2,128,256]{1,2,0:T(8,128)S(1)}, u32[]{:S(2)}, u32[]{:S(2)}) collective-permute-start(f32[2,128,256]{1,2,0:T(8,128)S(1)} %get-tuple-element.35), channel_id=1, source_target_pairs={{4,0},{8,4},{12,8},{16,12},{20,16},{24,20},{28,24},{32,28},{36,32}... | collective-permute-start | bytes 786440 | tf_op jit(solution)/shard_map/ppermute | solution.py:19
  123.0 1.7 broadcast_multiply_fusion.11
  124.7 1.6 broadcast_multiply_fusion.9
  127.3 3.2 fusion.131
  130.5 2.5 copy.125
  133.0 3.4 collective-permute-start.6
  136.5 2.5 copy.127
  139.0 2.4 collective-permute-start.7
  143.0 2.3 copy.126
  145.3 2.3 copy.128
  147.8 7.1 %maximum_maximum_fusion.1 = (f32[20,130,256]{1,2,0:T(8,128)}, f32[20,130,256]{1,2,0:T(8,128)}) fusion(f32[2,128,256]{1,2,0:T(8,128)S(1)} %collective-permute-done.5, f32[16,128,256]{1,2,0:T(8,128)S(1)} %copy-done.2, f32[2,128,256]{1,2,0:T(8,128)S(1)} %collective-permute-done.4, f32[20,2,256]{1,2,0:T(8,128)} %copy.126, f32[20,2,256]{1,2,0:T(8,128)} %copy.128), kind=kLoop, calls=%fused_computation.4 | loop fusion | flops 3993600 | bytes 8028160 | tf_op jit(solution)/shard_map/concatenate | solution.py:20
  155.0 36.6 %fusion.112 = f32[16,128,256]{1,2,0:T(8,128)S(1)} fusion(f32[16,128,4,64]{1,3,2,0:T(8,128)} %broadcast_multiply_fusion.8, f32[16,128,4,64]{1,3,2,0:T(8,128)} %broadcast_multiply_fusion.9, f32[16,128,4,64]{1,3,2,0:T(8,128)} %broadcast_multiply_fusion.10, f32[16,128,256]{1,2,0:T(8,128)} %copy-done, f32[16,128,256]{1,2,0:T(8,128)} %fusion.113, ...), kind=kLoop, calls=%fused_computation.257 | loop fusion | flops 31457280 | bytes 57966592 | tf_op jit(solution)/shard_map/mul | solution.py:51
  192.1 7.9 %collective-permute-start.9 = (f32[2,128,256]{1,2,0:T(8,128)S(1)}, f32[2,128,256]{1,2,0:T(8,128)S(1)}, u32[]{:S(2)}, u32[]{:S(2)}) collective-permute-start(f32[2,128,256]{1,2,0:T(8,128)S(1)} %get-tuple-element.29), channel_id=1, source_target_pairs={{4,0},{8,4},{12,8},{16,12},{20,16},{24,20},{28,24},{32,28},{36,32}... | collective-permute-start | bytes 786440 | tf_op jit(solution)/shard_map/ppermute | solution.py:19
  199.9 1.6 broadcast_multiply_fusion.5
  203.2 1.7 broadcast_multiply_fusion.7
  205.0 3.2 fusion.130
  208.2 3.1 copy.129
  211.3 3.5 collective-permute-start.10
  214.9 3.1 copy.131
  218.0 2.1 collective-permute-start.11
  220.1 2.4 broadcast_multiply_fusion.4
  222.4 3.0 copy.130
  225.5 3.0 copy.132
  228.6 7.0 %maximum_maximum_fusion.2 = (f32[20,130,256]{1,2,0:T(8,128)}, f32[20,130,256]{1,2,0:T(8,128)}) fusion(f32[2,128,256]{1,2,0:T(8,128)S(1)} %collective-permute-done.9, f32[16,128,256]{1,2,0:T(8,128)S(1)} %fusion.112, f32[2,128,256]{1,2,0:T(8,128)S(1)} %collective-permute-done.8, f32[20,2,256]{1,2,0:T(8,128)} %copy.130, f32[20,2,256]{1,2,0:T(8,128)} %copy.132), kind=kLoop, calls=%fused_computation.6 | loop fusion | flops 3993600 | bytes 8028160 | tf_op jit(solution)/shard_map/concatenate | solution.py:20
  235.8 33.4 %fusion.110 = f32[16,128,256]{1,2,0:T(8,128)} fusion(f32[16,128,256]{1,2,0:T(8,128)S(1)} %fusion.112, f32[16,128,4,64]{1,3,2,0:T(8,128)} %broadcast_multiply_fusion.4, f32[16,128,4,64]{1,3,2,0:T(8,128)} %broadcast_multiply_fusion.5, f32[16,128,4,64]{1,3,2,0:T(8,128)} %broadcast_multiply_fusion.6, f32[16,128,4,64]{1,3,2,0:T(8,128)} %broadcast_multiply_fusion.7, ...), kind=kLoop, calls=%fused_computation.252 | loop fusion | flops 30408704 | bytes 55869440 | tf_op jit(solution)/shard_map/add | solution.py:50
  270.2 1.7 fusion.134
  272.0 7.9 %collective-permute-start.13 = (f32[2,128,256]{1,2,0:T(8,128)S(1)}, f32[2,128,256]{1,2,0:T(8,128)S(1)}, u32[]{:S(2)}, u32[]{:S(2)}) collective-permute-start(f32[2,128,256]{1,2,0:T(8,128)S(1)} %get-tuple-element.23), channel_id=1, source_target_pairs={{4,0},{8,4},{12,8},{16,12},{20,16},{24,20},{28,24},{32,28},{36,32}... | collective-permute-start | bytes 786440 | tf_op jit(solution)/shard_map/ppermute | solution.py:19
  280.0 1.6 broadcast_multiply_fusion.1
  281.6 1.6 broadcast_multiply_fusion.2
  283.2 1.7 broadcast_multiply_fusion.3
  285.3 3.2 fusion.129
  288.5 3.1 copy.133
  291.6 3.9 collective-permute-start.14
  295.5 3.1 copy.135
  298.6 2.1 collective-permute-start.15
  300.8 2.4 broadcast_multiply_fusion
  303.1 3.0 copy.134
  306.2 3.0 copy.136
  309.3 7.7 %maximum_maximum_fusion.3 = (f32[20,130,256]{1,2,0:T(8,128)}, f32[20,130,256]{1,2,0:T(8,128)}) fusion(f32[2,128,256]{1,2,0:T(8,128)S(1)} %collective-permute-done.13, f32[16,128,256]{1,2,0:T(8,128)} %fusion.110, f32[2,128,256]{1,2,0:T(8,128)S(1)} %collective-permute-done.12, f32[20,2,256]{1,2,0:T(8,128)} %copy.134, f32[20,2,256]{1,2,0:T(8,128)} %copy.136), kind=kLoop, calls=%fused_computation.8 | loop fusion | flops 3993600 | bytes 8028160 | tf_op jit(solution)/shard_map/concatenate | solution.py:20
  317.1 36.2 %fusion.109 = f32[16,128,256]{1,2,0:T(8,128)} fusion(f32[16,128,4,64]{1,3,2,0:T(8,128)} %broadcast_multiply_fusion, f32[16,128,4,64]{1,3,2,0:T(8,128)} %broadcast_multiply_fusion.1, f32[16,128,4,64]{1,3,2,0:T(8,128)} %broadcast_multiply_fusion.2, f32[16,128,256]{1,2,0:T(8,128)S(1)} %fusion.112, f32[16,128,256]{1,2,0:T(8,128)} %fusion.110, ...), kind=kLoop, calls=%fused_computation.248 | loop fusion | flops 31457280 | bytes 57966592 | tf_op jit(solution)/shard_map/mul | solution.py:51
  353.3 1.9 copy.138
  355.2 4.7 gather_fusion.1
  359.9 5.9 %fusion.114 = f32[512,256]{1,0:T(8,128)} fusion(f32[1024,256]{1,0:T(8,128)} %gather_fusion.1, f32[1024]{0:T(1024)S(1)} %get-tuple-element.79, bf16[1024,512]{1,0:T(8,128)(2,1)S(1)} %copy-done.6, pred[1024]{0:T(1024)(128)(4,1)S(1)} %compare_and_fusion.1, pred[1024]{0:T(1024)(128)(4,1)S(1)} %get-tuple-element.80), kind=kOutput, calls=%fused_computation.264 | convolution fusion | flops 1612447744 | bytes 2627584 | tf_op jit(solution)/shard_map/dot_general | solution.py:57
  365.9 146.8 %all-reduce.2.cloned.1.call-done = f32[512,256]{1,0:T(8,128)} async-done(((f32[512,256]{1,0:T(8,128)}), f32[512,256]{1,0:T(8,128)}) %all-reduce.2.cloned.1.call-update) | async-done | bytes 524304 | tf_op jit(solution)/shard_map/psum | solution.py:58
  (284 shorter events, 17.0 us)
Async XLA Ops:
  7.2 505.5 %all-reduce.2.cloned.1.call-start = ((), (), s32[]{:S(2)}) async-start(), calls=%async_computation | async-start | bytes 1048576 | tf_op jit(solution)/shard_map/psum | solution.py:58
  9.1 68.6 %copy-start = (f32[16,128,256]{1,2,0:T(8,128)}, f32[16,128,256]{1,2,0:T(8,128)S(1)}, u32[]{:S(2)}) copy-start(f32[16,128,256]{1,2,0:T(8,128)S(1)} %copy.124) | copy-start | bytes 6291460
  10.0 32.3 %collective-permute-start = (f32[2,128,256]{1,2,0:T(8,128)}, f32[2,128,256]{1,2,0:T(8,128)S(1)}, u32[]{:S(2)}, u32[]{:S(2)}) collective-permute-start(f32[2,128,256]{1,2,0:T(8,128)} %get-tuple-element.40), channel_id=1, source_target_pairs={{0,4},{4,8},{8,12},{12,16},{16,20},{20,24},{24,28},{28,32},{32,36}... | collective-permute-start | bytes 786440 | tf_op jit(solution)/shard_map/ppermute | solution.py:16
  12.2 11.9 %copy-start.7 = (f32[4,29,16,128]{3,2,1,0:T(8,128)S(1)}, f32[4,29,16,128]{3,2,1,0:T(8,128)}, u32[]{:S(2)}) copy-start(f32[4,29,16,128]{3,2,1,0:T(8,128)} %param.7) | copy-start | bytes 2850820
  12.2 30.2 %collective-permute-start.1 = (f32[2,128,256]{1,2,0:T(8,128)}, f32[2,128,256]{1,2,0:T(8,128)}, u32[]{:S(2)}, u32[]{:S(2)}) collective-permute-start(f32[2,128,256]{1,2,0:T(8,128)} %get-tuple-element.41), channel_id=1, source_target_pairs={{4,0},{8,4},{12,8},{16,12},{20,16},{24,20},{28,24},{32,28},{36,32}... | collective-permute-start | bytes 786440 | tf_op jit(solution)/shard_map/ppermute | solution.py:19
  24.9 9.7 %copy-start.78 = (f32[16,128,4]{1,2,0:T(4,128)}, f32[16,128,4]{1,2,0:T(4,128)S(1)}, u32[]{:S(2)}) copy-start(f32[16,128,4]{1,2,0:T(4,128)S(1)} %copy.115) | copy-start | bytes 98308
  24.9 9.7 %copy-start.82 = (f32[16,128,4]{1,2,0:T(4,128)}, f32[16,128,4]{1,2,0:T(4,128)S(1)}, u32[]{:S(2)}) copy-start(f32[16,128,4]{1,2,0:T(4,128)S(1)} %copy.117) | copy-start | bytes 98308
  29.7 9.0 %copy-start.86 = (f32[16,128,4]{1,2,0:T(4,128)}, f32[16,128,4]{1,2,0:T(4,128)S(1)}, u32[]{:S(2)}) copy-start(f32[16,128,4]{1,2,0:T(4,128)S(1)} %copy.119) | copy-start | bytes 98308
  46.7 10.6 %copy-start.104 = (f32[16,128,4]{1,0,2:T(8,128)S(1)}, f32[16,128,4]{1,0,2:T(8,128)}, u32[]{:S(2)}) copy-start(f32[16,128,4]{1,0,2:T(8,128)} %get-tuple-element.63) | copy-start | bytes 98308
  46.7 10.6 %copy-start.103 = (f32[16,128,4]{1,0,2:T(8,128)S(1)}, f32[16,128,4]{1,0,2:T(8,128)}, u32[]{:S(2)}) copy-start(f32[16,128,4]{1,0,2:T(8,128)} %get-tuple-element.62) | copy-start | bytes 98308
  46.7 10.6 %copy-start.102 = (f32[16,128,4]{1,0,2:T(8,128)S(1)}, f32[16,128,4]{1,0,2:T(8,128)}, u32[]{:S(2)}) copy-start(f32[16,128,4]{1,0,2:T(8,128)} %get-tuple-element.61) | copy-start | bytes 98308
  49.2 8.2 %copy-start.100 = (f32[16,128,4]{1,0,2:T(8,128)S(1)}, f32[16,128,4]{1,0,2:T(8,128)}, u32[]{:S(2)}) copy-start(f32[16,128,4]{1,0,2:T(8,128)} %get-tuple-element.59) | copy-start | bytes 98308
  49.2 8.2 %copy-start.99 = (f32[16,128,4]{1,0,2:T(8,128)S(1)}, f32[16,128,4]{1,0,2:T(8,128)}, u32[]{:S(2)}) copy-start(f32[16,128,4]{1,0,2:T(8,128)} %get-tuple-element.58) | copy-start | bytes 98308
  49.2 8.3 %copy-start.98 = (f32[16,128,4]{1,0,2:T(8,128)S(1)}, f32[16,128,4]{1,0,2:T(8,128)}, u32[]{:S(2)}) copy-start(f32[16,128,4]{1,0,2:T(8,128)} %get-tuple-element.57) | copy-start | bytes 98308
  49.3 8.3 %copy-start.97 = (f32[16,128,4]{1,0,2:T(8,128)S(1)}, f32[16,128,4]{1,0,2:T(8,128)}, u32[]{:S(2)}) copy-start(f32[16,128,4]{1,0,2:T(8,128)} %get-tuple-element.56) | copy-start | bytes 98308
  49.3 8.3 %copy-start.96 = (f32[16,128,4]{1,0,2:T(8,128)S(1)}, f32[16,128,4]{1,0,2:T(8,128)}, u32[]{:S(2)}) copy-start(f32[16,128,4]{1,0,2:T(8,128)} %get-tuple-element.55) | copy-start | bytes 98308
  49.3 8.3 %copy-start.95 = (f32[16,128,4]{1,0,2:T(8,128)S(1)}, f32[16,128,4]{1,0,2:T(8,128)}, u32[]{:S(2)}) copy-start(f32[16,128,4]{1,0,2:T(8,128)} %get-tuple-element.54) | copy-start | bytes 98308
  49.3 8.4 %copy-start.94 = (f32[16,128,4]{1,0,2:T(8,128)S(1)}, f32[16,128,4]{1,0,2:T(8,128)}, u32[]{:S(2)}) copy-start(f32[16,128,4]{1,0,2:T(8,128)} %get-tuple-element.53) | copy-start | bytes 98308
  49.3 8.4 %copy-start.93 = (f32[16,128,4]{1,0,2:T(8,128)S(1)}, f32[16,128,4]{1,0,2:T(8,128)}, u32[]{:S(2)}) copy-start(f32[16,128,4]{1,0,2:T(8,128)} %get-tuple-element.52) | copy-start | bytes 98308
  49.3 8.4 %copy-start.92 = (f32[16,128,4]{1,0,2:T(8,128)S(1)}, f32[16,128,4]{1,0,2:T(8,128)}, u32[]{:S(2)}) copy-start(f32[16,128,4]{1,0,2:T(8,128)} %get-tuple-element.51) | copy-start | bytes 98308
  49.3 8.5 %copy-start.91 = (f32[16,128,4]{1,0,2:T(8,128)S(1)}, f32[16,128,4]{1,0,2:T(8,128)}, u32[]{:S(2)}) copy-start(f32[16,128,4]{1,0,2:T(8,128)} %get-tuple-element.46) | copy-start | bytes 98308
  49.3 8.5 %copy-start.90 = (f32[16,128,4]{1,0,2:T(8,128)S(1)}, f32[16,128,4]{1,0,2:T(8,128)}, u32[]{:S(2)}) copy-start(f32[16,128,4]{1,0,2:T(8,128)} %get-tuple-element.64) | copy-start | bytes 98308
  49.3 16.7 %collective-permute-start.2 = (f32[20,2,256]{2,1,0:T(2,128)S(1)}, f32[20,2,256]{2,1,0:T(2,128)S(1)}, u32[]{:S(2)}, u32[]{:S(2)}) collective-permute-start(f32[20,2,256]{2,1,0:T(2,128)S(1)} %copy.84), channel_id=1, source_target_pairs={{0,1},{1,2},{2,3},{4,5},{5,6},{6,7},{8,9},{9,10},{10,11},{12,13},{... | collective-permute-start | bytes 122888 | tf_op jit(solution)/shard_map/ppermute | solution.py:16
  55.0 13.3 %collective-permute-start.3 = (f32[20,2,256]{2,1,0:T(2,128)S(1)}, f32[20,2,256]{2,1,0:T(2,128)S(1)}, u32[]{:S(2)}, u32[]{:S(2)}) collective-permute-start(f32[20,2,256]{2,1,0:T(2,128)S(1)} %copy.90), channel_id=1, source_target_pairs={{1,0},{2,1},{3,2},{5,4},{6,5},{7,6},{9,8},{10,9},{11,10},{13,12},{... | collective-permute-start | bytes 122888 | tf_op jit(solution)/shard_map/ppermute | solution.py:19
  57.4 20.3 %copy-start.8 = (f32[16,128,4]{1,2,0:T(4,128)}, f32[16,128,4]{1,2,0:T(4,128)S(1)}, u32[]{:S(2)}) copy-start(f32[16,128,4]{1,2,0:T(4,128)S(1)} %copy.105) | copy-start | bytes 98308
  57.5 20.2 %copy-start.10 = (f32[16,128,4]{1,2,0:T(4,128)}, f32[16,128,4]{1,2,0:T(4,128)S(1)}, u32[]{:S(2)}) copy-start(f32[16,128,4]{1,2,0:T(4,128)S(1)} %copy.106) | copy-start | bytes 98308
  57.5 20.2 %copy-start.12 = (f32[16,128,4]{1,2,0:T(4,128)}, f32[16,128,4]{1,2,0:T(4,128)S(1)}, u32[]{:S(2)}) copy-start(f32[16,128,4]{1,2,0:T(4,128)S(1)} %copy.108) | copy-start | bytes 98308
  57.6 20.2 %copy-start.14 = (f32[16,128,4]{1,2,0:T(4,128)}, f32[16,128,4]{1,2,0:T(4,128)S(1)}, u32[]{:S(2)}) copy-start(f32[16,128,4]{1,2,0:T(4,128)S(1)} %copy.109) | copy-start | bytes 98308
  57.6 20.1 %copy-start.16 = (f32[16,128,4]{1,2,0:T(4,128)}, f32[16,128,4]{1,2,0:T(4,128)S(1)}, u32[]{:S(2)}) copy-start(f32[16,128,4]{1,2,0:T(4,128)S(1)} %copy.110) | copy-start | bytes 98308
  57.7 20.1 %copy-start.18 = (f32[16,128,4]{1,2,0:T(4,128)}, f32[16,128,4]{1,2,0:T(4,128)S(1)}, u32[]{:S(2)}) copy-start(f32[16,128,4]{1,2,0:T(4,128)S(1)} %copy.111) | copy-start | bytes 98308
  57.7 20.1 %copy-start.20 = (f32[16,128,4]{1,2,0:T(4,128)}, f32[16,128,4]{1,2,0:T(4,128)S(1)}, u32[]{:S(2)}) copy-start(f32[16,128,4]{1,2,0:T(4,128)S(1)} %copy.112) | copy-start | bytes 98308
  57.7 20.0 %copy-start.22 = (f32[16,128,4]{1,2,0:T(4,128)}, f32[16,128,4]{1,2,0:T(4,128)S(1)}, u32[]{:S(2)}) copy-start(f32[16,128,4]{1,2,0:T(4,128)S(1)} %copy.113) | copy-start | bytes 98308
  57.8 20.0 %copy-start.24 = (f32[16,128,4]{1,2,0:T(4,128)}, f32[16,128,4]{1,2,0:T(4,128)S(1)}, u32[]{:S(2)}) copy-start(f32[16,128,4]{1,2,0:T(4,128)S(1)} %copy.114) | copy-start | bytes 98308
  57.8 20.0 %copy-start.28 = (f32[16,128,4]{1,2,0:T(4,128)}, f32[16,128,4]{1,2,0:T(4,128)S(1)}, u32[]{:S(2)}) copy-start(f32[16,128,4]{1,2,0:T(4,128)S(1)} %copy.80) | copy-start | bytes 98308
  57.9 19.9 %copy-start.32 = (f32[16,128,4]{1,2,0:T(4,128)}, f32[16,128,4]{1,2,0:T(4,128)S(1)}, u32[]{:S(2)}) copy-start(f32[16,128,4]{1,2,0:T(4,128)S(1)} %copy.99) | copy-start | bytes 98308
  57.9 19.9 %copy-start.36 = (f32[16,128,4]{1,2,0:T(4,128)}, f32[16,128,4]{1,2,0:T(4,128)S(1)}, u32[]{:S(2)}) copy-start(f32[16,128,4]{1,2,0:T(4,128)S(1)} %copy.86) | copy-start | bytes 98308
  57.9 19.9 %copy-start.40 = (f32[16,128,4]{1,2,0:T(4,128)}, f32[16,128,4]{1,2,0:T(4,128)S(1)}, u32[]{:S(2)}) copy-start(f32[16,128,4]{1,2,0:T(4,128)S(1)} %copy.87) | copy-start | bytes 98308
  58.0 19.9 %copy-start.44 = (f32[16,128,4]{1,2,0:T(4,128)}, f32[16,128,4]{1,2,0:T(4,128)S(1)}, u32[]{:S(2)}) copy-start(f32[16,128,4]{1,2,0:T(4,128)S(1)} %copy.89) | copy-start | bytes 98308
  58.0 19.8 %copy-start.48 = (f32[16,128,4]{1,2,0:T(4,128)}, f32[16,128,4]{1,2,0:T(4,128)S(1)}, u32[]{:S(2)}) copy-start(f32[16,128,4]{1,2,0:T(4,128)S(1)} %copy.92) | copy-start | bytes 98308
  58.0 19.8 %copy-start.52 = (f32[16,128,4]{1,2,0:T(4,128)}, f32[16,128,4]{1,2,0:T(4,128)S(1)}, u32[]{:S(2)}) copy-start(f32[16,128,4]{1,2,0:T(4,128)S(1)} %copy.93) | copy-start | bytes 98308
  58.1 19.8 %copy-start.56 = (f32[16,128,4]{1,2,0:T(4,128)}, f32[16,128,4]{1,2,0:T(4,128)S(1)}, u32[]{:S(2)}) copy-start(f32[16,128,4]{1,2,0:T(4,128)S(1)} %copy.94) | copy-start | bytes 98308
  58.1 19.8 %copy-start.60 = (f32[16,128,4]{1,2,0:T(4,128)}, f32[16,128,4]{1,2,0:T(4,128)S(1)}, u32[]{:S(2)}) copy-start(f32[16,128,4]{1,2,0:T(4,128)S(1)} %copy.95) | copy-start | bytes 98308
  58.1 19.7 %copy-start.64 = (f32[16,128,4]{1,2,0:T(4,128)}, f32[16,128,4]{1,2,0:T(4,128)S(1)}, u32[]{:S(2)}) copy-start(f32[16,128,4]{1,2,0:T(4,128)S(1)} %copy.96) | copy-start | bytes 98308
  58.2 19.7 %copy-start.68 = (f32[16,128,4]{1,2,0:T(4,128)}, f32[16,128,4]{1,2,0:T(4,128)S(1)}, u32[]{:S(2)}) copy-start(f32[16,128,4]{1,2,0:T(4,128)S(1)} %copy.97) | copy-start | bytes 98308
  58.2 19.7 %copy-start.72 = (f32[16,128,4]{1,2,0:T(4,128)}, f32[16,128,4]{1,2,0:T(4,128)S(1)}, u32[]{:S(2)}) copy-start(f32[16,128,4]{1,2,0:T(4,128)S(1)} %copy.98) | copy-start | bytes 98308
  112.4 9.0 %copy-start.83 = (f32[16,128,4]{1,2,0:T(4,128)S(1)}, f32[16,128,4]{1,2,0:T(4,128)}, u32[]{:S(2)}) copy-start(f32[16,128,4]{1,2,0:T(4,128)} %copy-done.82) | copy-start | bytes 98308
  114.1 8.9 %copy-start.79 = (f32[16,128,4]{1,2,0:T(4,128)S(1)}, f32[16,128,4]{1,2,0:T(4,128)}, u32[]{:S(2)}) copy-start(f32[16,128,4]{1,2,0:T(4,128)} %copy-done.78) | copy-start | bytes 98308
  114.1 13.0 %collective-permute-start.4 = (f32[2,128,256]{1,2,0:T(8,128)S(1)}, f32[2,128,256]{1,2,0:T(8,128)S(1)}, u32[]{:S(2)}, u32[]{:S(2)}) collective-permute-start(f32[2,128,256]{1,2,0:T(8,128)S(1)} %get-tuple-element.34), channel_id=1, source_target_pairs={{0,4},{4,8},{8,12},{12,16},{16,20},{20,24},{24,28},{28,32},{32,36}... | collective-permute-start | bytes 786440 | tf_op jit(solution)/shard_map/ppermute | solution.py:16
  114.2 12.9 %collective-permute-start.5 = (f32[2,128,256]{1,2,0:T(8,128)S(1)}, f32[2,128,256]{1,2,0:T(8,128)S(1)}, u32[]{:S(2)}, u32[]{:S(2)}) collective-permute-start(f32[2,128,256]{1,2,0:T(8,128)S(1)} %get-tuple-element.35), channel_id=1, source_target_pairs={{4,0},{8,4},{12,8},{16,12},{20,16},{24,20},{28,24},{32,28},{36,32}... | collective-permute-start | bytes 786440 | tf_op jit(solution)/shard_map/ppermute | solution.py:19
  130.5 10.9 %copy-start.77 = (f32[16,128,4]{1,2,0:T(4,128)S(1)}, f32[16,128,4]{1,2,0:T(4,128)}, u32[]{:S(2)}) copy-start(f32[16,128,4]{1,2,0:T(4,128)} %copy-done.76) | copy-start | bytes 98308
  133.0 10.0 %collective-permute-start.6 = (f32[20,2,256]{2,1,0:T(2,128)S(1)}, f32[20,2,256]{2,1,0:T(2,128)S(1)}, u32[]{:S(2)}, u32[]{:S(2)}) collective-permute-start(f32[20,2,256]{2,1,0:T(2,128)S(1)} %copy.125), channel_id=1, source_target_pairs={{0,1},{1,2},{2,3},{4,5},{5,6},{6,7},{8,9},{9,10},{10,11},{12,13},{... | collective-permute-start | bytes 122888 | tf_op jit(solution)/shard_map/ppermute | solution.py:16
  139.0 6.3 %collective-permute-start.7 = (f32[20,2,256]{2,1,0:T(2,128)S(1)}, f32[20,2,256]{2,1,0:T(2,128)S(1)}, u32[]{:S(2)}, u32[]{:S(2)}) collective-permute-start(f32[20,2,256]{2,1,0:T(2,128)S(1)} %copy.127), channel_id=1, source_target_pairs={{1,0},{2,1},{3,2},{5,4},{6,5},{7,6},{9,8},{10,9},{11,10},{13,12},{... | collective-permute-start | bytes 122888 | tf_op jit(solution)/shard_map/ppermute | solution.py:19
  191.7 8.2 %copy-start.88 = (f32[16,128,4]{1,2,0:T(4,128)S(1)}, f32[16,128,4]{1,2,0:T(4,128)}, u32[]{:S(2)}) copy-start(f32[16,128,4]{1,2,0:T(4,128)} %copy-done.86) | copy-start | bytes 98308
  192.0 9.6 %copy-start.84 = (f32[16,128,4]{1,2,0:T(4,128)S(1)}, f32[16,128,4]{1,2,0:T(4,128)}, u32[]{:S(2)}) copy-start(f32[16,128,4]{1,2,0:T(4,128)} %copy-done.82) | copy-start | bytes 98308
  192.0 12.9 %collective-permute-start.8 = (f32[2,128,256]{1,2,0:T(8,128)S(1)}, f32[2,128,256]{1,2,0:T(8,128)S(1)}, u32[]{:S(2)}, u32[]{:S(2)}) collective-permute-start(f32[2,128,256]{1,2,0:T(8,128)S(1)} %get-tuple-element.28), channel_id=1, source_target_pairs={{0,4},{4,8},{8,12},{12,16},{16,20},{20,24},{24,28},{28,32},{32,36}... | collective-permute-start | bytes 786440 | tf_op jit(solution)/shard_map/ppermute | solution.py:16
  192.1 12.8 %collective-permute-start.9 = (f32[2,128,256]{1,2,0:T(8,128)S(1)}, f32[2,128,256]{1,2,0:T(8,128)S(1)}, u32[]{:S(2)}, u32[]{:S(2)}) collective-permute-start(f32[2,128,256]{1,2,0:T(8,128)S(1)} %get-tuple-element.29), channel_id=1, source_target_pairs={{4,0},{8,4},{12,8},{16,12},{20,16},{24,20},{28,24},{32,28},{36,32}... | collective-permute-start | bytes 786440 | tf_op jit(solution)/shard_map/ppermute | solution.py:19
  211.3 11.1 %collective-permute-start.10 = (f32[20,2,256]{2,1,0:T(2,128)}, f32[20,2,256]{2,1,0:T(2,128)}, u32[]{:S(2)}, u32[]{:S(2)}) collective-permute-start(f32[20,2,256]{2,1,0:T(2,128)} %copy.129), channel_id=1, source_target_pairs={{0,1},{1,2},{2,3},{4,5},{5,6},{6,7},{8,9},{9,10},{10,11},{12,13},{... | collective-permute-start | bytes 122888 | tf_op jit(solution)/shard_map/ppermute | solution.py:16
  218.0 7.5 %collective-permute-start.11 = (f32[20,2,256]{2,1,0:T(2,128)}, f32[20,2,256]{2,1,0:T(2,128)}, u32[]{:S(2)}, u32[]{:S(2)}) collective-permute-start(f32[20,2,256]{2,1,0:T(2,128)} %copy.131), channel_id=1, source_target_pairs={{1,0},{2,1},{3,2},{5,4},{6,5},{7,6},{9,8},{10,9},{11,10},{13,12},{... | collective-permute-start | bytes 122888 | tf_op jit(solution)/shard_map/ppermute | solution.py:19
  270.2 9.7 %copy-start.89 = (f32[16,128,4]{1,2,0:T(4,128)S(1)}, f32[16,128,4]{1,2,0:T(4,128)}, u32[]{:S(2)}) copy-start(f32[16,128,4]{1,2,0:T(4,128)} %copy-done.86) | copy-start | bytes 98308
  271.9 9.7 %copy-start.85 = (f32[16,128,4]{1,2,0:T(4,128)S(1)}, f32[16,128,4]{1,2,0:T(4,128)}, u32[]{:S(2)}) copy-start(f32[16,128,4]{1,2,0:T(4,128)} %copy-done.82) | copy-start | bytes 98308
  271.9 13.1 %collective-permute-start.12 = (f32[2,128,256]{1,2,0:T(8,128)S(1)}, f32[2,128,256]{1,2,0:T(8,128)S(1)}, u32[]{:S(2)}, u32[]{:S(2)}) collective-permute-start(f32[2,128,256]{1,2,0:T(8,128)S(1)} %get-tuple-element.22), channel_id=1, source_target_pairs={{0,4},{4,8},{8,12},{12,16},{16,20},{20,24},{24,28},{28,32},{32,36}... | collective-permute-start | bytes 786440 | tf_op jit(solution)/shard_map/ppermute | solution.py:16
  272.0 13.1 %collective-permute-start.13 = (f32[2,128,256]{1,2,0:T(8,128)S(1)}, f32[2,128,256]{1,2,0:T(8,128)S(1)}, u32[]{:S(2)}, u32[]{:S(2)}) collective-permute-start(f32[2,128,256]{1,2,0:T(8,128)S(1)} %get-tuple-element.23), channel_id=1, source_target_pairs={{4,0},{8,4},{12,8},{16,12},{20,16},{24,20},{28,24},{32,28},{36,32}... | collective-permute-start | bytes 786440 | tf_op jit(solution)/shard_map/ppermute | solution.py:19
  291.6 11.6 %collective-permute-start.14 = (f32[20,2,256]{2,1,0:T(2,128)}, f32[20,2,256]{2,1,0:T(2,128)}, u32[]{:S(2)}, u32[]{:S(2)}) collective-permute-start(f32[20,2,256]{2,1,0:T(2,128)} %copy.133), channel_id=1, source_target_pairs={{0,1},{1,2},{2,3},{4,5},{5,6},{6,7},{8,9},{9,10},{10,11},{12,13},{... | collective-permute-start | bytes 122888 | tf_op jit(solution)/shard_map/ppermute | solution.py:16
  298.6 7.5 %collective-permute-start.15 = (f32[20,2,256]{2,1,0:T(2,128)}, f32[20,2,256]{2,1,0:T(2,128)}, u32[]{:S(2)}, u32[]{:S(2)}) collective-permute-start(f32[20,2,256]{2,1,0:T(2,128)} %copy.135), channel_id=1, source_target_pairs={{1,0},{2,1},{3,2},{5,4},{6,5},{7,6},{9,8},{10,9},{11,10},{13,12},{... | collective-permute-start | bytes 122888 | tf_op jit(solution)/shard_map/ppermute | solution.py:19
  (60 other events, 407.3 us)
Sparse Core Ops, SparseCore 0:
  366.0 146.6 all-reduce.1
where the time goes:
time: 527 us; the launch traced here: 521 us
  other arithmetic  198 us (38%)
  waiting for transfers between devices  148 us (28%)
  local copies, waits for them, and re-layouts  96.9 us (18%)
  starting transfers between devices  55.7 us (11%)
  between operations  16.7 us (3%)
  matrix products  5.94 us (1%)
    psum x1, waiting for transfers between devices, body(): totals = lax.psum(term, ('azim', 'rad'))  147 us
    mul x2, other arithmetic, body(): state = 0.5 * (state + first + flux(rimmed(first), coefficients, first))  72.8 us
    add x2, other arithmetic, body(): first = state + flux(rimmed(state), coefficients, state)  66.8 us
    ppermute x8, starting transfers between devices, with_halo(): lax.ppermute(lax.slice_in_dim(block, 0, width, axis=dim), axis, backward)  39.2 us
    concatenate x8, other arithmetic, with_halo(): block = jnp.concatenate([low, block, high], axis=dim)  30.5 us
    mul x14, other arithmetic, flux(): total = total + weight * block  27.8 us
    slice x12, local copies, waits for them, and re-layouts, with_halo(): lax.slice_in_dim(block, block.shape[dim] - width, None, axis=dim)  27.1 us
    ppermute x8, starting transfers between devices, with_halo(): lax.ppermute(lax.slice_in_dim(block, block.shape[dim] - width, None, axis...  16.4 us
  transfers between devices with their start and end apart: 17, of which 3 were waited for; matrix products, arithmetic and copies ran while one was open for 14% of the time, Pallas kernels for 0%

commit v1 on v0

v1 whole, which is shorter than its diff:
```python
import jax
import jax.numpy as jnp
from jax import lax
from jax.experimental import pallas as pl
from jax.experimental.pallas import tpu as pltpu
from jax.sharding import PartitionSpec as P

STEPS = 2
VMEM_LIMIT = 32 * 1024 * 1024
F32 = jnp.float32
BF16 = jnp.bfloat16


def spec(block, index):
    return pl.BlockSpec(block, index)


def params(n):
    return pltpu.CompilerParams(
        vmem_limit_bytes=VMEM_LIMIT, dimension_semantics=("arbitrary",) * n
    )


def lanes(shape):
    return lax.broadcasted_iota(jnp.int32, shape, len(shape) - 1)


def pack_into(edge_ref, row, var, value):
    base = (row % 8) * 16 + var * 4
    lane = lanes(value.shape)
    here = (lane >= base) & (lane < base + 4)
    old = edge_ref[row // 8]
    edge_ref[row // 8] = jnp.where(here, pltpu.roll(value, base + 2, axis=1), old)


def enter(x_ref, u_ref, edge_ref):
    step = pl.program_id(0)

    @pl.when(step % 2 == 0)
    def _():
        edge_ref[...] = jnp.zeros_like(edge_ref)

    lane = lanes((64, 128))
    for k in range(4):
        turned = x_ref[k].T
        for v in range(4):
            piece = turned[64 * v : 64 * v + 64]
            u_ref[k, v] = piece
            base = ((step % 2) * 4 + k) * 16 + v * 4
            here = (lane >= base) & (lane < base + 4)
            edge_ref[0] = jnp.where(here, pltpu.roll(piece, base + 2, axis=1), edge_ref[0])


def call_enter(x):
    return pl.pallas_call(
        enter,
        grid=(4,),
        in_specs=[spec((4, 128, 256), lambda s: (s, 0, 0))],
        out_specs=[
            spec((4, 4, 64, 128), lambda s: (s, 0, 0, 0)),
            spec((1, 64, 128), lambda s: (s // 2, 0, 0)),
        ],
        out_shape=[
            jax.ShapeDtypeStruct((16, 4, 64, 128), F32),
            jax.ShapeDtypeStruct((2, 64, 128), F32),
        ],
        compiler_params=params(1),
        name="enter",
    )(x)


def stencil(count, source, rim, weight, finish):
    lane = lanes((32, 128))
    open_rows = {}
    for s in range(count + 4):
        u = source(s)
        edge = rim(s)
        shifted = [
            pltpu.roll(jnp.where(lane >= 126, edge, u), 2, axis=1),
            pltpu.roll(jnp.where(lane >= 127, edge, u), 1, axis=1),
            u,
            pltpu.roll(jnp.where(lane < 1, edge, u), 127, axis=1),
            pltpu.roll(jnp.where(lane < 2, edge, u), 126, axis=1),
        ]
        for i in range(5):
            row = s - i
            if 0 <= row < count:
                total = open_rows.get(row)
                for j in range(5):
                    term = weight(5 * i + j, row) * shifted[j]
                    total = term if total is None else total + term
                open_rows[row] = total
        if s >= 4:
            finish(s - 4, open_rows.pop(s - 4))


def first_stage(u_ref, top_ref, bot_ref, cl_ref, cr_ref, tl_ref, tr_ref, bl_ref, br_ref,
                coef_ref, ctop_ref, cbot_ref, y_ref, edge_ref):
    var = pl.program_id(1)

    @pl.when(var == 0)
    def _():
        edge_ref[...] = jnp.zeros_like(edge_ref)

    def at(s, v):
        if s < 4:
            return top_ref[s, v]
        if s < 20:
            return u_ref[s - 4, v]
        return bot_ref[s - 20, v]

    from_left = lanes((32, 128)) % 4 < 2

    def rim(s):
        row = (s - 4) % 16
        if s < 4:
            both = jnp.where(from_left, tl_ref[...], tr_ref[...])
        elif s < 20:
            both = jnp.where(from_left, cl_ref[row // 8], cr_ref[row // 8])
        else:
            both = jnp.where(from_left, bl_ref[...], br_ref[...])
        return pltpu.roll(both, lax.rem(254 - (row % 8) * 16 - var * 4, 128), axis=1)

    def weight(k, row):
        if row < 2:
            line = ctop_ref[0, k, row : row + 1]
        elif row < 18:
            line = coef_ref[0, k, row - 2 : row - 1]
        else:
            line = cbot_ref[0, k, row - 18 : row - 17]
        return jnp.broadcast_to(line, (32, 128))

    def finish(row, total):
        for w in range(4):
            total = total + weight(25 + w, row) * at(row + 2, w)
        value = at(row + 2, var) + 0.5 * total
        y_ref[row, 0] = value
        pack_into(edge_ref, row, var, value)

    stencil(20, lambda s: at(s, var), rim, weight, finish)


def second_stage(y_ref, left_ref, right_ref, base_ref, coef_ref, u_ref, edge_ref):
    var = pl.program_id(1)

    @pl.when(var == 0)
    def _():
        edge_ref[...] = jnp.zeros_like(edge_ref)

    from_left = lanes((32, 128)) % 4 < 2

    def rim(s):
        both = jnp.where(from_left, left_ref[s // 8], right_ref[s // 8])
        return pltpu.roll(both, lax.rem(254 - (s % 8) * 16 - var * 4, 128), axis=1)

    def weight(k, row):
        return jnp.broadcast_to(coef_ref[0, k, row : row + 1], (32, 128))

    def finish(row, total):
        for w in range(4):
            total = total + weight(25 + w, row) * y_ref[row + 2, w]
        value = base_ref[row, 0] + total
        u_ref[row, 0] = value
        pack_into(edge_ref, row, var, value)

    stencil(16, lambda s: y_ref[s, var], rim, weight, finish)


def column_half(*lead):
    return spec(lead + (32, 128), lambda h, v: (0,) * len(lead) + (h, 0))


def one_variable(rows):
    return spec((rows, 1, 32, 128), lambda h, v: (0, v, h, 0))


def weights_of(rows):
    return spec((1, 29, rows, 128), lambda h, v: (v, 0, 0, 0))


def stage_cost(rows):
    return pl.CostEstimate(flops=2 * 29 * rows * 128 * 256, bytes_accessed=8 << 20, transcendentals=0)


def call_first(u, top, bot, edges, coef, ctop, cbot):
    return pl.pallas_call(
        first_stage,
        grid=(2, 4),
        in_specs=[column_half(16, 4), column_half(4, 4), column_half(4, 4),
                  column_half(2), column_half(2)] + [column_half()] * 4
        + [weights_of(16), weights_of(2), weights_of(2)],
        out_specs=[one_variable(20), column_half(3)],
        out_shape=[
            jax.ShapeDtypeStruct((20, 4, 64, 128), F32),
            jax.ShapeDtypeStruct((3, 64, 128), F32),
        ],
        compiler_params=params(2),
        cost_estimate=stage_cost(20),
        name="first_stage",
    )(u, top, bot, *edges, coef, ctop, cbot)


def call_second(y, left, right, base, coef):
    return pl.pallas_call(
        second_stage,
        grid=(2, 4),
        in_specs=[column_half(20, 4), column_half(3), column_half(3), one_variable(16), weights_of(16)],
        out_specs=[one_variable(16), column_half(2)],
        out_shape=[
            jax.ShapeDtypeStruct((16, 4, 64, 128), F32),
            jax.ShapeDtypeStruct((2, 64, 128), F32),
        ],
        compiler_params=params(2),
        cost_estimate=stage_cost(16),
        name="second_stage",
    )(y, left, right, base, coef)


def spread(cells_ref, weights_ref, high_ref, low_ref):
    step = pl.program_id(0)
    cell = lax.broadcasted_iota(jnp.int32, (256, 1024), 0) + step * 256
    hit = jnp.where(cells_ref[...] == cell, 1.0, 0.0).astype(BF16)
    total = jnp.dot(hit, weights_ref[...], preferred_element_type=F32)
    high = total.astype(BF16)
    high_ref[...] = high
    low_ref[...] = (total - high.astype(F32)).astype(BF16)


def call_spread(cells, weights):
    return pl.pallas_call(
        spread,
        grid=(8,),
        in_specs=[spec((1, 1024), lambda s: (0, 0)), spec((1024, 512), lambda s: (0, 0))],
        out_specs=[spec((256, 512), lambda s: (s, 0))] * 2,
        out_shape=[jax.ShapeDtypeStruct((2048, 512), BF16)] * 2,
        compiler_params=params(1),
        cost_estimate=pl.CostEstimate(flops=2 << 30, bytes_accessed=6 << 20, transcendentals=0),
        name="spread",
    )(cells, weights)


def leave(u_ref, high_ref, low_ref, out_ref, markov_ref, total):
    step = pl.program_id(0)
    grid = pl.num_programs(0)

    @pl.when(step == 0)
    def _():
        total[...] = jnp.zeros_like(total)

    rows = [u_ref[k].reshape(256, 128) for k in range(4)]
    for k in range(4):
        out_ref[k] = rows[k].T
    sums = total[...]
    for k in range(2):
        u = jnp.concatenate([rows[2 * k], rows[2 * k + 1]], axis=1)
        u_high = u.astype(BF16)
        u_low = (u - u_high.astype(F32)).astype(BF16)
        w_high = high_ref[256 * k : 256 * k + 256]
        w_low = low_ref[256 * k : 256 * k + 256]
        sums = sums + jnp.dot(u_high, w_high, preferred_element_type=F32)
        sums = sums + jnp.dot(u_low, w_high, preferred_element_type=F32)
        sums = sums + jnp.dot(u_high, w_low, preferred_element_type=F32)
    total[...] = sums

    @pl.when(step == grid - 1)
    def _():
        markov_ref[...] = total[...].T


def call_leave(u, high, low):
    return pl.pallas_call(
        leave,
        grid=(4,),
        in_specs=[spec((4, 4, 64, 128), lambda s: (s, 0, 0, 0))]
        + [spec((512, 512), lambda s: (s, 0))] * 2,
        out_specs=[spec((4, 128, 256), lambda s: (s, 0, 0)), spec((512, 256), lambda s: (0, 0))],
        out_shape=[
            jax.ShapeDtypeStruct((16, 128, 256), F32),
            jax.ShapeDtypeStruct((512, 256), F32),
        ],
        scratch_shapes=[pltpu.VMEM((256, 512), F32)],
        compiler_params=params(1),
        cost_estimate=pl.CostEstimate(flops=2 << 30, bytes_accessed=8 << 20, transcendentals=0),
        name="leave",
    )(u, high, low)


def shifts(n_azim, n_rad, da, dr):
    pairs = []
    for a in range(n_azim):
        for r in range(n_rad):
            if 0 <= r + dr < n_rad:
                pairs.append((a * n_rad + r, ((a + da) % n_azim) * n_rad + r + dr))
    return pairs


def body(perturbation_in, coefficients, wall_cells, wall_count, mode_row, mode_table):
    n_azim, n_rad = lax.axis_size("azim"), lax.axis_size("rad")

    def send(block, da, dr):
        return lax.ppermute(block, ("azim", "rad"), shifts(n_azim, n_rad, da, dr))

    slots = wall_cells.shape[0]
    live = jnp.arange(slots, dtype=jnp.int32) < wall_count[0]
    weights = jnp.where(live[:, None], jnp.take(mode_table, mode_row, axis=0), jnp.zeros((), BF16))
    high, low = call_spread(wall_cells.reshape(1, slots), weights)

    ctop = send(coefficients[:, :, 14:], 1, 0)
    cbot = send(coefficients[:, :, :2], -1, 0)
    u, edge = call_enter(perturbation_in)
    for step in range(STEPS):
        top = send(u[12:], 1, 0)
        bot = send(u[:4], -1, 0)
        edges = [
            send(edge, 0, 1), send(edge, 0, -1),
            send(edge[1], 1, 1), send(edge[1], 1, -1),
            send(edge[0], -1, 1), send(edge[0], -1, -1),
        ]
        y, rims = call_first(u, top, bot, edges, coefficients, ctop, cbot)
        u, edge = call_second(y, send(rims, 0, 1), send(rims, 0, -1), u, coefficients)
    out, term = call_leave(u, high, low)
    count = n_azim * n_rad
    parts = lax.all_to_all(term.reshape(count, -1, term.shape[1]), ("azim", "rad"), 0, 0)
    return out, jnp.sum(parts, axis=0)


def solution(mesh):
    return jax.shard_map(
        body,
        mesh=mesh,
        in_specs=(
            P("azim", "rad", None),
            P(None, None, "azim", "rad"),
            P(("azim", "rad")),
            P(("azim", "rad")),
            P(("azim", "rad")),
            P(),
        ),
        out_specs=(P("azim", "rad", None), P(("azim", "rad"), None)),
        check_vma=False,
    )
```

time: 527 us -> 210 us (0.40)
  other arithmetic: 198 us -> 2.61 us
  waiting for transfers between devices: 148 us -> 12.4 us
  Pallas kernels: 0 us -> 86.2 us
  local copies, waits for them, and re-layouts: 96.9 us -> 10.9 us
  blocking collectives: 0 us -> 22.2 us
  starting transfers between devices: 55.7 us -> 73.1 us
  between operations: 16.7 us -> 1.65 us
  matrix products: 5.94 us -> 0 us
    psum x1 -> x0, waiting for transfers between devices: 147 us -> none  [body(): totals = lax.psum(term, ('azim', 'rad'))]
    mul x16 -> x0, other arithmetic: 101 us -> none  [the longest x2 72.8 us: body(): state = 0.5 * (state + first + flux(rimmed(first), coefficients, first))]
    pallas_call x0 -> x7, Pallas kernels: none -> 86.2 us  [the longest x2 44.2 us: call_first(): pl.pallas_call(first_stage, grid=(2, 4), in_specs=[column_half(16, 4), co...]
    add x2 -> x0, other arithmetic: 66.8 us -> none  [body(): first = state + flux(rimmed(state), coefficients, state)]
    slice x24 -> x3, local copies, waits for them, and re-layouts: 54.6 us -> 1.24 us  [the longest x2 1.15 us: body(): bot = send(u[:4], -1, 0)]
    concatenate x8 -> x0, other arithmetic: 30.5 us -> none  [with_halo(): block = jnp.concatenate([low, block, high], axis=dim)]
    all_to_all x0 -> x1, blocking collectives: none -> 22.2 us  [body(): lax.all_to_all(term.reshape(count, -1, term.shape[1]), ('azim', 'rad'), 0...]
    ppermute x8 -> x0, local copies, waits for them, and re-layouts: 21.2 us -> none  [the longest x4 10.6 us: with_halo(): lax.ppermute(lax.slice_in_dim(block, block.shape[dim] - width, None, axis...]
  transfers between devices with their start and end apart: 17 -> 22, of which waited for: 3 -> 4; matrix products, arithmetic and copies ran while one was open for 14% -> 5% of each run, Pallas kernels for 0% -> 2%
where the time goes in v1:
time: 210 us; the launch traced here: 209 us
  Pallas kernels  86.2 us (41%)
  starting transfers between devices  73.1 us (35%)
  blocking collectives  22.2 us (11%)
  waiting for transfers between devices  12.4 us (6%)
  local copies, waits for them, and re-layouts  10.9 us (5%)
  other arithmetic  2.61 us (1%)
    ppermute x22, starting transfers between devices, send(): return lax.ppermute(block, ('azim', 'rad'), shifts(n_azim, n_rad, da, dr))  73.1 us
    pallas_call x2, Pallas kernels, call_first(): pl.pallas_call(first_stage, grid=(2, 4), in_specs=[column_half(16, 4), co...  44.2 us
    pallas_call x2, Pallas kernels, call_second(): pl.pallas_call(second_stage, grid=(2, 4), in_specs=[column_half(20, 4), c...  33.4 us
    all_to_all x1, blocking collectives, body(): lax.all_to_all(term.reshape(count, -1, term.shape[1]), ('azim', 'rad'), 0...  22.2 us
    ppermute x22, waiting for transfers between devices, send(): return lax.ppermute(block, ('azim', 'rad'), shifts(n_azim, n_rad, da, dr))  12.4 us
    gather x1, local copies, waits for them, and re-layouts, body(): jnp.take(mode_table, mode_row, axis=0)  7.85 us
  transfers between devices with their start and end apart: 22, of which 4 were waited for; matrix products, arithmetic and copies ran while one was open for 5% of the time, Pallas kernels for 2%

profile of v1, /device:TPU:1, one launch (start us, length us, event | category | flops | bytes accessed | tf_op | source)
XLA Modules:
  0.0 209.2 jit_solution(13006209697319509620)
XLA Ops:
  0.6 0.0 copy-start
  0.6 0.0 copy-start.1
  0.6 1.7 copy-done.1
  2.3 1.5 enter.1
  3.8 0.1 fusion.2
  3.9 9.6 %collective-permute-start.1 = (f32[4,4,64,128]{3,2,1,0:T(8,128)S(1)}, f32[4,4,64,128]{3,2,1,0:T(8,128)S(1)}, u32[]{:S(2)}, u32[]{:S(2)}) collective-permute-start(f32[4,4,64,128]{3,2,1,0:T(8,128)S(1)} %get-tuple-element.30), channel_id=1, source_target_pairs={{0,124},{1,125},{2,126},{3,127},{4,0},{5,1},{6,2},{7,3},{8,4},{9,5... | collective-permute-start | bytes 1572872 | tf_op jit(solution)/shard_map/ppermute | solution.py:301
  13.5 0.0 collective-permute-start
  13.5 10.2 %collective-permute-start.7 = (f32[64,128]{1,0:T(8,128)S(1)}, f32[64,128]{1,0:T(8,128)S(1)}, u32[]{:S(2)}, u32[]{:S(2)}) collective-permute-start(f32[64,128]{1,0:T(8,128)S(1)} %get-tuple-element.36), channel_id=1, source_target_pairs={{1,124},{2,125},{3,126},{5,0},{6,1},{7,2},{9,4},{10,5},{11,6},{13,... | collective-permute-start | bytes 98312 | tf_op jit(solution)/shard_map/ppermute | solution.py:301
  23.7 1.9 collective-permute-start.6
  25.6 3.6 %collective-permute-start.5 = (f32[64,128]{1,0:T(8,128)S(1)}, f32[64,128]{1,0:T(8,128)S(1)}, u32[]{:S(2)}, u32[]{:S(2)}) collective-permute-start(f32[64,128]{1,0:T(8,128)S(1)} %get-tuple-element.37), channel_id=1, source_target_pairs={{1,4},{2,5},{3,6},{5,8},{6,9},{7,10},{9,12},{10,13},{11,14},{13,16... | collective-permute-start | bytes 98312 | tf_op jit(solution)/shard_map/ppermute | solution.py:301
  29.3 0.0 collective-permute-done.7.br_ref
  29.3 1.9 collective-permute-start.4
  31.2 0.0 collective-permute-done.6.bl_ref
  31.2 1.9 collective-permute-start.3
  33.2 0.0 copy-done
  33.2 0.1 fusion.3
  33.3 3.0 %collective-permute-done.5.tr_ref = f32[64,128]{1,0:T(8,128)S(1)} collective-permute-done((f32[64,128]{1,0:T(8,128)S(1)}, f32[64,128]{1,0:T(8,128)S(1)}, u32[]{:S(2)}, u32[]{:S(2)}) %collective-permute-start.5) | collective-permute-done | bytes 32800 | tf_op jit(solution)/shard_map/ppermute | solution.py:301
  36.3 4.6 %collective-permute-start.9 = (f32[4,29,2,128]{3,2,1,0:T(2,128)S(1)}, f32[4,29,2,128]{3,2,1,0:T(2,128)S(1)}, u32[]{:S(2)}, u32[]{:S(2)}) collective-permute-start(f32[4,29,2,128]{3,2,1,0:T(2,128)S(1)} %get-tuple-element.32), channel_id=1, source_target_pairs={{0,124},{1,125},{2,126},{3,127},{4,0},{5,1},{6,2},{7,3},{8,4},{9,5... | collective-permute-start | bytes 356360 | tf_op jit(solution)/shard_map/ppermute | solution.py:301
  40.9 0.0 collective-permute-done.4.tl_ref
  40.9 0.0 collective-permute-start.8
  40.9 0.0 collective-permute-done.3.cr_ref
  40.9 2.4 %collective-permute-start.2 = (f32[2,64,128]{2,1,0:T(8,128)S(1)}, f32[2,64,128]{2,1,0:T(8,128)S(1)}, u32[]{:S(2)}, u32[]{:S(2)}) collective-permute-start(f32[2,64,128]{2,1,0:T(8,128)S(1)} %get-tuple-element.16), channel_id=1, source_target_pairs={{0,1},{1,2},{2,3},{4,5},{5,6},{6,7},{8,9},{9,10},{10,11},{12,13},{... | collective-permute-start | bytes 196616 | tf_op jit(solution)/shard_map/ppermute | solution.py:301
  43.3 1.3 collective-permute-done.2.cl_ref
  44.6 0.0 collective-permute-done.9.cbot_ref
  44.6 7.1 %collective-permute-done.8.ctop_ref = f32[4,29,2,128]{3,2,1,0:T(2,128)S(1)} collective-permute-done((f32[4,29,2,128]{3,2,1,0:T(2,128)S(1)}, f32[4,29,2,128]{3,2,1,0:T(2,128)S(1)}, u32[]{:S(2)}, u32[]{:S(2)}) %collective-permute-start.8) | collective-permute-done | bytes 118816 | tf_op jit(solution)/shard_map/ppermute | solution.py:301
  51.7 0.0 collective-permute-done.1.bot_ref
  51.7 0.0 collective-permute-done.top_ref
  51.8 21.6 %first_stage.2 = (f32[20,4,64,128]{3,2,1,0:T(8,128)S(1)}, f32[3,64,128]{2,1,0:T(8,128)S(1)}) custom-call(f32[16,4,64,128]{3,2,1,0:T(8,128)S(1)} %get-tuple-element.15.u_ref.base_ref, f32[4,4,64,128]{3,2,1,0:T(8,128)S(1)} %collective-permute-done.top_ref, f32[4,4,64,128]{3,2,1,0:T(8,128)S(1)} %collective-permute-done.1.bot_ref, ...), custom_call_target="tpu_custom_call" | custom-call | flops 38010880 | bytes 8388608 | tf_op jit(solution)/shard_map/first_stage/pallas_call | solution.py:186
  73.4 2.4 %collective-permute-start.11 = (f32[3,64,128]{2,1,0:T(8,128)S(1)}, f32[3,64,128]{2,1,0:T(8,128)S(1)}, u32[]{:S(2)}, u32[]{:S(2)}) collective-permute-start(f32[3,64,128]{2,1,0:T(8,128)S(1)} %get-tuple-element.18), channel_id=1, source_target_pairs={{1,0},{2,1},{3,2},{5,4},{6,5},{7,6},{9,8},{10,9},{11,10},{13,12},{... | collective-permute-start | bytes 294920 | tf_op jit(solution)/shard_map/ppermute | solution.py:301
  75.8 3.1 %collective-permute-start.10 = (f32[3,64,128]{2,1,0:T(8,128)S(1)}, f32[3,64,128]{2,1,0:T(8,128)S(1)}, u32[]{:S(2)}, u32[]{:S(2)}) collective-permute-start(f32[3,64,128]{2,1,0:T(8,128)S(1)} %get-tuple-element.18), channel_id=1, source_target_pairs={{0,1},{1,2},{2,3},{4,5},{5,6},{6,7},{8,9},{9,10},{10,11},{12,13},{... | collective-permute-start | bytes 294920 | tf_op jit(solution)/shard_map/ppermute | solution.py:301
  79.6 0.0 collective-permute-done.11.right_ref
  79.6 0.9 collective-permute-done.10.left_ref
  80.6 16.3 %second_stage.2 = (f32[16,4,64,128]{3,2,1,0:T(8,128)S(1)}, f32[2,64,128]{2,1,0:T(8,128)S(1)}) custom-call(f32[20,4,64,128]{3,2,1,0:T(8,128)S(1)} %get-tuple-element.17.y_ref, f32[3,64,128]{2,1,0:T(8,128)S(1)} %collective-permute-done.10.left_ref, f32[3,64,128]{2,1,0:T(8,128)S(1)} %collective-permute-done.11.right_ref, ...), custom_call_target="tpu_custom_call" | custom-call | flops 30408704 | bytes 8388608 | tf_op jit(solution)/shard_map/second_stage/pallas_call | solution.py:204
  96.9 1.1 fusion.1
  98.0 1.6 collective-permute-start.13
  99.6 0.0 collective-permute-start.12
  99.6 7.0 %collective-permute-start.19 = (f32[64,128]{1,0:T(8,128)S(1)}, f32[64,128]{1,0:T(8,128)S(1)}, u32[]{:S(2)}, u32[]{:S(2)}) collective-permute-start(f32[64,128]{1,0:T(8,128)S(1)} %get-tuple-element.34), channel_id=1, source_target_pairs={{1,124},{2,125},{3,126},{5,0},{6,1},{7,2},{9,4},{10,5},{11,6},{13,... | collective-permute-start | bytes 98312 | tf_op jit(solution)/shard_map/ppermute | solution.py:301
  106.6 5.8 %collective-permute-start.18 = (f32[64,128]{1,0:T(8,128)S(1)}, f32[64,128]{1,0:T(8,128)S(1)}, u32[]{:S(2)}, u32[]{:S(2)}) collective-permute-start(f32[64,128]{1,0:T(8,128)S(1)} %get-tuple-element.34), channel_id=1, source_target_pairs={{0,125},{1,126},{2,127},{4,1},{5,2},{6,3},{8,5},{9,6},{10,7},{12,9... | collective-permute-start | bytes 98312 | tf_op jit(solution)/shard_map/ppermute | solution.py:301
  112.4 1.9 collective-permute-start.17
  114.3 7.8 %gather_fusion = bf16[1024,512]{1,0:T(8,128)(2,1)} fusion(bf16[4096,512]{1,0:T(8,128)(2,1)} %param.11, s32[1024]{0:T(1024)S(1)} %fusion), kind=kCustom, calls=%fused_computation | custom fusion | bytes 2101248 | tf_op jit(solution)/shard_map/jit(_take)/gather | solution.py:305
  122.2 0.0 collective-permute-done.19.br_ref
  122.2 3.9 %collective-permute-start.16 = (f32[64,128]{1,0:T(8,128)S(1)}, f32[64,128]{1,0:T(8,128)S(1)}, u32[]{:S(2)}, u32[]{:S(2)}) collective-permute-start(f32[64,128]{1,0:T(8,128)S(1)} %get-tuple-element.35), channel_id=1, source_target_pairs={{0,5},{1,6},{2,7},{4,9},{5,10},{6,11},{8,13},{9,14},{10,15},{12,17... | collective-permute-start | bytes 98312 | tf_op jit(solution)/shard_map/ppermute | solution.py:301
  126.1 0.0 collective-permute-done.18.bl_ref
  126.1 1.9 collective-permute-start.15
  128.1 0.0 collective-permute-done.17.tr_ref
  128.1 3.6 %collective-permute-start.14 = (f32[2,64,128]{2,1,0:T(8,128)S(1)}, f32[2,64,128]{2,1,0:T(8,128)S(1)}, u32[]{:S(2)}, u32[]{:S(2)}) collective-permute-start(f32[2,64,128]{2,1,0:T(8,128)S(1)} %get-tuple-element.20), channel_id=1, source_target_pairs={{0,1},{1,2},{2,3},{4,5},{5,6},{6,7},{8,9},{9,10},{10,11},{12,13},{... | collective-permute-start | bytes 196616 | tf_op jit(solution)/shard_map/ppermute | solution.py:301
  131.7 1.9 select_select_fusion.weights_ref
  133.6 0.0 copy-start.2
  133.6 0.0 collective-permute-done.16.tl_ref
  133.6 0.0 collective-permute-done.15.cr_ref
  133.6 0.0 collective-permute-done.14.cl_ref
  133.6 0.0 collective-permute-done.13.bot_ref
  133.6 0.0 collective-permute-done.12.top_ref
  133.6 22.6 %first_stage.3 = (f32[20,4,64,128]{3,2,1,0:T(8,128)S(1)}, f32[3,64,128]{2,1,0:T(8,128)S(1)}) custom-call(f32[16,4,64,128]{3,2,1,0:T(8,128)S(1)} %get-tuple-element.19.u_ref.base_ref, f32[4,4,64,128]{3,2,1,0:T(8,128)} %collective-permute-done.12.top_ref, f32[4,4,64,128]{3,2,1,0:T(8,128)} %collective-permute-done.13.bot_ref, ...), custom_call_target="tpu_custom_call" | custom-call | flops 38010880 | bytes 8388608 | tf_op jit(solution)/shard_map/first_stage/pallas_call | solution.py:186
  156.2 1.9 collective-permute-start.21
  158.2 3.6 %collective-permute-start.20 = (f32[3,64,128]{2,1,0:T(8,128)S(1)}, f32[3,64,128]{2,1,0:T(8,128)S(1)}, u32[]{:S(2)}, u32[]{:S(2)}) collective-permute-start(f32[3,64,128]{2,1,0:T(8,128)S(1)} %get-tuple-element.22), channel_id=1, source_target_pairs={{0,1},{1,2},{2,3},{4,5},{5,6},{6,7},{8,9},{9,10},{10,11},{12,13},{... | collective-permute-start | bytes 294920 | tf_op jit(solution)/shard_map/ppermute | solution.py:301
  161.8 3.6 %spread.1 = (bf16[2048,512]{1,0:T(8,128)(2,1)S(1)}, bf16[2048,512]{1,0:T(8,128)(2,1)S(1)}) custom-call(s32[1,1024]{1,0:T(1,128)S(1)} %bitcast.11, bf16[1024,512]{1,0:T(8,128)(2,1)S(1)} %select_select_fusion.weights_ref), custom_call_target="tpu_custom_call" | custom-call | flops 2147483648 | bytes 6291456 | tf_op jit(solution)/shard_map/spread/pallas_call | solution.py:230
  165.4 0.0 collective-permute-done.21.right_ref
  165.4 0.0 collective-permute-done.20.left_ref
  165.4 17.0 %second_stage.3 = (f32[16,4,64,128]{3,2,1,0:T(8,128)S(1)}, f32[2,64,128]{2,1,0:T(8,128)}) custom-call(f32[20,4,64,128]{3,2,1,0:T(8,128)S(1)} %get-tuple-element.21.y_ref, f32[3,64,128]{2,1,0:T(8,128)S(1)} %collective-permute-done.20.left_ref, f32[3,64,128]{2,1,0:T(8,128)S(1)} %collective-permute-done.21.right_ref, ...), custom_call_target="tpu_custom_call" | custom-call | flops 30408704 | bytes 8388608 | tf_op jit(solution)/shard_map/second_stage/pallas_call | solution.py:204
  182.4 3.6 %leave.1 = (f32[16,128,256]{2,1,0:T(8,128)}, f32[512,256]{1,0:T(8,128)S(1)}) custom-call(f32[16,4,64,128]{3,2,1,0:T(8,128)S(1)} %get-tuple-element.23.u_ref, bf16[2048,512]{1,0:T(8,128)(2,1)S(1)} %get-tuple-element.24.high_ref, bf16[2048,512]{1,0:T(8,128)(2,1)S(1)} %get-tuple-element.25.low_ref), custom_call_target="tpu_custom_call" | custom-call | flops 2147483648 | bytes 8388608 | tf_op jit(solution)/shard_map/leave/pallas_call | solution.py:271
  186.0 0.1 reshape.20
  186.2 22.2 %all_to_all.5 = f32[128,4,256]{2,1,0:T(4,128)S(1)} all-to-all(f32[128,4,256]{2,1,0:T(4,128)S(1)} %reshape.20), channel_id=1, replica_groups=mesh['azim'=32,'rad'=4] {'azim','rad'}, dimensions={0} | all-to-all | bytes 1048576 | tf_op jit(solution)/shard_map/all_to_all | solution.py:323
  208.4 0.7 reduce_sum.9
  (7 shorter events, 0.0 us)
Async XLA Ops:
  0.6 32.6 %copy-start = (f32[4,29,16,128]{3,2,1,0:T(8,128)S(1)}, f32[4,29,16,128]{3,2,1,0:T(8,128)}, u32[]{:S(2)}) copy-start(f32[4,29,16,128]{3,2,1,0:T(8,128)} %coef_ref.7) | copy-start | bytes 2850820
  0.6 1.7 copy-start.1
  3.9 47.8 %collective-permute-start.1 = (f32[4,4,64,128]{3,2,1,0:T(8,128)S(1)}, f32[4,4,64,128]{3,2,1,0:T(8,128)S(1)}, u32[]{:S(2)}, u32[]{:S(2)}) collective-permute-start(f32[4,4,64,128]{3,2,1,0:T(8,128)S(1)} %get-tuple-element.30), channel_id=1, source_target_pairs={{0,124},{1,125},{2,126},{3,127},{4,0},{5,1},{6,2},{7,3},{8,4},{9,5... | collective-permute-start | bytes 1572872 | tf_op jit(solution)/shard_map/ppermute | solution.py:301
  13.5 38.3 %collective-permute-start = (f32[4,4,64,128]{3,2,1,0:T(8,128)S(1)}, f32[4,4,64,128]{3,2,1,0:T(8,128)S(1)}, u32[]{:S(2)}, u32[]{:S(2)}) collective-permute-start(f32[4,4,64,128]{3,2,1,0:T(8,128)S(1)} %get-tuple-element.31), channel_id=1, source_target_pairs={{0,4},{1,5},{2,6},{3,7},{4,8},{5,9},{6,10},{7,11},{8,12},{9,13},{1... | collective-permute-start | bytes 1572872 | tf_op jit(solution)/shard_map/ppermute | solution.py:301
  13.5 15.8 %collective-permute-start.7 = (f32[64,128]{1,0:T(8,128)S(1)}, f32[64,128]{1,0:T(8,128)S(1)}, u32[]{:S(2)}, u32[]{:S(2)}) collective-permute-start(f32[64,128]{1,0:T(8,128)S(1)} %get-tuple-element.36), channel_id=1, source_target_pairs={{1,124},{2,125},{3,126},{5,0},{6,1},{7,2},{9,4},{10,5},{11,6},{13,... | collective-permute-start | bytes 98312 | tf_op jit(solution)/shard_map/ppermute | solution.py:301
  23.7 7.5 %collective-permute-start.6 = (f32[64,128]{1,0:T(8,128)S(1)}, f32[64,128]{1,0:T(8,128)S(1)}, u32[]{:S(2)}, u32[]{:S(2)}) collective-permute-start(f32[64,128]{1,0:T(8,128)S(1)} %get-tuple-element.36), channel_id=1, source_target_pairs={{0,125},{1,126},{2,127},{4,1},{5,2},{6,3},{8,5},{9,6},{10,7},{12,9... | collective-permute-start | bytes 98312 | tf_op jit(solution)/shard_map/ppermute | solution.py:301
  25.6 10.7 %collective-permute-start.5 = (f32[64,128]{1,0:T(8,128)S(1)}, f32[64,128]{1,0:T(8,128)S(1)}, u32[]{:S(2)}, u32[]{:S(2)}) collective-permute-start(f32[64,128]{1,0:T(8,128)S(1)} %get-tuple-element.37), channel_id=1, source_target_pairs={{1,4},{2,5},{3,6},{5,8},{6,9},{7,10},{9,12},{10,13},{11,14},{13,16... | collective-permute-start | bytes 98312 | tf_op jit(solution)/shard_map/ppermute | solution.py:301
  29.3 11.6 %collective-permute-start.4 = (f32[64,128]{1,0:T(8,128)S(1)}, f32[64,128]{1,0:T(8,128)S(1)}, u32[]{:S(2)}, u32[]{:S(2)}) collective-permute-start(f32[64,128]{1,0:T(8,128)S(1)} %get-tuple-element.37), channel_id=1, source_target_pairs={{0,5},{1,6},{2,7},{4,9},{5,10},{6,11},{8,13},{9,14},{10,15},{12,17... | collective-permute-start | bytes 98312 | tf_op jit(solution)/shard_map/ppermute | solution.py:301
  31.2 9.7 %collective-permute-start.3 = (f32[2,64,128]{2,1,0:T(8,128)S(1)}, f32[2,64,128]{2,1,0:T(8,128)S(1)}, u32[]{:S(2)}, u32[]{:S(2)}) collective-permute-start(f32[2,64,128]{2,1,0:T(8,128)S(1)} %get-tuple-element.16), channel_id=1, source_target_pairs={{1,0},{2,1},{3,2},{5,4},{6,5},{7,6},{9,8},{10,9},{11,10},{13,12},{... | collective-permute-start | bytes 196616 | tf_op jit(solution)/shard_map/ppermute | solution.py:301
  36.3 8.3 %collective-permute-start.9 = (f32[4,29,2,128]{3,2,1,0:T(2,128)S(1)}, f32[4,29,2,128]{3,2,1,0:T(2,128)S(1)}, u32[]{:S(2)}, u32[]{:S(2)}) collective-permute-start(f32[4,29,2,128]{3,2,1,0:T(2,128)S(1)} %get-tuple-element.32), channel_id=1, source_target_pairs={{0,124},{1,125},{2,126},{3,127},{4,0},{5,1},{6,2},{7,3},{8,4},{9,5... | collective-permute-start | bytes 356360 | tf_op jit(solution)/shard_map/ppermute | solution.py:301
  40.9 38.1 %copy-start.3 = (s32[1024]{0:T(1024)S(1)}, s32[1024]{0:T(1024)}, u32[]{:S(2)}) copy-start(s32[1024]{0:T(1024)} %param.10) | copy-start | bytes 12292
  40.9 10.9 %collective-permute-start.8 = (f32[4,29,2,128]{3,2,1,0:T(2,128)S(1)}, f32[4,29,2,128]{3,2,1,0:T(2,128)S(1)}, u32[]{:S(2)}, u32[]{:S(2)}) collective-permute-start(f32[4,29,2,128]{3,2,1,0:T(2,128)S(1)} %get-tuple-element.33), channel_id=1, source_target_pairs={{0,4},{1,5},{2,6},{3,7},{4,8},{5,9},{6,10},{7,11},{8,12},{9,13},{1... | collective-permute-start | bytes 356360 | tf_op jit(solution)/shard_map/ppermute | solution.py:301
  40.9 3.7 %collective-permute-start.2 = (f32[2,64,128]{2,1,0:T(8,128)S(1)}, f32[2,64,128]{2,1,0:T(8,128)S(1)}, u32[]{:S(2)}, u32[]{:S(2)}) collective-permute-start(f32[2,64,128]{2,1,0:T(8,128)S(1)} %get-tuple-element.16), channel_id=1, source_target_pairs={{0,1},{1,2},{2,3},{4,5},{5,6},{6,7},{8,9},{9,10},{10,11},{12,13},{... | collective-permute-start | bytes 196616 | tf_op jit(solution)/shard_map/ppermute | solution.py:301
  73.4 6.3 %collective-permute-start.11 = (f32[3,64,128]{2,1,0:T(8,128)S(1)}, f32[3,64,128]{2,1,0:T(8,128)S(1)}, u32[]{:S(2)}, u32[]{:S(2)}) collective-permute-start(f32[3,64,128]{2,1,0:T(8,128)S(1)} %get-tuple-element.18), channel_id=1, source_target_pairs={{1,0},{2,1},{3,2},{5,4},{6,5},{7,6},{9,8},{10,9},{11,10},{13,12},{... | collective-permute-start | bytes 294920 | tf_op jit(solution)/shard_map/ppermute | solution.py:301
  75.8 4.8 %collective-permute-start.10 = (f32[3,64,128]{2,1,0:T(8,128)S(1)}, f32[3,64,128]{2,1,0:T(8,128)S(1)}, u32[]{:S(2)}, u32[]{:S(2)}) collective-permute-start(f32[3,64,128]{2,1,0:T(8,128)S(1)} %get-tuple-element.18), channel_id=1, source_target_pairs={{0,1},{1,2},{2,3},{4,5},{5,6},{6,7},{8,9},{9,10},{10,11},{12,13},{... | collective-permute-start | bytes 294920 | tf_op jit(solution)/shard_map/ppermute | solution.py:301
  98.0 35.6 %collective-permute-start.13 = (f32[4,4,64,128]{3,2,1,0:T(8,128)}, f32[4,4,64,128]{3,2,1,0:T(8,128)}, u32[]{:S(2)}, u32[]{:S(2)}) collective-permute-start(f32[4,4,64,128]{3,2,1,0:T(8,128)} %get-tuple-element.28), channel_id=1, source_target_pairs={{0,124},{1,125},{2,126},{3,127},{4,0},{5,1},{6,2},{7,3},{8,4},{9,5... | collective-permute-start | bytes 1572872 | tf_op jit(solution)/shard_map/ppermute | solution.py:301
  99.6 34.1 %collective-permute-start.12 = (f32[4,4,64,128]{3,2,1,0:T(8,128)}, f32[4,4,64,128]{3,2,1,0:T(8,128)}, u32[]{:S(2)}, u32[]{:S(2)}) collective-permute-start(f32[4,4,64,128]{3,2,1,0:T(8,128)} %get-tuple-element.29), channel_id=1, source_target_pairs={{0,4},{1,5},{2,6},{3,7},{4,8},{5,9},{6,10},{7,11},{8,12},{9,13},{1... | collective-permute-start | bytes 1572872 | tf_op jit(solution)/shard_map/ppermute | solution.py:301
  99.6 22.6 %collective-permute-start.19 = (f32[64,128]{1,0:T(8,128)S(1)}, f32[64,128]{1,0:T(8,128)S(1)}, u32[]{:S(2)}, u32[]{:S(2)}) collective-permute-start(f32[64,128]{1,0:T(8,128)S(1)} %get-tuple-element.34), channel_id=1, source_target_pairs={{1,124},{2,125},{3,126},{5,0},{6,1},{7,2},{9,4},{10,5},{11,6},{13,... | collective-permute-start | bytes 98312 | tf_op jit(solution)/shard_map/ppermute | solution.py:301
  106.6 19.5 %collective-permute-start.18 = (f32[64,128]{1,0:T(8,128)S(1)}, f32[64,128]{1,0:T(8,128)S(1)}, u32[]{:S(2)}, u32[]{:S(2)}) collective-permute-start(f32[64,128]{1,0:T(8,128)S(1)} %get-tuple-element.34), channel_id=1, source_target_pairs={{0,125},{1,126},{2,127},{4,1},{5,2},{6,3},{8,5},{9,6},{10,7},{12,9... | collective-permute-start | bytes 98312 | tf_op jit(solution)/shard_map/ppermute | solution.py:301
  112.4 15.7 %collective-permute-start.17 = (f32[64,128]{1,0:T(8,128)S(1)}, f32[64,128]{1,0:T(8,128)S(1)}, u32[]{:S(2)}, u32[]{:S(2)}) collective-permute-start(f32[64,128]{1,0:T(8,128)S(1)} %get-tuple-element.35), channel_id=1, source_target_pairs={{1,4},{2,5},{3,6},{5,8},{6,9},{7,10},{9,12},{10,13},{11,14},{13,16... | collective-permute-start | bytes 98312 | tf_op jit(solution)/shard_map/ppermute | solution.py:301
  122.2 11.4 %collective-permute-start.16 = (f32[64,128]{1,0:T(8,128)S(1)}, f32[64,128]{1,0:T(8,128)S(1)}, u32[]{:S(2)}, u32[]{:S(2)}) collective-permute-start(f32[64,128]{1,0:T(8,128)S(1)} %get-tuple-element.35), channel_id=1, source_target_pairs={{0,5},{1,6},{2,7},{4,9},{5,10},{6,11},{8,13},{9,14},{10,15},{12,17... | collective-permute-start | bytes 98312 | tf_op jit(solution)/shard_map/ppermute | solution.py:301
  126.1 7.5 %collective-permute-start.15 = (f32[2,64,128]{2,1,0:T(8,128)S(1)}, f32[2,64,128]{2,1,0:T(8,128)S(1)}, u32[]{:S(2)}, u32[]{:S(2)}) collective-permute-start(f32[2,64,128]{2,1,0:T(8,128)S(1)} %get-tuple-element.20), channel_id=1, source_target_pairs={{1,0},{2,1},{3,2},{5,4},{6,5},{7,6},{9,8},{10,9},{11,10},{13,12},{... | collective-permute-start | bytes 196616 | tf_op jit(solution)/shard_map/ppermute | solution.py:301
  128.1 5.5 %collective-permute-start.14 = (f32[2,64,128]{2,1,0:T(8,128)S(1)}, f32[2,64,128]{2,1,0:T(8,128)S(1)}, u32[]{:S(2)}, u32[]{:S(2)}) collective-permute-start(f32[2,64,128]{2,1,0:T(8,128)S(1)} %get-tuple-element.20), channel_id=1, source_target_pairs={{0,1},{1,2},{2,3},{4,5},{5,6},{6,7},{8,9},{9,10},{10,11},{12,13},{... | collective-permute-start | bytes 196616 | tf_op jit(solution)/shard_map/ppermute | solution.py:301
  133.6 28.2 %copy-start.2 = (s32[1024]{0:T(1024)S(1)}, s32[1024]{0:T(1024)}, u32[]{:S(2)}) copy-start(s32[1024]{0:T(1024)} %param.8) | copy-start | bytes 12292
  156.2 9.2 %collective-permute-start.21 = (f32[3,64,128]{2,1,0:T(8,128)S(1)}, f32[3,64,128]{2,1,0:T(8,128)S(1)}, u32[]{:S(2)}, u32[]{:S(2)}) collective-permute-start(f32[3,64,128]{2,1,0:T(8,128)S(1)} %get-tuple-element.22), channel_id=1, source_target_pairs={{1,0},{2,1},{3,2},{5,4},{6,5},{7,6},{9,8},{10,9},{11,10},{13,12},{... | collective-permute-start | bytes 294920 | tf_op jit(solution)/shard_map/ppermute | solution.py:301
  158.2 7.3 %collective-permute-start.20 = (f32[3,64,128]{2,1,0:T(8,128)S(1)}, f32[3,64,128]{2,1,0:T(8,128)S(1)}, u32[]{:S(2)}, u32[]{:S(2)}) collective-permute-start(f32[3,64,128]{2,1,0:T(8,128)S(1)} %get-tuple-element.22), channel_id=1, source_target_pairs={{0,1},{1,2},{2,3},{4,5},{5,6},{6,7},{8,9},{9,10},{10,11},{12,13},{... | collective-permute-start | bytes 294920 | tf_op jit(solution)/shard_map/ppermute | solution.py:301

commit v2 on v0

v2 whole, which is shorter than its diff:
```python
import jax
import jax.numpy as jnp
from jax import lax
from jax.experimental import pallas as pl
from jax.experimental.pallas import tpu as pltpu
from jax.sharding import PartitionSpec as P

STEPS = 2
VMEM_LIMIT = 32 * 1024 * 1024
F32 = jnp.float32
BF16 = jnp.bfloat16


def spec(block, index):
    return pl.BlockSpec(block, index)


def whole(n):
    return [pl.BlockSpec(memory_space=pltpu.VMEM)] * n


def params(n=0):
    order = ("arbitrary",) * n if n else None
    return pltpu.CompilerParams(vmem_limit_bytes=VMEM_LIMIT, dimension_semantics=order)


def cost(rows):
    return pl.CostEstimate(flops=2 * 29 * rows * 128 * 256, bytes_accessed=rows << 18, transcendentals=0)


def arrays(*shapes):
    return [jax.ShapeDtypeStruct(shape, F32) for shape in shapes]


def lanes(shape):
    return lax.broadcasted_iota(jnp.int32, shape, len(shape) - 1)


ROWS = 256
TAIL = 4 * ROWS


def window(ref, row, var, half):
    start = pl.multiple_of(row * ROWS + var * 64 + half * 32, 32)
    return ref[pl.ds(start, 32), :]


def put(ref, row, var, half, value):
    start = pl.multiple_of(row * ROWS + var * 64 + half * 32, 32)
    ref[pl.ds(start, 32), :] = value


def pick(parts, row, var, half):
    for first, stop, ref in parts:
        if first <= row < stop:
            return window(ref, row - first, var, half)
    raise IndexError(row)


def place(pack, row, value):
    lane = lanes(value.shape)
    base = 4 * (row + 4)
    here = (lane >= base) & (lane < base + 4)
    return jnp.where(here, pltpu.roll(value, (base + 2) % 128, axis=1), pack)


def unplace(pack, row):
    lane = lanes(pack.shape)
    base = 4 * (row + 4)
    turned = pltpu.roll(pack, (126 - base) % 128, axis=1)
    return jnp.where((lane < 2) | (lane >= 126), turned, 0.0)


def each_part(body):
    @pl.loop(0, 8)
    def _(step):
        body(step // 2, step % 2)


def sweep(first, stop, source, weight, finish, shift_ref, block=4):
    lane = lanes((32, 128))
    for s in range(first - 2, stop + 2):
        u = source(s)
        k = s - first + 2
        shift_ref[0, k] = jnp.where(lane >= 2, pltpu.roll(u, 2, axis=1), 0.0)
        shift_ref[1, k] = jnp.where(lane >= 1, pltpu.roll(u, 1, axis=1), 0.0)
        shift_ref[2, k] = jnp.where(lane < 127, pltpu.roll(u, 127, axis=1), 0.0)
        shift_ref[3, k] = jnp.where(lane < 126, pltpu.roll(u, 126, axis=1), 0.0)
    for begin in range(first, stop, block):
        totals = [None] * block
        for s in range(begin - 2, begin + block + 2):
            k = s - first + 2
            for j in range(5):
                x = source(s) if j == 2 else shift_ref[j - (j > 2), k]
                for b in range(block):
                    i = s + 2 - begin - b
                    if 0 <= i < 5:
                        term = weight(5 * i + j, begin + b) * x
                        totals[b] = term if totals[b] is None else totals[b] + term
        for b in range(block):
            finish(begin + b, totals[b])


def line_of(coef_ref, var, k, row):
    return jnp.broadcast_to(coef_ref[var, k, row : row + 1], (32, 128))


def tail_line(ref, var, k, row):
    lines = ref.at[pl.ds(pl.multiple_of(TAIL + var * 64, 64), 64)]
    return jnp.broadcast_to(lines[2 * k + row : 2 * k + row + 1], (32, 128))


def enter(x_ref, coef_ref, low_ref, mid_ref, high_ref):
    low_ref[TAIL:] = jnp.zeros((256, 128), F32)
    high_ref[TAIL:] = jnp.zeros((256, 128), F32)

    @pl.loop(0, 4)
    def _(k):
        at = pl.ds(pl.multiple_of(k * ROWS, ROWS), ROWS)
        low_ref[at] = x_ref[k].T
        mid_ref[at] = x_ref[k + 4].T
        mid_ref[pl.ds(pl.multiple_of((k + 4) * ROWS, ROWS), ROWS)] = x_ref[k + 8].T
        high_ref[at] = x_ref[k + 12].T
        lines = pl.ds(pl.multiple_of(TAIL + k * 64, 64), 58)
        low_ref[lines] = coef_ref[k, :, 0:2].reshape(58, 128)
        high_ref[lines] = coef_ref[k, :, 14:16].reshape(58, 128)


def call_enter(x, coef):
    return pl.pallas_call(
        enter,
        in_specs=whole(2),
        out_specs=whole(3),
        out_shape=arrays((TAIL + 256, 128), (8 * ROWS, 128), (TAIL + 256, 128)),
        compiler_params=params(),
        name="enter",
    )(x, coef)


def inner_first(low_ref, mid_ref, high_ref, coef_ref, y_ref, edge_y_ref, edge_u_ref, shift_ref):
    parts = ((0, 4, low_ref), (4, 12, mid_ref), (12, 16, high_ref))

    def one(var, half):
        at = pl.ds(pl.multiple_of(half * 32, 32), 32)

        def finish(row, total):
            for w in range(4):
                total = total + line_of(coef_ref, var, 25 + w, row) * pick(parts, row, w, half)
            put(y_ref, row - 2, var, half, pick(parts, row, var, half) + 0.5 * total)

        sweep(
            2, 14, lambda s: pick(parts, s, var, half),
            lambda k, row: line_of(coef_ref, var, k, row), finish, shift_ref,
        )
        pack = jnp.zeros((32, 128), F32)
        for row in range(16):
            pack = place(pack, row, pick(parts, row, var, half))
        edge_u_ref[var, at] = pack
        pack = jnp.zeros((32, 128), F32)
        for row in range(2, 14):
            pack = place(pack, row, window(y_ref, row - 2, var, half))
        edge_y_ref[var, at] = pack

    each_part(one)


def call_inner_first(low, mid, high, coef):
    return pl.pallas_call(
        inner_first,
        in_specs=whole(4),
        out_specs=whole(3),
        out_shape=arrays((12 * ROWS, 128), (4, 64, 128), (4, 64, 128)),
        scratch_shapes=[pltpu.VMEM((4, 16, 32, 128), F32)],
        compiler_params=params(),
        cost_estimate=cost(12),
        name="inner_first",
    )(low, mid, high, coef)


def halo_edges(top_ref, bot_ref, edge_ref, out_ref):
    def one(var, half):
        at = pl.ds(pl.multiple_of(half * 32, 32), 32)
        pack = edge_ref[var, at]
        for k in range(4):
            pack = place(pack, k - 4, window(top_ref, k, var, half))
            pack = place(pack, k + 16, window(bot_ref, k, var, half))
        out_ref[var, at] = pack

    each_part(one)


def call_halo_edges(top, bot, edge):
    return pl.pallas_call(
        halo_edges,
        in_specs=whole(3),
        out_specs=whole(1)[0],
        out_shape=arrays((4, 64, 128))[0],
        compiler_params=params(),
        name="halo_edges",
    )(top, bot, edge)


def outer_first(top_ref, low_ref, high_ref, bot_ref, coef_ref, ctop_ref, cbot_ref, edge_ref,
                y_low_ref, y_high_ref, edge_y_ref, shift_ref):
    parts = ((-4, 0, top_ref), (0, 4, low_ref), (12, 16, high_ref), (16, 20, bot_ref))

    def one(var, half):
        at = pl.ds(pl.multiple_of(half * 32, 32), 32)

        def weight(k, row):
            if row < 0:
                return tail_line(ctop_ref, var, k, row + 2)
            if row < 16:
                return line_of(coef_ref, var, k, row)
            return tail_line(cbot_ref, var, k, row - 16)

        def finish(row, total):
            for w in range(4):
                total = total + weight(25 + w, row) * pick(parts, row, w, half)
            value = pick(parts, row, var, half) + 0.5 * total
            if row < 2:
                put(y_low_ref, row + 2, var, half, value)
            else:
                put(y_high_ref, row - 14, var, half, value)

        for first in (-2, 14):
            sweep(first, first + 4, lambda s: pick(parts, s, var, half), weight, finish, shift_ref)
        pack = edge_ref[var, at]
        for k in range(4):
            pack = place(pack, k - 2, window(y_low_ref, k, var, half))
            pack = place(pack, k + 14, window(y_high_ref, k, var, half))
        edge_y_ref[var, at] = pack

    each_part(one)


def call_outer_first(top, low, high, bot, coef, ctop, cbot, edge):
    return pl.pallas_call(
        outer_first,
        in_specs=whole(8),
        out_specs=whole(3),
        out_shape=arrays((4 * ROWS, 128), (4 * ROWS, 128), (4, 64, 128)),
        scratch_shapes=[pltpu.VMEM((4, 8, 32, 128), F32)],
        compiler_params=params(),
        cost_estimate=cost(8),
        name="outer_first",
    )(top, low, high, bot, coef, ctop, cbot, edge)


def edge_weights(coef_ref, ctop_ref, cbot_ref, out_ref):
    lane = lanes((1, 128))
    inner = (lane % 4 == 1) | (lane % 4 == 2)

    @pl.loop(0, 4)
    def _(var):
        top = ctop_ref.at[pl.ds(pl.multiple_of(TAIL + var * 64, 64), 64)]
        bot = cbot_ref.at[pl.ds(pl.multiple_of(TAIL + var * 64, 64), 64)]

        def line(k, row):
            if row < 0:
                return top[2 * k + row + 2 : 2 * k + row + 3]
            if row < 16:
                return coef_ref[var, k, row : row + 1]
            return bot[2 * k + row - 16 : 2 * k + row - 15]

        for i in range(5):
            far = jnp.zeros((1, 128), F32)
            near = jnp.zeros((1, 128), F32)
            for row in range(-2, 18):
                far = place(far, row, jnp.where(lane < 64, line(5 * i, row), line(5 * i + 4, row)))
                near = place(near, row, jnp.where(lane < 64, line(5 * i + 1, row), line(5 * i + 3, row)))
            out_ref[var, i : i + 1] = far
            out_ref[var, 5 + i : 6 + i] = jnp.where(inner, near, 0.0)


def call_edge_weights(coef, ctop, cbot):
    return pl.pallas_call(
        edge_weights,
        in_specs=whole(3),
        out_specs=whole(1)[0],
        out_shape=arrays((4, 10, 128))[0],
        compiler_params=params(),
        name="edge_weights",
    )(coef, ctop, cbot)


def beyond(left_ref, right_ref, weight_ref, var):
    lane = lanes((64, 128)) % 4
    rim = jnp.where(
        lane < 2, pltpu.roll(right_ref[var], 126, axis=1), pltpu.roll(left_ref[var], 2, axis=1)
    )
    other = jnp.where(lane == 1, pltpu.roll(rim, 1, axis=1), pltpu.roll(rim, 127, axis=1))
    total = jnp.zeros((64, 128), F32)
    for i in range(5):
        turn = (4 * (2 - i)) % 128
        far, near = rim, other
        if turn:
            far, near = pltpu.roll(rim, turn, axis=1), pltpu.roll(other, turn, axis=1)
        total = total + weight_ref[var, i : i + 1] * far
        total = total + weight_ref[var, 5 + i : 6 + i] * near
    return total


def mend_edges(left_ref, right_ref, weight_ref, edge_ref, out_ref, mend_ref):
    @pl.loop(0, 4)
    def _(var):
        mend = 0.5 * beyond(left_ref, right_ref, weight_ref, var)
        mend_ref[var] = mend
        out_ref[var] = edge_ref[var] + mend


def call_mend_edges(left, right, weights, edge):
    return pl.pallas_call(
        mend_edges,
        in_specs=whole(4),
        out_specs=whole(2),
        out_shape=arrays((4, 64, 128), (4, 64, 128)),
        compiler_params=params(),
        name="mend_edges",
    )(left, right, weights, edge)


def second(y_low_ref, y_mid_ref, y_high_ref, mend_ref, low_ref, mid_ref, high_ref, coef_ref,
           out_ref, y_ref, shift_ref):
    y_parts = ((-2, 2, y_low_ref), (2, 14, y_mid_ref), (14, 18, y_high_ref))
    u_parts = ((0, 4, low_ref), (4, 12, mid_ref), (12, 16, high_ref))
    whole_y = ((-2, 18, y_ref),)

    def mend(var, half):
        pack = mend_ref[var, pl.ds(pl.multiple_of(half * 32, 32), 32)]
        for row in range(-2, 18):
            put(y_ref, row + 2, var, half, pick(y_parts, row, var, half) + unplace(pack, row))

    each_part(mend)

    def one(var, half):
        def finish(row, total):
            for w in range(4):
                total = total + line_of(coef_ref, var, 25 + w, row) * pick(whole_y, row, w, half)
            put(out_ref, row, var, half, pick(u_parts, row, var, half) + total)

        sweep(
            0, 16, lambda s: pick(whole_y, s, var, half),
            lambda k, row: line_of(coef_ref, var, k, row), finish, shift_ref,
        )

    each_part(one)


def call_second(y_low, y_mid, y_high, mend, low, mid, high, coef):
    return pl.pallas_call(
        second,
        in_specs=whole(8),
        out_specs=whole(1)[0],
        out_shape=arrays((16 * ROWS, 128))[0],
        scratch_shapes=[pltpu.VMEM((20 * ROWS, 128), F32), pltpu.VMEM((4, 20, 32, 128), F32)],
        compiler_params=params(),
        cost_estimate=cost(16),
        name="second",
    )(y_low, y_mid, y_high, mend, low, mid, high, coef)


def mend_state(left_ref, right_ref, weight_ref, u_ref, low_ref, mid_ref, high_ref, mend_ref):
    @pl.loop(0, 4)
    def _(var):
        mend_ref[var] = beyond(left_ref, right_ref, weight_ref, var)

    def one(var, half):
        pack = mend_ref[var, pl.ds(pl.multiple_of(half * 32, 32), 32)]
        for row in range(16):
            value = window(u_ref, row, var, half) + unplace(pack, row)
            for first, stop, ref in ((0, 4, low_ref), (4, 12, mid_ref), (12, 16, high_ref)):
                if first <= row < stop:
                    put(ref, row - first, var, half, value)

    each_part(one)


def call_mend_state(left, right, weights, u):
    return pl.pallas_call(
        mend_state,
        in_specs=whole(4),
        out_specs=whole(3),
        out_shape=arrays((4 * ROWS, 128), (8 * ROWS, 128), (4 * ROWS, 128)),
        scratch_shapes=[pltpu.VMEM((4, 64, 128), F32)],
        compiler_params=params(),
        name="mend_state",
    )(left, right, weights, u)


def spread(cells_ref, weights_ref, high_ref, low_ref):
    step = pl.program_id(0)
    cell = lax.broadcasted_iota(jnp.int32, (256, 1024), 0) + step * 256
    hit = jnp.where(cells_ref[...] == cell, 1.0, 0.0).astype(BF16)
    total = jnp.dot(hit, weights_ref[...], preferred_element_type=F32)
    high = total.astype(BF16)
    high_ref[...] = high
    low_ref[...] = (total - high.astype(F32)).astype(BF16)


def call_spread(cells, weights):
    return pl.pallas_call(
        spread,
        grid=(8,),
        in_specs=[spec((1, 1024), lambda s: (0, 0)), spec((1024, 512), lambda s: (0, 0))],
        out_specs=[spec((256, 512), lambda s: (s, 0))] * 2,
        out_shape=[jax.ShapeDtypeStruct((2048, 512), BF16)] * 2,
        compiler_params=params(1),
        cost_estimate=pl.CostEstimate(flops=2 << 30, bytes_accessed=6 << 20, transcendentals=0),
        name="spread",
    )(cells, weights)


def leave(low_ref, mid_ref, high_ref, w_high_ref, w_low_ref, out_ref, markov_ref):
    parts = ((0, 4, low_ref), (4, 12, mid_ref), (12, 16, high_ref))
    sums = jnp.zeros((256, 512), F32)
    for k in range(8):
        rows = []
        for row in (2 * k, 2 * k + 1):
            for first, stop, ref in parts:
                if first <= row < stop:
                    rows.append(ref[(row - first) * ROWS : (row - first + 1) * ROWS])
            out_ref[row] = rows[-1].T
        u = jnp.concatenate(rows, axis=1)
        u_high = u.astype(BF16)
        u_low = (u - u_high.astype(F32)).astype(BF16)
        w_high = w_high_ref[256 * k : 256 * k + 256]
        w_low = w_low_ref[256 * k : 256 * k + 256]
        sums = sums + jnp.dot(u_high, w_high, preferred_element_type=F32)
        sums = sums + jnp.dot(u_low, w_high, preferred_element_type=F32)
        sums = sums + jnp.dot(u_high, w_low, preferred_element_type=F32)
    markov_ref[...] = sums.T


def call_leave(low, mid, high, w_high, w_low):
    return pl.pallas_call(
        leave,
        in_specs=whole(5),
        out_specs=whole(2),
        out_shape=arrays((16, 128, 256), (512, 256)),
        compiler_params=params(),
        cost_estimate=pl.CostEstimate(flops=2 << 30, bytes_accessed=8 << 20, transcendentals=0),
        name="leave",
    )(low, mid, high, w_high, w_low)


def shifts(n_azim, n_rad, da, dr):
    pairs = []
    for a in range(n_azim):
        for r in range(n_rad):
            if 0 <= r + dr < n_rad:
                pairs.append((a * n_rad + r, ((a + da) % n_azim) * n_rad + r + dr))
    return pairs


def body(perturbation_in, coefficients, wall_cells, wall_count, mode_row, mode_table):
    n_azim, n_rad = lax.axis_size("azim"), lax.axis_size("rad")

    def send(block, da, dr):
        return lax.ppermute(block, ("azim", "rad"), shifts(n_azim, n_rad, da, dr))

    slots = wall_cells.shape[0]
    live = jnp.arange(slots, dtype=jnp.int32) < wall_count[0]
    weights = jnp.where(live[:, None], jnp.take(mode_table, mode_row, axis=0), jnp.zeros((), BF16))
    w_high, w_low = call_spread(wall_cells.reshape(1, slots), weights)

    low, mid, high = call_enter(perturbation_in, coefficients)
    tails = None
    for step in range(STEPS):
        top, bot = send(high, 1, 0), send(low, -1, 0)
        if tails is None:
            tails = top, bot
            edge_w = call_edge_weights(coefficients, *tails)
        y_mid, edge_y, edge_u = call_inner_first(low, mid, high, coefficients)
        edge_u = call_halo_edges(top, bot, edge_u)
        left, right = send(edge_u, 0, 1), send(edge_u, 0, -1)
        y_low, y_high, edge_y = call_outer_first(top, low, high, bot, coefficients, *tails, edge_y)
        edge_y, mend = call_mend_edges(left, right, edge_w, edge_y)
        left, right = send(edge_y, 0, 1), send(edge_y, 0, -1)
        u = call_second(y_low, y_mid, y_high, mend, low, mid, high, coefficients)
        low, mid, high = call_mend_state(left, right, edge_w, u)
    out, term = call_leave(low, mid, high, w_high, w_low)
    count = n_azim * n_rad
    parts = lax.all_to_all(term.reshape(count, -1, term.shape[1]), ("azim", "rad"), 0, 0)
    return out, jnp.sum(parts, axis=0)


def solution(mesh):
    return jax.shard_map(
        body,
        mesh=mesh,
        in_specs=(
            P("azim", "rad", None),
            P(None, None, "azim", "rad"),
            P(("azim", "rad")),
            P(("azim", "rad")),
            P(("azim", "rad")),
            P(),
        ),
        out_specs=(P("azim", "rad", None), P(("azim", "rad"), None)),
        check_vma=False,
    )
```

time: 527 us -> 133 us (0.25); the launches traced: 521 us -> 133 us
  other arithmetic: 198 us -> 1.55 us
  waiting for transfers between devices: 148 us -> 9.76 us
  local copies, waits for them, and re-layouts: 96.9 us -> 13 us
  Pallas kernels: 0 us -> 47.9 us
  blocking collectives: 0 us -> 19.7 us
  starting transfers between devices: 55.7 us -> 39.3 us
  between operations: 16.7 us -> 1.61 us
  matrix products: 5.94 us -> 0 us
    psum x1 -> x0, waiting for transfers between devices: 147 us -> none  [body(): totals = lax.psum(term, ('azim', 'rad'))]
    mul x16 -> x0, other arithmetic: 101 us -> none  [the longest x2 72.8 us: body(): state = 0.5 * (state + first + flux(rimmed(first), coefficients, first))]
    add x2 -> x0, other arithmetic: 66.8 us -> none  [body(): first = state + flux(rimmed(state), coefficients, state)]
    slice x24 -> x0, local copies, waits for them, and re-layouts: 54.6 us -> none  [the longest x12 27.1 us: with_halo(): lax.slice_in_dim(block, block.shape[dim] - width, None, axis=dim)]
    pallas_call x0 -> x16, Pallas kernels: none -> 47.9 us  [the longest x2 12.5 us: call_second(): pl.pallas_call(second, in_specs=whole(8), out_specs=whole(1)[0], out_shap...]
    concatenate x8 -> x0, other arithmetic: 30.5 us -> none  [with_halo(): block = jnp.concatenate([low, block, high], axis=dim)]
    ppermute x8 -> x0, local copies, waits for them, and re-layouts: 21.2 us -> none  [the longest x4 10.6 us: with_halo(): lax.ppermute(lax.slice_in_dim(block, block.shape[dim] - width, None, axis...]
    all_to_all x0 -> x1, blocking collectives: none -> 19.7 us  [body(): lax.all_to_all(term.reshape(count, -1, term.shape[1]), ('azim', 'rad'), 0...]
  transfers between devices with their start and end apart: 17 -> 12, of which waited for: 3 -> 1; matrix products, arithmetic and copies ran while one was open for 14% -> 7% of each run, Pallas kernels for 0% -> 26%
where the time goes in v2:
time: 133 us
  Pallas kernels  47.9 us (36%)
  starting transfers between devices  39.3 us (30%)
  blocking collectives  19.7 us (15%)
  local copies, waits for them, and re-layouts  13 us (10%)
  waiting for transfers between devices  9.76 us (7%)
  between operations  1.61 us (1%)
  other arithmetic  1.55 us (1%)
    ppermute x12, starting transfers between devices, send(): return lax.ppermute(block, ('azim', 'rad'), shifts(n_azim, n_rad, da, dr))  39.3 us
    all_to_all x1, blocking collectives, body(): lax.all_to_all(term.reshape(count, -1, term.shape[1]), ('azim', 'rad'), 0...  19.7 us
    pallas_call x2, Pallas kernels, call_second(): pl.pallas_call(second, in_specs=whole(8), out_specs=whole(1)[0], out_shap...  12.5 us
    ppermute x12, waiting for transfers between devices, send(): return lax.ppermute(block, ('azim', 'rad'), shifts(n_azim, n_rad, da, dr))  9.76 us
    pallas_call x2, Pallas kernels, call_inner_first(): pl.pallas_call(inner_first, in_specs=whole(4), out_specs=whole(3), out_sh...  9.29 us
    pallas_call x2, Pallas kernels, call_outer_first(): pl.pallas_call(outer_first, in_specs=whole(8), out_specs=whole(3), out_sh...  8.24 us
    gather x1, local copies, waits for them, and re-layouts, body(): jnp.take(mode_table, mode_row, axis=0)  7.84 us
    unnamed x18, local copies, waits for them, and re-layouts  4.99 us
  transfers between devices with their start and end apart: 12, of which 1 were waited for; matrix products, arithmetic and copies ran while one was open for 7% of the time, Pallas kernels for 26%

profile of v2, /device:TPU:1, one launch (start us, length us, event | category | flops | bytes accessed | tf_op | source)
XLA Modules:
  0.0 132.9 jit_solution(10493516505081582100)
XLA Ops:
  0.6 0.0 copy-start
  0.6 1.2 copy-done
  1.8 0.0 copy-start.5
  1.8 1.6 %copy-done.5 = f32[16,128,256]{2,1,0:T(8,128)S(1)} copy-done((f32[16,128,256]{2,1,0:T(8,128)S(1)}, f32[16,128,256]{2,1,0:T(8,128)}, u32[]{:S(2)}) %copy-start.5) | copy-done | bytes 2097176
  3.4 0.0 copy-start.1
  3.4 0.8 enter.1
  4.3 2.2 %collective-permute-start = (f32[1280,128]{1,0:T(8,128)S(1)}, f32[1280,128]{1,0:T(8,128)S(1)}, u32[]{:S(2)}, u32[]{:S(2)}) collective-permute-start(f32[1280,128]{1,0:T(8,128)S(1)} %get-tuple-element.31.high_ref), channel_id=1, source_target_pairs={{0,4},{1,5},{2,6},{3,7},{4,8},{5,9},{6,10},{7,11},{8,12},{9,13},{1... | collective-permute-start | bytes 1966088 | tf_op jit(solution)/shard_map/ppermute | solution.py:460
  6.5 7.5 %collective-permute-start.1 = (f32[1280,128]{1,0:T(8,128)S(1)}, f32[1280,128]{1,0:T(8,128)S(1)}, u32[]{:S(2)}, u32[]{:S(2)}) collective-permute-start(f32[1280,128]{1,0:T(8,128)S(1)} %get-tuple-element.32.low_ref), channel_id=1, source_target_pairs={{0,124},{1,125},{2,126},{3,127},{4,0},{5,1},{6,2},{7,3},{8,4},{9,5... | collective-permute-start | bytes 1966088 | tf_op jit(solution)/shard_map/ppermute | solution.py:460
  13.9 0.0 copy-done.1
  13.9 4.6 %inner_first.2 = (f32[3072,128]{1,0:T(8,128)S(1)}, f32[4,64,128]{2,1,0:T(8,128)S(1)}, f32[4,64,128]{2,1,0:T(8,128)S(1)}) custom-call(f32[1280,128]{1,0:T(8,128)S(1)} %get-tuple-element.32.low_ref, f32[2048,128]{1,0:T(8,128)S(1)} %get-tuple-element.33.mid_ref, f32[1280,128]{1,0:T(8,128)S(1)} %get-tuple-element.31.high_ref, f32[4,29,16,128]{3,2,1,0:T(8,128)S(1)} %copy-done.1), custom_call_target="tpu_custom_call" | custom-call | flops 22806528 | bytes 3145728 | tf_op jit(solution)/shard_map/inner_first/pallas_call | solution.py:168
  18.6 9.7 %collective-permute-done.top_ref.ctop_ref = f32[1280,128]{1,0:T(8,128)S(1)} collective-permute-done((f32[1280,128]{1,0:T(8,128)S(1)}, f32[1280,128]{1,0:T(8,128)S(1)}, u32[]{:S(2)}, u32[]{:S(2)}) %collective-permute-start) | collective-permute-done | bytes 655392 | tf_op jit(solution)/shard_map/ppermute | solution.py:460
  28.3 0.0 collective-permute-done.1.bot_ref.cbot_ref
  28.3 0.8 halo_edges.2
  29.2 3.3 %collective-permute-start.2 = (f32[4,64,128]{2,1,0:T(8,128)S(1)}, f32[4,64,128]{2,1,0:T(8,128)S(1)}, u32[]{:S(2)}, u32[]{:S(2)}) collective-permute-start(f32[4,64,128]{2,1,0:T(8,128)S(1)} %halo_edges.2), channel_id=1, source_target_pairs={{0,1},{1,2},{2,3},{4,5},{5,6},{6,7},{8,9},{9,10},{10,11},{12,13},{... | collective-permute-start | bytes 393224 | tf_op jit(solution)/shard_map/ppermute | solution.py:460
  32.5 1.9 %collective-permute-start.3 = (f32[4,64,128]{2,1,0:T(8,128)S(1)}, f32[4,64,128]{2,1,0:T(8,128)S(1)}, u32[]{:S(2)}, u32[]{:S(2)}) collective-permute-start(f32[4,64,128]{2,1,0:T(8,128)S(1)} %halo_edges.2), channel_id=1, source_target_pairs={{1,0},{2,1},{3,2},{5,4},{6,5},{7,6},{9,8},{10,9},{11,10},{13,12},{... | collective-permute-start | bytes 393224 | tf_op jit(solution)/shard_map/ppermute | solution.py:460
  34.4 1.1 edge_weights.1.weight_ref
  35.6 3.5 %outer_first.2 = (f32[1024,128]{1,0:T(8,128)S(1)}, f32[1024,128]{1,0:T(8,128)S(1)}, f32[4,64,128]{2,1,0:T(8,128)S(1)}) custom-call(f32[1280,128]{1,0:T(8,128)S(1)} %collective-permute-done.top_ref.ctop_ref, f32[1280,128]{1,0:T(8,128)S(1)} %get-tuple-element.32.low_ref, f32[1280,128]{1,0:T(8,128)S(1)} %get-tuple-element.31.high_ref, ...), custom_call_target="tpu_custom_call" | custom-call | flops 15204352 | bytes 2097152 | tf_op jit(solution)/shard_map/outer_first/pallas_call | solution.py:238
  39.1 0.0 collective-permute-done.2.left_ref
  39.1 0.0 collective-permute-done.3.right_ref
  39.1 1.0 mend_edges.2
  40.1 3.6 %collective-permute-start.4 = (f32[4,64,128]{2,1,0:T(8,128)S(1)}, f32[4,64,128]{2,1,0:T(8,128)S(1)}, u32[]{:S(2)}, u32[]{:S(2)}) collective-permute-start(f32[4,64,128]{2,1,0:T(8,128)S(1)} %get-tuple-element.37), channel_id=1, source_target_pairs={{0,1},{1,2},{2,3},{4,5},{5,6},{6,7},{8,9},{9,10},{10,11},{12,13},{... | collective-permute-start | bytes 393224 | tf_op jit(solution)/shard_map/ppermute | solution.py:460
  43.8 1.9 %collective-permute-start.5 = (f32[4,64,128]{2,1,0:T(8,128)S(1)}, f32[4,64,128]{2,1,0:T(8,128)S(1)}, u32[]{:S(2)}, u32[]{:S(2)}) collective-permute-start(f32[4,64,128]{2,1,0:T(8,128)S(1)} %get-tuple-element.37), channel_id=1, source_target_pairs={{1,0},{2,1},{3,2},{5,4},{6,5},{7,6},{9,8},{10,9},{11,10},{13,12},{... | collective-permute-start | bytes 393224 | tf_op jit(solution)/shard_map/ppermute | solution.py:460
  45.7 6.3 %second.2.u_ref = f32[4096,128]{1,0:T(8,128)S(1)} custom-call(f32[1024,128]{1,0:T(8,128)S(1)} %get-tuple-element.38.y_low_ref, f32[3072,128]{1,0:T(8,128)S(1)} %get-tuple-element.39.y_mid_ref, f32[1024,128]{1,0:T(8,128)S(1)} %get-tuple-element.40.y_high_ref, f32[4,64,128]{2,1,0:T(8,128)S(1)} %get-tuple-element.41.mend_ref, ...), custom_call_target="tpu_custom_call" | custom-call | flops 30408704 | bytes 4194304 | tf_op jit(solution)/shard_map/second/pallas_call | solution.py:351
  52.0 0.0 copy-start.8
  52.0 0.0 collective-permute-done.4.left_ref
  52.0 0.0 collective-permute-done.5.right_ref
  52.0 2.1 %mend_state.2 = (f32[1024,128]{1,0:T(8,128)S(1)}, f32[2048,128]{1,0:T(8,128)S(1)}, f32[1024,128]{1,0:T(8,128)S(1)}) custom-call(f32[4,64,128]{2,1,0:T(8,128)S(1)} %collective-permute-done.4.left_ref, f32[4,64,128]{2,1,0:T(8,128)S(1)} %collective-permute-done.5.right_ref, f32[4,10,128]{2,1,0:T(8,128)S(1)} %edge_weights.1.weight_ref, f32[4096,128]{1,0:T(8,128)S(1)} %second.2.u_ref), custom_call_target="tpu_custom_call" | custom-call | tf_op jit(solution)/shard_map/mend_state/pallas_call | solution.py:380
  54.1 0.0 copy-start.2
  54.2 1.0 copy-done.2
  55.1 0.0 collective-permute-start.6
  55.1 7.9 %collective-permute-start.7 = (f32[1024,128]{1,0:T(8,128)S(1)}, f32[1024,128]{1,0:T(8,128)}, u32[]{:S(2)}, u32[]{:S(2)}) collective-permute-start(f32[1024,128]{1,0:T(8,128)S(1)} %get-tuple-element.43.low_ref), channel_id=1, source_target_pairs={{0,124},{1,125},{2,126},{3,127},{4,0},{5,1},{6,2},{7,3},{8,4},{9,5... | collective-permute-start | bytes 1572872 | tf_op jit(solution)/shard_map/ppermute | solution.py:460
  63.6 0.0 copy-done.8
  63.7 7.8 %gather_fusion = bf16[1024,512]{1,0:T(8,128)(2,1)} fusion(bf16[4096,512]{1,0:T(8,128)(2,1)} %param.11, s32[1024]{0:T(1024)S(1)} %fusion), kind=kCustom, calls=%fused_computation | custom fusion | bytes 2101248 | tf_op jit(solution)/shard_map/jit(_take)/gather | solution.py:464
  71.5 0.0 copy-start.3
  71.5 1.2 copy-done.3
  72.7 0.0 copy-start.7
  72.7 4.6 %inner_first.3 = (f32[3072,128]{1,0:T(8,128)S(1)}, f32[4,64,128]{2,1,0:T(8,128)S(1)}, f32[4,64,128]{2,1,0:T(8,128)S(1)}) custom-call(f32[1024,128]{1,0:T(8,128)S(1)} %get-tuple-element.43.low_ref, f32[2048,128]{1,0:T(8,128)S(1)} %copy-done.3, f32[1024,128]{1,0:T(8,128)S(1)} %get-tuple-element.42.high_ref, f32[4,29,16,128]{3,2,1,0:T(8,128)S(1)} %copy-done.1), custom_call_target="tpu_custom_call" | custom-call | flops 22806528 | bytes 3145728 | tf_op jit(solution)/shard_map/inner_first/pallas_call | solution.py:168
  77.4 0.0 collective-permute-done.6.top_ref
  77.4 0.0 collective-permute-done.7.bot_ref
  77.4 2.0 %halo_edges.3 = f32[4,64,128]{2,1,0:T(8,128)S(1)} custom-call(f32[1024,128]{1,0:T(8,128)} %collective-permute-done.6.top_ref, f32[1024,128]{1,0:T(8,128)} %collective-permute-done.7.bot_ref, f32[4,64,128]{2,1,0:T(8,128)S(1)} %get-tuple-element.45.edge_ref), custom_call_target="tpu_custom_call" | custom-call | tf_op jit(solution)/shard_map/halo_edges/pallas_call | solution.py:193
  79.5 3.5 %collective-permute-start.8 = (f32[4,64,128]{2,1,0:T(8,128)S(1)}, f32[4,64,128]{2,1,0:T(8,128)S(1)}, u32[]{:S(2)}, u32[]{:S(2)}) collective-permute-start(f32[4,64,128]{2,1,0:T(8,128)S(1)} %halo_edges.3), channel_id=1, source_target_pairs={{0,1},{1,2},{2,3},{4,5},{5,6},{6,7},{8,9},{9,10},{10,11},{12,13},{... | collective-permute-start | bytes 393224 | tf_op jit(solution)/shard_map/ppermute | solution.py:460
  83.0 1.9 %collective-permute-start.9 = (f32[4,64,128]{2,1,0:T(8,128)S(1)}, f32[4,64,128]{2,1,0:T(8,128)S(1)}, u32[]{:S(2)}, u32[]{:S(2)}) collective-permute-start(f32[4,64,128]{2,1,0:T(8,128)S(1)} %halo_edges.3), channel_id=1, source_target_pairs={{1,0},{2,1},{3,2},{5,4},{6,5},{7,6},{9,8},{10,9},{11,10},{13,12},{... | collective-permute-start | bytes 393224 | tf_op jit(solution)/shard_map/ppermute | solution.py:460
  84.9 0.0 copy-done.7
  84.9 0.8 select_select_fusion.weights_ref
  85.7 0.0 copy-start.6
  85.7 4.7 %outer_first.3 = (f32[1024,128]{1,0:T(8,128)S(1)}, f32[1024,128]{1,0:T(8,128)S(1)}, f32[4,64,128]{2,1,0:T(8,128)S(1)}) custom-call(f32[1024,128]{1,0:T(8,128)} %collective-permute-done.6.top_ref, f32[1024,128]{1,0:T(8,128)S(1)} %get-tuple-element.43.low_ref, f32[1024,128]{1,0:T(8,128)S(1)} %get-tuple-element.42.high_ref, ...), custom_call_target="tpu_custom_call" | custom-call | flops 15204352 | bytes 2097152 | tf_op jit(solution)/shard_map/outer_first/pallas_call | solution.py:238
  90.5 0.0 collective-permute-done.8.left_ref
  90.5 0.0 collective-permute-done.9.right_ref
  90.5 1.0 mend_edges.3
  91.5 3.6 %collective-permute-start.10 = (f32[4,64,128]{2,1,0:T(8,128)S(1)}, f32[4,64,128]{2,1,0:T(8,128)S(1)}, u32[]{:S(2)}, u32[]{:S(2)}) collective-permute-start(f32[4,64,128]{2,1,0:T(8,128)S(1)} %get-tuple-element.48), channel_id=1, source_target_pairs={{0,1},{1,2},{2,3},{4,5},{5,6},{6,7},{8,9},{9,10},{10,11},{12,13},{... | collective-permute-start | bytes 393224 | tf_op jit(solution)/shard_map/ppermute | solution.py:460
  95.2 1.9 %collective-permute-start.11 = (f32[4,64,128]{2,1,0:T(8,128)S(1)}, f32[4,64,128]{2,1,0:T(8,128)S(1)}, u32[]{:S(2)}, u32[]{:S(2)}) collective-permute-start(f32[4,64,128]{2,1,0:T(8,128)S(1)} %get-tuple-element.48), channel_id=1, source_target_pairs={{1,0},{2,1},{3,2},{5,4},{6,5},{7,6},{9,8},{10,9},{11,10},{13,12},{... | collective-permute-start | bytes 393224 | tf_op jit(solution)/shard_map/ppermute | solution.py:460
  97.1 0.0 copy-done.6
  97.1 0.0 copy-start.4
  97.1 3.6 %spread.1 = (bf16[2048,512]{1,0:T(8,128)(2,1)S(1)}, bf16[2048,512]{1,0:T(8,128)(2,1)S(1)}) custom-call(s32[1,1024]{1,0:T(1,128)S(1)} %bitcast.3, bf16[1024,512]{1,0:T(8,128)(2,1)S(1)} %select_select_fusion.weights_ref), custom_call_target="tpu_custom_call" | custom-call | flops 2147483648 | bytes 6291456 | tf_op jit(solution)/shard_map/spread/pallas_call | solution.py:402
  100.7 0.0 copy-done.4
  100.7 6.3 %second.3.u_ref = f32[4096,128]{1,0:T(8,128)S(1)} custom-call(f32[1024,128]{1,0:T(8,128)S(1)} %get-tuple-element.49.y_low_ref, f32[3072,128]{1,0:T(8,128)S(1)} %get-tuple-element.50.y_mid_ref, f32[1024,128]{1,0:T(8,128)S(1)} %get-tuple-element.51.y_high_ref, f32[4,64,128]{2,1,0:T(8,128)S(1)} %get-tuple-element.52.mend_ref, ...), custom_call_target="tpu_custom_call" | custom-call | flops 30408704 | bytes 4194304 | tf_op jit(solution)/shard_map/second/pallas_call | solution.py:351
  107.0 0.0 collective-permute-done.10.left_ref
  107.0 0.0 collective-permute-done.11.right_ref
  107.0 2.1 %mend_state.3 = (f32[1024,128]{1,0:T(8,128)S(1)}, f32[2048,128]{1,0:T(8,128)S(1)}, f32[1024,128]{1,0:T(8,128)S(1)}) custom-call(f32[4,64,128]{2,1,0:T(8,128)S(1)} %collective-permute-done.10.left_ref, f32[4,64,128]{2,1,0:T(8,128)S(1)} %collective-permute-done.11.right_ref, f32[4,10,128]{2,1,0:T(8,128)S(1)} %edge_weights.1.weight_ref, ...), custom_call_target="tpu_custom_call" | custom-call | tf_op jit(solution)/shard_map/mend_state/pallas_call | solution.py:380
  109.1 3.1 %leave.1 = (f32[16,128,256]{2,1,0:T(8,128)}, f32[512,256]{1,0:T(8,128)S(1)}) custom-call(f32[1024,128]{1,0:T(8,128)S(1)} %get-tuple-element.53.low_ref, f32[2048,128]{1,0:T(8,128)S(1)} %get-tuple-element.54.mid_ref, f32[1024,128]{1,0:T(8,128)S(1)} %get-tuple-element.55.high_ref, bf16[2048,512]{1,0:T(8,128)(2,1)S(1)} %get-tuple-element.56.w_high_ref, ...), custom_call_target="tpu_custom_call" | custom-call | flops 2147483648 | bytes 8388608 | tf_op jit(solution)/shard_map/leave/pallas_call | solution.py:436
  112.3 0.1 reshape.20
  112.4 19.7 %all_to_all.5 = f32[128,4,256]{2,1,0:T(4,128)S(1)} all-to-all(f32[128,4,256]{2,1,0:T(4,128)S(1)} %reshape.20), channel_id=1, replica_groups=mesh['azim'=32,'rad'=4] {'azim','rad'}, dimensions={0} | all-to-all | bytes 1048576 | tf_op jit(solution)/shard_map/all_to_all | solution.py:484
  132.1 0.7 reduce_sum.9
  (2 shorter events, 0.0 us)
Async XLA Ops:
  0.6 1.2 copy-start
  1.8 1.6 %copy-start.5 = (f32[16,128,256]{2,1,0:T(8,128)S(1)}, f32[16,128,256]{2,1,0:T(8,128)}, u32[]{:S(2)}) copy-start(f32[16,128,256]{2,1,0:T(8,128)} %x_ref.1) | copy-start | bytes 6291460
  3.4 10.5 %copy-start.1 = (f32[4,29,16,128]{3,2,1,0:T(8,128)S(1)}, f32[4,29,16,128]{3,2,1,0:T(8,128)}, u32[]{:S(2)}) copy-start(f32[4,29,16,128]{3,2,1,0:T(8,128)} %coef_ref.15) | copy-start | bytes 2850820
  4.3 24.0 %collective-permute-start = (f32[1280,128]{1,0:T(8,128)S(1)}, f32[1280,128]{1,0:T(8,128)S(1)}, u32[]{:S(2)}, u32[]{:S(2)}) collective-permute-start(f32[1280,128]{1,0:T(8,128)S(1)} %get-tuple-element.31.high_ref), channel_id=1, source_target_pairs={{0,4},{1,5},{2,6},{3,7},{4,8},{5,9},{6,10},{7,11},{8,12},{9,13},{1... | collective-permute-start | bytes 1966088 | tf_op jit(solution)/shard_map/ppermute | solution.py:460
  6.5 21.8 %collective-permute-start.1 = (f32[1280,128]{1,0:T(8,128)S(1)}, f32[1280,128]{1,0:T(8,128)S(1)}, u32[]{:S(2)}, u32[]{:S(2)}) collective-permute-start(f32[1280,128]{1,0:T(8,128)S(1)} %get-tuple-element.32.low_ref), channel_id=1, source_target_pairs={{0,124},{1,125},{2,126},{3,127},{4,0},{5,1},{6,2},{7,3},{8,4},{9,5... | collective-permute-start | bytes 1966088 | tf_op jit(solution)/shard_map/ppermute | solution.py:460
  29.2 9.9 %collective-permute-start.2 = (f32[4,64,128]{2,1,0:T(8,128)S(1)}, f32[4,64,128]{2,1,0:T(8,128)S(1)}, u32[]{:S(2)}, u32[]{:S(2)}) collective-permute-start(f32[4,64,128]{2,1,0:T(8,128)S(1)} %halo_edges.2), channel_id=1, source_target_pairs={{0,1},{1,2},{2,3},{4,5},{5,6},{6,7},{8,9},{9,10},{10,11},{12,13},{... | collective-permute-start | bytes 393224 | tf_op jit(solution)/shard_map/ppermute | solution.py:460
  32.5 6.6 %collective-permute-start.3 = (f32[4,64,128]{2,1,0:T(8,128)S(1)}, f32[4,64,128]{2,1,0:T(8,128)S(1)}, u32[]{:S(2)}, u32[]{:S(2)}) collective-permute-start(f32[4,64,128]{2,1,0:T(8,128)S(1)} %halo_edges.2), channel_id=1, source_target_pairs={{1,0},{2,1},{3,2},{5,4},{6,5},{7,6},{9,8},{10,9},{11,10},{13,12},{... | collective-permute-start | bytes 393224 | tf_op jit(solution)/shard_map/ppermute | solution.py:460
  40.1 11.9 %collective-permute-start.4 = (f32[4,64,128]{2,1,0:T(8,128)S(1)}, f32[4,64,128]{2,1,0:T(8,128)S(1)}, u32[]{:S(2)}, u32[]{:S(2)}) collective-permute-start(f32[4,64,128]{2,1,0:T(8,128)S(1)} %get-tuple-element.37), channel_id=1, source_target_pairs={{0,1},{1,2},{2,3},{4,5},{5,6},{6,7},{8,9},{9,10},{10,11},{12,13},{... | collective-permute-start | bytes 393224 | tf_op jit(solution)/shard_map/ppermute | solution.py:460
  43.8 8.2 %collective-permute-start.5 = (f32[4,64,128]{2,1,0:T(8,128)S(1)}, f32[4,64,128]{2,1,0:T(8,128)S(1)}, u32[]{:S(2)}, u32[]{:S(2)}) collective-permute-start(f32[4,64,128]{2,1,0:T(8,128)S(1)} %get-tuple-element.37), channel_id=1, source_target_pairs={{1,0},{2,1},{3,2},{5,4},{6,5},{7,6},{9,8},{10,9},{11,10},{13,12},{... | collective-permute-start | bytes 393224 | tf_op jit(solution)/shard_map/ppermute | solution.py:460
  52.0 11.7 %copy-start.8 = (s32[1024]{0:T(1024)S(1)}, s32[1024]{0:T(1024)}, u32[]{:S(2)}) copy-start(s32[1024]{0:T(1024)} %param.10) | copy-start | bytes 12292
  54.1 1.0 copy-start.2
  55.1 22.3 %collective-permute-start.6 = (f32[1024,128]{1,0:T(8,128)S(1)}, f32[1024,128]{1,0:T(8,128)}, u32[]{:S(2)}, u32[]{:S(2)}) collective-permute-start(f32[1024,128]{1,0:T(8,128)S(1)} %get-tuple-element.42.high_ref), channel_id=1, source_target_pairs={{0,4},{1,5},{2,6},{3,7},{4,8},{5,9},{6,10},{7,11},{8,12},{9,13},{1... | collective-permute-start | bytes 1572872 | tf_op jit(solution)/shard_map/ppermute | solution.py:460
  55.1 22.3 %collective-permute-start.7 = (f32[1024,128]{1,0:T(8,128)S(1)}, f32[1024,128]{1,0:T(8,128)}, u32[]{:S(2)}, u32[]{:S(2)}) collective-permute-start(f32[1024,128]{1,0:T(8,128)S(1)} %get-tuple-element.43.low_ref), channel_id=1, source_target_pairs={{0,124},{1,125},{2,126},{3,127},{4,0},{5,1},{6,2},{7,3},{8,4},{9,5... | collective-permute-start | bytes 1572872 | tf_op jit(solution)/shard_map/ppermute | solution.py:460
  71.5 1.2 copy-start.3
  72.7 12.2 %copy-start.7 = (bf16[1024,512]{1,0:T(8,128)(2,1)S(1)}, bf16[1024,512]{1,0:T(8,128)(2,1)}, u32[]{:S(2)}) copy-start(bf16[1024,512]{1,0:T(8,128)(2,1)} %gather_fusion) | copy-start | bytes 3145732
  79.5 11.0 %collective-permute-start.8 = (f32[4,64,128]{2,1,0:T(8,128)S(1)}, f32[4,64,128]{2,1,0:T(8,128)S(1)}, u32[]{:S(2)}, u32[]{:S(2)}) collective-permute-start(f32[4,64,128]{2,1,0:T(8,128)S(1)} %halo_edges.3), channel_id=1, source_target_pairs={{0,1},{1,2},{2,3},{4,5},{5,6},{6,7},{8,9},{9,10},{10,11},{12,13},{... | collective-permute-start | bytes 393224 | tf_op jit(solution)/shard_map/ppermute | solution.py:460
  83.0 7.5 %collective-permute-start.9 = (f32[4,64,128]{2,1,0:T(8,128)S(1)}, f32[4,64,128]{2,1,0:T(8,128)S(1)}, u32[]{:S(2)}, u32[]{:S(2)}) collective-permute-start(f32[4,64,128]{2,1,0:T(8,128)S(1)} %halo_edges.3), channel_id=1, source_target_pairs={{1,0},{2,1},{3,2},{5,4},{6,5},{7,6},{9,8},{10,9},{11,10},{13,12},{... | collective-permute-start | bytes 393224 | tf_op jit(solution)/shard_map/ppermute | solution.py:460
  85.7 11.4 %copy-start.6 = (s32[1024]{0:T(1024)S(1)}, s32[1024]{0:T(1024)}, u32[]{:S(2)}) copy-start(s32[1024]{0:T(1024)} %param.8) | copy-start | bytes 12292
  91.5 15.5 %collective-permute-start.10 = (f32[4,64,128]{2,1,0:T(8,128)S(1)}, f32[4,64,128]{2,1,0:T(8,128)S(1)}, u32[]{:S(2)}, u32[]{:S(2)}) collective-permute-start(f32[4,64,128]{2,1,0:T(8,128)S(1)} %get-tuple-element.48), channel_id=1, source_target_pairs={{0,1},{1,2},{2,3},{4,5},{5,6},{6,7},{8,9},{9,10},{10,11},{12,13},{... | collective-permute-start | bytes 393224 | tf_op jit(solution)/shard_map/ppermute | solution.py:460
  95.2 11.8 %collective-permute-start.11 = (f32[4,64,128]{2,1,0:T(8,128)S(1)}, f32[4,64,128]{2,1,0:T(8,128)S(1)}, u32[]{:S(2)}, u32[]{:S(2)}) collective-permute-start(f32[4,64,128]{2,1,0:T(8,128)S(1)} %get-tuple-element.48), channel_id=1, source_target_pairs={{1,0},{2,1},{3,2},{5,4},{6,5},{7,6},{9,8},{10,9},{11,10},{13,12},{... | collective-permute-start | bytes 393224 | tf_op jit(solution)/shard_map/ppermute | solution.py:460
  97.1 3.6 %copy-start.4 = (f32[2048,128]{1,0:T(8,128)S(1)}, f32[2048,128]{1,0:T(8,128)}, u32[]{:S(2)}) copy-start(f32[2048,128]{1,0:T(8,128)} %copy-done.2) | copy-start | bytes 3145732

commit v3 on v2

--- a/solution.py
+++ b/solution.py
@@ -1,3 +1,5 @@
+import functools
+
 import jax
 import jax.numpy as jnp
 from jax import lax
@@ -38,6 +40,7 @@
 
 ROWS = 256
 TAIL = 4 * ROWS
+COEF = 2 * ROWS
 
 
 def window(ref, row, var, half):
@@ -62,6 +65,13 @@
     base = 4 * (row + 4)
     here = (lane >= base) & (lane < base + 4)
     return jnp.where(here, pltpu.roll(value, (base + 2) % 128, axis=1), pack)
+
+
+def place_far(pack, row, value):
+    lane = lanes(value.shape)
+    base = 4 * (row + 4)
+    pack = jnp.where((lane >= base) & (lane < base + 2), pltpu.roll(value, (base + 4) % 128, axis=1), pack)
+    return jnp.where((lane >= base + 2) & (lane < base + 4), pltpu.roll(value, base, axis=1), pack)
 
 
 def unplace(pack, row):
@@ -137,12 +147,10 @@
     )(x, coef)
 
 
-def inner_first(low_ref, mid_ref, high_ref, coef_ref, y_ref, edge_y_ref, edge_u_ref, shift_ref):
+def inner_first(low_ref, mid_ref, high_ref, coef_ref, y_ref, edge_ref, shift_ref):
     parts = ((0, 4, low_ref), (4, 12, mid_ref), (12, 16, high_ref))
 
     def one(var, half):
-        at = pl.ds(pl.multiple_of(half * 32, 32), 32)
-
         def finish(row, total):
             for w in range(4):
                 total = total + line_of(coef_ref, var, 25 + w, row) * pick(parts, row, w, half)
@@ -152,14 +160,13 @@
             2, 14, lambda s: pick(parts, s, var, half),
             lambda k, row: line_of(coef_ref, var, k, row), finish, shift_ref,
         )
-        pack = jnp.zeros((32, 128), F32)
+        near = jnp.zeros((32, 128), F32)
+        far = jnp.zeros((32, 128), F32)
         for row in range(16):
-            pack = place(pack, row, pick(parts, row, var, half))
-        edge_u_ref[var, at] = pack
-        pack = jnp.zeros((32, 128), F32)
-        for row in range(2, 14):
-            pack = place(pack, row, window(y_ref, row - 2, var, half))
-        edge_y_ref[var, at] = pack
+            value = pick(parts, row, var, half)
+            near, far = place(near, row, value), place_far(far, row, value)
+        put(edge_ref, 0, var, half, near)
+        put(edge_ref, 1, var, half, far)
 
     each_part(one)
 
@@ -168,8 +175,8 @@
     return pl.pallas_call(
         inner_first,
         in_specs=whole(4),
-        out_specs=whole(3),
-        out_shape=arrays((12 * ROWS, 128), (4, 64, 128), (4, 64, 128)),
+        out_specs=whole(2),
+        out_shape=arrays((12 * ROWS, 128), (2 * ROWS, 128)),
         scratch_shapes=[pltpu.VMEM((4, 16, 32, 128), F32)],
         compiler_params=params(),
         cost_estimate=cost(12),
@@ -177,36 +184,67 @@
     )(low, mid, high, coef)
 
 
-def halo_edges(top_ref, bot_ref, edge_ref, out_ref):
+def coef_edges(coef_ref, out_ref):
+    out_ref[...] = jnp.zeros_like(out_ref)
+    for var in range(4):
+        pack = jnp.zeros((29, 128), F32)
+        for row in range(16):
+            pack = place(pack, row, coef_ref[pl.ds(var * 464 + row, 29, stride=16), :])
+        out_ref[32 * var : 32 * var + 29] = pack
+
+
+def call_coef_edges(coef):
+    return pl.pallas_call(
+        coef_edges,
+        in_specs=whole(1),
+        out_specs=whole(1)[0],
+        out_shape=arrays((128, 128))[0],
+        compiler_params=params(),
+        name="coef_edges",
+    )(coef.reshape(-1, 128))
+
+
+def halo_edges(top_ref, bot_ref, edge_ref, *refs):
+    out_ref = refs[-1]
+
     def one(var, half):
-        at = pl.ds(pl.multiple_of(half * 32, 32), 32)
-        pack = edge_ref[var, at]
+        near = window(edge_ref, 0, var, half)
+        far = window(edge_ref, 1, var, half)
         for k in range(4):
-            pack = place(pack, k - 4, window(top_ref, k, var, half))
-            pack = place(pack, k + 16, window(bot_ref, k, var, half))
-        out_ref[var, at] = pack
+            for row, ref in ((k - 4, top_ref), (k + 16, bot_ref)):
+                value = window(ref, k, var, half)
+                near, far = place(near, row, value), place_far(far, row, value)
+        put(out_ref, 0, var, half, near)
+        put(out_ref, 1, var, half, far)
 
     each_part(one)
-
-
-def call_halo_edges(top, bot, edge):
+    if len(refs) == 2:
+        for var in range(4):
+            pack = refs[0][32 * var : 32 * var + 29]
+            for k in range(2):
+                lines = pl.ds(TAIL + 64 * var + k, 29, stride=2)
+                pack = place(pack, k - 2, top_ref[lines, :])
+                pack = place(pack, k + 16, bot_ref[lines, :])
+            out_ref[COEF + 32 * var : COEF + 32 * var + 29] = pack
+            out_ref[COEF + 32 * var + 29 : COEF + 32 * var + 32] = jnp.zeros((3, 128), F32)
+
+
+def call_halo_edges(top, bot, edge, *coef_edge):
     return pl.pallas_call(
         halo_edges,
-        in_specs=whole(3),
+        in_specs=whole(3 + len(coef_edge)),
         out_specs=whole(1)[0],
-        out_shape=arrays((4, 64, 128))[0],
+        out_shape=arrays((COEF + 128 * len(coef_edge), 128))[0],
         compiler_params=params(),
         name="halo_edges",
-    )(top, bot, edge)
-
-
-def outer_first(top_ref, low_ref, high_ref, bot_ref, coef_ref, ctop_ref, cbot_ref, edge_ref,
-                y_low_ref, y_high_ref, edge_y_ref, shift_ref):
+    )(top, bot, edge, *coef_edge)
+
+
+def outer_first(top_ref, low_ref, high_ref, bot_ref, coef_ref, ctop_ref, cbot_ref,
+                y_low_ref, y_high_ref, shift_ref):
     parts = ((-4, 0, top_ref), (0, 4, low_ref), (12, 16, high_ref), (16, 20, bot_ref))
 
     def one(var, half):
-        at = pl.ds(pl.multiple_of(half * 32, 32), 32)
-
         def weight(k, row):
             if row < 0:
                 return tail_line(ctop_ref, var, k, row + 2)
@@ -225,167 +263,143 @@
 
         for first in (-2, 14):
             sweep(first, first + 4, lambda s: pick(parts, s, var, half), weight, finish, shift_ref)
-        pack = edge_ref[var, at]
-        for k in range(4):
-            pack = place(pack, k - 2, window(y_low_ref, k, var, half))
-            pack = place(pack, k + 14, window(y_high_ref, k, var, half))
-        edge_y_ref[var, at] = pack
 
     each_part(one)
 
 
-def call_outer_first(top, low, high, bot, coef, ctop, cbot, edge):
+def call_outer_first(top, low, high, bot, coef, ctop, cbot):
     return pl.pallas_call(
         outer_first,
-        in_specs=whole(8),
-        out_specs=whole(3),
-        out_shape=arrays((4 * ROWS, 128), (4 * ROWS, 128), (4, 64, 128)),
+        in_specs=whole(7),
+        out_specs=whole(2),
+        out_shape=arrays((4 * ROWS, 128), (4 * ROWS, 128)),
         scratch_shapes=[pltpu.VMEM((4, 8, 32, 128), F32)],
         compiler_params=params(),
         cost_estimate=cost(8),
         name="outer_first",
-    )(top, low, high, bot, coef, ctop, cbot, edge)
-
-
-def edge_weights(coef_ref, ctop_ref, cbot_ref, out_ref):
-    lane = lanes((1, 128))
-    inner = (lane % 4 == 1) | (lane % 4 == 2)
+    )(top, low, high, bot, coef, ctop, cbot)
+
+
+def strips(left_ref, right_ref, own_ref, coef_left_ref, coef_right_ref, coef_own_ref,
+           mend_y_ref, mend_u_ref, rim_ref):
+    entry = lanes((64, 128)) % 4
+    entry_line = lanes((32, 128)) % 4
+
+    def merge(entry, left, right):
+        return jnp.where(entry < 2, pltpu.roll(right, 126, axis=1), pltpu.roll(left, 2, axis=1))
+
+    def rows_on(pack, i):
+        turn = (4 * (2 - i)) % 128
+        return pltpu.roll(pack, turn, axis=1) if turn else pack
+
+    def pack_at(ref, kind, var):
+        return ref[pl.ds(pl.multiple_of(kind * ROWS + var * 64, 64), 64), :]
 
     @pl.loop(0, 4)
     def _(var):
-        top = ctop_ref.at[pl.ds(pl.multiple_of(TAIL + var * 64, 64), 64)]
-        bot = cbot_ref.at[pl.ds(pl.multiple_of(TAIL + var * 64, 64), 64)]
-
-        def line(k, row):
-            if row < 0:
-                return top[2 * k + row + 2 : 2 * k + row + 3]
-            if row < 16:
-                return coef_ref[var, k, row : row + 1]
-            return bot[2 * k + row - 16 : 2 * k + row - 15]
-
-        for i in range(5):
-            far = jnp.zeros((1, 128), F32)
-            near = jnp.zeros((1, 128), F32)
-            for row in range(-2, 18):
-                far = place(far, row, jnp.where(lane < 64, line(5 * i, row), line(5 * i + 4, row)))
-                near = place(near, row, jnp.where(lane < 64, line(5 * i + 1, row), line(5 * i + 3, row)))
-            out_ref[var, i : i + 1] = far
-            out_ref[var, 5 + i : 6 + i] = jnp.where(inner, near, 0.0)
-
-
-def call_edge_weights(coef, ctop, cbot):
-    return pl.pallas_call(
-        edge_weights,
-        in_specs=whole(3),
-        out_specs=whole(1)[0],
-        out_shape=arrays((4, 10, 128))[0],
-        compiler_params=params(),
-        name="edge_weights",
-    )(coef, ctop, cbot)
-
-
-def beyond(left_ref, right_ref, weight_ref, var):
-    lane = lanes((64, 128)) % 4
-    rim = jnp.where(
-        lane < 2, pltpu.roll(right_ref[var], 126, axis=1), pltpu.roll(left_ref[var], 2, axis=1)
-    )
-    other = jnp.where(lane == 1, pltpu.roll(rim, 1, axis=1), pltpu.roll(rim, 127, axis=1))
-    total = jnp.zeros((64, 128), F32)
-    for i in range(5):
-        turn = (4 * (2 - i)) % 128
-        far, near = rim, other
-        if turn:
-            far, near = pltpu.roll(rim, turn, axis=1), pltpu.roll(other, turn, axis=1)
-        total = total + weight_ref[var, i : i + 1] * far
-        total = total + weight_ref[var, 5 + i : 6 + i] * near
-    return total
-
-
-def mend_edges(left_ref, right_ref, weight_ref, edge_ref, out_ref, mend_ref):
+        rim_ref[var] = merge(entry, pack_at(left_ref, 0, var), pack_at(right_ref, 0, var))
+
     @pl.loop(0, 4)
     def _(var):
-        mend = 0.5 * beyond(left_ref, right_ref, weight_ref, var)
-        mend_ref[var] = mend
-        out_ref[var] = edge_ref[var] + mend
-
-
-def call_mend_edges(left, right, weights, edge):
-    return pl.pallas_call(
-        mend_edges,
-        in_specs=whole(4),
+        near = pack_at(own_ref, 0, var)
+        rim = rim_ref[var]
+        outer = merge(entry, pack_at(left_ref, 1, var), pack_at(right_ref, 1, var))
+        lines = pl.ds(pl.multiple_of(COEF + var * 32, 32), 32)
+        own = coef_own_ref[lines, :]
+        other = merge(entry_line, coef_left_ref[lines, :], coef_right_ref[lines, :])
+
+        def beyond(rim):
+            crossed = jnp.where(entry == 1, pltpu.roll(rim, 1, axis=1), pltpu.roll(rim, 127, axis=1))
+            total = jnp.zeros((64, 128), F32)
+            for i in range(5):
+                two = jnp.where(entry_line[0:1] < 2, own[5 * i + 4 : 5 * i + 5], own[5 * i : 5 * i + 1])
+                one = jnp.where(entry_line[0:1] == 1, own[5 * i + 3 : 5 * i + 4], 0.0)
+                one = jnp.where(entry_line[0:1] == 2, own[5 * i + 1 : 5 * i + 2], one)
+                total = total + two * rows_on(rim, i) + one * rows_on(crossed, i)
+            return total
+
+        before = jnp.where(
+            entry == 0, pltpu.roll(near, 127, axis=1),
+            jnp.where(entry == 2, pltpu.roll(outer, 127, axis=1), pltpu.roll(rim, 1, axis=1)),
+        )
+        after = jnp.where(
+            entry == 1, pltpu.roll(outer, 1, axis=1),
+            jnp.where(entry == 3, pltpu.roll(near, 1, axis=1), pltpu.roll(rim, 127, axis=1)),
+        )
+        shifted = (
+            jnp.where(entry < 2, near, outer), before, rim, after, jnp.where(entry < 2, outer, near),
+        )
+        total = jnp.zeros((64, 128), F32)
+        for i in range(5):
+            for j in range(5):
+                k = 5 * i + j
+                total = total + other[k : k + 1] * rows_on(shifted[j], i)
+        for w in range(4):
+            total = total + other[25 + w : 26 + w] * rim_ref[w]
+        mend_y_ref[var] = 0.5 * beyond(rim)
+        mend_u_ref[var] = beyond(rim + 0.5 * total)
+
+
+def call_strips(left, right, own, coef_left, coef_right, coef_own):
+    return pl.pallas_call(
+        strips,
+        in_specs=whole(6),
         out_specs=whole(2),
         out_shape=arrays((4, 64, 128), (4, 64, 128)),
-        compiler_params=params(),
-        name="mend_edges",
-    )(left, right, weights, edge)
-
-
-def second(y_low_ref, y_mid_ref, y_high_ref, mend_ref, low_ref, mid_ref, high_ref, coef_ref,
-           out_ref, y_ref, shift_ref):
-    y_parts = ((-2, 2, y_low_ref), (2, 14, y_mid_ref), (14, 18, y_high_ref))
-    u_parts = ((0, 4, low_ref), (4, 12, mid_ref), (12, 16, high_ref))
+        scratch_shapes=[pltpu.VMEM((4, 64, 128), F32)],
+        compiler_params=params(),
+        name="strips",
+    )(left, right, own, coef_left, coef_right, coef_own)
+
+
+def second(ranges, n_y, *refs):
+    y_refs, refs = refs[:n_y], refs[n_y:]
+    mend_y_ref, mend_u_ref, coef_ref = refs[:3]
+    u_refs, refs = refs[3 : 3 + len(ranges)], refs[3 + len(ranges) :]
+    out_refs, refs = refs[: len(ranges)], refs[len(ranges) :]
+    y_ref, shift_ref = refs
+    bounds = {1: ((2, 14),), 3: ((-2, 2), (2, 14), (14, 18))}[n_y]
+    y_parts = [(first, stop, ref) for (first, stop), ref in zip(bounds, y_refs)]
+    sources = sorted({s for first, stop in ranges for s in range(first - 2, stop + 2)})
     whole_y = ((-2, 18, y_ref),)
 
     def mend(var, half):
-        pack = mend_ref[var, pl.ds(pl.multiple_of(half * 32, 32), 32)]
-        for row in range(-2, 18):
+        pack = mend_y_ref[var, pl.ds(pl.multiple_of(half * 32, 32), 32)]
+        for row in sources:
             put(y_ref, row + 2, var, half, pick(y_parts, row, var, half) + unplace(pack, row))
 
     each_part(mend)
 
     def one(var, half):
-        def finish(row, total):
-            for w in range(4):
-                total = total + line_of(coef_ref, var, 25 + w, row) * pick(whole_y, row, w, half)
-            put(out_ref, row, var, half, pick(u_parts, row, var, half) + total)
-
-        sweep(
-            0, 16, lambda s: pick(whole_y, s, var, half),
-            lambda k, row: line_of(coef_ref, var, k, row), finish, shift_ref,
-        )
+        pack = mend_u_ref[var, pl.ds(pl.multiple_of(half * 32, 32), 32)]
+        for (first, stop), u_ref, out_ref in zip(ranges, u_refs, out_refs):
+
+            def finish(row, total):
+                for w in range(4):
+                    total = total + line_of(coef_ref, var, 25 + w, row) * pick(whole_y, row, w, half)
+                total = total + unplace(pack, row)
+                put(out_ref, row - first, var, half, window(u_ref, row - first, var, half) + total)
+
+            sweep(
+                first, stop, lambda s: pick(whole_y, s, var, half),
+                lambda k, row: line_of(coef_ref, var, k, row), finish, shift_ref,
+            )
 
     each_part(one)
 
 
-def call_second(y_low, y_mid, y_high, mend, low, mid, high, coef):
-    return pl.pallas_call(
-        second,
-        in_specs=whole(8),
-        out_specs=whole(1)[0],
-        out_shape=arrays((16 * ROWS, 128))[0],
-        scratch_shapes=[pltpu.VMEM((20 * ROWS, 128), F32), pltpu.VMEM((4, 20, 32, 128), F32)],
-        compiler_params=params(),
-        cost_estimate=cost(16),
+def call_second(ranges, ys, mend_y, mend_u, coef, us):
+    outs = [((stop - first) * ROWS, 128) for first, stop in ranges]
+    return pl.pallas_call(
+        functools.partial(second, ranges, len(ys)),
+        in_specs=whole(len(ys) + 3 + len(us)),
+        out_specs=whole(len(us)),
+        out_shape=arrays(*outs),
+        scratch_shapes=[pltpu.VMEM((20 * ROWS, 128), F32), pltpu.VMEM((4, 12, 32, 128), F32)],
+        compiler_params=params(),
+        cost_estimate=cost(8),
         name="second",
-    )(y_low, y_mid, y_high, mend, low, mid, high, coef)
-
-
-def mend_state(left_ref, right_ref, weight_ref, u_ref, low_ref, mid_ref, high_ref, mend_ref):
-    @pl.loop(0, 4)
-    def _(var):
-        mend_ref[var] = beyond(left_ref, right_ref, weight_ref, var)
-
-    def one(var, half):
-        pack = mend_ref[var, pl.ds(pl.multiple_of(half * 32, 32), 32)]
-        for row in range(16):
-            value = window(u_ref, row, var, half) + unplace(pack, row)
-            for first, stop, ref in ((0, 4, low_ref), (4, 12, mid_ref), (12, 16, high_ref)):
-                if first <= row < stop:
-                    put(ref, row - first, var, half, value)
-
-    each_part(one)
-
-
-def call_mend_state(left, right, weights, u):
-    return pl.pallas_call(
-        mend_state,
-        in_specs=whole(4),
-        out_specs=whole(3),
-        out_shape=arrays((4 * ROWS, 128), (8 * ROWS, 128), (4 * ROWS, 128)),
-        scratch_shapes=[pltpu.VMEM((4, 64, 128), F32)],
-        compiler_params=params(),
-        name="mend_state",
-    )(left, right, weights, u)
+    )(*ys, mend_y, mend_u, coef, *us)
 
 
 def spread(cells_ref, weights_ref, high_ref, low_ref):
@@ -465,20 +479,27 @@
     w_high, w_low = call_spread(wall_cells.reshape(1, slots), weights)
 
     low, mid, high = call_enter(perturbation_in, coefficients)
-    tails = None
+    tails = edge_coef = None
     for step in range(STEPS):
         top, bot = send(high, 1, 0), send(low, -1, 0)
-        if tails is None:
+        y_mid, edge = call_inner_first(low, mid, high, coefficients)
+        if step == 0:
             tails = top, bot
-            edge_w = call_edge_weights(coefficients, *tails)
-        y_mid, edge_y, edge_u = call_inner_first(low, mid, high, coefficients)
-        edge_u = call_halo_edges(top, bot, edge_u)
-        left, right = send(edge_u, 0, 1), send(edge_u, 0, -1)
-        y_low, y_high, edge_y = call_outer_first(top, low, high, bot, coefficients, *tails, edge_y)
-        edge_y, mend = call_mend_edges(left, right, edge_w, edge_y)
-        left, right = send(edge_y, 0, 1), send(edge_y, 0, -1)
-        u = call_second(y_low, y_mid, y_high, mend, low, mid, high, coefficients)
-        low, mid, high = call_mend_state(left, right, edge_w, u)
+            extra = (call_coef_edges(coefficients),)
+            edge, w_high = lax.optimization_barrier((edge, w_high))
+        else:
+            extra = ()
+        own = call_halo_edges(top, bot, edge, *extra)
+        left, right = send(own, 0, 1), send(own, 0, -1)
+        if step == 0:
+            edge_coef = left, right, own
+        y_low, y_high = call_outer_first(top, low, high, bot, coefficients, *tails)
+        mends = call_strips(left, right, own, *edge_coef)
+        new_low, new_high = call_second(
+            ((0, 4), (12, 16)), (y_low, y_mid, y_high), *mends, coefficients, (low, high)
+        )
+        (mid,) = call_second(((4, 12),), (y_mid,), *mends, coefficients, (mid,))
+        low, high = new_low, new_high
     out, term = call_leave(low, mid, high, w_high, w_low)
     count = n_azim * n_rad
     parts = lax.all_to_all(term.reshape(count, -1, term.shape[1]), ("azim", "rad"), 0, 0)

time: 133 us -> 125 us (0.940)
  starting transfers between devices: 39.3 us -> 27.9 us
  waiting for transfers between devices: 9.76 us -> 3.53 us
  Pallas kernels: 47.9 us -> 52.6 us
  blocking collectives: 19.7 us -> 23.3 us
    ppermute x12 -> x8, starting transfers between devices: 39.3 us -> 27.9 us  [send(): return lax.ppermute(block, ('azim', 'rad'), shifts(n_azim, n_rad, da, dr))]
    ppermute x12 -> x8, waiting for transfers between devices: 9.76 us -> 3.53 us  [send(): return lax.ppermute(block, ('azim', 'rad'), shifts(n_azim, n_rad, da, dr))]
    pallas_call x13, Pallas kernels: 40.4 us -> 44.2 us  [the longest x4 17.5 us: call_second(): pl.pallas_call(functools.partial(second, ranges, len(ys)), in_specs=whole...]
    all_to_all x1, blocking collectives: 19.7 us -> 23.3 us  [body(): lax.all_to_all(term.reshape(count, -1, term.shape[1]), ('azim', 'rad'), 0...]
  transfers between devices with their start and end apart: 12 -> 8, of which waited for: 1 -> 2; matrix products, arithmetic and copies ran while one was open for 7% -> 8% of each run, Pallas kernels for 26% -> 21%
where the time goes in v3:
time: 125 us; the launch traced here: 124 us
  Pallas kernels  52.6 us (42%)
  starting transfers between devices  27.9 us (22%)
  blocking collectives  23.3 us (19%)
  local copies, waits for them, and re-layouts  12.9 us (10%)
  waiting for transfers between devices  3.53 us (3%)
  other arithmetic  2.6 us (2%)
  between operations  1.55 us (1%)
    ppermute x8, starting transfers between devices, send(): return lax.ppermute(block, ('azim', 'rad'), shifts(n_azim, n_rad, da, dr))  27.9 us
    all_to_all x1, blocking collectives, body(): lax.all_to_all(term.reshape(count, -1, term.shape[1]), ('azim', 'rad'), 0...  23.3 us
    pallas_call x4, Pallas kernels, call_second(): pl.pallas_call(functools.partial(second, ranges, len(ys)), in_specs=whole...  17.5 us
    pallas_call x2, Pallas kernels, call_inner_first(): pl.pallas_call(inner_first, in_specs=whole(4), out_specs=whole(2), out_sh...  11.3 us
    gather x1, local copies, waits for them, and re-layouts, body(): jnp.take(mode_table, mode_row, axis=0)  7.83 us
    pallas_call x2, Pallas kernels, call_outer_first(): pl.pallas_call(outer_first, in_specs=whole(7), out_specs=whole(2), out_sh...  7.02 us
    pallas_call x2, Pallas kernels, call_strips(): pl.pallas_call(strips, in_specs=whole(6), out_specs=whole(2), out_shape=a...  5.2 us
    unnamed x18, local copies, waits for them, and re-layouts  4.95 us
  transfers between devices with their start and end apart: 8, of which 2 were waited for; matrix products, arithmetic and copies ran while one was open for 8% of the time, Pallas kernels for 21%

profile of v3, /device:TPU:1, one launch (start us, length us, event | category | flops | bytes accessed | tf_op | source)
XLA Modules:
  0.0 124.4 jit_solution(16960839076886098114)
XLA Ops:
  0.6 0.0 copy-start
  0.6 1.2 copy-done
  1.8 0.0 copy-start.6
  1.8 1.6 %copy-done.6 = f32[16,128,256]{2,1,0:T(8,128)S(1)} copy-done((f32[16,128,256]{2,1,0:T(8,128)S(1)}, f32[16,128,256]{2,1,0:T(8,128)}, u32[]{:S(2)}) %copy-start.6) | copy-done | bytes 2097176
  3.4 0.0 copy-start.8
  3.4 0.0 copy-start.1
  3.4 1.7 %enter.1 = (f32[1280,128]{1,0:T(8,128)S(1)}, f32[2048,128]{1,0:T(8,128)S(1)}, f32[1280,128]{1,0:T(8,128)}) custom-call(f32[16,128,256]{2,1,0:T(8,128)S(1)} %copy-done.6, f32[4,29,16,128]{3,2,1,0:T(8,128)S(1)} %copy-done), custom_call_target="tpu_custom_call" | custom-call | tf_op jit(solution)/shard_map/enter/pallas_call | solution.py:140
  5.1 2.1 %collective-permute-start = (f32[1280,128]{1,0:T(8,128)}, f32[1280,128]{1,0:T(8,128)S(1)}, u32[]{:S(2)}, u32[]{:S(2)}) collective-permute-start(f32[1280,128]{1,0:T(8,128)} %get-tuple-element.27.high_ref.refs_7_), channel_id=1, source_target_pairs={{0,4},{1,5},{2,6},{3,7},{4,8},{5,9},{6,10},{7,11},{8,12},{9,13},{1... | collective-permute-start | bytes 1966088 | tf_op jit(solution)/shard_map/ppermute | solution.py:474
  7.2 7.4 %collective-permute-start.1 = (f32[1280,128]{1,0:T(8,128)S(1)}, f32[1280,128]{1,0:T(8,128)S(1)}, u32[]{:S(2)}, u32[]{:S(2)}) collective-permute-start(f32[1280,128]{1,0:T(8,128)S(1)} %get-tuple-element.28.low_ref.refs_6_), channel_id=1, source_target_pairs={{0,124},{1,125},{2,126},{3,127},{4,0},{5,1},{6,2},{7,3},{8,4},{9,5... | collective-permute-start | bytes 1966088 | tf_op jit(solution)/shard_map/ppermute | solution.py:474
  15.3 0.0 copy-done.8
  15.3 0.4 coef_edges.1.refs_0_
  15.6 0.0 copy-done.1
  15.6 6.2 %inner_first.2 = (f32[3072,128]{1,0:T(8,128)S(1)}, f32[512,128]{1,0:T(8,128)S(1)}) custom-call(f32[1280,128]{1,0:T(8,128)S(1)} %get-tuple-element.28.low_ref.refs_6_, f32[2048,128]{1,0:T(8,128)S(1)} %get-tuple-element.30.mid_ref.refs_4_, f32[1280,128]{1,0:T(8,128)} %get-tuple-element.27.high_ref.refs_7_, f32[4,29,16,128]{3,2,1,0:T(8,128)S(1)} %copy-done.1), custom_call_target="tpu_custom_call" | custom-call | flops 22806528 | bytes 3145728 | tf_op jit(solution)/shard_map/inner_first/pallas_call | solution.py:175
  21.8 0.0 copy-start.2
  21.9 1.1 copy-done.2
  23.0 0.0 copy-start.4
  23.0 1.0 copy-done.4
  24.0 7.8 %gather_fusion = bf16[1024,512]{1,0:T(8,128)(2,1)} fusion(bf16[4096,512]{1,0:T(8,128)(2,1)} %param.11, s32[1024]{0:T(1024)S(1)} %fusion), kind=kCustom, calls=%fused_computation | custom fusion | bytes 2101248 | tf_op jit(solution)/shard_map/jit(_take)/gather | solution.py:478
  31.8 0.0 copy-start.7
  31.9 1.9 %select_select_fusion.weights_ref = bf16[1024,512]{1,0:T(8,128)(2,1)S(1)} fusion(bf16[1024,512]{1,0:T(8,128)(2,1)} %gather_fusion, pred[1024]{0:T(1024)(128)(4,1)S(1)} %get-tuple-element.53, pred[1024]{0:T(1024)(128)(4,1)S(1)} %get-tuple-element.52), kind=kLoop, calls=%fused_computation.1 | loop fusion | flops 1048576 | bytes 2099200 | tf_op jit(solution)/shard_map/jit(_where)/select_n | solution.py:478
  33.7 0.0 copy-done.7
  33.7 3.6 %spread.1 = (bf16[2048,512]{1,0:T(8,128)(2,1)S(1)}, bf16[2048,512]{1,0:T(8,128)(2,1)S(1)}) custom-call(s32[1,1024]{1,0:T(1,128)S(1)} %bitcast.5, bf16[1024,512]{1,0:T(8,128)(2,1)S(1)} %select_select_fusion.weights_ref), custom_call_target="tpu_custom_call" | custom-call | flops 2147483648 | bytes 6291456 | tf_op jit(solution)/shard_map/spread/pallas_call | solution.py:416
  37.3 0.0 collective-permute-done.top_ref.ctop_ref
  37.3 0.0 collective-permute-done.1.bot_ref.cbot_ref
  37.3 1.5 %halo_edges.2.own_ref.coef_own_ref = f32[640,128]{1,0:T(8,128)S(1)} custom-call(f32[1280,128]{1,0:T(8,128)S(1)} %collective-permute-done.top_ref.ctop_ref, f32[1280,128]{1,0:T(8,128)S(1)} %collective-permute-done.1.bot_ref.cbot_ref, f32[512,128]{1,0:T(8,128)S(1)} %get-tuple-element.35.edge_ref, f32[128,128]{1,0:T(8,128)S(1)} %coef_edges.1.refs_0_), custom_call_target="tpu_custom_call" | custom-call | tf_op jit(solution)/shard_map/halo_edges/pallas_call | solution.py:233
  38.8 2.9 %collective-permute-start.3 = (f32[640,128]{1,0:T(8,128)S(1)}, f32[640,128]{1,0:T(8,128)S(1)}, u32[]{:S(2)}, u32[]{:S(2)}) collective-permute-start(f32[640,128]{1,0:T(8,128)S(1)} %halo_edges.2.own_ref.coef_own_ref), channel_id=1, source_target_pairs={{1,0},{2,1},{3,2},{5,4},{6,5},{7,6},{9,8},{10,9},{11,10},{13,12},{... | collective-permute-start | bytes 983048 | tf_op jit(solution)/shard_map/ppermute | solution.py:474
  41.7 2.7 %collective-permute-start.2 = (f32[640,128]{1,0:T(8,128)S(1)}, f32[640,128]{1,0:T(8,128)S(1)}, u32[]{:S(2)}, u32[]{:S(2)}) collective-permute-start(f32[640,128]{1,0:T(8,128)S(1)} %halo_edges.2.own_ref.coef_own_ref), channel_id=1, source_target_pairs={{0,1},{1,2},{2,3},{4,5},{5,6},{6,7},{8,9},{9,10},{10,11},{12,13},{... | collective-permute-start | bytes 983048 | tf_op jit(solution)/shard_map/ppermute | solution.py:474
  44.4 4.1 %outer_first.2 = (f32[1024,128]{1,0:T(8,128)S(1)}, f32[1024,128]{1,0:T(8,128)S(1)}) custom-call(f32[1280,128]{1,0:T(8,128)S(1)} %collective-permute-done.top_ref.ctop_ref, f32[1280,128]{1,0:T(8,128)S(1)} %get-tuple-element.28.low_ref.refs_6_, f32[1280,128]{1,0:T(8,128)} %get-tuple-element.27.high_ref.refs_7_, ...), custom_call_target="tpu_custom_call" | custom-call | flops 15204352 | bytes 2097152 | tf_op jit(solution)/shard_map/outer_first/pallas_call | solution.py:271
  48.5 0.0 copy-start.3
  48.5 0.0 collective-permute-done.3.right_ref.coef_right_ref
  48.5 0.0 collective-permute-done.2.left_ref.coef_left_ref
  48.5 2.6 %strips.2 = (f32[4,64,128]{2,1,0:T(8,128)S(1)}, f32[4,64,128]{2,1,0:T(8,128)S(1)}) custom-call(f32[640,128]{1,0:T(8,128)S(1)} %collective-permute-done.2.left_ref.coef_left_ref, f32[640,128]{1,0:T(8,128)S(1)} %collective-permute-done.3.right_ref.coef_right_ref, f32[640,128]{1,0:T(8,128)S(1)} %halo_edges.2.own_ref.coef_own_ref, ...), custom_call_target="tpu_custom_call" | custom-call | tf_op jit(solution)/shard_map/strips/pallas_call | solution.py:344
  51.1 0.0 copy-done.3
  51.1 0.0 copy-start.5
  51.1 5.4 %second.4 = (f32[1024,128]{1,0:T(8,128)S(1)}, f32[1024,128]{1,0:T(8,128)S(1)}) custom-call(f32[1024,128]{1,0:T(8,128)S(1)} %get-tuple-element.29.refs_0_, f32[3072,128]{1,0:T(8,128)S(1)} %copy-done.3, f32[1024,128]{1,0:T(8,128)S(1)} %get-tuple-element.32.refs_2_, f32[4,64,128]{2,1,0:T(8,128)S(1)} %get-tuple-element.36.refs_3_.refs_1_, ...), custom_call_target="tpu_custom_call" | custom-call | flops 15204352 | bytes 2097152 | tf_op jit(solution)/shard_map/second/pallas_call | solution.py:393
  56.5 0.1 collective-permute-start.4
  56.6 7.2 %collective-permute-start.5 = (f32[1024,128]{1,0:T(8,128)S(1)}, f32[1024,128]{1,0:T(8,128)S(1)}, u32[]{:S(2)}, u32[]{:S(2)}) collective-permute-start(f32[1024,128]{1,0:T(8,128)S(1)} %get-tuple-element.39.low_ref.refs_6_), channel_id=1, source_target_pairs={{0,124},{1,125},{2,126},{3,127},{4,0},{5,1},{6,2},{7,3},{8,4},{9,5... | collective-permute-start | bytes 1572872 | tf_op jit(solution)/shard_map/ppermute | solution.py:474
  63.8 0.0 copy-done.5
  63.8 3.9 %second.5.mid_ref.refs_4_ = f32[2048,128]{1,0:T(8,128)S(1)} custom-call(f32[3072,128]{1,0:T(8,128)S(1)} %copy-done.3, f32[4,64,128]{2,1,0:T(8,128)S(1)} %get-tuple-element.36.refs_3_.refs_1_, f32[4,64,128]{2,1,0:T(8,128)S(1)} %get-tuple-element.37.refs_4_.refs_2_, f32[4,29,16,128]{3,2,1,0:T(8,128)S(1)} %copy-done.1, f32[2048,128]{1,0:T(8,128)S(1)} %copy-done.5), custom_call_target="tpu_custom_call" | custom-call | flops 15204352 | bytes 2097152 | tf_op jit(solution)/shard_map/second/pallas_call | solution.py:393
  67.7 5.1 %inner_first.3 = (f32[3072,128]{1,0:T(8,128)S(1)}, f32[512,128]{1,0:T(8,128)S(1)}) custom-call(f32[1024,128]{1,0:T(8,128)S(1)} %get-tuple-element.39.low_ref.refs_6_, f32[2048,128]{1,0:T(8,128)S(1)} %second.5.mid_ref.refs_4_, f32[1024,128]{1,0:T(8,128)S(1)} %get-tuple-element.38.high_ref.refs_7_, f32[4,29,16,128]{3,2,1,0:T(8,128)S(1)} %copy-done.1), custom_call_target="tpu_custom_call" | custom-call | flops 22806528 | bytes 3145728 | tf_op jit(solution)/shard_map/inner_first/pallas_call | solution.py:175
  72.8 3.2 %collective-permute-done.4.top_ref = f32[1024,128]{1,0:T(8,128)S(1)} collective-permute-done((f32[1024,128]{1,0:T(8,128)S(1)}, f32[1024,128]{1,0:T(8,128)S(1)}, u32[]{:S(2)}, u32[]{:S(2)}) %collective-permute-start.4) | collective-permute-done | bytes 524320 | tf_op jit(solution)/shard_map/ppermute | solution.py:474
  76.0 0.0 collective-permute-done.5.bot_ref
  76.0 1.4 %halo_edges.3.own_ref = f32[512,128]{1,0:T(8,128)S(1)} custom-call(f32[1024,128]{1,0:T(8,128)S(1)} %collective-permute-done.4.top_ref, f32[1024,128]{1,0:T(8,128)S(1)} %collective-permute-done.5.bot_ref, f32[512,128]{1,0:T(8,128)S(1)} %get-tuple-element.43.edge_ref), custom_call_target="tpu_custom_call" | custom-call | tf_op jit(solution)/shard_map/halo_edges/pallas_call | solution.py:233
  77.4 2.5 %collective-permute-start.7 = (f32[512,128]{1,0:T(8,128)S(1)}, f32[512,128]{1,0:T(8,128)S(1)}, u32[]{:S(2)}, u32[]{:S(2)}) collective-permute-start(f32[512,128]{1,0:T(8,128)S(1)} %halo_edges.3.own_ref), channel_id=1, source_target_pairs={{1,0},{2,1},{3,2},{5,4},{6,5},{7,6},{9,8},{10,9},{11,10},{13,12},{... | collective-permute-start | bytes 786440 | tf_op jit(solution)/shard_map/ppermute | solution.py:474
  79.9 3.1 %collective-permute-start.6 = (f32[512,128]{1,0:T(8,128)S(1)}, f32[512,128]{1,0:T(8,128)S(1)}, u32[]{:S(2)}, u32[]{:S(2)}) collective-permute-start(f32[512,128]{1,0:T(8,128)S(1)} %halo_edges.3.own_ref), channel_id=1, source_target_pairs={{0,1},{1,2},{2,3},{4,5},{5,6},{6,7},{8,9},{9,10},{10,11},{12,13},{... | collective-permute-start | bytes 786440 | tf_op jit(solution)/shard_map/ppermute | solution.py:474
  83.0 3.0 %outer_first.3 = (f32[1024,128]{1,0:T(8,128)S(1)}, f32[1024,128]{1,0:T(8,128)S(1)}) custom-call(f32[1024,128]{1,0:T(8,128)S(1)} %collective-permute-done.4.top_ref, f32[1024,128]{1,0:T(8,128)S(1)} %get-tuple-element.39.low_ref.refs_6_, f32[1024,128]{1,0:T(8,128)S(1)} %get-tuple-element.38.high_ref.refs_7_, f32[1024,128]{1,0:T(8,128)S(1)} %collective-permute-done.5.bot_ref, ...), custom_call_target="tpu_custom_call" | custom-call | flops 15204352 | bytes 2097152 | tf_op jit(solution)/shard_map/outer_first/pallas_call | solution.py:271
  86.0 0.0 collective-permute-done.7.right_ref
  86.0 0.3 collective-permute-done.6.left_ref
  86.3 2.6 %strips.3 = (f32[4,64,128]{2,1,0:T(8,128)S(1)}, f32[4,64,128]{2,1,0:T(8,128)S(1)}) custom-call(f32[512,128]{1,0:T(8,128)S(1)} %collective-permute-done.6.left_ref, f32[512,128]{1,0:T(8,128)S(1)} %collective-permute-done.7.right_ref, f32[512,128]{1,0:T(8,128)S(1)} %halo_edges.3.own_ref, f32[640,128]{1,0:T(8,128)S(1)} %collective-permute-done.2.left_ref.coef_left_ref, ...), custom_call_target="tpu_custom_call" | custom-call | tf_op jit(solution)/shard_map/strips/pallas_call | solution.py:344
  88.9 3.9 %second.7.mid_ref = f32[2048,128]{1,0:T(8,128)S(1)} custom-call(f32[3072,128]{1,0:T(8,128)S(1)} %get-tuple-element.41.refs_1_.refs_0_, f32[4,64,128]{2,1,0:T(8,128)S(1)} %get-tuple-element.44.refs_3_.refs_1_, f32[4,64,128]{2,1,0:T(8,128)S(1)} %get-tuple-element.45.refs_4_.refs_2_, f32[4,29,16,128]{3,2,1,0:T(8,128)S(1)} %copy-done.1, ...), custom_call_target="tpu_custom_call" | custom-call | flops 15204352 | bytes 2097152 | tf_op jit(solution)/shard_map/second/pallas_call | solution.py:393
  92.8 4.2 %second.6 = (f32[1024,128]{1,0:T(8,128)S(1)}, f32[1024,128]{1,0:T(8,128)S(1)}) custom-call(f32[1024,128]{1,0:T(8,128)S(1)} %get-tuple-element.40.refs_0_, f32[3072,128]{1,0:T(8,128)S(1)} %get-tuple-element.41.refs_1_.refs_0_, f32[1024,128]{1,0:T(8,128)S(1)} %get-tuple-element.42.refs_2_, f32[4,64,128]{2,1,0:T(8,128)S(1)} %get-tuple-element.44.refs_3_.refs_1_, ...), custom_call_target="tpu_custom_call" | custom-call | flops 15204352 | bytes 2097152 | tf_op jit(solution)/shard_map/second/pallas_call | solution.py:393
  97.0 3.1 %leave.1 = (f32[16,128,256]{2,1,0:T(8,128)}, f32[512,256]{1,0:T(8,128)S(1)}) custom-call(f32[1024,128]{1,0:T(8,128)S(1)} %get-tuple-element.46.low_ref, f32[2048,128]{1,0:T(8,128)S(1)} %second.7.mid_ref, f32[1024,128]{1,0:T(8,128)S(1)} %get-tuple-element.47.high_ref, bf16[2048,512]{1,0:T(8,128)(2,1)S(1)} %get-tuple-element.48.w_high_ref, ...), custom_call_target="tpu_custom_call" | custom-call | flops 2147483648 | bytes 8388608 | tf_op jit(solution)/shard_map/leave/pallas_call | solution.py:450
  100.2 0.1 reshape.24
  100.3 23.3 %all_to_all.5 = f32[128,4,256]{2,1,0:T(4,128)S(1)} all-to-all(f32[128,4,256]{2,1,0:T(4,128)S(1)} %reshape.24), channel_id=1, replica_groups=mesh['azim'=32,'rad'=4] {'azim','rad'}, dimensions={0} | all-to-all | bytes 1048576 | tf_op jit(solution)/shard_map/all_to_all | solution.py:505
  123.6 0.7 reduce_sum.9
  (2 shorter events, 0.0 us)
Async XLA Ops:
  0.6 1.2 copy-start
  1.8 1.6 %copy-start.6 = (f32[16,128,256]{2,1,0:T(8,128)S(1)}, f32[16,128,256]{2,1,0:T(8,128)}, u32[]{:S(2)}) copy-start(f32[16,128,256]{2,1,0:T(8,128)} %x_ref.1) | copy-start | bytes 6291460
  3.4 11.9 %copy-start.8 = (s32[1024]{0:T(1024)S(1)}, s32[1024]{0:T(1024)}, u32[]{:S(2)}) copy-start(s32[1024]{0:T(1024)} %param.10) | copy-start | bytes 12292
  3.4 12.2 %copy-start.1 = (f32[4,29,16,128]{3,2,1,0:T(8,128)S(1)}, f32[4,29,16,128]{3,2,1,0:T(8,128)}, u32[]{:S(2)}) copy-start(f32[4,29,16,128]{3,2,1,0:T(8,128)} %refs_3_.3) | copy-start | bytes 2850820
  5.1 32.2 %collective-permute-start = (f32[1280,128]{1,0:T(8,128)}, f32[1280,128]{1,0:T(8,128)S(1)}, u32[]{:S(2)}, u32[]{:S(2)}) collective-permute-start(f32[1280,128]{1,0:T(8,128)} %get-tuple-element.27.high_ref.refs_7_), channel_id=1, source_target_pairs={{0,4},{1,5},{2,6},{3,7},{4,8},{5,9},{6,10},{7,11},{8,12},{9,13},{1... | collective-permute-start | bytes 1966088 | tf_op jit(solution)/shard_map/ppermute | solution.py:474
  7.2 30.1 %collective-permute-start.1 = (f32[1280,128]{1,0:T(8,128)S(1)}, f32[1280,128]{1,0:T(8,128)S(1)}, u32[]{:S(2)}, u32[]{:S(2)}) collective-permute-start(f32[1280,128]{1,0:T(8,128)S(1)} %get-tuple-element.28.low_ref.refs_6_), channel_id=1, source_target_pairs={{0,124},{1,125},{2,126},{3,127},{4,0},{5,1},{6,2},{7,3},{8,4},{9,5... | collective-permute-start | bytes 1966088 | tf_op jit(solution)/shard_map/ppermute | solution.py:474
  21.8 1.1 copy-start.2
  23.0 1.0 copy-start.4
  31.8 1.9 %copy-start.7 = (s32[1024]{0:T(1024)S(1)}, s32[1024]{0:T(1024)}, u32[]{:S(2)}) copy-start(s32[1024]{0:T(1024)} %param.8) | copy-start | bytes 12292
  38.8 9.7 %collective-permute-start.3 = (f32[640,128]{1,0:T(8,128)S(1)}, f32[640,128]{1,0:T(8,128)S(1)}, u32[]{:S(2)}, u32[]{:S(2)}) collective-permute-start(f32[640,128]{1,0:T(8,128)S(1)} %halo_edges.2.own_ref.coef_own_ref), channel_id=1, source_target_pairs={{1,0},{2,1},{3,2},{5,4},{6,5},{7,6},{9,8},{10,9},{11,10},{13,12},{... | collective-permute-start | bytes 983048 | tf_op jit(solution)/shard_map/ppermute | solution.py:474
  41.7 6.8 %collective-permute-start.2 = (f32[640,128]{1,0:T(8,128)S(1)}, f32[640,128]{1,0:T(8,128)S(1)}, u32[]{:S(2)}, u32[]{:S(2)}) collective-permute-start(f32[640,128]{1,0:T(8,128)S(1)} %halo_edges.2.own_ref.coef_own_ref), channel_id=1, source_target_pairs={{0,1},{1,2},{2,3},{4,5},{5,6},{6,7},{8,9},{9,10},{10,11},{12,13},{... | collective-permute-start | bytes 983048 | tf_op jit(solution)/shard_map/ppermute | solution.py:474
  48.5 2.6 %copy-start.3 = (f32[3072,128]{1,0:T(8,128)S(1)}, f32[3072,128]{1,0:T(8,128)}, u32[]{:S(2)}) copy-start(f32[3072,128]{1,0:T(8,128)} %copy-done.2) | copy-start | bytes 4718596
  51.1 12.6 %copy-start.5 = (f32[2048,128]{1,0:T(8,128)S(1)}, f32[2048,128]{1,0:T(8,128)}, u32[]{:S(2)}) copy-start(f32[2048,128]{1,0:T(8,128)} %copy-done.4) | copy-start | bytes 3145732
  56.5 19.5 %collective-permute-start.4 = (f32[1024,128]{1,0:T(8,128)S(1)}, f32[1024,128]{1,0:T(8,128)S(1)}, u32[]{:S(2)}, u32[]{:S(2)}) collective-permute-start(f32[1024,128]{1,0:T(8,128)S(1)} %get-tuple-element.38.high_ref.refs_7_), channel_id=1, source_target_pairs={{0,4},{1,5},{2,6},{3,7},{4,8},{5,9},{6,10},{7,11},{8,12},{9,13},{1... | collective-permute-start | bytes 1572872 | tf_op jit(solution)/shard_map/ppermute | solution.py:474
  56.6 19.5 %collective-permute-start.5 = (f32[1024,128]{1,0:T(8,128)S(1)}, f32[1024,128]{1,0:T(8,128)S(1)}, u32[]{:S(2)}, u32[]{:S(2)}) collective-permute-start(f32[1024,128]{1,0:T(8,128)S(1)} %get-tuple-element.39.low_ref.refs_6_), channel_id=1, source_target_pairs={{0,124},{1,125},{2,126},{3,127},{4,0},{5,1},{6,2},{7,3},{8,4},{9,5... | collective-permute-start | bytes 1572872 | tf_op jit(solution)/shard_map/ppermute | solution.py:474
  77.4 8.6 %collective-permute-start.7 = (f32[512,128]{1,0:T(8,128)S(1)}, f32[512,128]{1,0:T(8,128)S(1)}, u32[]{:S(2)}, u32[]{:S(2)}) collective-permute-start(f32[512,128]{1,0:T(8,128)S(1)} %halo_edges.3.own_ref), channel_id=1, source_target_pairs={{1,0},{2,1},{3,2},{5,4},{6,5},{7,6},{9,8},{10,9},{11,10},{13,12},{... | collective-permute-start | bytes 786440 | tf_op jit(solution)/shard_map/ppermute | solution.py:474
  79.9 6.4 %collective-permute-start.6 = (f32[512,128]{1,0:T(8,128)S(1)}, f32[512,128]{1,0:T(8,128)S(1)}, u32[]{:S(2)}, u32[]{:S(2)}) collective-permute-start(f32[512,128]{1,0:T(8,128)S(1)} %halo_edges.3.own_ref), channel_id=1, source_target_pairs={{0,1},{1,2},{2,3},{4,5},{5,6},{6,7},{8,9},{9,10},{10,11},{12,13},{... | collective-permute-start | bytes 786440 | tf_op jit(solution)/shard_map/ppermute | solution.py:474

commit v4 on v3

--- a/solution.py
+++ b/solution.py
@@ -9,6 +9,7 @@
 
 STEPS = 2
 VMEM_LIMIT = 32 * 1024 * 1024
+ENTER_LIMIT = 58 * 1024 * 1024
 F32 = jnp.float32
 BF16 = jnp.bfloat16
 
@@ -88,14 +89,13 @@
 
 
 def sweep(first, stop, source, weight, finish, shift_ref, block=4):
-    lane = lanes((32, 128))
     for s in range(first - 2, stop + 2):
         u = source(s)
         k = s - first + 2
-        shift_ref[0, k] = jnp.where(lane >= 2, pltpu.roll(u, 2, axis=1), 0.0)
-        shift_ref[1, k] = jnp.where(lane >= 1, pltpu.roll(u, 1, axis=1), 0.0)
-        shift_ref[2, k] = jnp.where(lane < 127, pltpu.roll(u, 127, axis=1), 0.0)
-        shift_ref[3, k] = jnp.where(lane < 126, pltpu.roll(u, 126, axis=1), 0.0)
+        shift_ref[0, k] = pltpu.roll(u, 2, axis=1)
+        shift_ref[1, k] = pltpu.roll(u, 1, axis=1)
+        shift_ref[2, k] = pltpu.roll(u, 127, axis=1)
+        shift_ref[3, k] = pltpu.roll(u, 126, axis=1)
     for begin in range(first, stop, block):
         totals = [None] * block
         for s in range(begin - 2, begin + block + 2):
@@ -111,40 +111,99 @@
             finish(begin + b, totals[b])
 
 
+def inside(lane, k, line):
+    if k >= 25 or k % 5 == 2:
+        return line
+    keep = (lane >= 2, lane >= 1, None, lane < 127, lane < 126)[k % 5]
+    return jnp.where(keep, line, 0.0)
+
+
 def line_of(coef_ref, var, k, row):
     return jnp.broadcast_to(coef_ref[var, k, row : row + 1], (32, 128))
 
 
 def tail_line(ref, var, k, row):
     lines = ref.at[pl.ds(pl.multiple_of(TAIL + var * 64, 64), 64)]
-    return jnp.broadcast_to(lines[2 * k + row : 2 * k + row + 1], (32, 128))
-
-
-def enter(x_ref, coef_ref, low_ref, mid_ref, high_ref):
+    line = inside(lanes((1, 128)), k, lines[2 * k + row : 2 * k + row + 1])
+    return jnp.broadcast_to(line, (32, 128))
+
+
+def sort_sides(index, even_ref, odd_ref, below_ref, above_ref):
+    even_is_above = index % 2 == 0
+
+    @pl.when(even_is_above)
+    def _():
+        odd_ref[...], even_ref[...] = below_ref[...], above_ref[...]
+
+    @pl.when(jnp.logical_not(even_is_above))
+    def _():
+        even_ref[...], odd_ref[...] = below_ref[...], above_ref[...]
+
+
+def enter_outer(x_ref, coef_ref, low_ref, high_ref, even_ref, odd_ref, x_in, coef_in, sems):
+    copies = [
+        pltpu.make_async_copy(x_ref.at[pl.ds(0, 4)], x_in.at[0], sems.at[0]),
+        pltpu.make_async_copy(x_ref.at[pl.ds(12, 4)], x_in.at[1], sems.at[1]),
+        pltpu.make_async_copy(coef_ref, coef_in, sems.at[2]),
+    ]
+    for copy in copies:
+        copy.start()
     low_ref[TAIL:] = jnp.zeros((256, 128), F32)
     high_ref[TAIL:] = jnp.zeros((256, 128), F32)
+    for side, ref in ((0, low_ref), (1, high_ref)):
+        copies[side].wait()
+
+        @pl.loop(0, 4)
+        def _(k):
+            ref[pl.ds(pl.multiple_of(k * ROWS, ROWS), ROWS)] = x_in[side, k].T
+
+    copies[2].wait()
 
     @pl.loop(0, 4)
     def _(k):
-        at = pl.ds(pl.multiple_of(k * ROWS, ROWS), ROWS)
-        low_ref[at] = x_ref[k].T
-        mid_ref[at] = x_ref[k + 4].T
-        mid_ref[pl.ds(pl.multiple_of((k + 4) * ROWS, ROWS), ROWS)] = x_ref[k + 8].T
-        high_ref[at] = x_ref[k + 12].T
         lines = pl.ds(pl.multiple_of(TAIL + k * 64, 64), 58)
-        low_ref[lines] = coef_ref[k, :, 0:2].reshape(58, 128)
-        high_ref[lines] = coef_ref[k, :, 14:16].reshape(58, 128)
-
-
-def call_enter(x, coef):
-    return pl.pallas_call(
-        enter,
-        in_specs=whole(2),
-        out_specs=whole(3),
-        out_shape=arrays((TAIL + 256, 128), (8 * ROWS, 128), (TAIL + 256, 128)),
-        compiler_params=params(),
-        name="enter",
+        low_ref[lines] = coef_in[k, :, 0:2].reshape(58, 128)
+        high_ref[lines] = coef_in[k, :, 14:16].reshape(58, 128)
+
+    sort_sides(lax.axis_index("azim"), even_ref, odd_ref, low_ref, high_ref)
+
+
+def call_enter_outer(x, coef):
+    return pl.pallas_call(
+        enter_outer,
+        in_specs=[pl.BlockSpec(memory_space=pltpu.HBM)] * 2,
+        out_specs=whole(4),
+        out_shape=arrays(*[(TAIL + 256, 128)] * 4),
+        scratch_shapes=[
+            pltpu.VMEM((2, 4, 128, 256), F32),
+            pltpu.VMEM((4, 29, 16, 128), F32),
+            pltpu.SemaphoreType.DMA((3,)),
+        ],
+        compiler_params=pltpu.CompilerParams(vmem_limit_bytes=ENTER_LIMIT),
+        name="enter_outer",
     )(x, coef)
+
+
+def enter_inner(x_ref, mid_ref, x_in, sem):
+    copy = pltpu.make_async_copy(x_ref.at[pl.ds(4, 8)], x_in, sem)
+    copy.start()
+    copy.wait()
+
+    @pl.loop(0, 8)
+    def _(k):
+        mid_ref[pl.ds(pl.multiple_of(k * ROWS, ROWS), ROWS)] = x_in[k].T
+
+
+def call_enter_inner(x):
+    return pl.pallas_call(
+        enter_inner,
+        in_specs=[pl.BlockSpec(memory_space=pltpu.HBM)],
+        out_specs=whole(1)[0],
+        out_shape=arrays((8 * ROWS, 128))[0],
+        scratch_shapes=[pltpu.VMEM((8, 128, 256), F32), pltpu.SemaphoreType.DMA],
+        compiler_params=params(),
+        name="enter_inner",
+    )(x)
 
 
 def inner_first(low_ref, mid_ref, high_ref, coef_ref, y_ref, edge_ref, shift_ref):
@@ -184,7 +243,15 @@
     )(low, mid, high, coef)
 
 
-def coef_edges(coef_ref, out_ref):
+def coef_edges(coef_ref, out_ref, inside_ref):
+    lane = lanes((16, 128))
+
+    @pl.loop(0, 4)
+    def _(var):
+        for k in range(29):
+            lines = pl.ds(pl.multiple_of(var * 464 + k * 16, 16), 16)
+            inside_ref[var, k] = inside(lane, k, coef_ref[lines, :])
+
     out_ref[...] = jnp.zeros_like(out_ref)
     for var in range(4):
         pack = jnp.zeros((29, 128), F32)
@@ -197,15 +264,24 @@
     return pl.pallas_call(
         coef_edges,
         in_specs=whole(1),
-        out_specs=whole(1)[0],
-        out_shape=arrays((128, 128))[0],
+        out_specs=whole(2),
+        out_shape=arrays((128, 128), coef.shape),
         compiler_params=params(),
         name="coef_edges",
     )(coef.reshape(-1, 128))
 
 
-def halo_edges(top_ref, bot_ref, edge_ref, *refs):
-    out_ref = refs[-1]
+def halo_edges(even_ref, odd_ref, edge_ref, *refs):
+    top_ref, bot_ref, out_ref = refs[-3:]
+    even_is_above = lax.axis_index("azim") % 2 == 0
+
+    @pl.when(even_is_above)
+    def _():
+        top_ref[...], bot_ref[...] = odd_ref[...], even_ref[...]
+
+    @pl.when(jnp.logical_not(even_is_above))
+    def _():
+        top_ref[...], bot_ref[...] = even_ref[...], odd_ref[...]
 
     def one(var, half):
         near = window(edge_ref, 0, var, half)
@@ -218,7 +294,7 @@
         put(out_ref, 1, var, half, far)
 
     each_part(one)
-    if len(refs) == 2:
+    if len(refs) == 4:
         for var in range(4):
             pack = refs[0][32 * var : 32 * var + 29]
             for k in range(2):
@@ -229,15 +305,15 @@
             out_ref[COEF + 32 * var + 29 : COEF + 32 * var + 32] = jnp.zeros((3, 128), F32)
 
 
-def call_halo_edges(top, bot, edge, *coef_edge):
+def call_halo_edges(even, odd, edge, *coef_edge):
     return pl.pallas_call(
         halo_edges,
         in_specs=whole(3 + len(coef_edge)),
-        out_specs=whole(1)[0],
-        out_shape=arrays((COEF + 128 * len(coef_edge), 128))[0],
+        out_specs=whole(3),
+        out_shape=arrays(even.shape, odd.shape, (COEF + 128 * len(coef_edge), 128)),
         compiler_params=params(),
         name="halo_edges",
-    )(top, bot, edge, *coef_edge)
+    )(even, odd, edge, *coef_edge)
 
 
 def outer_first(top_ref, low_ref, high_ref, bot_ref, coef_ref, ctop_ref, cbot_ref,
@@ -280,44 +356,56 @@
     )(top, low, high, bot, coef, ctop, cbot)
 
 
-def strips(left_ref, right_ref, own_ref, coef_left_ref, coef_right_ref, coef_own_ref,
-           mend_y_ref, mend_u_ref, rim_ref):
-    entry = lanes((64, 128)) % 4
-    entry_line = lanes((32, 128)) % 4
-
-    def merge(entry, left, right):
+def strips(even_ref, odd_ref, own_ref, coef_even_ref, coef_odd_ref, coef_own_ref,
+           mend_y_ref, mend_u_ref, rim_ref, line_ref):
+    entry = lanes((32, 128)) % 4
+    entry_line = lanes((1, 128)) % 4
+    even_is_right = lanes((32, 128)) * 0 + lax.axis_index("rad") % 2 == 0
+
+    def merge(even, odd):
+        right = jnp.where(even_is_right, even, odd)
+        left = jnp.where(even_is_right, odd, even)
         return jnp.where(entry < 2, pltpu.roll(right, 126, axis=1), pltpu.roll(left, 2, axis=1))
 
     def rows_on(pack, i):
         turn = (4 * (2 - i)) % 128
         return pltpu.roll(pack, turn, axis=1) if turn else pack
 
-    def pack_at(ref, kind, var):
-        return ref[pl.ds(pl.multiple_of(kind * ROWS + var * 64, 64), 64), :]
+    def rim_of(var, half):
+        at = pl.ds(pl.multiple_of(half * 32, 32), 32)
+        rim_ref[var, at] = merge(window(even_ref, 0, var, half), window(odd_ref, 0, var, half))
+
+    each_part(rim_of)
 
     @pl.loop(0, 4)
     def _(var):
-        rim_ref[var] = merge(entry, pack_at(left_ref, 0, var), pack_at(right_ref, 0, var))
-
-    @pl.loop(0, 4)
-    def _(var):
-        near = pack_at(own_ref, 0, var)
-        rim = rim_ref[var]
-        outer = merge(entry, pack_at(left_ref, 1, var), pack_at(right_ref, 1, var))
         lines = pl.ds(pl.multiple_of(COEF + var * 32, 32), 32)
-        own = coef_own_ref[lines, :]
-        other = merge(entry_line, coef_left_ref[lines, :], coef_right_ref[lines, :])
+        own = coef_own_ref.at[lines]
+        line_ref[var, 0:32] = merge(coef_even_ref[lines, :], coef_odd_ref[lines, :])
+        for i in range(5):
+            k = 5 * i
+            two = jnp.where(entry_line < 2, own[k + 4 : k + 5], own[k : k + 1])
+            one = jnp.where(entry_line == 1, own[k + 3 : k + 4], 0.0)
+            one = jnp.where(entry_line == 2, own[k + 1 : k + 2], one)
+            line_ref[var, 32 + i : 33 + i] = two
+            line_ref[var, 37 + i : 38 + i] = one
+
+    def one_part(var, half):
+        at = pl.ds(pl.multiple_of(half * 32, 32), 32)
+
+        def line(k):
+            return jnp.broadcast_to(line_ref[var, k : k + 1], (32, 128))
 
         def beyond(rim):
             crossed = jnp.where(entry == 1, pltpu.roll(rim, 1, axis=1), pltpu.roll(rim, 127, axis=1))
-            total = jnp.zeros((64, 128), F32)
-            for i in range(5):
-                two = jnp.where(entry_line[0:1] < 2, own[5 * i + 4 : 5 * i + 5], own[5 * i : 5 * i + 1])
-                one = jnp.where(entry_line[0:1] == 1, own[5 * i + 3 : 5 * i + 4], 0.0)
-                one = jnp.where(entry_line[0:1] == 2, own[5 * i + 1 : 5 * i + 2], one)
-                total = total + two * rows_on(rim, i) + one * rows_on(crossed, i)
+            total = line(32) * rows_on(rim, 0) + line(37) * rows_on(crossed, 0)
+            for i in range(1, 5):
+                total = total + line(32 + i) * rows_on(rim, i) + line(37 + i) * rows_on(crossed, i)
             return total
 
+        near = window(own_ref, 0, var, half)
+        rim = rim_ref[var, at]
+        outer = merge(window(even_ref, 1, var, half), window(odd_ref, 1, var, half))
         before = jnp.where(
             entry == 0, pltpu.roll(near, 127, axis=1),
             jnp.where(entry == 2, pltpu.roll(outer, 127, axis=1), pltpu.roll(rim, 1, axis=1)),
@@ -329,37 +417,42 @@
         shifted = (
             jnp.where(entry < 2, near, outer), before, rim, after, jnp.where(entry < 2, outer, near),
         )
-        total = jnp.zeros((64, 128), F32)
-        for i in range(5):
-            for j in range(5):
-                k = 5 * i + j
-                total = total + other[k : k + 1] * rows_on(shifted[j], i)
-        for w in range(4):
-            total = total + other[25 + w : 26 + w] * rim_ref[w]
-        mend_y_ref[var] = 0.5 * beyond(rim)
-        mend_u_ref[var] = beyond(rim + 0.5 * total)
-
-
-def call_strips(left, right, own, coef_left, coef_right, coef_own):
+        total = line(25) * rim_ref[0, at]
+        for w in range(1, 4):
+            total = total + line(25 + w) * rim_ref[w, at]
+        for j in range(5):
+            for i in range(5):
+                total = total + line(5 * i + j) * rows_on(shifted[j], i)
+        mend_y_ref[var, at] = 0.5 * beyond(rim)
+        mend_u_ref[var, at] = beyond(rim + 0.5 * total)
+
+    each_part(one_part)
+
+
+def call_strips(even, odd, own, coef_even, coef_odd, coef_own):
     return pl.pallas_call(
         strips,
         in_specs=whole(6),
         out_specs=whole(2),
         out_shape=arrays((4, 64, 128), (4, 64, 128)),
-        scratch_shapes=[pltpu.VMEM((4, 64, 128), F32)],
+        scratch_shapes=[pltpu.VMEM((4, 64, 128), F32), pltpu.VMEM((4, 48, 128), F32)],
         compiler_params=params(),
         name="strips",
-    )(left, right, own, coef_left, coef_right, coef_own)
-
-
-def second(ranges, n_y, *refs):
+    )(even, odd, own, coef_even, coef_odd, coef_own)
+
+
+PARTS = ((0, 4), (4, 12), (12, 16))
+
+
+def second(ranges, parts, n_y, sides, *refs):
     y_refs, refs = refs[:n_y], refs[n_y:]
     mend_y_ref, mend_u_ref, coef_ref = refs[:3]
-    u_refs, refs = refs[3 : 3 + len(ranges)], refs[3 + len(ranges) :]
-    out_refs, refs = refs[: len(ranges)], refs[len(ranges) :]
-    y_ref, shift_ref = refs
+    u_refs, refs = refs[3 : 3 + len(parts)], refs[3 + len(parts) :]
+    out_refs, refs = refs[: len(parts)], refs[len(parts) :]
+    y_ref, shift_ref = refs[-2:]
     bounds = {1: ((2, 14),), 3: ((-2, 2), (2, 14), (14, 18))}[n_y]
     y_parts = [(first, stop, ref) for (first, stop), ref in zip(bounds, y_refs)]
+    u_parts = [(first, stop, ref) for (first, stop), ref in zip(parts, u_refs)]
     sources = sorted({s for first, stop in ranges for s in range(first - 2, stop + 2)})
     whole_y = ((-2, 18, y_ref),)
 
@@ -372,57 +465,96 @@
 
     def one(var, half):
         pack = mend_u_ref[var, pl.ds(pl.multiple_of(half * 32, 32), 32)]
-        for (first, stop), u_ref, out_ref in zip(ranges, u_refs, out_refs):
-
-            def finish(row, total):
-                for w in range(4):
-                    total = total + line_of(coef_ref, var, 25 + w, row) * pick(whole_y, row, w, half)
-                total = total + unplace(pack, row)
-                put(out_ref, row - first, var, half, window(u_ref, row - first, var, half) + total)
-
+
+        def finish(row, total):
+            for w in range(4):
+                total = total + line_of(coef_ref, var, 25 + w, row) * pick(whole_y, row, w, half)
+            total = total + unplace(pack, row)
+            for (first, stop), ref in zip(parts, out_refs):
+                if first <= row < stop:
+                    put(ref, row - first, var, half, pick(u_parts, row, var, half) + total)
+
+        for first, stop in ranges:
             sweep(
                 first, stop, lambda s: pick(whole_y, s, var, half),
                 lambda k, row: line_of(coef_ref, var, k, row), finish, shift_ref,
             )
 
     each_part(one)
-
-
-def call_second(ranges, ys, mend_y, mend_u, coef, us):
-    outs = [((stop - first) * ROWS, 128) for first, stop in ranges]
-    return pl.pallas_call(
-        functools.partial(second, ranges, len(ys)),
+    if sides:
+        sort_sides(lax.axis_index("azim"), refs[0], refs[1], out_refs[0], out_refs[-1])
+
+
+def call_second(ranges, parts, ys, mend_y, mend_u, coef, us, sides=False):
+    outs = [((stop - first) * ROWS, 128) for first, stop in parts]
+    outs += [outs[0]] * (2 * sides)
+    most = max(stop - first for first, stop in ranges)
+    return pl.pallas_call(
+        functools.partial(second, ranges, parts, len(ys), sides),
         in_specs=whole(len(ys) + 3 + len(us)),
-        out_specs=whole(len(us)),
+        out_specs=whole(len(outs)),
         out_shape=arrays(*outs),
-        scratch_shapes=[pltpu.VMEM((20 * ROWS, 128), F32), pltpu.VMEM((4, 12, 32, 128), F32)],
+        scratch_shapes=[pltpu.VMEM((20 * ROWS, 128), F32), pltpu.VMEM((4, most + 4, 32, 128), F32)],
         compiler_params=params(),
         cost_estimate=cost(8),
         name="second",
     )(*ys, mend_y, mend_u, coef, *us)
 
 
-def spread(cells_ref, weights_ref, high_ref, low_ref):
+def gather(rows_ref, table_ref, out_ref, wide_ref, picked_ref):
+    @pl.loop(0, 16)
+    def _(k):
+        at = pl.ds(pl.multiple_of(k * 256, 256), 256)
+        wide_ref[at] = table_ref[at].astype(F32)
+
+    @pl.loop(0, 32)
+    def _(k):
+        for t in range(32):
+            slot = k * 32 + t
+            picked_ref[pl.ds(slot, 1)] = wide_ref[pl.ds(rows_ref[slot], 1)]
+
+    @pl.loop(0, 4)
+    def _(k):
+        at = pl.ds(pl.multiple_of(k * 256, 256), 256)
+        out_ref[at] = picked_ref[at].astype(BF16)
+
+
+def call_gather(rows, table):
+    return pl.pallas_call(
+        gather,
+        in_specs=[pl.BlockSpec(memory_space=pltpu.SMEM)] + whole(1),
+        out_specs=whole(1)[0],
+        out_shape=jax.ShapeDtypeStruct((rows.shape[0], table.shape[1]), BF16),
+        scratch_shapes=[pltpu.VMEM((4096, 512), F32), pltpu.VMEM((1024, 512), F32)],
+        compiler_params=params(),
+        name="gather",
+    )(rows, table)
+
+
+def spread(count_ref, cells_ref, weights_ref, high_ref, low_ref):
     step = pl.program_id(0)
     cell = lax.broadcasted_iota(jnp.int32, (256, 1024), 0) + step * 256
-    hit = jnp.where(cells_ref[...] == cell, 1.0, 0.0).astype(BF16)
+    live = lax.broadcasted_iota(jnp.int32, (1, 1024), 1) < count_ref[0]
+    cells = jnp.where(live, cells_ref[...], -1)
+    hit = jnp.where(cells == cell, 1.0, 0.0).astype(BF16)
     total = jnp.dot(hit, weights_ref[...], preferred_element_type=F32)
     high = total.astype(BF16)
     high_ref[...] = high
     low_ref[...] = (total - high.astype(F32)).astype(BF16)
 
 
-def call_spread(cells, weights):
+def call_spread(count, cells, weights):
     return pl.pallas_call(
         spread,
         grid=(8,),
-        in_specs=[spec((1, 1024), lambda s: (0, 0)), spec((1024, 512), lambda s: (0, 0))],
+        in_specs=[pl.BlockSpec(memory_space=pltpu.SMEM)]
+        + [spec((1, 1024), lambda s: (0, 0)), spec((1024, 512), lambda s: (0, 0))],
         out_specs=[spec((256, 512), lambda s: (s, 0))] * 2,
         out_shape=[jax.ShapeDtypeStruct((2048, 512), BF16)] * 2,
         compiler_params=params(1),
         cost_estimate=pl.CostEstimate(flops=2 << 30, bytes_accessed=6 << 20, transcendentals=0),
         name="spread",
-    )(cells, weights)
+    )(count, cells, weights)
 
 
 def leave(low_ref, mid_ref, high_ref, w_high_ref, w_low_ref, out_ref, markov_ref):
@@ -458,48 +590,49 @@
     )(low, mid, high, w_high, w_low)
 
 
-def shifts(n_azim, n_rad, da, dr):
-    pairs = []
-    for a in range(n_azim):
-        for r in range(n_rad):
-            if 0 <= r + dr < n_rad:
-                pairs.append((a * n_rad + r, ((a + da) % n_azim) * n_rad + r + dr))
-    return pairs
+def swaps(count, first, periodic):
+    pairs = [(k, (k + 1) % count) for k in range(first, count, 2) if periodic or k + 1 < count]
+    return pairs + [(target, source) for source, target in pairs]
 
 
 def body(perturbation_in, coefficients, wall_cells, wall_count, mode_row, mode_table):
     n_azim, n_rad = lax.axis_size("azim"), lax.axis_size("rad")
 
-    def send(block, da, dr):
-        return lax.ppermute(block, ("azim", "rad"), shifts(n_azim, n_rad, da, dr))
+    def swap(block, axis, odd):
+        count = lax.axis_size(axis)
+        return lax.ppermute(block, axis, swaps(count, odd, axis == "azim"))
 
     slots = wall_cells.shape[0]
-    live = jnp.arange(slots, dtype=jnp.int32) < wall_count[0]
-    weights = jnp.where(live[:, None], jnp.take(mode_table, mode_row, axis=0), jnp.zeros((), BF16))
-    w_high, w_low = call_spread(wall_cells.reshape(1, slots), weights)
-
-    low, mid, high = call_enter(perturbation_in, coefficients)
-    tails = edge_coef = None
+    weights = call_gather(mode_row, mode_table)
+    w_high, w_low = call_spread(wall_count, wall_cells.reshape(1, slots), weights)
+
+    low, high, even, odd = call_enter_outer(perturbation_in, coefficients)
+    mid = call_enter_inner(perturbation_in)
+    coef_edge, coef = call_coef_edges(coefficients)
     for step in range(STEPS):
-        top, bot = send(high, 1, 0), send(low, -1, 0)
-        y_mid, edge = call_inner_first(low, mid, high, coefficients)
+        even = swap(even, "azim", 0)
+        odd = swap(odd, "azim", 1)
+        y_mid, edge = call_inner_first(low, mid, high, coef)
         if step == 0:
+            edge, w_high = lax.optimization_barrier((edge, w_high))
+            top, bot, own = call_halo_edges(even, odd, edge, coef_edge)
             tails = top, bot
-            extra = (call_coef_edges(coefficients),)
-            edge, w_high = lax.optimization_barrier((edge, w_high))
         else:
-            extra = ()
-        own = call_halo_edges(top, bot, edge, *extra)
-        left, right = send(own, 0, 1), send(own, 0, -1)
+            top, bot, own = call_halo_edges(even, odd, edge)
+        sides = swap(own, "rad", 0), swap(own, "rad", 1), own
         if step == 0:
-            edge_coef = left, right, own
-        y_low, y_high = call_outer_first(top, low, high, bot, coefficients, *tails)
-        mends = call_strips(left, right, own, *edge_coef)
-        new_low, new_high = call_second(
-            ((0, 4), (12, 16)), (y_low, y_mid, y_high), *mends, coefficients, (low, high)
-        )
-        (mid,) = call_second(((4, 12),), (y_mid,), *mends, coefficients, (mid,))
-        low, high = new_low, new_high
+            coef_sides = sides
+        ys = call_outer_first(top, low, high, bot, coef, *tails)
+        ys = ys[0], y_mid, ys[1]
+        mends = call_strips(*sides, *coef_sides)
+        if step < STEPS - 1:
+            (new_mid,) = call_second(((4, 12),), PARTS[1:2], ys[1:2], *mends, coef, (mid,))
+            low, high, even, odd = call_second(
+                (PARTS[0], PARTS[2]), (PARTS[0], PARTS[2]), ys, *mends, coef, (low, high), sides=True
+            )
+            mid = new_mid
+        else:
+            low, mid, high = call_second(((0, 16),), PARTS, ys, *mends, coef, (low, mid, high))
     out, term = call_leave(low, mid, high, w_high, w_low)
     count = n_azim * n_rad
     parts = lax.all_to_all(term.reshape(count, -1, term.shape[1]), ("azim", "rad"), 0, 0)

time: 125 us -> 113 us (0.904)
  local copies, waits for them, and re-layouts: 12.9 us -> 2.36 us
  starting transfers between devices: 27.9 us -> 20.4 us
  waiting for transfers between devices: 3.53 us -> 9.64 us
  Pallas kernels: 52.6 us -> 58 us
  blocking collectives: 23.3 us -> 20.1 us
  other arithmetic: 2.6 us -> 0.74 us
    gather x1 -> x0, local copies, waits for them, and re-layouts: 7.83 us -> none  [body(): jnp.take(mode_table, mode_row, axis=0)]
    ppermute x8, starting transfers between devices: 27.9 us -> 20.4 us  [swap(): return lax.ppermute(block, axis, swaps(count, odd, axis == 'azim'))]
    ppermute x8, waiting for transfers between devices: 3.53 us -> 9.64 us  [swap(): return lax.ppermute(block, axis, swaps(count, odd, axis == 'azim'))]
    pallas_call x7 -> x8, Pallas kernels: 23.1 us -> 27.6 us  [the longest x3 14.4 us: call_second(): pl.pallas_call(functools.partial(second, ranges, parts, len(ys), sides),...]
    pallas_call x2, Pallas kernels: 5.2 us -> 8.66 us  [call_strips(): pl.pallas_call(strips, in_specs=whole(6), out_specs=whole(2), out_shape=a...]
    all_to_all x1, blocking collectives: 23.3 us -> 20.1 us  [body(): lax.all_to_all(term.reshape(count, -1, term.shape[1]), ('azim', 'rad'), 0...]
    unnamed x18 -> x14, local copies, waits for them, and re-layouts: 4.95 us -> 2.21 us
    select_n x1 -> x0, other arithmetic: 1.85 us -> none  [body(): jnp.where(live[:, None], jnp.take(mode_table, mode_row, axis=0), jnp.zero...]
  transfers between devices with their start and end apart: 8 -> 8, of which waited for: 2 -> 3; matrix products, arithmetic and copies ran while one was open for 8% -> 0% of each run, Pallas kernels for 21% -> 26%
where the time goes in v4:
time: 113 us
  Pallas kernels  58 us (51%)
  starting transfers between devices  20.4 us (18%)
  blocking collectives  20.1 us (18%)
  waiting for transfers between devices  9.64 us (9%)
  local copies, waits for them, and re-layouts  2.36 us (2%)
  between operations  1.54 us (1%)
    ppermute x8, starting transfers between devices, swap(): return lax.ppermute(block, axis, swaps(count, odd, axis == 'azim'))  20.4 us
    all_to_all x1, blocking collectives, body(): lax.all_to_all(term.reshape(count, -1, term.shape[1]), ('azim', 'rad'), 0...  20.1 us
    pallas_call x3, Pallas kernels, call_second(): pl.pallas_call(functools.partial(second, ranges, parts, len(ys), sides),...  14.4 us
    pallas_call x2, Pallas kernels, call_inner_first(): pl.pallas_call(inner_first, in_specs=whole(4), out_specs=whole(2), out_sh...  9.88 us
    ppermute x8, waiting for transfers between devices, swap(): return lax.ppermute(block, axis, swaps(count, odd, axis == 'azim'))  9.64 us
    pallas_call x2, Pallas kernels, call_strips(): pl.pallas_call(strips, in_specs=whole(6), out_specs=whole(2), out_shape=a...  8.66 us
    pallas_call x2, Pallas kernels, call_outer_first(): pl.pallas_call(outer_first, in_specs=whole(7), out_specs=whole(2), out_sh...  5.75 us
    pallas_call x1, Pallas kernels, call_gather(): pl.pallas_call(gather, in_specs=[pl.BlockSpec(memory_space=pltpu.SMEM)] +...  4.63 us
  transfers between devices with their start and end apart: 8, of which 3 were waited for; matrix products, arithmetic and copies ran while one was open for 0% of the time, Pallas kernels for 26%

profile of v4, /device:TPU:1, one launch (start us, length us, event | category | flops | bytes accessed | tf_op | source)
XLA Modules:
  0.0 112.7 jit_solution(8960300951988311346)
XLA Ops:
  0.6 0.0 copy-start
  0.6 3.7 %enter_outer.1 = (f32[1280,128]{1,0:T(8,128)}, f32[1280,128]{1,0:T(8,128)}, f32[1280,128]{1,0:T(8,128)}, f32[1280,128]{1,0:T(8,128)}) custom-call(f32[16,128,256]{2,1,0:T(8,128)} %x_ref.3, f32[4,29,16,128]{3,2,1,0:T(8,128)} %coef_ref.1), custom_call_target="tpu_custom_call" | custom-call | tf_op jit(solution)/shard_map/enter_outer/pallas_call | solution.py:172
  4.3 0.0 copy-start.4
  4.3 0.0 copy-start.5
  4.3 2.2 %collective-permute-start = (f32[1280,128]{1,0:T(8,128)}, f32[1280,128]{1,0:T(8,128)S(1)}, u32[]{:S(2)}, u32[]{:S(2)}) collective-permute-start(f32[1280,128]{1,0:T(8,128)} %get-tuple-element.39), channel_id=1, source_target_pairs={{0,4},{8,12},{16,20},{24,28},{32,36},{40,44},{48,52},{56,60},{64,6... | collective-permute-start | bytes 1966088 | tf_op jit(solution)/shard_map/ppermute | solution.py:603
  6.6 7.8 %collective-permute-start.1 = (f32[1280,128]{1,0:T(8,128)}, f32[1280,128]{1,0:T(8,128)S(1)}, u32[]{:S(2)}, u32[]{:S(2)}) collective-permute-start(f32[1280,128]{1,0:T(8,128)} %get-tuple-element.40), channel_id=1, source_target_pairs={{4,8},{12,16},{20,24},{28,32},{36,40},{44,48},{52,56},{60,64},{68,... | collective-permute-start | bytes 1966088 | tf_op jit(solution)/shard_map/ppermute | solution.py:603
  14.4 0.0 copy-done
  14.4 0.9 enter_inner.1.mid_ref.refs_4_
  15.9 0.0 copy-done.4
  15.9 0.4 coef_edges.1
  16.4 0.0 copy-done.5
  16.4 0.0 copy-start.3
  16.4 2.2 %copy-done.3 = bf16[4096,512]{1,0:T(8,128)(2,1)S(1)} copy-done((bf16[4096,512]{1,0:T(8,128)(2,1)S(1)}, bf16[4096,512]{1,0:T(8,128)(2,1)}, u32[]{:S(2)}) %copy-start.3) | copy-done | bytes 4194328
  18.6 0.0 copy-start.1
  18.6 0.0 copy-start.2
  18.6 4.6 %gather.1.weights_ref = bf16[1024,512]{1,0:T(8,128)(2,1)S(1)} custom-call(s32[1024]{0:T(1024)S(1)} %copy-done.5, bf16[4096,512]{1,0:T(8,128)(2,1)S(1)} %copy-done.3), custom_call_target="tpu_custom_call" | custom-call | tf_op jit(solution)/shard_map/gather/pallas_call | solution.py:523
  23.2 0.0 copy-start.6
  23.2 0.0 copy-done.1
  23.2 0.0 copy-done.2
  23.2 4.9 %inner_first.2 = (f32[3072,128]{1,0:T(8,128)S(1)}, f32[512,128]{1,0:T(8,128)S(1)}) custom-call(f32[1280,128]{1,0:T(8,128)S(1)} %copy-done.1, f32[2048,128]{1,0:T(8,128)S(1)} %enter_inner.1.mid_ref.refs_4_, f32[1280,128]{1,0:T(8,128)S(1)} %copy-done.2, f32[4,29,16,128]{3,2,1,0:T(8,128)S(1)} %get-tuple-element.43.coef_ref.refs_5_.refs_3_), custom_call_target="tpu_custom_call" | custom-call | flops 22806528 | bytes 3145728 | tf_op jit(solution)/shard_map/inner_first/pallas_call | solution.py:234
  28.2 0.0 copy-done.6
  28.2 3.6 %spread.1 = (bf16[2048,512]{1,0:T(8,128)(2,1)S(1)}, bf16[2048,512]{1,0:T(8,128)(2,1)S(1)}) custom-call(s32[1]{0:T(128)S(6)} %copy.8.count_ref, s32[1,1024]{1,0:T(1,128)S(1)} %bitcast.3, bf16[1024,512]{1,0:T(8,128)(2,1)S(1)} %gather.1.weights_ref), custom_call_target="tpu_custom_call" | custom-call | flops 2147483648 | bytes 6291456 | tf_op jit(solution)/shard_map/spread/pallas_call | solution.py:547
  31.8 0.0 collective-permute-done.even_ref
  31.8 0.0 collective-permute-done.1.odd_ref
  31.8 1.6 %halo_edges.2 = (f32[1280,128]{1,0:T(8,128)S(1)}, f32[1280,128]{1,0:T(8,128)S(1)}, f32[640,128]{1,0:T(8,128)S(1)}) custom-call(f32[1280,128]{1,0:T(8,128)S(1)} %collective-permute-done.even_ref, f32[1280,128]{1,0:T(8,128)S(1)} %collective-permute-done.1.odd_ref, f32[512,128]{1,0:T(8,128)S(1)} %get-tuple-element.46.edge_ref, ...), custom_call_target="tpu_custom_call" | custom-call | tf_op jit(solution)/shard_map/halo_edges/pallas_call | solution.py:309
  33.4 3.3 %collective-permute-start.3 = (f32[640,128]{1,0:T(8,128)S(1)}, f32[640,128]{1,0:T(8,128)S(1)}, u32[]{:S(2)}, u32[]{:S(2)}) collective-permute-start(f32[640,128]{1,0:T(8,128)S(1)} %get-tuple-element.53.own_ref.coef_own_ref), channel_id=1, source_target_pairs={{1,2},{2,1},{5,6},{6,5},{9,10},{10,9},{13,14},{14,13},{17,18},{18,... | collective-permute-start | bytes 983048 | tf_op jit(solution)/shard_map/ppermute | solution.py:603
  36.7 0.1 collective-permute-start.2
  36.8 2.9 %outer_first.2 = (f32[1024,128]{1,0:T(8,128)S(1)}, f32[1024,128]{1,0:T(8,128)S(1)}) custom-call(f32[1280,128]{1,0:T(8,128)S(1)} %get-tuple-element.48.top_ref.ctop_ref, f32[1280,128]{1,0:T(8,128)S(1)} %copy-done.1, f32[1280,128]{1,0:T(8,128)S(1)} %copy-done.2, f32[1280,128]{1,0:T(8,128)S(1)} %get-tuple-element.49.bot_ref.cbot_ref, ...), custom_call_target="tpu_custom_call" | custom-call | flops 15204352 | bytes 2097152 | tf_op jit(solution)/shard_map/outer_first/pallas_call | solution.py:347
  39.7 2.1 %collective-permute-done.3.odd_ref.coef_odd_ref = f32[640,128]{1,0:T(8,128)S(1)} collective-permute-done((f32[640,128]{1,0:T(8,128)S(1)}, f32[640,128]{1,0:T(8,128)S(1)}, u32[]{:S(2)}, u32[]{:S(2)}) %collective-permute-start.3) | collective-permute-done | bytes 327712 | tf_op jit(solution)/shard_map/ppermute | solution.py:603
  41.8 0.0 collective-permute-done.2.even_ref.coef_even_ref
  41.8 4.3 %strips.2 = (f32[4,64,128]{2,1,0:T(8,128)S(1)}, f32[4,64,128]{2,1,0:T(8,128)S(1)}) custom-call(f32[640,128]{1,0:T(8,128)S(1)} %collective-permute-done.2.even_ref.coef_even_ref, f32[640,128]{1,0:T(8,128)S(1)} %collective-permute-done.3.odd_ref.coef_odd_ref, f32[640,128]{1,0:T(8,128)S(1)} %get-tuple-element.53.own_ref.coef_own_ref, ...), custom_call_target="tpu_custom_call" | custom-call | tf_op jit(solution)/shard_map/strips/pallas_call | solution.py:433
  46.1 4.3 %second.3 = (f32[1024,128]{1,0:T(8,128)S(1)}, f32[1024,128]{1,0:T(8,128)S(1)}, f32[1024,128]{1,0:T(8,128)S(1)}, f32[1024,128]{1,0:T(8,128)S(1)}) custom-call(f32[1024,128]{1,0:T(8,128)S(1)} %get-tuple-element.50.refs_0_, f32[3072,128]{1,0:T(8,128)S(1)} %get-tuple-element.51.refs_1_.refs_0_, f32[1024,128]{1,0:T(8,128)S(1)} %get-tuple-element.52.refs_2_, ...), custom_call_target="tpu_custom_call" | custom-call | flops 15204352 | bytes 2097152 | tf_op jit(solution)/shard_map/second/pallas_call | solution.py:492
  50.4 0.1 collective-permute-start.4
  50.5 4.8 %collective-permute-start.5 = (f32[1024,128]{1,0:T(8,128)S(1)}, f32[1024,128]{1,0:T(8,128)S(1)}, u32[]{:S(2)}, u32[]{:S(2)}) collective-permute-start(f32[1024,128]{1,0:T(8,128)S(1)} %get-tuple-element.57), channel_id=1, source_target_pairs={{4,8},{12,16},{20,24},{28,32},{36,40},{44,48},{52,56},{60,64},{68,... | collective-permute-start | bytes 1572872 | tf_op jit(solution)/shard_map/ppermute | solution.py:603
  55.3 3.8 %second.4.mid_ref.refs_7_ = f32[2048,128]{1,0:T(8,128)S(1)} custom-call(f32[3072,128]{1,0:T(8,128)S(1)} %get-tuple-element.51.refs_1_.refs_0_, f32[4,64,128]{2,1,0:T(8,128)S(1)} %get-tuple-element.54.refs_3_.refs_1_, f32[4,64,128]{2,1,0:T(8,128)S(1)} %get-tuple-element.55.refs_4_.refs_2_, f32[4,29,16,128]{3,2,1,0:T(8,128)S(1)} %get-tuple-element.43.coef_ref.refs_5_.refs_3_, ...), custom_call_target="tpu_custom_call" | custom-call | flops 15204352 | bytes 2097152 | tf_op jit(solution)/shard_map/second/pallas_call | solution.py:492
  59.1 4.9 %inner_first.3 = (f32[3072,128]{1,0:T(8,128)S(1)}, f32[512,128]{1,0:T(8,128)S(1)}) custom-call(f32[1024,128]{1,0:T(8,128)S(1)} %get-tuple-element.58.low_ref.refs_6_, f32[2048,128]{1,0:T(8,128)S(1)} %second.4.mid_ref.refs_7_, f32[1024,128]{1,0:T(8,128)S(1)} %get-tuple-element.59.high_ref.refs_8_, ...), custom_call_target="tpu_custom_call" | custom-call | flops 22806528 | bytes 3145728 | tf_op jit(solution)/shard_map/inner_first/pallas_call | solution.py:234
  64.1 0.0 collective-permute-done.4.even_ref
  64.1 4.8 %collective-permute-done.5.odd_ref = f32[1024,128]{1,0:T(8,128)S(1)} collective-permute-done((f32[1024,128]{1,0:T(8,128)S(1)}, f32[1024,128]{1,0:T(8,128)S(1)}, u32[]{:S(2)}, u32[]{:S(2)}) %collective-permute-start.5) | collective-permute-done | bytes 524320 | tf_op jit(solution)/shard_map/ppermute | solution.py:603
  68.9 1.4 %halo_edges.3 = (f32[1024,128]{1,0:T(8,128)S(1)}, f32[1024,128]{1,0:T(8,128)S(1)}, f32[512,128]{1,0:T(8,128)S(1)}) custom-call(f32[1024,128]{1,0:T(8,128)S(1)} %collective-permute-done.4.even_ref, f32[1024,128]{1,0:T(8,128)S(1)} %collective-permute-done.5.odd_ref, f32[512,128]{1,0:T(8,128)S(1)} %get-tuple-element.60.edge_ref), custom_call_target="tpu_custom_call" | custom-call | tf_op jit(solution)/shard_map/halo_edges/pallas_call | solution.py:309
  70.3 1.9 %collective-permute-start.7 = (f32[512,128]{1,0:T(8,128)S(1)}, f32[512,128]{1,0:T(8,128)S(1)}, u32[]{:S(2)}, u32[]{:S(2)}) collective-permute-start(f32[512,128]{1,0:T(8,128)S(1)} %get-tuple-element.66.own_ref), channel_id=1, source_target_pairs={{1,2},{2,1},{5,6},{6,5},{9,10},{10,9},{13,14},{14,13},{17,18},{18,... | collective-permute-start | bytes 786440 | tf_op jit(solution)/shard_map/ppermute | solution.py:603
  72.3 0.1 collective-permute-start.6
  72.4 2.9 %outer_first.3 = (f32[1024,128]{1,0:T(8,128)S(1)}, f32[1024,128]{1,0:T(8,128)S(1)}) custom-call(f32[1024,128]{1,0:T(8,128)S(1)} %get-tuple-element.61.top_ref, f32[1024,128]{1,0:T(8,128)S(1)} %get-tuple-element.58.low_ref.refs_6_, f32[1024,128]{1,0:T(8,128)S(1)} %get-tuple-element.59.high_ref.refs_8_, f32[1024,128]{1,0:T(8,128)S(1)} %get-tuple-element.62.bot_ref, ...), custom_call_target="tpu_custom_call" | custom-call | flops 15204352 | bytes 2097152 | tf_op jit(solution)/shard_map/outer_first/pallas_call | solution.py:347
  75.3 2.8 %collective-permute-done.7.odd_ref = f32[512,128]{1,0:T(8,128)S(1)} collective-permute-done((f32[512,128]{1,0:T(8,128)S(1)}, f32[512,128]{1,0:T(8,128)S(1)}, u32[]{:S(2)}, u32[]{:S(2)}) %collective-permute-start.7) | collective-permute-done | bytes 262176 | tf_op jit(solution)/shard_map/ppermute | solution.py:603
  78.0 0.0 collective-permute-done.6.even_ref
  78.0 4.3 %strips.3 = (f32[4,64,128]{2,1,0:T(8,128)S(1)}, f32[4,64,128]{2,1,0:T(8,128)S(1)}) custom-call(f32[512,128]{1,0:T(8,128)S(1)} %collective-permute-done.6.even_ref, f32[512,128]{1,0:T(8,128)S(1)} %collective-permute-done.7.odd_ref, f32[512,128]{1,0:T(8,128)S(1)} %get-tuple-element.66.own_ref, f32[640,128]{1,0:T(8,128)S(1)} %collective-permute-done.2.even_ref.coef_even_ref, ...), custom_call_target="tpu_custom_call" | custom-call | tf_op jit(solution)/shard_map/strips/pallas_call | solution.py:433
  82.4 6.3 %second.5 = (f32[1024,128]{1,0:T(8,128)S(1)}, f32[2048,128]{1,0:T(8,128)S(1)}, f32[1024,128]{1,0:T(8,128)S(1)}) custom-call(f32[1024,128]{1,0:T(8,128)S(1)} %get-tuple-element.63.refs_0_, f32[3072,128]{1,0:T(8,128)S(1)} %get-tuple-element.64.refs_1_, f32[1024,128]{1,0:T(8,128)S(1)} %get-tuple-element.65.refs_2_, ...), custom_call_target="tpu_custom_call" | custom-call | flops 15204352 | bytes 2097152 | tf_op jit(solution)/shard_map/second/pallas_call | solution.py:492
  88.6 3.1 %leave.1 = (f32[16,128,256]{2,1,0:T(8,128)}, f32[512,256]{1,0:T(8,128)S(1)}) custom-call(f32[1024,128]{1,0:T(8,128)S(1)} %get-tuple-element.69.low_ref, f32[2048,128]{1,0:T(8,128)S(1)} %get-tuple-element.70.mid_ref, f32[1024,128]{1,0:T(8,128)S(1)} %get-tuple-element.71.high_ref, bf16[2048,512]{1,0:T(8,128)(2,1)S(1)} %get-tuple-element.72.w_high_ref, ...), custom_call_target="tpu_custom_call" | custom-call | flops 2147483648 | bytes 8388608 | tf_op jit(solution)/shard_map/leave/pallas_call | solution.py:582
  91.8 0.1 reshape.15
  91.9 20.1 %all_to_all.5 = f32[128,4,256]{2,1,0:T(4,128)S(1)} all-to-all(f32[128,4,256]{2,1,0:T(4,128)S(1)} %reshape.15), channel_id=1, replica_groups=mesh['azim'=32,'rad'=4] {'azim','rad'}, dimensions={0} | all-to-all | bytes 1048576 | tf_op jit(solution)/shard_map/all_to_all | solution.py:638
  112.0 0.7 reduce_sum.9
Async XLA Ops:
  0.6 13.8 %copy-start = (f32[16,128,256]{2,1,0:T(8,128)S(1)}, f32[16,128,256]{2,1,0:T(8,128)}, u32[]{:S(2)}) copy-start(f32[16,128,256]{2,1,0:T(8,128)} %x_ref.3) | copy-start | bytes 6291460
  4.3 11.6 %copy-start.4 = (f32[4,29,16,128]{3,2,1,0:T(8,128)S(1)}, f32[4,29,16,128]{3,2,1,0:T(8,128)}, u32[]{:S(2)}) copy-start(f32[4,29,16,128]{3,2,1,0:T(8,128)} %coef_ref.1) | copy-start | bytes 2850820
  4.3 12.0 %copy-start.5 = (s32[1024]{0:T(1024)S(1)}, s32[1024]{0:T(1024)}, u32[]{:S(2)}) copy-start(s32[1024]{0:T(1024)} %rows_ref.1) | copy-start | bytes 12292
  4.3 27.4 %collective-permute-start = (f32[1280,128]{1,0:T(8,128)}, f32[1280,128]{1,0:T(8,128)S(1)}, u32[]{:S(2)}, u32[]{:S(2)}) collective-permute-start(f32[1280,128]{1,0:T(8,128)} %get-tuple-element.39), channel_id=1, source_target_pairs={{0,4},{8,12},{16,20},{24,28},{32,36},{40,44},{48,52},{56,60},{64,6... | collective-permute-start | bytes 1966088 | tf_op jit(solution)/shard_map/ppermute | solution.py:603
  6.6 25.2 %collective-permute-start.1 = (f32[1280,128]{1,0:T(8,128)}, f32[1280,128]{1,0:T(8,128)S(1)}, u32[]{:S(2)}, u32[]{:S(2)}) collective-permute-start(f32[1280,128]{1,0:T(8,128)} %get-tuple-element.40), channel_id=1, source_target_pairs={{4,8},{12,16},{20,24},{28,32},{36,40},{44,48},{52,56},{60,64},{68,... | collective-permute-start | bytes 1966088 | tf_op jit(solution)/shard_map/ppermute | solution.py:603
  16.4 2.2 %copy-start.3 = (bf16[4096,512]{1,0:T(8,128)(2,1)S(1)}, bf16[4096,512]{1,0:T(8,128)(2,1)}, u32[]{:S(2)}) copy-start(bf16[4096,512]{1,0:T(8,128)(2,1)} %table_ref.1) | copy-start | bytes 12582916
  18.6 4.7 %copy-start.1 = (f32[1280,128]{1,0:T(8,128)S(1)}, f32[1280,128]{1,0:T(8,128)}, u32[]{:S(2)}) copy-start(f32[1280,128]{1,0:T(8,128)} %get-tuple-element.41.low_ref.refs_6_) | copy-start | bytes 1966084
  18.6 4.7 %copy-start.2 = (f32[1280,128]{1,0:T(8,128)S(1)}, f32[1280,128]{1,0:T(8,128)}, u32[]{:S(2)}) copy-start(f32[1280,128]{1,0:T(8,128)} %get-tuple-element.42.high_ref.refs_7_) | copy-start | bytes 1966084
  23.2 5.0 %copy-start.6 = (s32[1024]{0:T(1024)S(1)}, s32[1024]{0:T(1024)}, u32[]{:S(2)}) copy-start(s32[1024]{0:T(1024)} %param.8) | copy-start | bytes 12292
  33.4 8.4 %collective-permute-start.3 = (f32[640,128]{1,0:T(8,128)S(1)}, f32[640,128]{1,0:T(8,128)S(1)}, u32[]{:S(2)}, u32[]{:S(2)}) collective-permute-start(f32[640,128]{1,0:T(8,128)S(1)} %get-tuple-element.53.own_ref.coef_own_ref), channel_id=1, source_target_pairs={{1,2},{2,1},{5,6},{6,5},{9,10},{10,9},{13,14},{14,13},{17,18},{18,... | collective-permute-start | bytes 983048 | tf_op jit(solution)/shard_map/ppermute | solution.py:603
  36.7 5.0 %collective-permute-start.2 = (f32[640,128]{1,0:T(8,128)S(1)}, f32[640,128]{1,0:T(8,128)S(1)}, u32[]{:S(2)}, u32[]{:S(2)}) collective-permute-start(f32[640,128]{1,0:T(8,128)S(1)} %get-tuple-element.53.own_ref.coef_own_ref), channel_id=1, source_target_pairs={{0,1},{2,3},{1,0},{3,2},{4,5},{6,7},{5,4},{7,6},{8,9},{10,11},{9,8... | collective-permute-start | bytes 983048 | tf_op jit(solution)/shard_map/ppermute | solution.py:603
  50.4 13.7 %collective-permute-start.4 = (f32[1024,128]{1,0:T(8,128)S(1)}, f32[1024,128]{1,0:T(8,128)S(1)}, u32[]{:S(2)}, u32[]{:S(2)}) collective-permute-start(f32[1024,128]{1,0:T(8,128)S(1)} %get-tuple-element.56), channel_id=1, source_target_pairs={{0,4},{8,12},{16,20},{24,28},{32,36},{40,44},{48,52},{56,60},{64,6... | collective-permute-start | bytes 1572872 | tf_op jit(solution)/shard_map/ppermute | solution.py:603
  50.5 18.4 %collective-permute-start.5 = (f32[1024,128]{1,0:T(8,128)S(1)}, f32[1024,128]{1,0:T(8,128)S(1)}, u32[]{:S(2)}, u32[]{:S(2)}) collective-permute-start(f32[1024,128]{1,0:T(8,128)S(1)} %get-tuple-element.57), channel_id=1, source_target_pairs={{4,8},{12,16},{20,24},{28,32},{36,40},{44,48},{52,56},{60,64},{68,... | collective-permute-start | bytes 1572872 | tf_op jit(solution)/shard_map/ppermute | solution.py:603
  70.3 7.7 %collective-permute-start.7 = (f32[512,128]{1,0:T(8,128)S(1)}, f32[512,128]{1,0:T(8,128)S(1)}, u32[]{:S(2)}, u32[]{:S(2)}) collective-permute-start(f32[512,128]{1,0:T(8,128)S(1)} %get-tuple-element.66.own_ref), channel_id=1, source_target_pairs={{1,2},{2,1},{5,6},{6,5},{9,10},{10,9},{13,14},{14,13},{17,18},{18,... | collective-permute-start | bytes 786440 | tf_op jit(solution)/shard_map/ppermute | solution.py:603
  72.3 5.7 %collective-permute-start.6 = (f32[512,128]{1,0:T(8,128)S(1)}, f32[512,128]{1,0:T(8,128)S(1)}, u32[]{:S(2)}, u32[]{:S(2)}) collective-permute-start(f32[512,128]{1,0:T(8,128)S(1)} %get-tuple-element.66.own_ref), channel_id=1, source_target_pairs={{0,1},{2,3},{1,0},{3,2},{4,5},{6,7},{5,4},{7,6},{8,9},{10,11},{9,8... | collective-permute-start | bytes 786440 | tf_op jit(solution)/shard_map/ppermute | solution.py:603

commit v5 on v4

--- a/solution.py
+++ b/solution.py
@@ -40,18 +40,20 @@
 
 
 ROWS = 256
+WIDTH = 32
+UNROLL = 8
 TAIL = 4 * ROWS
 COEF = 2 * ROWS
 
 
 def window(ref, row, var, half):
-    start = pl.multiple_of(row * ROWS + var * 64 + half * 32, 32)
-    return ref[pl.ds(start, 32), :]
+    start = pl.multiple_of(row * ROWS + var * 64 + half * WIDTH, 8)
+    return ref[pl.ds(start, WIDTH), :]
 
 
 def put(ref, row, var, half, value):
-    start = pl.multiple_of(row * ROWS + var * 64 + half * 32, 32)
-    ref[pl.ds(start, 32), :] = value
+    start = pl.multiple_of(row * ROWS + var * 64 + half * WIDTH, 8)
+    ref[pl.ds(start, WIDTH), :] = value
 
 
 def pick(parts, row, var, half):
@@ -61,18 +63,11 @@
     raise IndexError(row)
 
 
-def place(pack, row, value):
+def place(pack, row, value, cell):
     lane = lanes(value.shape)
     base = 4 * (row + 4)
     here = (lane >= base) & (lane < base + 4)
-    return jnp.where(here, pltpu.roll(value, (base + 2) % 128, axis=1), pack)
-
-
-def place_far(pack, row, value):
-    lane = lanes(value.shape)
-    base = 4 * (row + 4)
-    pack = jnp.where((lane >= base) & (lane < base + 2), pltpu.roll(value, (base + 4) % 128, axis=1), pack)
-    return jnp.where((lane >= base + 2) & (lane < base + 4), pltpu.roll(value, base, axis=1), pack)
+    return jnp.where(here, pltpu.roll(value, (base - cell) % 128, axis=1), pack)
 
 
 def unplace(pack, row):
@@ -83,49 +78,42 @@
 
 
 def each_part(body):
-    @pl.loop(0, 8)
+    halves = 64 // WIDTH
+
+    @pl.loop(0, 4 * halves, unroll=UNROLL)
     def _(step):
-        body(step // 2, step % 2)
-
-
-def sweep(first, stop, source, weight, finish, shift_ref, block=4):
-    for s in range(first - 2, stop + 2):
-        u = source(s)
-        k = s - first + 2
-        shift_ref[0, k] = pltpu.roll(u, 2, axis=1)
-        shift_ref[1, k] = pltpu.roll(u, 1, axis=1)
-        shift_ref[2, k] = pltpu.roll(u, 127, axis=1)
-        shift_ref[3, k] = pltpu.roll(u, 126, axis=1)
-    for begin in range(first, stop, block):
-        totals = [None] * block
-        for s in range(begin - 2, begin + block + 2):
-            k = s - first + 2
+        body(step // halves, step % halves)
+
+
+def sweep(first, stop, source, weight, finish):
+    for row in range(first, stop):
+        sums = [None] * 5
+        for i in range(5):
+            u = source(row + i - 2)
             for j in range(5):
-                x = source(s) if j == 2 else shift_ref[j - (j > 2), k]
-                for b in range(block):
-                    i = s + 2 - begin - b
-                    if 0 <= i < 5:
-                        term = weight(5 * i + j, begin + b) * x
-                        totals[b] = term if totals[b] is None else totals[b] + term
-        for b in range(block):
-            finish(begin + b, totals[b])
-
-
-def inside(lane, k, line):
+                term = weight(5 * i + j, row) * u
+                sums[j] = term if i == 0 else sums[j] + term
+        total = sums[2]
+        for j in (0, 1, 3, 4):
+            total = total + pltpu.roll(sums[j], (2 - j) % 128, axis=1)
+        finish(row, total)
+
+
+def turned(k, line):
     if k >= 25 or k % 5 == 2:
         return line
-    keep = (lane >= 2, lane >= 1, None, lane < 127, lane < 126)[k % 5]
-    return jnp.where(keep, line, 0.0)
+    lane = lanes(line.shape)
+    keep = (lane < 126, lane < 127, None, lane >= 1, lane >= 2)[k % 5]
+    return jnp.where(keep, pltpu.roll(line, (k % 5 - 2) % 128, axis=1), 0.0)
 
 
 def line_of(coef_ref, var, k, row):
-    return jnp.broadcast_to(coef_ref[var, k, row : row + 1], (32, 128))
+    return jnp.broadcast_to(coef_ref[var, k, row : row + 1], (WIDTH, 128))
 
 
 def tail_line(ref, var, k, row):
-    lines = ref.at[pl.ds(pl.multiple_of(TAIL + var * 64, 64), 64)]
-    line = inside(lanes((1, 128)), k, lines[2 * k + row : 2 * k + row + 1])
-    return jnp.broadcast_to(line, (32, 128))
+    lines = ref.at[pl.ds(pl.multiple_of(var * 64, 64), 64)]
+    return jnp.broadcast_to(lines[2 * k + row : 2 * k + row + 1], (WIDTH, 128))
 
 
 def sort_sides(index, even_ref, odd_ref, below_ref, above_ref):
@@ -206,7 +194,7 @@
     )(x)
 
 
-def inner_first(low_ref, mid_ref, high_ref, coef_ref, y_ref, edge_ref, shift_ref):
+def inner_first(low_ref, mid_ref, high_ref, coef_ref, y_ref, edge_ref):
     parts = ((0, 4, low_ref), (4, 12, mid_ref), (12, 16, high_ref))
 
     def one(var, half):
@@ -217,15 +205,15 @@
 
         sweep(
             2, 14, lambda s: pick(parts, s, var, half),
-            lambda k, row: line_of(coef_ref, var, k, row), finish, shift_ref,
+            lambda k, row: line_of(coef_ref, var, k, row), finish,
         )
-        near = jnp.zeros((32, 128), F32)
-        far = jnp.zeros((32, 128), F32)
+        tail = jnp.zeros((WIDTH, 128), F32)
+        head = jnp.zeros((WIDTH, 128), F32)
         for row in range(16):
             value = pick(parts, row, var, half)
-            near, far = place(near, row, value), place_far(far, row, value)
-        put(edge_ref, 0, var, half, near)
-        put(edge_ref, 1, var, half, far)
+            tail, head = place(tail, row, value, 124), place(head, row, value, 0)
+        put(edge_ref, 0, var, half, tail)
+        put(edge_ref, 1, var, half, head)
 
     each_part(one)
 
@@ -236,27 +224,24 @@
         in_specs=whole(4),
         out_specs=whole(2),
         out_shape=arrays((12 * ROWS, 128), (2 * ROWS, 128)),
-        scratch_shapes=[pltpu.VMEM((4, 16, 32, 128), F32)],
         compiler_params=params(),
         cost_estimate=cost(12),
         name="inner_first",
     )(low, mid, high, coef)
 
 
-def coef_edges(coef_ref, out_ref, inside_ref):
-    lane = lanes((16, 128))
-
+def coef_edges(coef_ref, out_ref, turned_ref):
     @pl.loop(0, 4)
     def _(var):
         for k in range(29):
             lines = pl.ds(pl.multiple_of(var * 464 + k * 16, 16), 16)
-            inside_ref[var, k] = inside(lane, k, coef_ref[lines, :])
+            turned_ref[var, k] = turned(k, coef_ref[lines, :])
 
     out_ref[...] = jnp.zeros_like(out_ref)
     for var in range(4):
         pack = jnp.zeros((29, 128), F32)
         for row in range(16):
-            pack = place(pack, row, coef_ref[pl.ds(var * 464 + row, 29, stride=16), :])
+            pack = place(pack, row, coef_ref[pl.ds(var * 464 + row, 29, stride=16), :], 126)
         out_ref[32 * var : 32 * var + 29] = pack
 
 
@@ -272,52 +257,75 @@
 
 
 def halo_edges(even_ref, odd_ref, edge_ref, *refs):
-    top_ref, bot_ref, out_ref = refs[-3:]
+    top_ref, bot_ref, out_ref = refs[len(refs) > 3 :][:3]
     even_is_above = lax.axis_index("azim") % 2 == 0
 
     @pl.when(even_is_above)
     def _():
-        top_ref[...], bot_ref[...] = odd_ref[...], even_ref[...]
+        top_ref[...], bot_ref[...] = odd_ref[:TAIL], even_ref[:TAIL]
 
     @pl.when(jnp.logical_not(even_is_above))
     def _():
-        top_ref[...], bot_ref[...] = even_ref[...], odd_ref[...]
+        top_ref[...], bot_ref[...] = even_ref[:TAIL], odd_ref[:TAIL]
 
     def one(var, half):
-        near = window(edge_ref, 0, var, half)
-        far = window(edge_ref, 1, var, half)
+        tail = window(edge_ref, 0, var, half)
+        head = window(edge_ref, 1, var, half)
         for k in range(4):
             for row, ref in ((k - 4, top_ref), (k + 16, bot_ref)):
                 value = window(ref, k, var, half)
-                near, far = place(near, row, value), place_far(far, row, value)
-        put(out_ref, 0, var, half, near)
-        put(out_ref, 1, var, half, far)
+                tail, head = place(tail, row, value, 124), place(head, row, value, 0)
+        put(out_ref, 0, var, half, tail)
+        put(out_ref, 1, var, half, head)
 
     each_part(one)
-    if len(refs) == 4:
+    if len(refs) > 3:
+        coef_edge_ref, (ctop_ref, cbot_ref) = refs[0], refs[4:]
+
+        @pl.when(even_is_above)
+        def _():
+            ctop_ref[...], cbot_ref[...] = odd_ref[TAIL:], even_ref[TAIL:]
+
+        @pl.when(jnp.logical_not(even_is_above))
+        def _():
+            ctop_ref[...], cbot_ref[...] = even_ref[TAIL:], odd_ref[TAIL:]
+
+        number = lax.broadcasted_iota(jnp.int32, (64, 128), 0) // 2
         for var in range(4):
-            pack = refs[0][32 * var : 32 * var + 29]
+            pack = coef_edge_ref[32 * var : 32 * var + 29]
             for k in range(2):
-                lines = pl.ds(TAIL + 64 * var + k, 29, stride=2)
-                pack = place(pack, k - 2, top_ref[lines, :])
-                pack = place(pack, k + 16, bot_ref[lines, :])
+                lines = pl.ds(64 * var + k, 29, stride=2)
+                pack = place(pack, k - 2, ctop_ref[lines, :], 126)
+                pack = place(pack, k + 16, cbot_ref[lines, :], 126)
             out_ref[COEF + 32 * var : COEF + 32 * var + 29] = pack
             out_ref[COEF + 32 * var + 29 : COEF + 32 * var + 32] = jnp.zeros((3, 128), F32)
+        for var in range(4):
+            at = slice(64 * var, 64 * var + 64)
+            for ref in (ctop_ref, cbot_ref):
+                lines = ref[at]
+                result = lines
+                for j in (0, 1, 3, 4):
+                    here = (number % 5 == j) & (number < 25)
+                    result = jnp.where(here, turned(j, lines), result)
+                ref[at] = result
 
 
 def call_halo_edges(even, odd, edge, *coef_edge):
     return pl.pallas_call(
         halo_edges,
         in_specs=whole(3 + len(coef_edge)),
-        out_specs=whole(3),
-        out_shape=arrays(even.shape, odd.shape, (COEF + 128 * len(coef_edge), 128)),
+        out_specs=whole(3 + 2 * len(coef_edge)),
+        out_shape=arrays(
+            (TAIL, 128), (TAIL, 128), (COEF + 128 * len(coef_edge), 128),
+            *[(256, 128)] * (2 * len(coef_edge)),
+        ),
         compiler_params=params(),
         name="halo_edges",
     )(even, odd, edge, *coef_edge)
 
 
 def outer_first(top_ref, low_ref, high_ref, bot_ref, coef_ref, ctop_ref, cbot_ref,
-                y_low_ref, y_high_ref, shift_ref):
+                y_low_ref, y_high_ref):
     parts = ((-4, 0, top_ref), (0, 4, low_ref), (12, 16, high_ref), (16, 20, bot_ref))
 
     def one(var, half):
@@ -338,7 +346,7 @@
                 put(y_high_ref, row - 14, var, half, value)
 
         for first in (-2, 14):
-            sweep(first, first + 4, lambda s: pick(parts, s, var, half), weight, finish, shift_ref)
+            sweep(first, first + 4, lambda s: pick(parts, s, var, half), weight, finish)
 
     each_part(one)
 
@@ -349,96 +357,125 @@
         in_specs=whole(7),
         out_specs=whole(2),
         out_shape=arrays((4 * ROWS, 128), (4 * ROWS, 128)),
-        scratch_shapes=[pltpu.VMEM((4, 8, 32, 128), F32)],
         compiler_params=params(),
         cost_estimate=cost(8),
         name="outer_first",
     )(top, low, high, bot, coef, ctop, cbot)
 
 
-def strips(even_ref, odd_ref, own_ref, coef_even_ref, coef_odd_ref, coef_own_ref,
-           mend_y_ref, mend_u_ref, rim_ref, line_ref):
+def strip_lines(even_ref, odd_ref, own_ref, out_ref):
     entry = lanes((32, 128)) % 4
-    entry_line = lanes((1, 128)) % 4
     even_is_right = lanes((32, 128)) * 0 + lax.axis_index("rad") % 2 == 0
-
-    def merge(even, odd):
+    number = lax.broadcasted_iota(jnp.int32, (32, 128), 0)
+    for var in range(4):
+        at = slice(COEF + 32 * var, COEF + 32 * var + 32)
+        even, odd = even_ref[at], odd_ref[at]
         right = jnp.where(even_is_right, even, odd)
         left = jnp.where(even_is_right, odd, even)
-        return jnp.where(entry < 2, pltpu.roll(right, 126, axis=1), pltpu.roll(left, 2, axis=1))
-
-    def rows_on(pack, i):
-        turn = (4 * (2 - i)) % 128
-        return pltpu.roll(pack, turn, axis=1) if turn else pack
-
-    def rim_of(var, half):
-        at = pl.ds(pl.multiple_of(half * 32, 32), 32)
-        rim_ref[var, at] = merge(window(even_ref, 0, var, half), window(odd_ref, 0, var, half))
-
-    each_part(rim_of)
-
-    @pl.loop(0, 4)
-    def _(var):
-        lines = pl.ds(pl.multiple_of(COEF + var * 32, 32), 32)
-        own = coef_own_ref.at[lines]
-        line_ref[var, 0:32] = merge(coef_even_ref[lines, :], coef_odd_ref[lines, :])
+        lines = jnp.where(entry < 2, pltpu.roll(right, 126, axis=1), pltpu.roll(left, 2, axis=1))
+        result = lines
+        for i in (0, 1, 3, 4):
+            here = (number >= 5 * i) & (number < 5 * i + 5)
+            result = jnp.where(here, pltpu.roll(lines, (4 * (i - 2)) % 128, axis=1), result)
+        out_ref[var, 0:32] = result
+        own = own_ref.at[at]
+        one_entry = entry[0:1]
         for i in range(5):
             k = 5 * i
-            two = jnp.where(entry_line < 2, own[k + 4 : k + 5], own[k : k + 1])
-            one = jnp.where(entry_line == 1, own[k + 3 : k + 4], 0.0)
-            one = jnp.where(entry_line == 2, own[k + 1 : k + 2], one)
-            line_ref[var, 32 + i : 33 + i] = two
-            line_ref[var, 37 + i : 38 + i] = one
-
-    def one_part(var, half):
-        at = pl.ds(pl.multiple_of(half * 32, 32), 32)
-
-        def line(k):
-            return jnp.broadcast_to(line_ref[var, k : k + 1], (32, 128))
-
-        def beyond(rim):
-            crossed = jnp.where(entry == 1, pltpu.roll(rim, 1, axis=1), pltpu.roll(rim, 127, axis=1))
-            total = line(32) * rows_on(rim, 0) + line(37) * rows_on(crossed, 0)
-            for i in range(1, 5):
-                total = total + line(32 + i) * rows_on(rim, i) + line(37 + i) * rows_on(crossed, i)
-            return total
-
-        near = window(own_ref, 0, var, half)
-        rim = rim_ref[var, at]
-        outer = merge(window(even_ref, 1, var, half), window(odd_ref, 1, var, half))
-        before = jnp.where(
-            entry == 0, pltpu.roll(near, 127, axis=1),
-            jnp.where(entry == 2, pltpu.roll(outer, 127, axis=1), pltpu.roll(rim, 1, axis=1)),
+            two = jnp.where(one_entry < 2, own[k + 4 : k + 5], own[k : k + 1])
+            one = jnp.where(one_entry == 1, own[k + 3 : k + 4], 0.0)
+            one = jnp.where(one_entry == 2, own[k + 1 : k + 2], one)
+            turn = (4 * (i - 2)) % 128
+            out_ref[var, 32 + i : 33 + i] = pltpu.roll(two, turn, axis=1) if turn else two
+            out_ref[var, 37 + i : 38 + i] = pltpu.roll(one, turn, axis=1) if turn else one
+        out_ref[var, 42:48] = jnp.zeros((6, 128), F32)
+
+
+def call_strip_lines(even, odd, own):
+    return pl.pallas_call(
+        strip_lines,
+        in_specs=whole(3),
+        out_specs=whole(1)[0],
+        out_shape=arrays((4, 48, 128))[0],
+        compiler_params=params(),
+        name="strip_lines",
+    )(even, odd, own)
+
+
+def strips(even_ref, odd_ref, own_ref, line_ref, mend_y_ref, mend_u_ref, shift_ref):
+    entry = lanes((32, 128)) % 4
+    even_is_right = lanes((32, 128)) * 0 + lax.axis_index("rad") % 2 == 0
+    every = [(var, half) for var in range(4) for half in range(2)]
+
+    def part(ref, kind, var, half):
+        start = kind * ROWS + var * 64 + half * 32
+        return ref[start : start + 32]
+
+    def line(var, k):
+        return jnp.broadcast_to(line_ref[var, k : k + 1], (32, 128))
+
+    def turn(pack, by):
+        return pltpu.roll(pack, by % 128, axis=1)
+
+    def over_rows(sums):
+        total = sums[2]
+        for i in (0, 1, 3, 4):
+            total = total + turn(sums[i], 4 * (2 - i))
+        return total
+
+    def beyond(var, rim, crossed):
+        return over_rows([line(var, 32 + i) * rim + line(var, 37 + i) * crossed for i in range(5)])
+
+    for var, half in every:
+        at = slice(32 * half, 32 * half + 32)
+        tail = jnp.where(even_is_right, part(odd_ref, 0, var, half), part(even_ref, 0, var, half))
+        head = jnp.where(even_is_right, part(even_ref, 1, var, half), part(odd_ref, 1, var, half))
+        rim = jnp.where(entry < 2, head, tail)
+        outer = jnp.where(entry < 2, tail, head)
+        own = jnp.where(entry < 2, part(own_ref, 1, var, half), part(own_ref, 0, var, half))
+        up, down = turn(rim, 1), turn(rim, -1)
+        shift_ref[0, var, at] = jnp.where(entry < 2, turn(own, -2), turn(outer, 2))
+        shift_ref[1, var, at] = jnp.where(
+            entry == 0, turn(own, -3), jnp.where(entry == 2, turn(outer, 1), up)
         )
-        after = jnp.where(
-            entry == 1, pltpu.roll(outer, 1, axis=1),
-            jnp.where(entry == 3, pltpu.roll(near, 1, axis=1), pltpu.roll(rim, 127, axis=1)),
+        shift_ref[2, var, at] = rim
+        shift_ref[3, var, at] = jnp.where(
+            entry == 3, turn(own, 3), jnp.where(entry == 1, turn(outer, -1), down)
         )
-        shifted = (
-            jnp.where(entry < 2, near, outer), before, rim, after, jnp.where(entry < 2, outer, near),
-        )
-        total = line(25) * rim_ref[0, at]
-        for w in range(1, 4):
-            total = total + line(25 + w) * rim_ref[w, at]
-        for j in range(5):
-            for i in range(5):
-                total = total + line(5 * i + j) * rows_on(shifted[j], i)
-        mend_y_ref[var, at] = 0.5 * beyond(rim)
-        mend_u_ref[var, at] = beyond(rim + 0.5 * total)
-
-    each_part(one_part)
-
-
-def call_strips(even, odd, own, coef_even, coef_odd, coef_own):
+        shift_ref[4, var, at] = jnp.where(entry < 2, turn(outer, -2), turn(own, 2))
+        shift_ref[5, var, at] = jnp.where(entry == 1, up, down)
+    for var, half in every:
+        at = slice(32 * half, 32 * half + 32)
+        mend_y_ref[var, at] = 0.5 * beyond(var, shift_ref[2, var, at], shift_ref[5, var, at])
+    for var, half in every:
+        at = slice(32 * half, 32 * half + 32)
+        sums = []
+        for i in range(5):
+            total = line(var, 5 * i) * shift_ref[0, var, at]
+            for j in range(1, 5):
+                total = total + line(var, 5 * i + j) * shift_ref[j, var, at]
+            sums.append(total)
+        total = over_rows(sums)
+        for w in range(4):
+            total = total + line(var, 25 + w) * shift_ref[2, w, at]
+        shift_ref[6, var, at] = shift_ref[2, var, at] + 0.5 * total
+    for var, half in every:
+        at = slice(32 * half, 32 * half + 32)
+        rim = shift_ref[6, var, at]
+        crossed = jnp.where(entry == 1, turn(rim, 1), turn(rim, -1))
+        mend_u_ref[var, at] = beyond(var, rim, crossed)
+
+
+def call_strips(even, odd, own, lines):
     return pl.pallas_call(
         strips,
-        in_specs=whole(6),
+        in_specs=whole(4),
         out_specs=whole(2),
         out_shape=arrays((4, 64, 128), (4, 64, 128)),
-        scratch_shapes=[pltpu.VMEM((4, 64, 128), F32), pltpu.VMEM((4, 48, 128), F32)],
+        scratch_shapes=[pltpu.VMEM((7, 4, 64, 128), F32)],
         compiler_params=params(),
         name="strips",
-    )(even, odd, own, coef_even, coef_odd, coef_own)
+    )(even, odd, own, lines)
 
 
 PARTS = ((0, 4), (4, 12), (12, 16))
@@ -449,7 +486,7 @@
     mend_y_ref, mend_u_ref, coef_ref = refs[:3]
     u_refs, refs = refs[3 : 3 + len(parts)], refs[3 + len(parts) :]
     out_refs, refs = refs[: len(parts)], refs[len(parts) :]
-    y_ref, shift_ref = refs[-2:]
+    y_ref = refs[-1]
     bounds = {1: ((2, 14),), 3: ((-2, 2), (2, 14), (14, 18))}[n_y]
     y_parts = [(first, stop, ref) for (first, stop), ref in zip(bounds, y_refs)]
     u_parts = [(first, stop, ref) for (first, stop), ref in zip(parts, u_refs)]
@@ -457,14 +494,14 @@
     whole_y = ((-2, 18, y_ref),)
 
     def mend(var, half):
-        pack = mend_y_ref[var, pl.ds(pl.multiple_of(half * 32, 32), 32)]
+        pack = mend_y_ref[var, pl.ds(pl.multiple_of(half * WIDTH, WIDTH), WIDTH)]
         for row in sources:
             put(y_ref, row + 2, var, half, pick(y_parts, row, var, half) + unplace(pack, row))
 
     each_part(mend)
 
     def one(var, half):
-        pack = mend_u_ref[var, pl.ds(pl.multiple_of(half * 32, 32), 32)]
+        pack = mend_u_ref[var, pl.ds(pl.multiple_of(half * WIDTH, WIDTH), WIDTH)]
 
         def finish(row, total):
             for w in range(4):
@@ -477,7 +514,7 @@
         for first, stop in ranges:
             sweep(
                 first, stop, lambda s: pick(whole_y, s, var, half),
-                lambda k, row: line_of(coef_ref, var, k, row), finish, shift_ref,
+                lambda k, row: line_of(coef_ref, var, k, row), finish,
             )
 
     each_part(one)
@@ -488,13 +525,12 @@
 def call_second(ranges, parts, ys, mend_y, mend_u, coef, us, sides=False):
     outs = [((stop - first) * ROWS, 128) for first, stop in parts]
     outs += [outs[0]] * (2 * sides)
-    most = max(stop - first for first, stop in ranges)
     return pl.pallas_call(
         functools.partial(second, ranges, parts, len(ys), sides),
         in_specs=whole(len(ys) + 3 + len(us)),
         out_specs=whole(len(outs)),
         out_shape=arrays(*outs),
-        scratch_shapes=[pltpu.VMEM((20 * ROWS, 128), F32), pltpu.VMEM((4, most + 4, 32, 128), F32)],
+        scratch_shapes=[pltpu.VMEM((20 * ROWS, 128), F32)],
         compiler_params=params(),
         cost_estimate=cost(8),
         name="second",
@@ -557,17 +593,19 @@
     )(count, cells, weights)
 
 
-def leave(low_ref, mid_ref, high_ref, w_high_ref, w_low_ref, out_ref, markov_ref):
-    parts = ((0, 4, low_ref), (4, 12, mid_ref), (12, 16, high_ref))
+def leave(low_ref, mid_ref, high_ref, w_high_ref, w_low_ref, out_ref, markov_ref, turned_ref, sems):
+    copies = []
+    rows = []
+    for k, ((first, stop), ref) in enumerate(zip(PARTS, (low_ref, mid_ref, high_ref))):
+        for row in range(first, stop):
+            rows.append(ref.at[(row - first) * ROWS : (row - first + 1) * ROWS])
+            turned_ref[row] = rows[-1][...].T
+        at = pl.ds(first, stop - first)
+        copies.append(pltpu.make_async_copy(turned_ref.at[at], out_ref.at[at], sems.at[k]))
+        copies[-1].start()
     sums = jnp.zeros((256, 512), F32)
     for k in range(8):
-        rows = []
-        for row in (2 * k, 2 * k + 1):
-            for first, stop, ref in parts:
-                if first <= row < stop:
-                    rows.append(ref[(row - first) * ROWS : (row - first + 1) * ROWS])
-            out_ref[row] = rows[-1].T
-        u = jnp.concatenate(rows, axis=1)
+        u = jnp.concatenate([rows[2 * k][...], rows[2 * k + 1][...]], axis=1)
         u_high = u.astype(BF16)
         u_low = (u - u_high.astype(F32)).astype(BF16)
         w_high = w_high_ref[256 * k : 256 * k + 256]
@@ -576,14 +614,17 @@
         sums = sums + jnp.dot(u_low, w_high, preferred_element_type=F32)
         sums = sums + jnp.dot(u_high, w_low, preferred_element_type=F32)
     markov_ref[...] = sums.T
+    for copy in copies:
+        copy.wait()
 
 
 def call_leave(low, mid, high, w_high, w_low):
     return pl.pallas_call(
         leave,
         in_specs=whole(5),
-        out_specs=whole(2),
+        out_specs=[pl.BlockSpec(memory_space=pltpu.HBM)] + whole(1),
         out_shape=arrays((16, 128, 256), (512, 256)),
+        scratch_shapes=[pltpu.VMEM((16, 128, 256), F32), pltpu.SemaphoreType.DMA((3,))],
         compiler_params=params(),
         cost_estimate=pl.CostEstimate(flops=2 << 30, bytes_accessed=8 << 20, transcendentals=0),
         name="leave",
@@ -615,16 +656,15 @@
         y_mid, edge = call_inner_first(low, mid, high, coef)
         if step == 0:
             edge, w_high = lax.optimization_barrier((edge, w_high))
-            top, bot, own = call_halo_edges(even, odd, edge, coef_edge)
-            tails = top, bot
+            top, bot, own, *tails = call_halo_edges(even, odd, edge, coef_edge)
         else:
             top, bot, own = call_halo_edges(even, odd, edge)
         sides = swap(own, "rad", 0), swap(own, "rad", 1), own
-        if step == 0:
-            coef_sides = sides
         ys = call_outer_first(top, low, high, bot, coef, *tails)
         ys = ys[0], y_mid, ys[1]
-        mends = call_strips(*sides, *coef_sides)
+        if step == 0:
+            lines = call_strip_lines(*sides)
+        mends = call_strips(*sides, lines)
         if step < STEPS - 1:
             (new_mid,) = call_second(((4, 12),), PARTS[1:2], ys[1:2], *mends, coef, (mid,))
             low, high, even, odd = call_second(

time: 113 us -> 101 us (0.89)
  Pallas kernels: 58 us -> 41.2 us
  waiting for transfers between devices: 9.64 us -> 12.1 us
  starting transfers between devices: 20.4 us -> 22.1 us
    pallas_call x3 -> x4, Pallas kernels: 11.8 us -> 5.58 us  [the longest x1 2.8 us: call_leave(): pl.pallas_call(leave, in_specs=whole(5), out_specs=[pl.BlockSpec(memory_s...]
    pallas_call x3, Pallas kernels: 14.4 us -> 9.3 us  [call_second(): pl.pallas_call(functools.partial(second, ranges, parts, len(ys), sides),...]
    pallas_call x2, Pallas kernels: 9.88 us -> 7.03 us  [call_inner_first(): pl.pallas_call(inner_first, in_specs=whole(4), out_specs=whole(2), out_sh...]
    ppermute x8, waiting for transfers between devices: 9.64 us -> 12.1 us  [swap(): return lax.ppermute(block, axis, swaps(count, odd, axis == 'azim'))]
    ppermute x8, starting transfers between devices: 20.4 us -> 22.1 us  [swap(): return lax.ppermute(block, axis, swaps(count, odd, axis == 'azim'))]
    pallas_call x2, Pallas kernels: 5.75 us -> 4.08 us  [call_outer_first(): pl.pallas_call(outer_first, in_specs=whole(7), out_specs=whole(2), out_sh...]
    pallas_call x2, Pallas kernels: 3 us -> 1.69 us  [call_halo_edges(): pl.pallas_call(halo_edges, in_specs=whole(3 + len(coef_edge)), out_specs=...]
  transfers between devices with their start and end apart: 8 -> 8, of which waited for: 3 -> 4; matrix products, arithmetic and copies ran while one was open for 0% -> 0% of each run, Pallas kernels for 26% -> 23%
where the time goes in v5:
time: 101 us
  Pallas kernels  41.2 us (41%)
  starting transfers between devices  22.1 us (22%)
  blocking collectives  21.1 us (21%)
  waiting for transfers between devices  12.1 us (12%)
  local copies, waits for them, and re-layouts  2.36 us (2%)
  between operations  1.55 us (2%)
    ppermute x8, starting transfers between devices, swap(): return lax.ppermute(block, axis, swaps(count, odd, axis == 'azim'))  22.1 us
    all_to_all x1, blocking collectives, body(): lax.all_to_all(term.reshape(count, -1, term.shape[1]), ('azim', 'rad'), 0...  21.1 us
    ppermute x8, waiting for transfers between devices, swap(): return lax.ppermute(block, axis, swaps(count, odd, axis == 'azim'))  12.1 us
    pallas_call x3, Pallas kernels, call_second(): pl.pallas_call(functools.partial(second, ranges, parts, len(ys), sides),...  9.3 us
    pallas_call x2, Pallas kernels, call_inner_first(): pl.pallas_call(inner_first, in_specs=whole(4), out_specs=whole(2), out_sh...  7.03 us
    pallas_call x1, Pallas kernels, call_gather(): pl.pallas_call(gather, in_specs=[pl.BlockSpec(memory_space=pltpu.SMEM)] +...  4.63 us
    pallas_call x2, Pallas kernels, call_outer_first(): pl.pallas_call(outer_first, in_specs=whole(7), out_specs=whole(2), out_sh...  4.08 us
    pallas_call x1, Pallas kernels, call_enter_outer(): pl.pallas_call(enter_outer, in_specs=[pl.BlockSpec(memory_space=pltpu.HBM...  3.67 us
  transfers between devices with their start and end apart: 8, of which 4 were waited for; matrix products, arithmetic and copies ran while one was open for 0% of the time, Pallas kernels for 23%

profile of v5, /device:TPU:1, one launch (start us, length us, event | category | flops | bytes accessed | tf_op | source)
XLA Modules:
  0.0 101.2 jit_solution(10714907421025572714)
XLA Ops:
  0.6 0.0 copy-start
  0.6 3.7 %enter_outer.1 = (f32[1280,128]{1,0:T(8,128)}, f32[1280,128]{1,0:T(8,128)}, f32[1280,128]{1,0:T(8,128)}, f32[1280,128]{1,0:T(8,128)}) custom-call(f32[16,128,256]{2,1,0:T(8,128)} %x_ref.3, f32[4,29,16,128]{3,2,1,0:T(8,128)} %coef_ref.1), custom_call_target="tpu_custom_call" | custom-call | tf_op jit(solution)/shard_map/enter_outer/pallas_call | solution.py:160
  4.3 0.0 copy-start.4
  4.3 0.0 copy-start.5
  4.3 2.2 %collective-permute-start = (f32[1280,128]{1,0:T(8,128)}, f32[1280,128]{1,0:T(8,128)S(1)}, u32[]{:S(2)}, u32[]{:S(2)}) collective-permute-start(f32[1280,128]{1,0:T(8,128)} %get-tuple-element.41), channel_id=1, source_target_pairs={{0,4},{8,12},{16,20},{24,28},{32,36},{40,44},{48,52},{56,60},{64,6... | collective-permute-start | bytes 1966088 | tf_op jit(solution)/shard_map/ppermute | solution.py:644
  6.6 7.8 %collective-permute-start.1 = (f32[1280,128]{1,0:T(8,128)}, f32[1280,128]{1,0:T(8,128)S(1)}, u32[]{:S(2)}, u32[]{:S(2)}) collective-permute-start(f32[1280,128]{1,0:T(8,128)} %get-tuple-element.42), channel_id=1, source_target_pairs={{4,8},{12,16},{20,24},{28,32},{36,40},{44,48},{52,56},{60,64},{68,... | collective-permute-start | bytes 1966088 | tf_op jit(solution)/shard_map/ppermute | solution.py:644
  14.4 0.0 copy-done
  14.4 0.9 enter_inner.1.mid_ref.refs_4_
  15.9 0.0 copy-done.4
  15.9 0.8 coef_edges.1
  16.7 0.0 copy-done.5
  16.7 0.0 copy-start.3
  16.7 2.2 %copy-done.3 = bf16[4096,512]{1,0:T(8,128)(2,1)S(1)} copy-done((bf16[4096,512]{1,0:T(8,128)(2,1)S(1)}, bf16[4096,512]{1,0:T(8,128)(2,1)}, u32[]{:S(2)}) %copy-start.3) | copy-done | bytes 4194328
  18.9 0.0 copy-start.1
  18.9 0.0 copy-start.2
  18.9 4.6 %gather.1.weights_ref = bf16[1024,512]{1,0:T(8,128)(2,1)S(1)} custom-call(s32[1024]{0:T(1024)S(1)} %copy-done.5, bf16[4096,512]{1,0:T(8,128)(2,1)S(1)} %copy-done.3), custom_call_target="tpu_custom_call" | custom-call | tf_op jit(solution)/shard_map/gather/pallas_call | solution.py:559
  23.6 0.0 copy-start.6
  23.6 0.0 copy-done.1
  23.6 0.0 copy-done.2
  23.6 3.5 %inner_first.2 = (f32[3072,128]{1,0:T(8,128)S(1)}, f32[512,128]{1,0:T(8,128)S(1)}) custom-call(f32[1280,128]{1,0:T(8,128)S(1)} %copy-done.1, f32[2048,128]{1,0:T(8,128)S(1)} %enter_inner.1.mid_ref.refs_4_, f32[1280,128]{1,0:T(8,128)S(1)} %copy-done.2, f32[4,29,16,128]{3,2,1,0:T(8,128)S(1)} %get-tuple-element.45.coef_ref.refs_5_.refs_3_), custom_call_target="tpu_custom_call" | custom-call | flops 22806528 | bytes 3145728 | tf_op jit(solution)/shard_map/inner_first/pallas_call | solution.py:222
  27.1 0.0 copy-done.6
  27.1 3.6 %spread.1 = (bf16[2048,512]{1,0:T(8,128)(2,1)S(1)}, bf16[2048,512]{1,0:T(8,128)(2,1)S(1)}) custom-call(s32[1]{0:T(128)S(6)} %copy.8.count_ref, s32[1,1024]{1,0:T(1,128)S(1)} %bitcast.3, bf16[1024,512]{1,0:T(8,128)(2,1)S(1)} %gather.1.weights_ref), custom_call_target="tpu_custom_call" | custom-call | flops 2147483648 | bytes 6291456 | tf_op jit(solution)/shard_map/spread/pallas_call | solution.py:583
  30.7 0.0 collective-permute-done.even_ref
  30.7 0.0 collective-permute-done.1.odd_ref
  30.7 1.0 %halo_edges.2 = (f32[1024,128]{1,0:T(8,128)S(1)}, f32[1024,128]{1,0:T(8,128)S(1)}, f32[640,128]{1,0:T(8,128)S(1)}, f32[256,128]{1,0:T(8,128)S(1)}, f32[256,128]{1,0:T(8,128)S(1)}) custom-call(f32[1280,128]{1,0:T(8,128)S(1)} %collective-permute-done.even_ref, f32[1280,128]{1,0:T(8,128)S(1)} %collective-permute-done.1.odd_ref, ...), custom_call_target="tpu_custom_call" | custom-call | tf_op jit(solution)/shard_map/halo_edges/pallas_call | solution.py:314
  31.8 3.3 %collective-permute-start.3 = (f32[640,128]{1,0:T(8,128)S(1)}, f32[640,128]{1,0:T(8,128)S(1)}, u32[]{:S(2)}, u32[]{:S(2)}) collective-permute-start(f32[640,128]{1,0:T(8,128)S(1)} %get-tuple-element.57.own_ref), channel_id=1, source_target_pairs={{1,2},{2,1},{5,6},{6,5},{9,10},{10,9},{13,14},{14,13},{17,18},{18,... | collective-permute-start | bytes 983048 | tf_op jit(solution)/shard_map/ppermute | solution.py:644
  35.1 0.3 collective-permute-start.2
  35.4 2.0 %outer_first.2 = (f32[1024,128]{1,0:T(8,128)S(1)}, f32[1024,128]{1,0:T(8,128)S(1)}) custom-call(f32[1024,128]{1,0:T(8,128)S(1)} %get-tuple-element.50.top_ref, f32[1280,128]{1,0:T(8,128)S(1)} %copy-done.1, f32[1280,128]{1,0:T(8,128)S(1)} %copy-done.2, f32[1024,128]{1,0:T(8,128)S(1)} %get-tuple-element.51.bot_ref, ...), custom_call_target="tpu_custom_call" | custom-call | flops 15204352 | bytes 2097152 | tf_op jit(solution)/shard_map/outer_first/pallas_call | solution.py:355
  37.5 2.7 %collective-permute-done.3.odd_ref = f32[640,128]{1,0:T(8,128)S(1)} collective-permute-done((f32[640,128]{1,0:T(8,128)S(1)}, f32[640,128]{1,0:T(8,128)S(1)}, u32[]{:S(2)}, u32[]{:S(2)}) %collective-permute-start.3) | collective-permute-done | bytes 327712 | tf_op jit(solution)/shard_map/ppermute | solution.py:644
  40.2 0.0 collective-permute-done.2.even_ref
  40.2 0.2 strip_lines.1.line_ref
  40.4 1.3 %strips.2 = (f32[4,64,128]{2,1,0:T(8,128)S(1)}, f32[4,64,128]{2,1,0:T(8,128)S(1)}) custom-call(f32[640,128]{1,0:T(8,128)S(1)} %collective-permute-done.2.even_ref, f32[640,128]{1,0:T(8,128)S(1)} %collective-permute-done.3.odd_ref, f32[640,128]{1,0:T(8,128)S(1)} %get-tuple-element.57.own_ref, f32[4,48,128]{2,1,0:T(8,128)S(1)} %strip_lines.1.line_ref), custom_call_target="tpu_custom_call" | custom-call | tf_op jit(solution)/shard_map/strips/pallas_call | solution.py:470
  41.7 2.5 %second.3 = (f32[1024,128]{1,0:T(8,128)S(1)}, f32[1024,128]{1,0:T(8,128)S(1)}, f32[1024,128]{1,0:T(8,128)S(1)}, f32[1024,128]{1,0:T(8,128)S(1)}) custom-call(f32[1024,128]{1,0:T(8,128)S(1)} %get-tuple-element.54.refs_0_, f32[3072,128]{1,0:T(8,128)S(1)} %get-tuple-element.55.refs_1_.refs_0_, f32[1024,128]{1,0:T(8,128)S(1)} %get-tuple-element.56.refs_2_, ...), custom_call_target="tpu_custom_call" | custom-call | flops 15204352 | bytes 2097152 | tf_op jit(solution)/shard_map/second/pallas_call | solution.py:528
  44.2 0.1 collective-permute-start.4
  44.3 6.1 %collective-permute-start.5 = (f32[1024,128]{1,0:T(8,128)S(1)}, f32[1024,128]{1,0:T(8,128)S(1)}, u32[]{:S(2)}, u32[]{:S(2)}) collective-permute-start(f32[1024,128]{1,0:T(8,128)S(1)} %get-tuple-element.61), channel_id=1, source_target_pairs={{4,8},{12,16},{20,24},{28,32},{36,40},{44,48},{52,56},{60,64},{68,... | collective-permute-start | bytes 1572872 | tf_op jit(solution)/shard_map/ppermute | solution.py:644
  50.4 2.3 %second.4.mid_ref.refs_7_ = f32[2048,128]{1,0:T(8,128)S(1)} custom-call(f32[3072,128]{1,0:T(8,128)S(1)} %get-tuple-element.55.refs_1_.refs_0_, f32[4,64,128]{2,1,0:T(8,128)S(1)} %get-tuple-element.58.refs_3_.refs_1_, f32[4,64,128]{2,1,0:T(8,128)S(1)} %get-tuple-element.59.refs_4_.refs_2_, f32[4,29,16,128]{3,2,1,0:T(8,128)S(1)} %get-tuple-element.45.coef_ref.refs_5_.refs_3_, ...), custom_call_target="tpu_custom_call" | custom-call | flops 15204352 | bytes 2097152 | tf_op jit(solution)/shard_map/second/pallas_call | solution.py:528
  52.7 3.5 %inner_first.3 = (f32[3072,128]{1,0:T(8,128)S(1)}, f32[512,128]{1,0:T(8,128)S(1)}) custom-call(f32[1024,128]{1,0:T(8,128)S(1)} %get-tuple-element.62.low_ref.refs_6_, f32[2048,128]{1,0:T(8,128)S(1)} %second.4.mid_ref.refs_7_, f32[1024,128]{1,0:T(8,128)S(1)} %get-tuple-element.63.high_ref.refs_8_, ...), custom_call_target="tpu_custom_call" | custom-call | flops 22806528 | bytes 3145728 | tf_op jit(solution)/shard_map/inner_first/pallas_call | solution.py:222
  56.2 0.2 collective-permute-done.4.even_ref
  56.5 5.7 %collective-permute-done.5.odd_ref = f32[1024,128]{1,0:T(8,128)S(1)} collective-permute-done((f32[1024,128]{1,0:T(8,128)S(1)}, f32[1024,128]{1,0:T(8,128)S(1)}, u32[]{:S(2)}, u32[]{:S(2)}) %collective-permute-start.5) | collective-permute-done | bytes 524320 | tf_op jit(solution)/shard_map/ppermute | solution.py:644
  62.2 0.6 halo_edges.3
  62.9 1.9 %collective-permute-start.7 = (f32[512,128]{1,0:T(8,128)S(1)}, f32[512,128]{1,0:T(8,128)S(1)}, u32[]{:S(2)}, u32[]{:S(2)}) collective-permute-start(f32[512,128]{1,0:T(8,128)S(1)} %get-tuple-element.70.own_ref), channel_id=1, source_target_pairs={{1,2},{2,1},{5,6},{6,5},{9,10},{10,9},{13,14},{14,13},{17,18},{18,... | collective-permute-start | bytes 786440 | tf_op jit(solution)/shard_map/ppermute | solution.py:644
  64.8 0.3 collective-permute-start.6
  65.2 2.0 %outer_first.3 = (f32[1024,128]{1,0:T(8,128)S(1)}, f32[1024,128]{1,0:T(8,128)S(1)}) custom-call(f32[1024,128]{1,0:T(8,128)S(1)} %get-tuple-element.65.top_ref, f32[1024,128]{1,0:T(8,128)S(1)} %get-tuple-element.62.low_ref.refs_6_, f32[1024,128]{1,0:T(8,128)S(1)} %get-tuple-element.63.high_ref.refs_8_, f32[1024,128]{1,0:T(8,128)S(1)} %get-tuple-element.66.bot_ref, ...), custom_call_target="tpu_custom_call" | custom-call | flops 15204352 | bytes 2097152 | tf_op jit(solution)/shard_map/outer_first/pallas_call | solution.py:355
  67.2 3.3 %collective-permute-done.7.odd_ref = f32[512,128]{1,0:T(8,128)S(1)} collective-permute-done((f32[512,128]{1,0:T(8,128)S(1)}, f32[512,128]{1,0:T(8,128)S(1)}, u32[]{:S(2)}, u32[]{:S(2)}) %collective-permute-start.7) | collective-permute-done | bytes 262176 | tf_op jit(solution)/shard_map/ppermute | solution.py:644
  70.6 0.0 collective-permute-done.6.even_ref
  70.6 1.3 %strips.3 = (f32[4,64,128]{2,1,0:T(8,128)S(1)}, f32[4,64,128]{2,1,0:T(8,128)S(1)}) custom-call(f32[512,128]{1,0:T(8,128)S(1)} %collective-permute-done.6.even_ref, f32[512,128]{1,0:T(8,128)S(1)} %collective-permute-done.7.odd_ref, f32[512,128]{1,0:T(8,128)S(1)} %get-tuple-element.70.own_ref, f32[4,48,128]{2,1,0:T(8,128)S(1)} %strip_lines.1.line_ref), custom_call_target="tpu_custom_call" | custom-call | tf_op jit(solution)/shard_map/strips/pallas_call | solution.py:470
  71.8 4.5 %second.5 = (f32[1024,128]{1,0:T(8,128)S(1)}, f32[2048,128]{1,0:T(8,128)S(1)}, f32[1024,128]{1,0:T(8,128)S(1)}) custom-call(f32[1024,128]{1,0:T(8,128)S(1)} %get-tuple-element.67.refs_0_, f32[3072,128]{1,0:T(8,128)S(1)} %get-tuple-element.68.refs_1_, f32[1024,128]{1,0:T(8,128)S(1)} %get-tuple-element.69.refs_2_, ...), custom_call_target="tpu_custom_call" | custom-call | flops 15204352 | bytes 2097152 | tf_op jit(solution)/shard_map/second/pallas_call | solution.py:528
  76.4 2.8 %leave.1 = (f32[16,128,256]{2,1,0:T(8,128)}, f32[512,256]{1,0:T(8,128)S(1)}) custom-call(f32[1024,128]{1,0:T(8,128)S(1)} %get-tuple-element.73.low_ref, f32[2048,128]{1,0:T(8,128)S(1)} %get-tuple-element.74.mid_ref, f32[1024,128]{1,0:T(8,128)S(1)} %get-tuple-element.75.high_ref, bf16[2048,512]{1,0:T(8,128)(2,1)S(1)} %get-tuple-element.76.w_high_ref, ...), custom_call_target="tpu_custom_call" | custom-call | flops 2147483648 | bytes 8388608 | tf_op jit(solution)/shard_map/leave/pallas_call | solution.py:622
  79.2 0.1 reshape.15
  79.3 21.1 %all_to_all.5 = f32[128,4,256]{2,1,0:T(4,128)S(1)} all-to-all(f32[128,4,256]{2,1,0:T(4,128)S(1)} %reshape.15), channel_id=1, replica_groups=mesh['azim'=32,'rad'=4] {'azim','rad'}, dimensions={0} | all-to-all | bytes 1048576 | tf_op jit(solution)/shard_map/all_to_all | solution.py:678
  100.5 0.7 reduce_sum.9
Async XLA Ops:
  0.6 13.8 %copy-start = (f32[16,128,256]{2,1,0:T(8,128)S(1)}, f32[16,128,256]{2,1,0:T(8,128)}, u32[]{:S(2)}) copy-start(f32[16,128,256]{2,1,0:T(8,128)} %x_ref.3) | copy-start | bytes 6291460
  4.3 11.6 %copy-start.4 = (f32[4,29,16,128]{3,2,1,0:T(8,128)S(1)}, f32[4,29,16,128]{3,2,1,0:T(8,128)}, u32[]{:S(2)}) copy-start(f32[4,29,16,128]{3,2,1,0:T(8,128)} %coef_ref.1) | copy-start | bytes 2850820
  4.3 12.4 %copy-start.5 = (s32[1024]{0:T(1024)S(1)}, s32[1024]{0:T(1024)}, u32[]{:S(2)}) copy-start(s32[1024]{0:T(1024)} %rows_ref.1) | copy-start | bytes 12292
  4.3 26.4 %collective-permute-start = (f32[1280,128]{1,0:T(8,128)}, f32[1280,128]{1,0:T(8,128)S(1)}, u32[]{:S(2)}, u32[]{:S(2)}) collective-permute-start(f32[1280,128]{1,0:T(8,128)} %get-tuple-element.41), channel_id=1, source_target_pairs={{0,4},{8,12},{16,20},{24,28},{32,36},{40,44},{48,52},{56,60},{64,6... | collective-permute-start | bytes 1966088 | tf_op jit(solution)/shard_map/ppermute | solution.py:644
  6.6 24.2 %collective-permute-start.1 = (f32[1280,128]{1,0:T(8,128)}, f32[1280,128]{1,0:T(8,128)S(1)}, u32[]{:S(2)}, u32[]{:S(2)}) collective-permute-start(f32[1280,128]{1,0:T(8,128)} %get-tuple-element.42), channel_id=1, source_target_pairs={{4,8},{12,16},{20,24},{28,32},{36,40},{44,48},{52,56},{60,64},{68,... | collective-permute-start | bytes 1966088 | tf_op jit(solution)/shard_map/ppermute | solution.py:644
  16.7 2.2 %copy-start.3 = (bf16[4096,512]{1,0:T(8,128)(2,1)S(1)}, bf16[4096,512]{1,0:T(8,128)(2,1)}, u32[]{:S(2)}) copy-start(bf16[4096,512]{1,0:T(8,128)(2,1)} %table_ref.1) | copy-start | bytes 12582916
  18.9 4.7 %copy-start.1 = (f32[1280,128]{1,0:T(8,128)S(1)}, f32[1280,128]{1,0:T(8,128)}, u32[]{:S(2)}) copy-start(f32[1280,128]{1,0:T(8,128)} %get-tuple-element.43.low_ref.refs_6_) | copy-start | bytes 1966084
  18.9 4.7 %copy-start.2 = (f32[1280,128]{1,0:T(8,128)S(1)}, f32[1280,128]{1,0:T(8,128)}, u32[]{:S(2)}) copy-start(f32[1280,128]{1,0:T(8,128)} %get-tuple-element.44.high_ref.refs_7_) | copy-start | bytes 1966084
  23.6 3.6 %copy-start.6 = (s32[1024]{0:T(1024)S(1)}, s32[1024]{0:T(1024)}, u32[]{:S(2)}) copy-start(s32[1024]{0:T(1024)} %param.8) | copy-start | bytes 12292
  31.8 8.4 %collective-permute-start.3 = (f32[640,128]{1,0:T(8,128)S(1)}, f32[640,128]{1,0:T(8,128)S(1)}, u32[]{:S(2)}, u32[]{:S(2)}) collective-permute-start(f32[640,128]{1,0:T(8,128)S(1)} %get-tuple-element.57.own_ref), channel_id=1, source_target_pairs={{1,2},{2,1},{5,6},{6,5},{9,10},{10,9},{13,14},{14,13},{17,18},{18,... | collective-permute-start | bytes 983048 | tf_op jit(solution)/shard_map/ppermute | solution.py:644
  35.1 5.0 %collective-permute-start.2 = (f32[640,128]{1,0:T(8,128)S(1)}, f32[640,128]{1,0:T(8,128)S(1)}, u32[]{:S(2)}, u32[]{:S(2)}) collective-permute-start(f32[640,128]{1,0:T(8,128)S(1)} %get-tuple-element.57.own_ref), channel_id=1, source_target_pairs={{0,1},{2,3},{1,0},{3,2},{4,5},{6,7},{5,4},{7,6},{8,9},{10,11},{9,8... | collective-permute-start | bytes 983048 | tf_op jit(solution)/shard_map/ppermute | solution.py:644
  44.2 12.3 %collective-permute-start.4 = (f32[1024,128]{1,0:T(8,128)S(1)}, f32[1024,128]{1,0:T(8,128)S(1)}, u32[]{:S(2)}, u32[]{:S(2)}) collective-permute-start(f32[1024,128]{1,0:T(8,128)S(1)} %get-tuple-element.60), channel_id=1, source_target_pairs={{0,4},{8,12},{16,20},{24,28},{32,36},{40,44},{48,52},{56,60},{64,6... | collective-permute-start | bytes 1572872 | tf_op jit(solution)/shard_map/ppermute | solution.py:644
  44.3 17.9 %collective-permute-start.5 = (f32[1024,128]{1,0:T(8,128)S(1)}, f32[1024,128]{1,0:T(8,128)S(1)}, u32[]{:S(2)}, u32[]{:S(2)}) collective-permute-start(f32[1024,128]{1,0:T(8,128)S(1)} %get-tuple-element.61), channel_id=1, source_target_pairs={{4,8},{12,16},{20,24},{28,32},{36,40},{44,48},{52,56},{60,64},{68,... | collective-permute-start | bytes 1572872 | tf_op jit(solution)/shard_map/ppermute | solution.py:644
  62.9 7.7 %collective-permute-start.7 = (f32[512,128]{1,0:T(8,128)S(1)}, f32[512,128]{1,0:T(8,128)S(1)}, u32[]{:S(2)}, u32[]{:S(2)}) collective-permute-start(f32[512,128]{1,0:T(8,128)S(1)} %get-tuple-element.70.own_ref), channel_id=1, source_target_pairs={{1,2},{2,1},{5,6},{6,5},{9,10},{10,9},{13,14},{14,13},{17,18},{18,... | collective-permute-start | bytes 786440 | tf_op jit(solution)/shard_map/ppermute | solution.py:644
  64.8 5.7 %collective-permute-start.6 = (f32[512,128]{1,0:T(8,128)S(1)}, f32[512,128]{1,0:T(8,128)S(1)}, u32[]{:S(2)}, u32[]{:S(2)}) collective-permute-start(f32[512,128]{1,0:T(8,128)S(1)} %get-tuple-element.70.own_ref), channel_id=1, source_target_pairs={{0,1},{2,3},{1,0},{3,2},{4,5},{6,7},{5,4},{7,6},{8,9},{10,11},{9,8... | collective-permute-start | bytes 786440 | tf_op jit(solution)/shard_map/ppermute | solution.py:644

commit v6 on v5

--- a/solution.py
+++ b/solution.py
@@ -44,6 +44,7 @@
 UNROLL = 8
 TAIL = 4 * ROWS
 COEF = 2 * ROWS
+LINES = 3 * ROWS
 
 
 def window(ref, row, var, half):
@@ -194,7 +195,7 @@
     )(x)
 
 
-def inner_first(low_ref, mid_ref, high_ref, coef_ref, y_ref, edge_ref):
+def inner_first(low_ref, mid_ref, high_ref, coef_ref, y_ref):
     parts = ((0, 4, low_ref), (4, 12, mid_ref), (12, 16, high_ref))
 
     def one(var, half):
@@ -207,13 +208,6 @@
             2, 14, lambda s: pick(parts, s, var, half),
             lambda k, row: line_of(coef_ref, var, k, row), finish,
         )
-        tail = jnp.zeros((WIDTH, 128), F32)
-        head = jnp.zeros((WIDTH, 128), F32)
-        for row in range(16):
-            value = pick(parts, row, var, half)
-            tail, head = place(tail, row, value, 124), place(head, row, value, 0)
-        put(edge_ref, 0, var, half, tail)
-        put(edge_ref, 1, var, half, head)
 
     each_part(one)
 
@@ -222,8 +216,8 @@
     return pl.pallas_call(
         inner_first,
         in_specs=whole(4),
-        out_specs=whole(2),
-        out_shape=arrays((12 * ROWS, 128), (2 * ROWS, 128)),
+        out_specs=whole(1)[0],
+        out_shape=arrays((12 * ROWS, 128))[0],
         compiler_params=params(),
         cost_estimate=cost(12),
         name="inner_first",
@@ -256,49 +250,154 @@
     )(coef.reshape(-1, 128))
 
 
-def halo_edges(even_ref, odd_ref, edge_ref, *refs):
-    top_ref, bot_ref, out_ref = refs[len(refs) > 3 :][:3]
-    even_is_above = lax.axis_index("azim") % 2 == 0
-
-    @pl.when(even_is_above)
-    def _():
-        top_ref[...], bot_ref[...] = odd_ref[:TAIL], even_ref[:TAIL]
-
-    @pl.when(jnp.logical_not(even_is_above))
-    def _():
-        top_ref[...], bot_ref[...] = even_ref[:TAIL], odd_ref[:TAIL]
+def edges(low_ref, mid_ref, high_ref, *refs):
+    out_ref = refs[-1]
+    parts = ((0, 4, low_ref), (4, 12, mid_ref), (12, 16, high_ref))
 
     def one(var, half):
-        tail = window(edge_ref, 0, var, half)
-        head = window(edge_ref, 1, var, half)
-        for k in range(4):
-            for row, ref in ((k - 4, top_ref), (k + 16, bot_ref)):
-                value = window(ref, k, var, half)
-                tail, head = place(tail, row, value, 124), place(head, row, value, 0)
+        tail = jnp.zeros((WIDTH, 128), F32)
+        head = jnp.zeros((WIDTH, 128), F32)
+        for row in range(16):
+            value = pick(parts, row, var, half)
+            tail, head = place(tail, row, value, 124), place(head, row, value, 0)
         put(out_ref, 0, var, half, tail)
         put(out_ref, 1, var, half, head)
 
     each_part(one)
-    if len(refs) > 3:
-        coef_edge_ref, (ctop_ref, cbot_ref) = refs[0], refs[4:]
-
-        @pl.when(even_is_above)
-        def _():
-            ctop_ref[...], cbot_ref[...] = odd_ref[TAIL:], even_ref[TAIL:]
-
-        @pl.when(jnp.logical_not(even_is_above))
-        def _():
-            ctop_ref[...], cbot_ref[...] = even_ref[TAIL:], odd_ref[TAIL:]
-
+    if len(refs) > 1:
+        out_ref[COEF:] = refs[0][...]
+
+
+def call_edges(low, mid, high, *coef_edge):
+    return pl.pallas_call(
+        edges,
+        in_specs=whole(3 + len(coef_edge)),
+        out_specs=whole(1)[0],
+        out_shape=arrays((COEF + 128 * len(coef_edge), 128))[0],
+        compiler_params=params(),
+        name="edges",
+    )(low, mid, high, *coef_edge)
+
+
+def corner(even_ref, odd_ref, own_ref, pack_ref, *refs):
+    fold_even_ref, fold_odd_ref, low_ref, high_ref = refs
+    entry = lanes((32, 128)) % 4
+    even_is_right = lanes((32, 128)) * 0 + lax.axis_index("rad") % 2 == 0
+    lane = lanes((32, 128))
+
+    def turn(pack, by):
+        return pltpu.roll(pack, by % 128, axis=1) if by % 128 else pack
+
+    folds = {}
+    for var in range(4):
+        for half in range(2):
+            at = slice(var * 64 + half * 32, var * 64 + half * 32 + 32)
+            below = slice(ROWS + at.start, ROWS + at.stop)
+            tail = jnp.where(even_is_right, odd_ref[at], even_ref[at])
+            head = jnp.where(even_is_right, even_ref[below], odd_ref[below])
+            rims = jnp.where(entry < 2, head, tail), jnp.where(entry < 2, tail, head)
+            pack_ref[at] = rims[0]
+            pack_ref[below] = rims[1]
+            pack_ref[2 * ROWS + at.start : 2 * ROWS + at.stop] = jnp.where(
+                entry < 2, turn(own_ref[at], -2), turn(own_ref[below], 2)
+            )
+            for side, first in (("low", 16), ("high", 64)):
+                fold = folds.get((side, half), jnp.zeros((32, 128), F32))
+                for k in range(2):
+                    to = 32 * var + 16 * k
+                    here = (lane >= to) & (lane < to + 16)
+                    fold = jnp.where(here, turn(rims[k], to - first), fold)
+                folds[side, half] = fold
+    for half in range(2):
+        at = slice(32 * half, 32 * half + 32)
+        low_ref[at], high_ref[at] = folds["low", half], folds["high", half]
+    if own_ref.shape[0] > COEF:
+        fold = {"low": jnp.zeros((32, 128), F32), "high": jnp.zeros((32, 128), F32)}
+        for var in range(4):
+            at = slice(COEF + 32 * var, COEF + 32 * var + 32)
+            right = jnp.where(even_is_right, even_ref[at], odd_ref[at])
+            left = jnp.where(even_is_right, odd_ref[at], even_ref[at])
+            lines = jnp.where(entry < 2, turn(right, 126), turn(left, 2))
+            pack_ref[LINES + 32 * var : LINES + 32 * var + 32] = lines
+            for side, first in (("low", 16), ("high", 72)):
+                here = (lane >= 32 * var) & (lane < 32 * var + 8)
+                fold[side] = jnp.where(here, turn(lines, 32 * var - first), fold[side])
+        low_ref[64:96], high_ref[64:96] = fold["low"], fold["high"]
+    sort_sides(lax.axis_index("azim"), fold_even_ref, fold_odd_ref, low_ref, high_ref)
+
+
+def call_corner(even, odd, own):
+    first = own.shape[0] > COEF
+    fold = (64 + 32 * first, 128)
+    return pl.pallas_call(
+        corner,
+        in_specs=whole(3),
+        out_specs=whole(3),
+        out_shape=arrays((LINES + 128 * first, 128), fold, fold),
+        scratch_shapes=[pltpu.VMEM(fold, F32)] * 2,
+        compiler_params=params(),
+        name="corner",
+    )(even, odd, own)
+
+
+def halo(even_ref, odd_ref, fold_even_ref, fold_odd_ref, pack_ref, *refs):
+    first_step = len(refs) > 5
+    coef_edge_ref = refs[0] if first_step else None
+    refs = refs[first_step:]
+    top_ref, bot_ref, out_ref = refs[:3]
+    fold_top_ref, fold_bot_ref = refs[-2:]
+    even_is_above = lax.axis_index("azim") % 2 == 0
+    lane = lanes((32, 128))
+
+    def turn(pack, by):
+        return pltpu.roll(pack, by % 128, axis=1) if by % 128 else pack
+
+    def sorted_sides(above):
+        below_from, above_from = (odd_ref, even_ref) if above else (even_ref, odd_ref)
+        folds = (fold_odd_ref, fold_even_ref) if above else (fold_even_ref, fold_odd_ref)
+        top_ref[...], bot_ref[...] = below_from[:TAIL], above_from[:TAIL]
+        fold_top_ref[...], fold_bot_ref[...] = folds[0][...], folds[1][...]
+        if first_step:
+            refs[3][...], refs[4][...] = below_from[TAIL:], above_from[TAIL:]
+
+    pl.when(even_is_above)(lambda: sorted_sides(True))
+    pl.when(jnp.logical_not(even_is_above))(lambda: sorted_sides(False))
+    for var in range(4):
+        for half in range(2):
+            at = slice(var * 64 + half * 32, var * 64 + half * 32 + 32)
+            c = slice(half * 32, half * 32 + 32)
+            for k in range(2):
+                here = slice(ROWS * k + at.start, ROWS * k + at.stop)
+                source = 32 * var + 16 * k
+                pack = jnp.where(lane < 16, turn(fold_top_ref[c], -source), pack_ref[here])
+                out_ref[here] = jnp.where(
+                    (lane >= 80) & (lane < 96), turn(fold_bot_ref[c], 80 - source), pack
+                )
+            here = slice(2 * ROWS + at.start, 2 * ROWS + at.stop)
+            seam = pack_ref[here]
+            for k in range(4):
+                rows = slice(ROWS * k + at.start, ROWS * k + at.stop)
+                seam = place(seam, k - 4, top_ref[rows], 126)
+                seam = place(seam, k + 16, bot_ref[rows], 126)
+            out_ref[here] = seam
+    if first_step:
+        ctop_ref, cbot_ref = refs[3:5]
         number = lax.broadcasted_iota(jnp.int32, (64, 128), 0) // 2
         for var in range(4):
+            here = slice(LINES + 32 * var, LINES + 32 * var + 32)
+            pack = pack_ref[here]
+            pack = jnp.where((lane >= 8) & (lane < 16), turn(fold_top_ref[64:96], 8 - 32 * var), pack)
+            out_ref[here] = jnp.where(
+                (lane >= 80) & (lane < 88), turn(fold_bot_ref[64:96], 80 - 32 * var), pack
+            )
             pack = coef_edge_ref[32 * var : 32 * var + 29]
             for k in range(2):
                 lines = pl.ds(64 * var + k, 29, stride=2)
                 pack = place(pack, k - 2, ctop_ref[lines, :], 126)
                 pack = place(pack, k + 16, cbot_ref[lines, :], 126)
-            out_ref[COEF + 32 * var : COEF + 32 * var + 29] = pack
-            out_ref[COEF + 32 * var + 29 : COEF + 32 * var + 32] = jnp.zeros((3, 128), F32)
+            start = LINES + 128 + 32 * var
+            out_ref[start : start + 29] = pack
+            out_ref[start + 29 : start + 32] = jnp.zeros((3, 128), F32)
         for var in range(4):
             at = slice(64 * var, 64 * var + 64)
             for ref in (ctop_ref, cbot_ref):
@@ -310,18 +409,19 @@
                 ref[at] = result
 
 
-def call_halo_edges(even, odd, edge, *coef_edge):
-    return pl.pallas_call(
-        halo_edges,
-        in_specs=whole(3 + len(coef_edge)),
+def call_halo(even, odd, fold_even, fold_odd, pack, *coef_edge):
+    return pl.pallas_call(
+        halo,
+        in_specs=whole(5 + len(coef_edge)),
         out_specs=whole(3 + 2 * len(coef_edge)),
         out_shape=arrays(
-            (TAIL, 128), (TAIL, 128), (COEF + 128 * len(coef_edge), 128),
+            (TAIL, 128), (TAIL, 128), (LINES + 256 * len(coef_edge), 128),
             *[(256, 128)] * (2 * len(coef_edge)),
         ),
-        compiler_params=params(),
-        name="halo_edges",
-    )(even, odd, edge, *coef_edge)
+        scratch_shapes=[pltpu.VMEM(fold_even.shape, F32)] * 2,
+        compiler_params=params(),
+        name="halo",
+    )(even, odd, fold_even, fold_odd, pack, *coef_edge)
 
 
 def outer_first(top_ref, low_ref, high_ref, bot_ref, coef_ref, ctop_ref, cbot_ref,
@@ -363,53 +463,47 @@
     )(top, low, high, bot, coef, ctop, cbot)
 
 
-def strip_lines(even_ref, odd_ref, own_ref, out_ref):
-    entry = lanes((32, 128)) % 4
-    even_is_right = lanes((32, 128)) * 0 + lax.axis_index("rad") % 2 == 0
+def strip_lines(pack_ref, out_ref):
+    entry = lanes((1, 128)) % 4
     number = lax.broadcasted_iota(jnp.int32, (32, 128), 0)
     for var in range(4):
-        at = slice(COEF + 32 * var, COEF + 32 * var + 32)
-        even, odd = even_ref[at], odd_ref[at]
-        right = jnp.where(even_is_right, even, odd)
-        left = jnp.where(even_is_right, odd, even)
-        lines = jnp.where(entry < 2, pltpu.roll(right, 126, axis=1), pltpu.roll(left, 2, axis=1))
+        lines = pack_ref[LINES + 32 * var : LINES + 32 * var + 32]
         result = lines
         for i in (0, 1, 3, 4):
             here = (number >= 5 * i) & (number < 5 * i + 5)
             result = jnp.where(here, pltpu.roll(lines, (4 * (i - 2)) % 128, axis=1), result)
         out_ref[var, 0:32] = result
-        own = own_ref.at[at]
-        one_entry = entry[0:1]
+        start = LINES + 128 + 32 * var
+        own = pack_ref.at[start : start + 32]
         for i in range(5):
             k = 5 * i
-            two = jnp.where(one_entry < 2, own[k + 4 : k + 5], own[k : k + 1])
-            one = jnp.where(one_entry == 1, own[k + 3 : k + 4], 0.0)
-            one = jnp.where(one_entry == 2, own[k + 1 : k + 2], one)
+            two = jnp.where(entry < 2, own[k + 4 : k + 5], own[k : k + 1])
+            one = jnp.where(entry == 1, own[k + 3 : k + 4], 0.0)
+            one = jnp.where(entry == 2, own[k + 1 : k + 2], one)
             turn = (4 * (i - 2)) % 128
             out_ref[var, 32 + i : 33 + i] = pltpu.roll(two, turn, axis=1) if turn else two
             out_ref[var, 37 + i : 38 + i] = pltpu.roll(one, turn, axis=1) if turn else one
         out_ref[var, 42:48] = jnp.zeros((6, 128), F32)
 
 
-def call_strip_lines(even, odd, own):
+def call_strip_lines(pack):
     return pl.pallas_call(
         strip_lines,
-        in_specs=whole(3),
+        in_specs=whole(1),
         out_specs=whole(1)[0],
         out_shape=arrays((4, 48, 128))[0],
         compiler_params=params(),
         name="strip_lines",
-    )(even, odd, own)
-
-
-def strips(even_ref, odd_ref, own_ref, line_ref, mend_y_ref, mend_u_ref, shift_ref):
+    )(pack)
+
+
+def strips(pack_ref, line_ref, mend_y_ref, mend_u_ref, shift_ref):
     entry = lanes((32, 128)) % 4
-    even_is_right = lanes((32, 128)) * 0 + lax.axis_index("rad") % 2 == 0
     every = [(var, half) for var in range(4) for half in range(2)]
 
-    def part(ref, kind, var, half):
+    def part(kind, var, half):
         start = kind * ROWS + var * 64 + half * 32
-        return ref[start : start + 32]
+        return pack_ref[start : start + 32]
 
     def line(var, k):
         return jnp.broadcast_to(line_ref[var, k : k + 1], (32, 128))
@@ -428,21 +522,17 @@
 
     for var, half in every:
         at = slice(32 * half, 32 * half + 32)
-        tail = jnp.where(even_is_right, part(odd_ref, 0, var, half), part(even_ref, 0, var, half))
-        head = jnp.where(even_is_right, part(even_ref, 1, var, half), part(odd_ref, 1, var, half))
-        rim = jnp.where(entry < 2, head, tail)
-        outer = jnp.where(entry < 2, tail, head)
-        own = jnp.where(entry < 2, part(own_ref, 1, var, half), part(own_ref, 0, var, half))
+        rim, outer, seam = (part(kind, var, half) for kind in range(3))
         up, down = turn(rim, 1), turn(rim, -1)
-        shift_ref[0, var, at] = jnp.where(entry < 2, turn(own, -2), turn(outer, 2))
+        shift_ref[0, var, at] = jnp.where(entry < 2, seam, turn(outer, 2))
         shift_ref[1, var, at] = jnp.where(
-            entry == 0, turn(own, -3), jnp.where(entry == 2, turn(outer, 1), up)
+            entry == 0, turn(seam, -1), jnp.where(entry == 2, turn(outer, 1), up)
         )
         shift_ref[2, var, at] = rim
         shift_ref[3, var, at] = jnp.where(
-            entry == 3, turn(own, 3), jnp.where(entry == 1, turn(outer, -1), down)
+            entry == 3, turn(seam, 1), jnp.where(entry == 1, turn(outer, -1), down)
         )
-        shift_ref[4, var, at] = jnp.where(entry < 2, turn(outer, -2), turn(own, 2))
+        shift_ref[4, var, at] = jnp.where(entry < 2, turn(outer, -2), seam)
         shift_ref[5, var, at] = jnp.where(entry == 1, up, down)
     for var, half in every:
         at = slice(32 * half, 32 * half + 32)
@@ -466,16 +556,16 @@
         mend_u_ref[var, at] = beyond(var, rim, crossed)
 
 
-def call_strips(even, odd, own, lines):
+def call_strips(pack, lines):
     return pl.pallas_call(
         strips,
-        in_specs=whole(4),
+        in_specs=whole(2),
         out_specs=whole(2),
         out_shape=arrays((4, 64, 128), (4, 64, 128)),
         scratch_shapes=[pltpu.VMEM((7, 4, 64, 128), F32)],
         compiler_params=params(),
         name="strips",
-    )(even, odd, own, lines)
+    )(pack, lines)
 
 
 PARTS = ((0, 4), (4, 12), (12, 16))
@@ -653,18 +743,21 @@
     for step in range(STEPS):
         even = swap(even, "azim", 0)
         odd = swap(odd, "azim", 1)
-        y_mid, edge = call_inner_first(low, mid, high, coef)
+        extra = (coef_edge,) if step == 0 else ()
+        own = call_edges(low, mid, high, *extra)
+        sides = swap(own, "rad", 0), swap(own, "rad", 1)
+        y_mid = call_inner_first(low, mid, high, coef)
+        pack, fold_even, fold_odd = call_corner(*sides, own)
+        fold_even = swap(fold_even, "azim", 0)
+        fold_odd = swap(fold_odd, "azim", 1)
         if step == 0:
-            edge, w_high = lax.optimization_barrier((edge, w_high))
-            top, bot, own, *tails = call_halo_edges(even, odd, edge, coef_edge)
-        else:
-            top, bot, own = call_halo_edges(even, odd, edge)
-        sides = swap(own, "rad", 0), swap(own, "rad", 1), own
+            pack, w_high = lax.optimization_barrier((pack, w_high))
+        top, bot, pack, *rest = call_halo(even, odd, fold_even, fold_odd, pack, *extra)
+        if step == 0:
+            tails, lines = rest, call_strip_lines(pack)
         ys = call_outer_first(top, low, high, bot, coef, *tails)
         ys = ys[0], y_mid, ys[1]
-        if step == 0:
-            lines = call_strip_lines(*sides)
-        mends = call_strips(*sides, lines)
+        mends = call_strips(pack, lines)
         if step < STEPS - 1:
             (new_mid,) = call_second(((4, 12),), PARTS[1:2], ys[1:2], *mends, coef, (mid,))
             low, high, even, odd = call_second(

time: 101 us -> 109 us (1.079)
  starting transfers between devices: 22.1 us -> 27.2 us
  waiting for transfers between devices: 12.1 us -> 16.1 us
  local copies, waits for them, and re-layouts: 2.36 us -> 0.19 us
  Pallas kernels: 41.2 us -> 42.9 us
  blocking collectives: 21.1 us -> 19.9 us
    ppermute x8 -> x12, starting transfers between devices: 22.1 us -> 27.2 us  [swap(): return lax.ppermute(block, axis, swaps(count, odd, axis == 'azim'))]
    ppermute x8 -> x12, waiting for transfers between devices: 12.1 us -> 16.1 us  [swap(): return lax.ppermute(block, axis, swaps(count, odd, axis == 'azim'))]
    unnamed x14, local copies, waits for them, and re-layouts: 2.21 us -> 0.04 us
    pallas_call x7 -> x11, Pallas kernels: 11.5 us -> 13.2 us  [the longest x2 6.07 us: call_inner_first(): pl.pallas_call(inner_first, in_specs=whole(4), out_specs=whole(1)[0], out...]
    all_to_all x1, blocking collectives: 21.1 us -> 19.9 us  [body(): lax.all_to_all(term.reshape(count, -1, term.shape[1]), ('azim', 'rad'), 0...]
  transfers between devices with their start and end apart: 8 -> 12, of which waited for: 4 -> 4; matrix products, arithmetic and copies ran while one was open for 0% -> 0% of each run, Pallas kernels for 23% -> 19%
where the time goes in v6:
time: 109 us
  Pallas kernels  42.9 us (39%)
  starting transfers between devices  27.2 us (25%)
  blocking collectives  19.9 us (18%)
  waiting for transfers between devices  16.1 us (15%)
  between operations  1.6 us (1%)
    ppermute x12, starting transfers between devices, swap(): return lax.ppermute(block, axis, swaps(count, odd, axis == 'azim'))  27.2 us
    all_to_all x1, blocking collectives, body(): lax.all_to_all(term.reshape(count, -1, term.shape[1]), ('azim', 'rad'), 0...  19.9 us
    ppermute x12, waiting for transfers between devices, swap(): return lax.ppermute(block, axis, swaps(count, odd, axis == 'azim'))  16.1 us
    pallas_call x3, Pallas kernels, call_second(): pl.pallas_call(functools.partial(second, ranges, parts, len(ys), sides),...  9.3 us
    pallas_call x2, Pallas kernels, call_inner_first(): pl.pallas_call(inner_first, in_specs=whole(4), out_specs=whole(1)[0], out...  6.07 us
    pallas_call x1, Pallas kernels, call_gather(): pl.pallas_call(gather, in_specs=[pl.BlockSpec(memory_space=pltpu.SMEM)] +...  4.63 us
    pallas_call x2, Pallas kernels, call_outer_first(): pl.pallas_call(outer_first, in_specs=whole(7), out_specs=whole(2), out_sh...  4.08 us
    pallas_call x1, Pallas kernels, call_enter_outer(): pl.pallas_call(enter_outer, in_specs=[pl.BlockSpec(memory_space=pltpu.HBM...  3.67 us
  transfers between devices with their start and end apart: 12, of which 4 were waited for; matrix products, arithmetic and copies ran while one was open for 0% of the time, Pallas kernels for 19%

profile of v6, /device:TPU:1, one launch (start us, length us, event | category | flops | bytes accessed | tf_op | source)
XLA Modules:
  0.0 108.6 jit_solution(11102075161004536116)
XLA Ops:
  0.6 0.0 copy-start.2
  0.6 3.7 %enter_outer.1 = (f32[1280,128]{1,0:T(8,128)}, f32[1280,128]{1,0:T(8,128)}, f32[1280,128]{1,0:T(8,128)}, f32[1280,128]{1,0:T(8,128)}) custom-call(f32[16,128,256]{2,1,0:T(8,128)} %x_ref.3, f32[4,29,16,128]{3,2,1,0:T(8,128)} %coef_ref.1), custom_call_target="tpu_custom_call" | custom-call | tf_op jit(solution)/shard_map/enter_outer/pallas_call | solution.py:161
  4.3 0.0 copy-start.4
  4.3 0.0 copy-start
  4.3 0.0 copy-start.1
  4.4 2.2 %collective-permute-start = (f32[1280,128]{1,0:T(8,128)}, f32[1280,128]{1,0:T(8,128)S(1)}, u32[]{:S(2)}, u32[]{:S(2)}) collective-permute-start(f32[1280,128]{1,0:T(8,128)} %get-tuple-element.43), channel_id=1, source_target_pairs={{0,4},{8,12},{16,20},{24,28},{32,36},{40,44},{48,52},{56,60},{64,6... | collective-permute-start | bytes 1966088 | tf_op jit(solution)/shard_map/ppermute | solution.py:734
  6.6 7.8 %collective-permute-start.1 = (f32[1280,128]{1,0:T(8,128)}, f32[1280,128]{1,0:T(8,128)S(1)}, u32[]{:S(2)}, u32[]{:S(2)}) collective-permute-start(f32[1280,128]{1,0:T(8,128)} %get-tuple-element.44), channel_id=1, source_target_pairs={{4,8},{12,16},{20,24},{28,32},{36,40},{44,48},{52,56},{60,64},{68,... | collective-permute-start | bytes 1966088 | tf_op jit(solution)/shard_map/ppermute | solution.py:734
  14.4 0.0 copy-done.2
  14.4 0.0 copy-start.3
  14.4 0.9 enter_inner.1.mid_ref.refs_4_
  15.3 0.0 copy-start.5
  15.3 0.0 copy-done.4
  15.3 0.8 coef_edges.1
  16.1 0.0 copy-done
  16.1 0.0 copy-done.1
  16.1 1.1 %edges.2.own_ref = f32[640,128]{1,0:T(8,128)S(1)} custom-call(f32[1280,128]{1,0:T(8,128)S(1)} %copy-done, f32[2048,128]{1,0:T(8,128)S(1)} %enter_inner.1.mid_ref.refs_4_, f32[1280,128]{1,0:T(8,128)S(1)} %copy-done.1, f32[128,128]{1,0:T(8,128)S(1)} %get-tuple-element.47.refs_0_), custom_call_target="tpu_custom_call" | custom-call | tf_op jit(solution)/shard_map/edges/pallas_call | solution.py:272
  17.3 3.3 %collective-permute-start.3 = (f32[640,128]{1,0:T(8,128)S(1)}, f32[640,128]{1,0:T(8,128)S(1)}, u32[]{:S(2)}, u32[]{:S(2)}) collective-permute-start(f32[640,128]{1,0:T(8,128)S(1)} %edges.2.own_ref), channel_id=1, source_target_pairs={{1,2},{2,1},{5,6},{6,5},{9,10},{10,9},{13,14},{14,13},{17,18},{18,... | collective-permute-start | bytes 983048 | tf_op jit(solution)/shard_map/ppermute | solution.py:734
  20.6 0.1 collective-permute-start.2
  21.3 0.0 copy-done.3
  21.4 0.0 copy-done.5
  21.4 0.0 copy-start.6
  21.4 4.6 %gather.1.weights_ref = bf16[1024,512]{1,0:T(8,128)(2,1)S(1)} custom-call(s32[1024]{0:T(1024)S(1)} %copy-done.5, bf16[4096,512]{1,0:T(8,128)(2,1)S(1)} %copy-done.3), custom_call_target="tpu_custom_call" | custom-call | tf_op jit(solution)/shard_map/gather/pallas_call | solution.py:649
  26.0 8.2 %collective-permute-done.3.odd_ref = f32[640,128]{1,0:T(8,128)S(1)} collective-permute-done((f32[640,128]{1,0:T(8,128)S(1)}, f32[640,128]{1,0:T(8,128)S(1)}, u32[]{:S(2)}, u32[]{:S(2)}) %collective-permute-start.3) | collective-permute-done | bytes 327712 | tf_op jit(solution)/shard_map/ppermute | solution.py:734
  34.2 0.0 collective-permute-done.2.even_ref
  34.2 0.4 corner.2
  34.6 0.1 collective-permute-start.4
  34.7 0.4 collective-permute-start.5
  35.1 0.0 copy-done.6
  35.1 3.6 %spread.1 = (bf16[2048,512]{1,0:T(8,128)(2,1)S(1)}, bf16[2048,512]{1,0:T(8,128)(2,1)S(1)}) custom-call(s32[1]{0:T(128)S(6)} %copy.8.count_ref, s32[1,1024]{1,0:T(1,128)S(1)} %bitcast.3, bf16[1024,512]{1,0:T(8,128)(2,1)S(1)} %gather.1.weights_ref), custom_call_target="tpu_custom_call" | custom-call | flops 2147483648 | bytes 6291456 | tf_op jit(solution)/shard_map/spread/pallas_call | solution.py:673
  38.7 3.0 %inner_first.2.refs_1_.refs_0_ = f32[3072,128]{1,0:T(8,128)S(1)} custom-call(f32[1280,128]{1,0:T(8,128)S(1)} %copy-done, f32[2048,128]{1,0:T(8,128)S(1)} %enter_inner.1.mid_ref.refs_4_, f32[1280,128]{1,0:T(8,128)S(1)} %copy-done.1, f32[4,29,16,128]{3,2,1,0:T(8,128)S(1)} %get-tuple-element.55.coef_ref.refs_5_.refs_3_), custom_call_target="tpu_custom_call" | custom-call | flops 22806528 | bytes 3145728 | tf_op jit(solution)/shard_map/inner_first/pallas_call | solution.py:216
  41.8 0.0 collective-permute-done.4.fold_even_ref
  41.8 1.7 %collective-permute-done.5.fold_odd_ref = f32[96,128]{1,0:T(8,128)S(1)} collective-permute-done((f32[96,128]{1,0:T(8,128)S(1)}, f32[96,128]{1,0:T(8,128)S(1)}, u32[]{:S(2)}, u32[]{:S(2)}) %collective-permute-start.5) | collective-permute-done | bytes 49184 | tf_op jit(solution)/shard_map/ppermute | solution.py:734
  43.5 0.0 collective-permute-done.even_ref
  43.5 0.0 collective-permute-done.1.odd_ref
  43.5 1.1 halo.2
  44.5 0.1 strip_lines.1.line_ref
  44.7 1.2 %strips.2 = (f32[4,64,128]{2,1,0:T(8,128)S(1)}, f32[4,64,128]{2,1,0:T(8,128)S(1)}) custom-call(f32[1024,128]{1,0:T(8,128)S(1)} %get-tuple-element.60.pack_ref, f32[4,48,128]{2,1,0:T(8,128)S(1)} %strip_lines.1.line_ref), custom_call_target="tpu_custom_call" | custom-call | tf_op jit(solution)/shard_map/strips/pallas_call | solution.py:560
  45.9 2.0 %outer_first.2 = (f32[1024,128]{1,0:T(8,128)S(1)}, f32[1024,128]{1,0:T(8,128)S(1)}) custom-call(f32[1024,128]{1,0:T(8,128)S(1)} %get-tuple-element.53.top_ref, f32[1280,128]{1,0:T(8,128)S(1)} %copy-done, f32[1280,128]{1,0:T(8,128)S(1)} %copy-done.1, f32[1024,128]{1,0:T(8,128)S(1)} %get-tuple-element.54.bot_ref, ...), custom_call_target="tpu_custom_call" | custom-call | flops 15204352 | bytes 2097152 | tf_op jit(solution)/shard_map/outer_first/pallas_call | solution.py:455
  48.0 2.5 %second.3 = (f32[1024,128]{1,0:T(8,128)S(1)}, f32[1024,128]{1,0:T(8,128)S(1)}, f32[1024,128]{1,0:T(8,128)S(1)}, f32[1024,128]{1,0:T(8,128)S(1)}) custom-call(f32[1024,128]{1,0:T(8,128)S(1)} %get-tuple-element.58.refs_0_, f32[3072,128]{1,0:T(8,128)S(1)} %inner_first.2.refs_1_.refs_0_, f32[1024,128]{1,0:T(8,128)S(1)} %get-tuple-element.59.refs_2_, ...), custom_call_target="tpu_custom_call" | custom-call | flops 15204352 | bytes 2097152 | tf_op jit(solution)/shard_map/second/pallas_call | solution.py:618
  50.5 0.1 collective-permute-start.6
  50.6 5.3 %collective-permute-start.7 = (f32[1024,128]{1,0:T(8,128)S(1)}, f32[1024,128]{1,0:T(8,128)S(1)}, u32[]{:S(2)}, u32[]{:S(2)}) collective-permute-start(f32[1024,128]{1,0:T(8,128)S(1)} %get-tuple-element.64), channel_id=1, source_target_pairs={{4,8},{12,16},{20,24},{28,32},{36,40},{44,48},{52,56},{60,64},{68,... | collective-permute-start | bytes 1572872 | tf_op jit(solution)/shard_map/ppermute | solution.py:734
  55.8 2.3 %second.4.mid_ref.refs_7_ = f32[2048,128]{1,0:T(8,128)S(1)} custom-call(f32[3072,128]{1,0:T(8,128)S(1)} %inner_first.2.refs_1_.refs_0_, f32[4,64,128]{2,1,0:T(8,128)S(1)} %get-tuple-element.61.refs_3_.refs_1_, f32[4,64,128]{2,1,0:T(8,128)S(1)} %get-tuple-element.62.refs_4_.refs_2_, f32[4,29,16,128]{3,2,1,0:T(8,128)S(1)} %get-tuple-element.55.coef_ref.refs_5_.refs_3_, ...), custom_call_target="tpu_custom_call" | custom-call | flops 15204352 | bytes 2097152 | tf_op jit(solution)/shard_map/second/pallas_call | solution.py:618
  58.1 1.1 %edges.3.own_ref = f32[512,128]{1,0:T(8,128)S(1)} custom-call(f32[1024,128]{1,0:T(8,128)S(1)} %get-tuple-element.65.low_ref.refs_6_, f32[2048,128]{1,0:T(8,128)S(1)} %second.4.mid_ref.refs_7_, f32[1024,128]{1,0:T(8,128)S(1)} %get-tuple-element.66.high_ref.refs_8_), custom_call_target="tpu_custom_call" | custom-call | tf_op jit(solution)/shard_map/edges/pallas_call | solution.py:272
  59.3 3.9 %collective-permute-start.9 = (f32[512,128]{1,0:T(8,128)S(1)}, f32[512,128]{1,0:T(8,128)S(1)}, u32[]{:S(2)}, u32[]{:S(2)}) collective-permute-start(f32[512,128]{1,0:T(8,128)S(1)} %edges.3.own_ref), channel_id=1, source_target_pairs={{1,2},{2,1},{5,6},{6,5},{9,10},{10,9},{13,14},{14,13},{17,18},{18,... | collective-permute-start | bytes 786440 | tf_op jit(solution)/shard_map/ppermute | solution.py:734
  63.2 0.1 collective-permute-start.8
  63.3 4.2 %collective-permute-done.9.odd_ref = f32[512,128]{1,0:T(8,128)S(1)} collective-permute-done((f32[512,128]{1,0:T(8,128)S(1)}, f32[512,128]{1,0:T(8,128)S(1)}, u32[]{:S(2)}, u32[]{:S(2)}) %collective-permute-start.9) | collective-permute-done | bytes 262176 | tf_op jit(solution)/shard_map/ppermute | solution.py:734
  67.5 0.0 collective-permute-done.8.even_ref
  67.5 0.3 corner.3
  67.8 0.1 collective-permute-start.10
  67.9 3.8 %collective-permute-start.11 = (f32[64,128]{1,0:T(8,128)S(1)}, f32[64,128]{1,0:T(8,128)S(1)}, u32[]{:S(2)}, u32[]{:S(2)}) collective-permute-start(f32[64,128]{1,0:T(8,128)S(1)} %get-tuple-element.68), channel_id=1, source_target_pairs={{4,8},{12,16},{20,24},{28,32},{36,40},{44,48},{52,56},{60,64},{68,... | collective-permute-start | bytes 98312 | tf_op jit(solution)/shard_map/ppermute | solution.py:734
  71.6 3.0 %inner_first.3.refs_1_ = f32[3072,128]{1,0:T(8,128)S(1)} custom-call(f32[1024,128]{1,0:T(8,128)S(1)} %get-tuple-element.65.low_ref.refs_6_, f32[2048,128]{1,0:T(8,128)S(1)} %second.4.mid_ref.refs_7_, f32[1024,128]{1,0:T(8,128)S(1)} %get-tuple-element.66.high_ref.refs_8_, f32[4,29,16,128]{3,2,1,0:T(8,128)S(1)} %get-tuple-element.55.coef_ref.refs_5_.refs_3_), custom_call_target="tpu_custom_call" | custom-call | flops 22806528 | bytes 3145728 | tf_op jit(solution)/shard_map/inner_first/pallas_call | solution.py:216
  74.7 0.0 collective-permute-done.10.fold_even_ref
  74.7 2.0 %collective-permute-done.11.fold_odd_ref = f32[64,128]{1,0:T(8,128)S(1)} collective-permute-done((f32[64,128]{1,0:T(8,128)S(1)}, f32[64,128]{1,0:T(8,128)S(1)}, u32[]{:S(2)}, u32[]{:S(2)}) %collective-permute-start.11) | collective-permute-done | bytes 32800 | tf_op jit(solution)/shard_map/ppermute | solution.py:734
  76.7 0.0 collective-permute-done.6.even_ref
  76.7 0.0 collective-permute-done.7.odd_ref
  76.7 0.5 halo.3
  77.2 1.2 %strips.3 = (f32[4,64,128]{2,1,0:T(8,128)S(1)}, f32[4,64,128]{2,1,0:T(8,128)S(1)}) custom-call(f32[768,128]{1,0:T(8,128)S(1)} %get-tuple-element.74.pack_ref, f32[4,48,128]{2,1,0:T(8,128)S(1)} %strip_lines.1.line_ref), custom_call_target="tpu_custom_call" | custom-call | tf_op jit(solution)/shard_map/strips/pallas_call | solution.py:560
  78.5 2.0 %outer_first.3 = (f32[1024,128]{1,0:T(8,128)S(1)}, f32[1024,128]{1,0:T(8,128)S(1)}) custom-call(f32[1024,128]{1,0:T(8,128)S(1)} %get-tuple-element.70.top_ref, f32[1024,128]{1,0:T(8,128)S(1)} %get-tuple-element.65.low_ref.refs_6_, f32[1024,128]{1,0:T(8,128)S(1)} %get-tuple-element.66.high_ref.refs_8_, f32[1024,128]{1,0:T(8,128)S(1)} %get-tuple-element.71.bot_ref, ...), custom_call_target="tpu_custom_call" | custom-call | flops 15204352 | bytes 2097152 | tf_op jit(solution)/shard_map/outer_first/pallas_call | solution.py:455
  80.5 4.5 %second.5 = (f32[1024,128]{1,0:T(8,128)S(1)}, f32[2048,128]{1,0:T(8,128)S(1)}, f32[1024,128]{1,0:T(8,128)S(1)}) custom-call(f32[1024,128]{1,0:T(8,128)S(1)} %get-tuple-element.72.refs_0_, f32[3072,128]{1,0:T(8,128)S(1)} %inner_first.3.refs_1_, f32[1024,128]{1,0:T(8,128)S(1)} %get-tuple-element.73.refs_2_, f32[4,64,128]{2,1,0:T(8,128)S(1)} %get-tuple-element.75.refs_3_, ...), custom_call_target="tpu_custom_call" | custom-call | flops 15204352 | bytes 2097152 | tf_op jit(solution)/shard_map/second/pallas_call | solution.py:618
  85.0 2.8 %leave.1 = (f32[16,128,256]{2,1,0:T(8,128)}, f32[512,256]{1,0:T(8,128)S(1)}) custom-call(f32[1024,128]{1,0:T(8,128)S(1)} %get-tuple-element.77.low_ref, f32[2048,128]{1,0:T(8,128)S(1)} %get-tuple-element.78.mid_ref, f32[1024,128]{1,0:T(8,128)S(1)} %get-tuple-element.79.high_ref, bf16[2048,512]{1,0:T(8,128)(2,1)S(1)} %get-tuple-element.80.w_high_ref, ...), custom_call_target="tpu_custom_call" | custom-call | flops 2147483648 | bytes 8388608 | tf_op jit(solution)/shard_map/leave/pallas_call | solution.py:712
  87.8 0.1 reshape.15
  88.0 19.9 %all_to_all.5 = f32[128,4,256]{2,1,0:T(4,128)S(1)} all-to-all(f32[128,4,256]{2,1,0:T(4,128)S(1)} %reshape.15), channel_id=1, replica_groups=mesh['azim'=32,'rad'=4] {'azim','rad'}, dimensions={0} | all-to-all | bytes 1048576 | tf_op jit(solution)/shard_map/all_to_all | solution.py:771
  107.9 0.7 reduce_sum.9
Async XLA Ops:
  0.6 13.8 %copy-start.2 = (f32[16,128,256]{2,1,0:T(8,128)S(1)}, f32[16,128,256]{2,1,0:T(8,128)}, u32[]{:S(2)}) copy-start(f32[16,128,256]{2,1,0:T(8,128)} %x_ref.3) | copy-start | bytes 6291460
  4.3 11.0 %copy-start.4 = (f32[4,29,16,128]{3,2,1,0:T(8,128)S(1)}, f32[4,29,16,128]{3,2,1,0:T(8,128)}, u32[]{:S(2)}) copy-start(f32[4,29,16,128]{3,2,1,0:T(8,128)} %coef_ref.1) | copy-start | bytes 2850820
  4.3 11.8 %copy-start = (f32[1280,128]{1,0:T(8,128)S(1)}, f32[1280,128]{1,0:T(8,128)}, u32[]{:S(2)}) copy-start(f32[1280,128]{1,0:T(8,128)} %get-tuple-element.45.low_ref.refs_6_) | copy-start | bytes 1966084
  4.3 11.8 %copy-start.1 = (f32[1280,128]{1,0:T(8,128)S(1)}, f32[1280,128]{1,0:T(8,128)}, u32[]{:S(2)}) copy-start(f32[1280,128]{1,0:T(8,128)} %get-tuple-element.46.high_ref.refs_7_) | copy-start | bytes 1966084
  4.4 39.1 %collective-permute-start = (f32[1280,128]{1,0:T(8,128)}, f32[1280,128]{1,0:T(8,128)S(1)}, u32[]{:S(2)}, u32[]{:S(2)}) collective-permute-start(f32[1280,128]{1,0:T(8,128)} %get-tuple-element.43), channel_id=1, source_target_pairs={{0,4},{8,12},{16,20},{24,28},{32,36},{40,44},{48,52},{56,60},{64,6... | collective-permute-start | bytes 1966088 | tf_op jit(solution)/shard_map/ppermute | solution.py:734
  6.6 36.9 %collective-permute-start.1 = (f32[1280,128]{1,0:T(8,128)}, f32[1280,128]{1,0:T(8,128)S(1)}, u32[]{:S(2)}, u32[]{:S(2)}) collective-permute-start(f32[1280,128]{1,0:T(8,128)} %get-tuple-element.44), channel_id=1, source_target_pairs={{4,8},{12,16},{20,24},{28,32},{36,40},{44,48},{52,56},{60,64},{68,... | collective-permute-start | bytes 1966088 | tf_op jit(solution)/shard_map/ppermute | solution.py:734
  14.4 6.9 %copy-start.3 = (bf16[4096,512]{1,0:T(8,128)(2,1)S(1)}, bf16[4096,512]{1,0:T(8,128)(2,1)}, u32[]{:S(2)}) copy-start(bf16[4096,512]{1,0:T(8,128)(2,1)} %table_ref.1) | copy-start | bytes 12582916
  15.3 6.1 %copy-start.5 = (s32[1024]{0:T(1024)S(1)}, s32[1024]{0:T(1024)}, u32[]{:S(2)}) copy-start(s32[1024]{0:T(1024)} %rows_ref.1) | copy-start | bytes 12292
  17.3 17.0 %collective-permute-start.3 = (f32[640,128]{1,0:T(8,128)S(1)}, f32[640,128]{1,0:T(8,128)S(1)}, u32[]{:S(2)}, u32[]{:S(2)}) collective-permute-start(f32[640,128]{1,0:T(8,128)S(1)} %edges.2.own_ref), channel_id=1, source_target_pairs={{1,2},{2,1},{5,6},{6,5},{9,10},{10,9},{13,14},{14,13},{17,18},{18,... | collective-permute-start | bytes 983048 | tf_op jit(solution)/shard_map/ppermute | solution.py:734
  20.6 13.6 %collective-permute-start.2 = (f32[640,128]{1,0:T(8,128)S(1)}, f32[640,128]{1,0:T(8,128)S(1)}, u32[]{:S(2)}, u32[]{:S(2)}) collective-permute-start(f32[640,128]{1,0:T(8,128)S(1)} %edges.2.own_ref), channel_id=1, source_target_pairs={{0,1},{2,3},{1,0},{3,2},{4,5},{6,7},{5,4},{7,6},{8,9},{10,11},{9,8... | collective-permute-start | bytes 983048 | tf_op jit(solution)/shard_map/ppermute | solution.py:734
  21.4 13.8 %copy-start.6 = (s32[1024]{0:T(1024)S(1)}, s32[1024]{0:T(1024)}, u32[]{:S(2)}) copy-start(s32[1024]{0:T(1024)} %param.8) | copy-start | bytes 12292
  34.6 7.1 %collective-permute-start.4 = (f32[96,128]{1,0:T(8,128)S(1)}, f32[96,128]{1,0:T(8,128)S(1)}, u32[]{:S(2)}, u32[]{:S(2)}) collective-permute-start(f32[96,128]{1,0:T(8,128)S(1)} %get-tuple-element.48), channel_id=1, source_target_pairs={{0,4},{8,12},{16,20},{24,28},{32,36},{40,44},{48,52},{56,60},{64,6... | collective-permute-start | bytes 147464 | tf_op jit(solution)/shard_map/ppermute | solution.py:734
  34.7 8.7 %collective-permute-start.5 = (f32[96,128]{1,0:T(8,128)S(1)}, f32[96,128]{1,0:T(8,128)S(1)}, u32[]{:S(2)}, u32[]{:S(2)}) collective-permute-start(f32[96,128]{1,0:T(8,128)S(1)} %get-tuple-element.49), channel_id=1, source_target_pairs={{4,8},{12,16},{20,24},{28,32},{36,40},{44,48},{52,56},{60,64},{68,... | collective-permute-start | bytes 147464 | tf_op jit(solution)/shard_map/ppermute | solution.py:734
  50.5 26.2 %collective-permute-start.6 = (f32[1024,128]{1,0:T(8,128)S(1)}, f32[1024,128]{1,0:T(8,128)S(1)}, u32[]{:S(2)}, u32[]{:S(2)}) collective-permute-start(f32[1024,128]{1,0:T(8,128)S(1)} %get-tuple-element.63), channel_id=1, source_target_pairs={{0,4},{8,12},{16,20},{24,28},{32,36},{40,44},{48,52},{56,60},{64,6... | collective-permute-start | bytes 1572872 | tf_op jit(solution)/shard_map/ppermute | solution.py:734
  50.6 26.1 %collective-permute-start.7 = (f32[1024,128]{1,0:T(8,128)S(1)}, f32[1024,128]{1,0:T(8,128)S(1)}, u32[]{:S(2)}, u32[]{:S(2)}) collective-permute-start(f32[1024,128]{1,0:T(8,128)S(1)} %get-tuple-element.64), channel_id=1, source_target_pairs={{4,8},{12,16},{20,24},{28,32},{36,40},{44,48},{52,56},{60,64},{68,... | collective-permute-start | bytes 1572872 | tf_op jit(solution)/shard_map/ppermute | solution.py:734
  59.3 8.2 %collective-permute-start.9 = (f32[512,128]{1,0:T(8,128)S(1)}, f32[512,128]{1,0:T(8,128)S(1)}, u32[]{:S(2)}, u32[]{:S(2)}) collective-permute-start(f32[512,128]{1,0:T(8,128)S(1)} %edges.3.own_ref), channel_id=1, source_target_pairs={{1,2},{2,1},{5,6},{6,5},{9,10},{10,9},{13,14},{14,13},{17,18},{18,... | collective-permute-start | bytes 786440 | tf_op jit(solution)/shard_map/ppermute | solution.py:734
  63.2 4.3 %collective-permute-start.8 = (f32[512,128]{1,0:T(8,128)S(1)}, f32[512,128]{1,0:T(8,128)S(1)}, u32[]{:S(2)}, u32[]{:S(2)}) collective-permute-start(f32[512,128]{1,0:T(8,128)S(1)} %edges.3.own_ref), channel_id=1, source_target_pairs={{0,1},{2,3},{1,0},{3,2},{4,5},{6,7},{5,4},{7,6},{8,9},{10,11},{9,8... | collective-permute-start | bytes 786440 | tf_op jit(solution)/shard_map/ppermute | solution.py:734
  67.8 6.9 %collective-permute-start.10 = (f32[64,128]{1,0:T(8,128)S(1)}, f32[64,128]{1,0:T(8,128)S(1)}, u32[]{:S(2)}, u32[]{:S(2)}) collective-permute-start(f32[64,128]{1,0:T(8,128)S(1)} %get-tuple-element.67), channel_id=1, source_target_pairs={{0,4},{8,12},{16,20},{24,28},{32,36},{40,44},{48,52},{56,60},{64,6... | collective-permute-start | bytes 98312 | tf_op jit(solution)/shard_map/ppermute | solution.py:734
  67.9 8.8 %collective-permute-start.11 = (f32[64,128]{1,0:T(8,128)S(1)}, f32[64,128]{1,0:T(8,128)S(1)}, u32[]{:S(2)}, u32[]{:S(2)}) collective-permute-start(f32[64,128]{1,0:T(8,128)S(1)} %get-tuple-element.68), channel_id=1, source_target_pairs={{4,8},{12,16},{20,24},{28,32},{36,40},{44,48},{52,56},{60,64},{68,... | collective-permute-start | bytes 98312 | tf_op jit(solution)/shard_map/ppermute | solution.py:734

commit v7 on v5

--- a/solution.py
+++ b/solution.py
@@ -43,6 +43,7 @@
 WIDTH = 32
 UNROLL = 8
 TAIL = 4 * ROWS
+PARTS = ((0, 4), (4, 12), (12, 16))
 COEF = 2 * ROWS
 
 
@@ -112,8 +113,8 @@
 
 
 def tail_line(ref, var, k, row):
-    lines = ref.at[pl.ds(pl.multiple_of(var * 64, 64), 64)]
-    return jnp.broadcast_to(lines[2 * k + row : 2 * k + row + 1], (WIDTH, 128))
+    lines = ref.at[pl.ds(pl.multiple_of(row * 128 + var * 32, 32), 32)]
+    return jnp.broadcast_to(lines[k : k + 1], (WIDTH, 128))
 
 
 def sort_sides(index, even_ref, odd_ref, below_ref, above_ref):
@@ -128,69 +129,65 @@
         even_ref[...], odd_ref[...] = below_ref[...], above_ref[...]
 
 
-def enter_outer(x_ref, coef_ref, low_ref, high_ref, even_ref, odd_ref, x_in, coef_in, sems):
-    copies = [
-        pltpu.make_async_copy(x_ref.at[pl.ds(0, 4)], x_in.at[0], sems.at[0]),
-        pltpu.make_async_copy(x_ref.at[pl.ds(12, 4)], x_in.at[1], sems.at[1]),
-        pltpu.make_async_copy(coef_ref, coef_in, sems.at[2]),
-    ]
-    for copy in copies:
-        copy.start()
-    low_ref[TAIL:] = jnp.zeros((256, 128), F32)
-    high_ref[TAIL:] = jnp.zeros((256, 128), F32)
-    for side, ref in ((0, low_ref), (1, high_ref)):
-        copies[side].wait()
-
-        @pl.loop(0, 4)
-        def _(k):
-            ref[pl.ds(pl.multiple_of(k * ROWS, ROWS), ROWS)] = x_in[side, k].T
-
-    copies[2].wait()
-
-    @pl.loop(0, 4)
-    def _(k):
-        lines = pl.ds(pl.multiple_of(TAIL + k * 64, 64), 58)
-        low_ref[lines] = coef_in[k, :, 0:2].reshape(58, 128)
-        high_ref[lines] = coef_in[k, :, 14:16].reshape(58, 128)
-
-    sort_sides(lax.axis_index("azim"), even_ref, odd_ref, low_ref, high_ref)
-
-
-def call_enter_outer(x, coef):
-    return pl.pallas_call(
-        enter_outer,
-        in_specs=[pl.BlockSpec(memory_space=pltpu.HBM)] * 2,
-        out_specs=whole(4),
-        out_shape=arrays(*[(TAIL + 256, 128)] * 4),
+def ship(odd, x_ref, coef_ref, out_ref, coef_in, lines, sems):
+    goes_up = lax.axis_index("azim") % 2 == odd
+    row = jnp.where(goes_up, 12, 0)
+    coef_row = pl.multiple_of(jnp.where(goes_up, 8, 0), 8)
+    state = pltpu.make_async_copy(x_ref.at[pl.ds(row, 4)], out_ref.at[pl.ds(0, 4)], sems.at[0])
+    state.start()
+    load = pltpu.make_async_copy(coef_ref.at[:, pl.ds(coef_row, 8)], coef_in, sems.at[1])
+    load.start()
+    lines[...] = jnp.zeros_like(lines)
+    load.wait()
+
+    def fill(first):
+        for var in range(4):
+            for k in range(2):
+                lines[32 * var : 32 * var + 29, 128 * k : 128 * k + 128] = coef_in[
+                    29 * var : 29 * var + 29, first + k, :
+                ]
+
+    pl.when(goes_up)(lambda: fill(6))
+    pl.when(jnp.logical_not(goes_up))(lambda: fill(0))
+    store = pltpu.make_async_copy(lines, out_ref.at[4], sems.at[2])
+    store.start()
+    state.wait()
+    store.wait()
+
+
+def call_ship(odd, x, coef):
+    hbm = pl.BlockSpec(memory_space=pltpu.HBM)
+    return pl.pallas_call(
+        functools.partial(ship, odd),
+        in_specs=[hbm] * 2,
+        out_specs=hbm,
+        out_shape=arrays((5, 128, 256))[0],
         scratch_shapes=[
-            pltpu.VMEM((2, 4, 128, 256), F32),
-            pltpu.VMEM((4, 29, 16, 128), F32),
+            pltpu.VMEM((116, 8, 128), F32),
+            pltpu.VMEM((128, 256), F32),
             pltpu.SemaphoreType.DMA((3,)),
         ],
         compiler_params=pltpu.CompilerParams(vmem_limit_bytes=ENTER_LIMIT),
-        name="enter_outer",
-    )(x, coef)
-
-
-def enter_inner(x_ref, mid_ref, x_in, sem):
-    copy = pltpu.make_async_copy(x_ref.at[pl.ds(4, 8)], x_in, sem)
-    copy.start()
-    copy.wait()
-
-    @pl.loop(0, 8)
-    def _(k):
-        mid_ref[pl.ds(pl.multiple_of(k * ROWS, ROWS), ROWS)] = x_in[k].T
-
-
-def call_enter_inner(x):
-    return pl.pallas_call(
-        enter_inner,
-        in_specs=[pl.BlockSpec(memory_space=pltpu.HBM)],
-        out_specs=whole(1)[0],
-        out_shape=arrays((8 * ROWS, 128))[0],
-        scratch_shapes=[pltpu.VMEM((8, 128, 256), F32), pltpu.SemaphoreType.DMA],
-        compiler_params=params(),
-        name="enter_inner",
+        name="ship",
+    )(x, coef.reshape(116, 16, 128))
+
+
+def enter(x_ref, low_ref, mid_ref, high_ref):
+    for (first, stop), ref in zip(PARTS, (low_ref, mid_ref, high_ref)):
+
+        @pl.loop(0, stop - first)
+        def _(k):
+            ref[pl.ds(pl.multiple_of(k * ROWS, ROWS), ROWS)] = x_ref[first + k].T
+
+
+def call_enter(x):
+    return pl.pallas_call(
+        enter,
+        in_specs=whole(1),
+        out_specs=whole(3),
+        out_shape=arrays((4 * ROWS, 128), (8 * ROWS, 128), (4 * ROWS, 128)),
+        compiler_params=params(),
+        name="enter",
     )(x)
 
 
@@ -256,17 +253,26 @@
     )(coef.reshape(-1, 128))
 
 
-def halo_edges(even_ref, odd_ref, edge_ref, *refs):
+def halo_edges(odd_ref, even_ref, edge_ref, *refs):
     top_ref, bot_ref, out_ref = refs[len(refs) > 3 :][:3]
+    first_step = len(refs) > 3
     even_is_above = lax.axis_index("azim") % 2 == 0
 
-    @pl.when(even_is_above)
-    def _():
-        top_ref[...], bot_ref[...] = odd_ref[:TAIL], even_ref[:TAIL]
-
-    @pl.when(jnp.logical_not(even_is_above))
-    def _():
-        top_ref[...], bot_ref[...] = even_ref[:TAIL], odd_ref[:TAIL]
+    def sorted_sides(above):
+        sides = (odd_ref, even_ref) if above else (even_ref, odd_ref)
+        for side, ref in zip(sides, (top_ref, bot_ref)):
+            if first_step:
+                for k in range(4):
+                    ref[ROWS * k : ROWS * k + ROWS] = side[k].T
+            else:
+                ref[...] = side[...]
+        if first_step:
+            for side, ref in zip(sides, refs[4:]):
+                for k in range(2):
+                    ref[128 * k : 128 * k + 128] = side[4, :, 128 * k : 128 * k + 128]
+
+    pl.when(even_is_above)(lambda: sorted_sides(True))
+    pl.when(jnp.logical_not(even_is_above))(lambda: sorted_sides(False))
 
     def one(var, half):
         tail = window(edge_ref, 0, var, half)
@@ -279,35 +285,22 @@
         put(out_ref, 1, var, half, head)
 
     each_part(one)
-    if len(refs) > 3:
+    if first_step:
         coef_edge_ref, (ctop_ref, cbot_ref) = refs[0], refs[4:]
-
-        @pl.when(even_is_above)
-        def _():
-            ctop_ref[...], cbot_ref[...] = odd_ref[TAIL:], even_ref[TAIL:]
-
-        @pl.when(jnp.logical_not(even_is_above))
-        def _():
-            ctop_ref[...], cbot_ref[...] = even_ref[TAIL:], odd_ref[TAIL:]
-
-        number = lax.broadcasted_iota(jnp.int32, (64, 128), 0) // 2
+        number = lax.broadcasted_iota(jnp.int32, (32, 128), 0)
         for var in range(4):
-            pack = coef_edge_ref[32 * var : 32 * var + 29]
+            pack = coef_edge_ref[32 * var : 32 * var + 32]
             for k in range(2):
-                lines = pl.ds(64 * var + k, 29, stride=2)
-                pack = place(pack, k - 2, ctop_ref[lines, :], 126)
-                pack = place(pack, k + 16, cbot_ref[lines, :], 126)
-            out_ref[COEF + 32 * var : COEF + 32 * var + 29] = pack
-            out_ref[COEF + 32 * var + 29 : COEF + 32 * var + 32] = jnp.zeros((3, 128), F32)
-        for var in range(4):
-            at = slice(64 * var, 64 * var + 64)
-            for ref in (ctop_ref, cbot_ref):
-                lines = ref[at]
-                result = lines
-                for j in (0, 1, 3, 4):
-                    here = (number % 5 == j) & (number < 25)
-                    result = jnp.where(here, turned(j, lines), result)
-                ref[at] = result
+                at = slice(128 * k + 32 * var, 128 * k + 32 * var + 32)
+                for ref, row in ((ctop_ref, k - 2), (cbot_ref, k + 16)):
+                    lines = ref[at]
+                    pack = place(pack, row, lines, 126)
+                    result = lines
+                    for j in (0, 1, 3, 4):
+                        here = (number % 5 == j) & (number < 25)
+                        result = jnp.where(here, turned(j, lines), result)
+                    ref[at] = result
+            out_ref[COEF + 32 * var : COEF + 32 * var + 32] = pack
 
 
 def call_halo_edges(even, odd, edge, *coef_edge):
@@ -321,7 +314,7 @@
         ),
         compiler_params=params(),
         name="halo_edges",
-    )(even, odd, edge, *coef_edge)
+    )(odd, even, edge, *coef_edge)
 
 
 def outer_first(top_ref, low_ref, high_ref, bot_ref, coef_ref, ctop_ref, cbot_ref,
@@ -478,9 +471,6 @@
     )(even, odd, own, lines)
 
 
-PARTS = ((0, 4), (4, 12), (12, 16))
-
-
 def second(ranges, parts, n_y, sides, *refs):
     y_refs, refs = refs[:n_y], refs[n_y:]
     mend_y_ref, mend_u_ref, coef_ref = refs[:3]
@@ -647,8 +637,9 @@
     weights = call_gather(mode_row, mode_table)
     w_high, w_low = call_spread(wall_count, wall_cells.reshape(1, slots), weights)
 
-    low, high, even, odd = call_enter_outer(perturbation_in, coefficients)
-    mid = call_enter_inner(perturbation_in)
+    odd = call_ship(1, perturbation_in, coefficients)
+    even = call_ship(0, perturbation_in, coefficients)
+    low, mid, high = call_enter(perturbation_in)
     coef_edge, coef = call_coef_edges(coefficients)
     for step in range(STEPS):
         even = swap(even, "azim", 0)

time: 101 us -> 127 us (1.26)
  Pallas kernels: 41.2 us -> 72.5 us
  starting transfers between devices: 22.1 us -> 17.4 us
  blocking collectives: 21.1 us -> 16.8 us
  waiting for transfers between devices: 12.1 us -> 15.8 us
    pallas_call x2 -> x3, Pallas kernels: 4.56 us -> 35.6 us  [the longest x2 34 us: call_ship(): pl.pallas_call(functools.partial(ship, odd), in_specs=[hbm] * 2, out_spec...]
    ppermute x8, starting transfers between devices: 22.1 us -> 17.4 us  [swap(): return lax.ppermute(block, axis, swaps(count, odd, axis == 'azim'))]
    all_to_all x1, blocking collectives: 21.1 us -> 16.8 us  [body(): lax.all_to_all(term.reshape(count, -1, term.shape[1]), ('azim', 'rad'), 0...]
    ppermute x8, waiting for transfers between devices: 12.1 us -> 15.8 us  [swap(): return lax.ppermute(block, axis, swaps(count, odd, axis == 'azim'))]
  transfers between devices with their start and end apart: 8 -> 8, of which waited for: 4 -> 3; matrix products, arithmetic and copies ran while one was open for 0% -> 0% of each run, Pallas kernels for 23% -> 32%
where the time goes in v7:
time: 127 us
  Pallas kernels  72.5 us (57%)
  starting transfers between devices  17.4 us (14%)
  blocking collectives  16.8 us (13%)
  waiting for transfers between devices  15.8 us (12%)
  local copies, waits for them, and re-layouts  2.36 us (2%)
  between operations  1.56 us (1%)
    pallas_call x2, Pallas kernels, call_ship(): pl.pallas_call(functools.partial(ship, odd), in_specs=[hbm] * 2, out_spec...  34 us
    ppermute x8, starting transfers between devices, swap(): return lax.ppermute(block, axis, swaps(count, odd, axis == 'azim'))  17.4 us
    all_to_all x1, blocking collectives, body(): lax.all_to_all(term.reshape(count, -1, term.shape[1]), ('azim', 'rad'), 0...  16.8 us
    ppermute x8, waiting for transfers between devices, swap(): return lax.ppermute(block, axis, swaps(count, odd, axis == 'azim'))  15.8 us
    pallas_call x3, Pallas kernels, call_second(): pl.pallas_call(functools.partial(second, ranges, parts, len(ys), sides),...  9.3 us
    pallas_call x2, Pallas kernels, call_inner_first(): pl.pallas_call(inner_first, in_specs=whole(4), out_specs=whole(2), out_sh...  7.03 us
    pallas_call x1, Pallas kernels, call_gather(): pl.pallas_call(gather, in_specs=[pl.BlockSpec(memory_space=pltpu.SMEM)] +...  4.63 us
    pallas_call x2, Pallas kernels, call_outer_first(): pl.pallas_call(outer_first, in_specs=whole(7), out_specs=whole(2), out_sh...  4.08 us
  transfers between devices with their start and end apart: 8, of which 3 were waited for; matrix products, arithmetic and copies ran while one was open for 0% of the time, Pallas kernels for 32%

profile of v7, /device:TPU:1, one launch (start us, length us, event | category | flops | bytes accessed | tf_op | source)
XLA Modules:
  0.0 127.2 jit_solution(16528329493902654139)
XLA Ops:
  0.6 17.0 %ship.2 = f32[5,128,256]{2,1,0:T(8,128)} custom-call(f32[16,128,256]{2,1,0:T(8,128)} %x_ref.5, f32[116,16,128]{2,1,0:T(8,128)} %bitcast.3), custom_call_target="tpu_custom_call" | custom-call | tf_op jit(solution)/shard_map/ship/pallas_call | solution.py:160
  17.7 0.0 copy-start
  17.7 0.0 copy-start.1
  17.7 9.6 %collective-permute-start = (f32[5,128,256]{2,1,0:T(8,128)}, f32[5,128,256]{2,1,0:T(8,128)S(1)}, u32[]{:S(2)}, u32[]{:S(2)}) collective-permute-start(f32[5,128,256]{2,1,0:T(8,128)} %ship.2), channel_id=1, source_target_pairs={{4,8},{12,16},{20,24},{28,32},{36,40},{44,48},{52,56},{60,64},{68,... | collective-permute-start | bytes 1966088 | tf_op jit(solution)/shard_map/ppermute | solution.py:634
  27.3 17.0 %ship.3 = f32[5,128,256]{2,1,0:T(8,128)} custom-call(f32[16,128,256]{2,1,0:T(8,128)} %x_ref.5, f32[116,16,128]{2,1,0:T(8,128)} %bitcast.4), custom_call_target="tpu_custom_call" | custom-call | tf_op jit(solution)/shard_map/ship/pallas_call | solution.py:160
  44.3 0.0 copy-start.3
  44.3 0.1 collective-permute-start.1
  44.4 0.0 copy-done
  44.4 1.6 %enter.1 = (f32[1024,128]{1,0:T(8,128)S(1)}, f32[2048,128]{1,0:T(8,128)S(1)}, f32[1024,128]{1,0:T(8,128)S(1)}) custom-call(f32[16,128,256]{2,1,0:T(8,128)S(1)} %copy-done), custom_call_target="tpu_custom_call" | custom-call | tf_op jit(solution)/shard_map/enter/pallas_call | solution.py:184
  46.7 0.0 copy-done.1
  46.7 0.8 coef_edges.1
  47.4 0.0 copy-done.3
  47.5 0.0 copy-start.2
  47.5 2.2 %copy-done.2 = bf16[4096,512]{1,0:T(8,128)(2,1)S(1)} copy-done((bf16[4096,512]{1,0:T(8,128)(2,1)S(1)}, bf16[4096,512]{1,0:T(8,128)(2,1)}, u32[]{:S(2)}) %copy-start.2) | copy-done | bytes 4194328
  49.6 4.6 %gather.1.weights_ref = bf16[1024,512]{1,0:T(8,128)(2,1)S(1)} custom-call(s32[1024]{0:T(1024)S(1)} %copy-done.3, bf16[4096,512]{1,0:T(8,128)(2,1)S(1)} %copy-done.2), custom_call_target="tpu_custom_call" | custom-call | tf_op jit(solution)/shard_map/gather/pallas_call | solution.py:549
  54.3 0.0 copy-start.4
  54.3 3.5 %inner_first.2 = (f32[3072,128]{1,0:T(8,128)S(1)}, f32[512,128]{1,0:T(8,128)S(1)}) custom-call(f32[1024,128]{1,0:T(8,128)S(1)} %get-tuple-element.40.low_ref.refs_6_, f32[2048,128]{1,0:T(8,128)S(1)} %get-tuple-element.41.mid_ref.refs_4_, f32[1024,128]{1,0:T(8,128)S(1)} %get-tuple-element.42.high_ref.refs_7_, ...), custom_call_target="tpu_custom_call" | custom-call | flops 22806528 | bytes 3145728 | tf_op jit(solution)/shard_map/inner_first/pallas_call | solution.py:219
  57.8 0.0 copy-done.4
  57.8 3.6 %spread.1 = (bf16[2048,512]{1,0:T(8,128)(2,1)S(1)}, bf16[2048,512]{1,0:T(8,128)(2,1)S(1)}) custom-call(s32[1]{0:T(128)S(6)} %copy.8.count_ref, s32[1,1024]{1,0:T(1,128)S(1)} %bitcast.6, bf16[1024,512]{1,0:T(8,128)(2,1)S(1)} %gather.1.weights_ref), custom_call_target="tpu_custom_call" | custom-call | flops 2147483648 | bytes 6291456 | tf_op jit(solution)/shard_map/spread/pallas_call | solution.py:573
  61.4 0.0 collective-permute-done.odd_ref
  61.4 0.0 collective-permute-done.1.even_ref
  61.4 1.3 halo_edges.2
  62.7 3.1 %collective-permute-start.3 = (f32[640,128]{1,0:T(8,128)S(1)}, f32[640,128]{1,0:T(8,128)S(1)}, u32[]{:S(2)}, u32[]{:S(2)}) collective-permute-start(f32[640,128]{1,0:T(8,128)S(1)} %get-tuple-element.55.own_ref), channel_id=1, source_target_pairs={{1,2},{2,1},{5,6},{6,5},{9,10},{10,9},{13,14},{14,13},{17,18},{18,... | collective-permute-start | bytes 983048 | tf_op jit(solution)/shard_map/ppermute | solution.py:634
  65.8 0.3 collective-permute-start.2
  66.1 2.0 %outer_first.2 = (f32[1024,128]{1,0:T(8,128)S(1)}, f32[1024,128]{1,0:T(8,128)S(1)}) custom-call(f32[1024,128]{1,0:T(8,128)S(1)} %get-tuple-element.48.top_ref, f32[1024,128]{1,0:T(8,128)S(1)} %get-tuple-element.40.low_ref.refs_6_, f32[1024,128]{1,0:T(8,128)S(1)} %get-tuple-element.42.high_ref.refs_7_, f32[1024,128]{1,0:T(8,128)S(1)} %get-tuple-element.49.bot_ref, ...), custom_call_target="tpu_custom_call" | custom-call | flops 15204352 | bytes 2097152 | tf_op jit(solution)/shard_map/outer_first/pallas_call | solution.py:348
  68.1 3.0 %collective-permute-done.3.odd_ref = f32[640,128]{1,0:T(8,128)S(1)} collective-permute-done((f32[640,128]{1,0:T(8,128)S(1)}, f32[640,128]{1,0:T(8,128)S(1)}, u32[]{:S(2)}, u32[]{:S(2)}) %collective-permute-start.3) | collective-permute-done | bytes 327712 | tf_op jit(solution)/shard_map/ppermute | solution.py:634
  71.1 0.0 collective-permute-done.2.even_ref
  71.1 0.2 strip_lines.1.line_ref
  71.3 1.3 %strips.2 = (f32[4,64,128]{2,1,0:T(8,128)S(1)}, f32[4,64,128]{2,1,0:T(8,128)S(1)}) custom-call(f32[640,128]{1,0:T(8,128)S(1)} %collective-permute-done.2.even_ref, f32[640,128]{1,0:T(8,128)S(1)} %collective-permute-done.3.odd_ref, f32[640,128]{1,0:T(8,128)S(1)} %get-tuple-element.55.own_ref, f32[4,48,128]{2,1,0:T(8,128)S(1)} %strip_lines.1.line_ref), custom_call_target="tpu_custom_call" | custom-call | tf_op jit(solution)/shard_map/strips/pallas_call | solution.py:463
  72.6 2.5 %second.3 = (f32[1024,128]{1,0:T(8,128)S(1)}, f32[1024,128]{1,0:T(8,128)S(1)}, f32[1024,128]{1,0:T(8,128)S(1)}, f32[1024,128]{1,0:T(8,128)S(1)}) custom-call(f32[1024,128]{1,0:T(8,128)S(1)} %get-tuple-element.52.refs_0_, f32[3072,128]{1,0:T(8,128)S(1)} %get-tuple-element.53.refs_1_.refs_0_, f32[1024,128]{1,0:T(8,128)S(1)} %get-tuple-element.54.refs_2_, ...), custom_call_target="tpu_custom_call" | custom-call | flops 15204352 | bytes 2097152 | tf_op jit(solution)/shard_map/second/pallas_call | solution.py:518
  75.1 1.0 collective-permute-start.4
  76.1 0.8 collective-permute-start.5
  77.0 2.3 %second.4.mid_ref.refs_7_ = f32[2048,128]{1,0:T(8,128)S(1)} custom-call(f32[3072,128]{1,0:T(8,128)S(1)} %get-tuple-element.53.refs_1_.refs_0_, f32[4,64,128]{2,1,0:T(8,128)S(1)} %get-tuple-element.56.refs_3_.refs_1_, f32[4,64,128]{2,1,0:T(8,128)S(1)} %get-tuple-element.57.refs_4_.refs_2_, f32[4,29,16,128]{3,2,1,0:T(8,128)S(1)} %get-tuple-element.43.coef_ref.refs_5_.refs_3_, ...), custom_call_target="tpu_custom_call" | custom-call | flops 15204352 | bytes 2097152 | tf_op jit(solution)/shard_map/second/pallas_call | solution.py:518
  79.3 3.5 %inner_first.3 = (f32[3072,128]{1,0:T(8,128)S(1)}, f32[512,128]{1,0:T(8,128)S(1)}) custom-call(f32[1024,128]{1,0:T(8,128)S(1)} %get-tuple-element.60.low_ref.refs_6_, f32[2048,128]{1,0:T(8,128)S(1)} %second.4.mid_ref.refs_7_, f32[1024,128]{1,0:T(8,128)S(1)} %get-tuple-element.61.high_ref.refs_8_, ...), custom_call_target="tpu_custom_call" | custom-call | flops 22806528 | bytes 3145728 | tf_op jit(solution)/shard_map/inner_first/pallas_call | solution.py:219
  82.8 9.7 %collective-permute-done.4.odd_ref = f32[1024,128]{1,0:T(8,128)S(1)} collective-permute-done((f32[1024,128]{1,0:T(8,128)S(1)}, f32[1024,128]{1,0:T(8,128)S(1)}, u32[]{:S(2)}, u32[]{:S(2)}) %collective-permute-start.4) | collective-permute-done | bytes 524320 | tf_op jit(solution)/shard_map/ppermute | solution.py:634
  92.5 0.0 collective-permute-done.5.even_ref
  92.5 0.6 halo_edges.3
  93.2 2.2 %collective-permute-start.7 = (f32[512,128]{1,0:T(8,128)S(1)}, f32[512,128]{1,0:T(8,128)S(1)}, u32[]{:S(2)}, u32[]{:S(2)}) collective-permute-start(f32[512,128]{1,0:T(8,128)S(1)} %get-tuple-element.68.own_ref), channel_id=1, source_target_pairs={{1,2},{2,1},{5,6},{6,5},{9,10},{10,9},{13,14},{14,13},{17,18},{18,... | collective-permute-start | bytes 786440 | tf_op jit(solution)/shard_map/ppermute | solution.py:634
  95.4 0.3 collective-permute-start.6
  95.8 2.0 %outer_first.3 = (f32[1024,128]{1,0:T(8,128)S(1)}, f32[1024,128]{1,0:T(8,128)S(1)}) custom-call(f32[1024,128]{1,0:T(8,128)S(1)} %get-tuple-element.63.top_ref, f32[1024,128]{1,0:T(8,128)S(1)} %get-tuple-element.60.low_ref.refs_6_, f32[1024,128]{1,0:T(8,128)S(1)} %get-tuple-element.61.high_ref.refs_8_, f32[1024,128]{1,0:T(8,128)S(1)} %get-tuple-element.64.bot_ref, ...), custom_call_target="tpu_custom_call" | custom-call | flops 15204352 | bytes 2097152 | tf_op jit(solution)/shard_map/outer_first/pallas_call | solution.py:348
  97.8 3.1 %collective-permute-done.7.odd_ref = f32[512,128]{1,0:T(8,128)S(1)} collective-permute-done((f32[512,128]{1,0:T(8,128)S(1)}, f32[512,128]{1,0:T(8,128)S(1)}, u32[]{:S(2)}, u32[]{:S(2)}) %collective-permute-start.7) | collective-permute-done | bytes 262176 | tf_op jit(solution)/shard_map/ppermute | solution.py:634
  100.9 0.0 collective-permute-done.6.even_ref
  100.9 1.3 %strips.3 = (f32[4,64,128]{2,1,0:T(8,128)S(1)}, f32[4,64,128]{2,1,0:T(8,128)S(1)}) custom-call(f32[512,128]{1,0:T(8,128)S(1)} %collective-permute-done.6.even_ref, f32[512,128]{1,0:T(8,128)S(1)} %collective-permute-done.7.odd_ref, f32[512,128]{1,0:T(8,128)S(1)} %get-tuple-element.68.own_ref, f32[4,48,128]{2,1,0:T(8,128)S(1)} %strip_lines.1.line_ref), custom_call_target="tpu_custom_call" | custom-call | tf_op jit(solution)/shard_map/strips/pallas_call | solution.py:463
  102.2 4.5 %second.5 = (f32[1024,128]{1,0:T(8,128)S(1)}, f32[2048,128]{1,0:T(8,128)S(1)}, f32[1024,128]{1,0:T(8,128)S(1)}) custom-call(f32[1024,128]{1,0:T(8,128)S(1)} %get-tuple-element.65.refs_0_, f32[3072,128]{1,0:T(8,128)S(1)} %get-tuple-element.66.refs_1_, f32[1024,128]{1,0:T(8,128)S(1)} %get-tuple-element.67.refs_2_, ...), custom_call_target="tpu_custom_call" | custom-call | flops 15204352 | bytes 2097152 | tf_op jit(solution)/shard_map/second/pallas_call | solution.py:518
  106.7 2.8 %leave.1 = (f32[16,128,256]{2,1,0:T(8,128)}, f32[512,256]{1,0:T(8,128)S(1)}) custom-call(f32[1024,128]{1,0:T(8,128)S(1)} %get-tuple-element.71.low_ref, f32[2048,128]{1,0:T(8,128)S(1)} %get-tuple-element.72.mid_ref, f32[1024,128]{1,0:T(8,128)S(1)} %get-tuple-element.73.high_ref, bf16[2048,512]{1,0:T(8,128)(2,1)S(1)} %get-tuple-element.74.w_high_ref, ...), custom_call_target="tpu_custom_call" | custom-call | flops 2147483648 | bytes 8388608 | tf_op jit(solution)/shard_map/leave/pallas_call | solution.py:612
  109.5 0.1 reshape.20
  109.7 16.8 %all_to_all.5 = f32[128,4,256]{2,1,0:T(4,128)S(1)} all-to-all(f32[128,4,256]{2,1,0:T(4,128)S(1)} %reshape.20), channel_id=1, replica_groups=mesh['azim'=32,'rad'=4] {'azim','rad'}, dimensions={0} | all-to-all | bytes 1048576 | tf_op jit(solution)/shard_map/all_to_all | solution.py:669
  126.4 0.7 reduce_sum.9
Async XLA Ops:
  17.7 26.7 %copy-start = (f32[16,128,256]{2,1,0:T(8,128)S(1)}, f32[16,128,256]{2,1,0:T(8,128)}, u32[]{:S(2)}) copy-start(f32[16,128,256]{2,1,0:T(8,128)} %x_ref.5) | copy-start | bytes 6291460
  17.7 29.0 %copy-start.1 = (f32[4,29,16,128]{3,2,1,0:T(8,128)S(1)}, f32[4,29,16,128]{3,2,1,0:T(8,128)}, u32[]{:S(2)}) copy-start(f32[4,29,16,128]{3,2,1,0:T(8,128)} %param.7) | copy-start | bytes 2850820
  17.7 43.7 %collective-permute-start = (f32[5,128,256]{2,1,0:T(8,128)}, f32[5,128,256]{2,1,0:T(8,128)S(1)}, u32[]{:S(2)}, u32[]{:S(2)}) collective-permute-start(f32[5,128,256]{2,1,0:T(8,128)} %ship.2), channel_id=1, source_target_pairs={{4,8},{12,16},{20,24},{28,32},{36,40},{44,48},{52,56},{60,64},{68,... | collective-permute-start | bytes 1966088 | tf_op jit(solution)/shard_map/ppermute | solution.py:634
  44.3 3.2 %copy-start.3 = (s32[1024]{0:T(1024)S(1)}, s32[1024]{0:T(1024)}, u32[]{:S(2)}) copy-start(s32[1024]{0:T(1024)} %rows_ref.1) | copy-start | bytes 12292
  44.3 17.1 %collective-permute-start.1 = (f32[5,128,256]{2,1,0:T(8,128)}, f32[5,128,256]{2,1,0:T(8,128)S(1)}, u32[]{:S(2)}, u32[]{:S(2)}) collective-permute-start(f32[5,128,256]{2,1,0:T(8,128)} %ship.3), channel_id=1, source_target_pairs={{0,4},{8,12},{16,20},{24,28},{32,36},{40,44},{48,52},{56,60},{64,6... | collective-permute-start | bytes 1966088 | tf_op jit(solution)/shard_map/ppermute | solution.py:634
  47.5 2.2 %copy-start.2 = (bf16[4096,512]{1,0:T(8,128)(2,1)S(1)}, bf16[4096,512]{1,0:T(8,128)(2,1)}, u32[]{:S(2)}) copy-start(bf16[4096,512]{1,0:T(8,128)(2,1)} %table_ref.1) | copy-start | bytes 12582916
  54.3 3.5 %copy-start.4 = (s32[1024]{0:T(1024)S(1)}, s32[1024]{0:T(1024)}, u32[]{:S(2)}) copy-start(s32[1024]{0:T(1024)} %param.8) | copy-start | bytes 12292
  62.7 8.4 %collective-permute-start.3 = (f32[640,128]{1,0:T(8,128)S(1)}, f32[640,128]{1,0:T(8,128)S(1)}, u32[]{:S(2)}, u32[]{:S(2)}) collective-permute-start(f32[640,128]{1,0:T(8,128)S(1)} %get-tuple-element.55.own_ref), channel_id=1, source_target_pairs={{1,2},{2,1},{5,6},{6,5},{9,10},{10,9},{13,14},{14,13},{17,18},{18,... | collective-permute-start | bytes 983048 | tf_op jit(solution)/shard_map/ppermute | solution.py:634
  65.8 5.3 %collective-permute-start.2 = (f32[640,128]{1,0:T(8,128)S(1)}, f32[640,128]{1,0:T(8,128)S(1)}, u32[]{:S(2)}, u32[]{:S(2)}) collective-permute-start(f32[640,128]{1,0:T(8,128)S(1)} %get-tuple-element.55.own_ref), channel_id=1, source_target_pairs={{0,1},{2,3},{1,0},{3,2},{4,5},{6,7},{5,4},{7,6},{8,9},{10,11},{9,8... | collective-permute-start | bytes 983048 | tf_op jit(solution)/shard_map/ppermute | solution.py:634
  75.1 17.4 %collective-permute-start.4 = (f32[1024,128]{1,0:T(8,128)S(1)}, f32[1024,128]{1,0:T(8,128)S(1)}, u32[]{:S(2)}, u32[]{:S(2)}) collective-permute-start(f32[1024,128]{1,0:T(8,128)S(1)} %get-tuple-element.58), channel_id=1, source_target_pairs={{4,8},{12,16},{20,24},{28,32},{36,40},{44,48},{52,56},{60,64},{68,... | collective-permute-start | bytes 1572872 | tf_op jit(solution)/shard_map/ppermute | solution.py:634
  76.1 16.4 %collective-permute-start.5 = (f32[1024,128]{1,0:T(8,128)S(1)}, f32[1024,128]{1,0:T(8,128)S(1)}, u32[]{:S(2)}, u32[]{:S(2)}) collective-permute-start(f32[1024,128]{1,0:T(8,128)S(1)} %get-tuple-element.59), channel_id=1, source_target_pairs={{0,4},{8,12},{16,20},{24,28},{32,36},{40,44},{48,52},{56,60},{64,6... | collective-permute-start | bytes 1572872 | tf_op jit(solution)/shard_map/ppermute | solution.py:634
  93.2 7.7 %collective-permute-start.7 = (f32[512,128]{1,0:T(8,128)S(1)}, f32[512,128]{1,0:T(8,128)S(1)}, u32[]{:S(2)}, u32[]{:S(2)}) collective-permute-start(f32[512,128]{1,0:T(8,128)S(1)} %get-tuple-element.68.own_ref), channel_id=1, source_target_pairs={{1,2},{2,1},{5,6},{6,5},{9,10},{10,9},{13,14},{14,13},{17,18},{18,... | collective-permute-start | bytes 786440 | tf_op jit(solution)/shard_map/ppermute | solution.py:634
  95.4 5.5 %collective-permute-start.6 = (f32[512,128]{1,0:T(8,128)S(1)}, f32[512,128]{1,0:T(8,128)S(1)}, u32[]{:S(2)}, u32[]{:S(2)}) collective-permute-start(f32[512,128]{1,0:T(8,128)S(1)} %get-tuple-element.68.own_ref), channel_id=1, source_target_pairs={{0,1},{2,3},{1,0},{3,2},{4,5},{6,7},{5,4},{7,6},{8,9},{10,11},{9,8... | collective-permute-start | bytes 786440 | tf_op jit(solution)/shard_map/ppermute | solution.py:634

commit v8 on v7

--- a/solution.py
+++ b/solution.py
@@ -129,7 +129,7 @@
         even_ref[...], odd_ref[...] = below_ref[...], above_ref[...]
 
 
-def ship(odd, x_ref, coef_ref, out_ref, coef_in, lines, sems):
+def ship(odd, x_ref, coef_ref, out_ref, coef_in, sems):
     goes_up = lax.axis_index("azim") % 2 == odd
     row = jnp.where(goes_up, 12, 0)
     coef_row = pl.multiple_of(jnp.where(goes_up, 8, 0), 8)
@@ -137,22 +137,19 @@
     state.start()
     load = pltpu.make_async_copy(coef_ref.at[:, pl.ds(coef_row, 8)], coef_in, sems.at[1])
     load.start()
-    lines[...] = jnp.zeros_like(lines)
+    out_ref[4] = jnp.zeros((128, 256), F32)
     load.wait()
 
     def fill(first):
         for var in range(4):
             for k in range(2):
-                lines[32 * var : 32 * var + 29, 128 * k : 128 * k + 128] = coef_in[
+                out_ref[4, 32 * var : 32 * var + 29, 128 * k : 128 * k + 128] = coef_in[
                     29 * var : 29 * var + 29, first + k, :
                 ]
 
     pl.when(goes_up)(lambda: fill(6))
     pl.when(jnp.logical_not(goes_up))(lambda: fill(0))
-    store = pltpu.make_async_copy(lines, out_ref.at[4], sems.at[2])
-    store.start()
     state.wait()
-    store.wait()
 
 
 def call_ship(odd, x, coef):
@@ -160,13 +157,9 @@
     return pl.pallas_call(
         functools.partial(ship, odd),
         in_specs=[hbm] * 2,
-        out_specs=hbm,
+        out_specs=whole(1)[0],
         out_shape=arrays((5, 128, 256))[0],
-        scratch_shapes=[
-            pltpu.VMEM((116, 8, 128), F32),
-            pltpu.VMEM((128, 256), F32),
-            pltpu.SemaphoreType.DMA((3,)),
-        ],
+        scratch_shapes=[pltpu.VMEM((116, 8, 128), F32), pltpu.SemaphoreType.DMA((2,))],
         compiler_params=pltpu.CompilerParams(vmem_limit_bytes=ENTER_LIMIT),
         name="ship",
     )(x, coef.reshape(116, 16, 128))
@@ -254,8 +247,9 @@
 
 
 def halo_edges(odd_ref, even_ref, edge_ref, *refs):
-    top_ref, bot_ref, out_ref = refs[len(refs) > 3 :][:3]
-    first_step = len(refs) > 3
+    first_step = len(refs) > 5
+    top_ref, bot_ref, out_ref = refs[first_step:][:3]
+    rad_even_ref, rad_odd_ref = refs[-2:]
     even_is_above = lax.axis_index("azim") % 2 == 0
 
     def sorted_sides(above):
@@ -267,7 +261,7 @@
             else:
                 ref[...] = side[...]
         if first_step:
-            for side, ref in zip(sides, refs[4:]):
+            for side, ref in zip(sides, refs[4:6]):
                 for k in range(2):
                     ref[128 * k : 128 * k + 128] = side[4, :, 128 * k : 128 * k + 128]
 
@@ -286,7 +280,7 @@
 
     each_part(one)
     if first_step:
-        coef_edge_ref, (ctop_ref, cbot_ref) = refs[0], refs[4:]
+        coef_edge_ref, ctop_ref, cbot_ref = refs[0], refs[4], refs[5]
         number = lax.broadcasted_iota(jnp.int32, (32, 128), 0)
         for var in range(4):
             pack = coef_edge_ref[32 * var : 32 * var + 32]
@@ -301,16 +295,28 @@
                         result = jnp.where(here, turned(j, lines), result)
                     ref[at] = result
             out_ref[COEF + 32 * var : COEF + 32 * var + 32] = pack
+        rad_even_ref[ROWS:] = out_ref[COEF:]
+        rad_odd_ref[ROWS:] = out_ref[COEF:]
+    even_is_right = lax.axis_index("rad") % 2 == 0
+
+    @pl.when(even_is_right)
+    def _():
+        rad_even_ref[:ROWS], rad_odd_ref[:ROWS] = out_ref[:ROWS], out_ref[ROWS:COEF]
+
+    @pl.when(jnp.logical_not(even_is_right))
+    def _():
+        rad_odd_ref[:ROWS], rad_even_ref[:ROWS] = out_ref[:ROWS], out_ref[ROWS:COEF]
 
 
 def call_halo_edges(even, odd, edge, *coef_edge):
     return pl.pallas_call(
         halo_edges,
         in_specs=whole(3 + len(coef_edge)),
-        out_specs=whole(3 + 2 * len(coef_edge)),
+        out_specs=whole(5 + 2 * len(coef_edge)),
         out_shape=arrays(
             (TAIL, 128), (TAIL, 128), (COEF + 128 * len(coef_edge), 128),
             *[(256, 128)] * (2 * len(coef_edge)),
+            *[(ROWS + 128 * len(coef_edge), 128)] * 2,
         ),
         compiler_params=params(),
         name="halo_edges",
@@ -362,7 +368,8 @@
     number = lax.broadcasted_iota(jnp.int32, (32, 128), 0)
     for var in range(4):
         at = slice(COEF + 32 * var, COEF + 32 * var + 32)
-        even, odd = even_ref[at], odd_ref[at]
+        there = slice(ROWS + 32 * var, ROWS + 32 * var + 32)
+        even, odd = even_ref[there], odd_ref[there]
         right = jnp.where(even_is_right, even, odd)
         left = jnp.where(even_is_right, odd, even)
         lines = jnp.where(entry < 2, pltpu.roll(right, 126, axis=1), pltpu.roll(left, 2, axis=1))
@@ -422,7 +429,7 @@
     for var, half in every:
         at = slice(32 * half, 32 * half + 32)
         tail = jnp.where(even_is_right, part(odd_ref, 0, var, half), part(even_ref, 0, var, half))
-        head = jnp.where(even_is_right, part(even_ref, 1, var, half), part(odd_ref, 1, var, half))
+        head = jnp.where(even_is_right, part(even_ref, 0, var, half), part(odd_ref, 0, var, half))
         rim = jnp.where(entry < 2, head, tail)
         outer = jnp.where(entry < 2, tail, head)
         own = jnp.where(entry < 2, part(own_ref, 1, var, half), part(own_ref, 0, var, half))
@@ -647,10 +654,10 @@
         y_mid, edge = call_inner_first(low, mid, high, coef)
         if step == 0:
             edge, w_high = lax.optimization_barrier((edge, w_high))
-            top, bot, own, *tails = call_halo_edges(even, odd, edge, coef_edge)
+            top, bot, own, *tails, rad_even, rad_odd = call_halo_edges(even, odd, edge, coef_edge)
         else:
-            top, bot, own = call_halo_edges(even, odd, edge)
-        sides = swap(own, "rad", 0), swap(own, "rad", 1), own
+            top, bot, own, rad_even, rad_odd = call_halo_edges(even, odd, edge)
+        sides = swap(rad_even, "rad", 0), swap(rad_odd, "rad", 1), own
         ys = call_outer_first(top, low, high, bot, coef, *tails)
         ys = ys[0], y_mid, ys[1]
         if step == 0:

time: 127 us -> 95.6 us (0.75)
  Pallas kernels: 72.5 us -> 43 us
  waiting for transfers between devices: 15.8 us -> 11.6 us
    pallas_call x2, Pallas kernels: 34 us -> 4.25 us  [call_ship(): pl.pallas_call(functools.partial(ship, odd), in_specs=[hbm] * 2, out_spec...]
    ppermute x8, waiting for transfers between devices: 15.8 us -> 11.6 us  [swap(): return lax.ppermute(block, axis, swaps(count, odd, axis == 'azim'))]
  transfers between devices with their start and end apart: 8 -> 8, of which waited for: 3 -> 3; matrix products, arithmetic and copies ran while one was open for 0% -> 0% of each run, Pallas kernels for 32% -> 28%
where the time goes in v8:
time: 95.6 us; the launch traced here: 95.4 us
  Pallas kernels  43 us (45%)
  starting transfers between devices  18.4 us (19%)
  blocking collectives  17.7 us (19%)
  waiting for transfers between devices  11.6 us (12%)
  local copies, waits for them, and re-layouts  2.36 us (2%)
  between operations  1.56 us (2%)
    ppermute x8, starting transfers between devices, swap(): return lax.ppermute(block, axis, swaps(count, odd, axis == 'azim'))  18.4 us
    all_to_all x1, blocking collectives, body(): lax.all_to_all(term.reshape(count, -1, term.shape[1]), ('azim', 'rad'), 0...  17.7 us
    ppermute x8, waiting for transfers between devices, swap(): return lax.ppermute(block, axis, swaps(count, odd, axis == 'azim'))  11.6 us
    pallas_call x3, Pallas kernels, call_second(): pl.pallas_call(functools.partial(second, ranges, parts, len(ys), sides),...  9.32 us
    pallas_call x2, Pallas kernels, call_inner_first(): pl.pallas_call(inner_first, in_specs=whole(4), out_specs=whole(2), out_sh...  7.17 us
    pallas_call x1, Pallas kernels, call_gather(): pl.pallas_call(gather, in_specs=[pl.BlockSpec(memory_space=pltpu.SMEM)] +...  4.63 us
    pallas_call x2, Pallas kernels, call_ship(): pl.pallas_call(functools.partial(ship, odd), in_specs=[hbm] * 2, out_spec...  4.25 us
    pallas_call x2, Pallas kernels, call_outer_first(): pl.pallas_call(outer_first, in_specs=whole(7), out_specs=whole(2), out_sh...  4.15 us
  transfers between devices with their start and end apart: 8, of which 3 were waited for; matrix products, arithmetic and copies ran while one was open for 0% of the time, Pallas kernels for 28%

profile of v8, /device:TPU:1, one launch (start us, length us, event | category | flops | bytes accessed | tf_op | source)
XLA Modules:
  0.0 95.4 jit_solution(16774328072145665076)
XLA Ops:
  0.6 2.1 %ship.2 = f32[5,128,256]{2,1,0:T(8,128)} custom-call(f32[16,128,256]{2,1,0:T(8,128)} %x_ref.5, f32[116,16,128]{2,1,0:T(8,128)} %bitcast.3), custom_call_target="tpu_custom_call" | custom-call | tf_op jit(solution)/shard_map/ship/pallas_call | solution.py:157
  2.8 0.0 copy-start
  2.8 0.0 copy-start.1
  2.8 9.6 %collective-permute-start = (f32[5,128,256]{2,1,0:T(8,128)}, f32[5,128,256]{2,1,0:T(8,128)S(1)}, u32[]{:S(2)}, u32[]{:S(2)}) collective-permute-start(f32[5,128,256]{2,1,0:T(8,128)} %ship.2), channel_id=1, source_target_pairs={{4,8},{12,16},{20,24},{28,32},{36,40},{44,48},{52,56},{60,64},{68,... | collective-permute-start | bytes 1966088 | tf_op jit(solution)/shard_map/ppermute | solution.py:641
  12.4 2.1 %ship.3 = f32[5,128,256]{2,1,0:T(8,128)} custom-call(f32[16,128,256]{2,1,0:T(8,128)} %x_ref.5, f32[116,16,128]{2,1,0:T(8,128)} %bitcast.4), custom_call_target="tpu_custom_call" | custom-call | tf_op jit(solution)/shard_map/ship/pallas_call | solution.py:157
  14.5 0.0 copy-start.3
  14.5 0.1 collective-permute-start.1
  14.6 0.0 copy-done
  14.6 1.6 %enter.1 = (f32[1024,128]{1,0:T(8,128)S(1)}, f32[2048,128]{1,0:T(8,128)S(1)}, f32[1024,128]{1,0:T(8,128)S(1)}) custom-call(f32[16,128,256]{2,1,0:T(8,128)S(1)} %copy-done), custom_call_target="tpu_custom_call" | custom-call | tf_op jit(solution)/shard_map/enter/pallas_call | solution.py:177
  16.9 0.0 copy-done.1
  16.9 0.8 coef_edges.1
  17.7 0.0 copy-done.3
  17.7 0.0 copy-start.2
  17.7 2.2 %copy-done.2 = bf16[4096,512]{1,0:T(8,128)(2,1)S(1)} copy-done((bf16[4096,512]{1,0:T(8,128)(2,1)S(1)}, bf16[4096,512]{1,0:T(8,128)(2,1)}, u32[]{:S(2)}) %copy-start.2) | copy-done | bytes 4194328
  19.9 4.6 %gather.1.weights_ref = bf16[1024,512]{1,0:T(8,128)(2,1)S(1)} custom-call(s32[1024]{0:T(1024)S(1)} %copy-done.3, bf16[4096,512]{1,0:T(8,128)(2,1)S(1)} %copy-done.2), custom_call_target="tpu_custom_call" | custom-call | tf_op jit(solution)/shard_map/gather/pallas_call | solution.py:556
  24.5 0.0 copy-start.4
  24.5 3.7 %inner_first.2 = (f32[3072,128]{1,0:T(8,128)S(1)}, f32[512,128]{1,0:T(8,128)S(1)}) custom-call(f32[1024,128]{1,0:T(8,128)S(1)} %get-tuple-element.44.low_ref.refs_6_, f32[2048,128]{1,0:T(8,128)S(1)} %get-tuple-element.45.mid_ref.refs_4_, f32[1024,128]{1,0:T(8,128)S(1)} %get-tuple-element.46.high_ref.refs_7_, ...), custom_call_target="tpu_custom_call" | custom-call | flops 22806528 | bytes 3145728 | tf_op jit(solution)/shard_map/inner_first/pallas_call | solution.py:212
  28.2 0.0 copy-done.4
  28.2 3.6 %spread.1 = (bf16[2048,512]{1,0:T(8,128)(2,1)S(1)}, bf16[2048,512]{1,0:T(8,128)(2,1)S(1)}) custom-call(s32[1]{0:T(128)S(6)} %copy.8.count_ref, s32[1,1024]{1,0:T(1,128)S(1)} %bitcast.6, bf16[1024,512]{1,0:T(8,128)(2,1)S(1)} %gather.1.weights_ref), custom_call_target="tpu_custom_call" | custom-call | flops 2147483648 | bytes 6291456 | tf_op jit(solution)/shard_map/spread/pallas_call | solution.py:580
  31.8 0.0 collective-permute-done.odd_ref
  31.8 0.0 collective-permute-done.1.even_ref
  31.8 1.3 %halo_edges.2 = (f32[1024,128]{1,0:T(8,128)S(1)}, f32[1024,128]{1,0:T(8,128)S(1)}, f32[640,128]{1,0:T(8,128)S(1)}, f32[256,128]{1,0:T(8,128)S(1)}, f32[256,128]{...) custom-call(f32[5,128,256]{2,1,0:T(8,128)S(1)} %collective-permute-done.odd_ref, ...), custom_call_target="tpu_custom_call" | custom-call | tf_op jit(solution)/shard_map/halo_edges/pallas_call | solution.py:312
  33.1 1.0 %collective-permute-start.2 = (f32[384,128]{1,0:T(8,128)S(1)}, f32[384,128]{1,0:T(8,128)S(1)}, u32[]{:S(2)}, u32[]{:S(2)}) collective-permute-start(f32[384,128]{1,0:T(8,128)S(1)} %get-tuple-element.59), channel_id=1, source_target_pairs={{0,1},{2,3},{1,0},{3,2},{4,5},{6,7},{5,4},{7,6},{8,9},{10,11},{9,8... | collective-permute-start | bytes 589832 | tf_op jit(solution)/shard_map/ppermute | solution.py:641
  34.1 2.3 %collective-permute-start.3 = (f32[384,128]{1,0:T(8,128)S(1)}, f32[384,128]{1,0:T(8,128)S(1)}, u32[]{:S(2)}, u32[]{:S(2)}) collective-permute-start(f32[384,128]{1,0:T(8,128)S(1)} %get-tuple-element.60), channel_id=1, source_target_pairs={{1,2},{2,1},{5,6},{6,5},{9,10},{10,9},{13,14},{14,13},{17,18},{18,... | collective-permute-start | bytes 589832 | tf_op jit(solution)/shard_map/ppermute | solution.py:641
  36.4 2.1 %outer_first.2 = (f32[1024,128]{1,0:T(8,128)S(1)}, f32[1024,128]{1,0:T(8,128)S(1)}) custom-call(f32[1024,128]{1,0:T(8,128)S(1)} %get-tuple-element.52.top_ref, f32[1024,128]{1,0:T(8,128)S(1)} %get-tuple-element.44.low_ref.refs_6_, f32[1024,128]{1,0:T(8,128)S(1)} %get-tuple-element.46.high_ref.refs_7_, f32[1024,128]{1,0:T(8,128)S(1)} %get-tuple-element.53.bot_ref, ...), custom_call_target="tpu_custom_call" | custom-call | flops 15204352 | bytes 2097152 | tf_op jit(solution)/shard_map/outer_first/pallas_call | solution.py:354
  38.5 0.0 collective-permute-done.2.even_ref
  38.6 2.5 %collective-permute-done.3.odd_ref = f32[384,128]{1,0:T(8,128)S(1)} collective-permute-done((f32[384,128]{1,0:T(8,128)S(1)}, f32[384,128]{1,0:T(8,128)S(1)}, u32[]{:S(2)}, u32[]{:S(2)}) %collective-permute-start.3) | collective-permute-done | bytes 196640 | tf_op jit(solution)/shard_map/ppermute | solution.py:641
  41.1 0.2 strip_lines.1.line_ref
  41.3 1.3 %strips.2 = (f32[4,64,128]{2,1,0:T(8,128)S(1)}, f32[4,64,128]{2,1,0:T(8,128)S(1)}) custom-call(f32[384,128]{1,0:T(8,128)S(1)} %collective-permute-done.2.even_ref, f32[384,128]{1,0:T(8,128)S(1)} %collective-permute-done.3.odd_ref, f32[640,128]{1,0:T(8,128)S(1)} %get-tuple-element.61.own_ref, f32[4,48,128]{2,1,0:T(8,128)S(1)} %strip_lines.1.line_ref), custom_call_target="tpu_custom_call" | custom-call | tf_op jit(solution)/shard_map/strips/pallas_call | solution.py:470
  42.6 2.5 %second.3 = (f32[1024,128]{1,0:T(8,128)S(1)}, f32[1024,128]{1,0:T(8,128)S(1)}, f32[1024,128]{1,0:T(8,128)S(1)}, f32[1024,128]{1,0:T(8,128)S(1)}) custom-call(f32[1024,128]{1,0:T(8,128)S(1)} %get-tuple-element.56.refs_0_, f32[3072,128]{1,0:T(8,128)S(1)} %get-tuple-element.57.refs_1_.refs_0_, f32[1024,128]{1,0:T(8,128)S(1)} %get-tuple-element.58.refs_2_, ...), custom_call_target="tpu_custom_call" | custom-call | flops 15204352 | bytes 2097152 | tf_op jit(solution)/shard_map/second/pallas_call | solution.py:525
  45.1 2.8 %collective-permute-start.4 = (f32[1024,128]{1,0:T(8,128)S(1)}, f32[1024,128]{1,0:T(8,128)S(1)}, u32[]{:S(2)}, u32[]{:S(2)}) collective-permute-start(f32[1024,128]{1,0:T(8,128)S(1)} %get-tuple-element.64), channel_id=1, source_target_pairs={{4,8},{12,16},{20,24},{28,32},{36,40},{44,48},{52,56},{60,64},{68,... | collective-permute-start | bytes 1572872 | tf_op jit(solution)/shard_map/ppermute | solution.py:641
  47.9 0.0 collective-permute-start.5
  47.9 2.3 %second.4.mid_ref.refs_7_ = f32[2048,128]{1,0:T(8,128)S(1)} custom-call(f32[3072,128]{1,0:T(8,128)S(1)} %get-tuple-element.57.refs_1_.refs_0_, f32[4,64,128]{2,1,0:T(8,128)S(1)} %get-tuple-element.62.refs_3_.refs_1_, f32[4,64,128]{2,1,0:T(8,128)S(1)} %get-tuple-element.63.refs_4_.refs_2_, f32[4,29,16,128]{3,2,1,0:T(8,128)S(1)} %get-tuple-element.47.coef_ref.refs_5_.refs_3_, ...), custom_call_target="tpu_custom_call" | custom-call | flops 15204352 | bytes 2097152 | tf_op jit(solution)/shard_map/second/pallas_call | solution.py:525
  50.2 3.5 %inner_first.3 = (f32[3072,128]{1,0:T(8,128)S(1)}, f32[512,128]{1,0:T(8,128)S(1)}) custom-call(f32[1024,128]{1,0:T(8,128)S(1)} %get-tuple-element.66.low_ref.refs_6_, f32[2048,128]{1,0:T(8,128)S(1)} %second.4.mid_ref.refs_7_, f32[1024,128]{1,0:T(8,128)S(1)} %get-tuple-element.67.high_ref.refs_8_, ...), custom_call_target="tpu_custom_call" | custom-call | flops 22806528 | bytes 3145728 | tf_op jit(solution)/shard_map/inner_first/pallas_call | solution.py:212
  53.7 7.3 %collective-permute-done.4.odd_ref = f32[1024,128]{1,0:T(8,128)S(1)} collective-permute-done((f32[1024,128]{1,0:T(8,128)S(1)}, f32[1024,128]{1,0:T(8,128)S(1)}, u32[]{:S(2)}, u32[]{:S(2)}) %collective-permute-start.4) | collective-permute-done | bytes 524320 | tf_op jit(solution)/shard_map/ppermute | solution.py:641
  61.1 0.0 collective-permute-done.5.even_ref
  61.1 0.7 halo_edges.3
  61.8 0.1 collective-permute-start.6
  61.9 2.6 %collective-permute-start.7 = (f32[256,128]{1,0:T(8,128)S(1)}, f32[256,128]{1,0:T(8,128)S(1)}, u32[]{:S(2)}, u32[]{:S(2)}) collective-permute-start(f32[256,128]{1,0:T(8,128)S(1)} %get-tuple-element.75), channel_id=1, source_target_pairs={{1,2},{2,1},{5,6},{6,5},{9,10},{10,9},{13,14},{14,13},{17,18},{18,... | collective-permute-start | bytes 393224 | tf_op jit(solution)/shard_map/ppermute | solution.py:641
  64.4 2.0 %outer_first.3 = (f32[1024,128]{1,0:T(8,128)S(1)}, f32[1024,128]{1,0:T(8,128)S(1)}) custom-call(f32[1024,128]{1,0:T(8,128)S(1)} %get-tuple-element.69.top_ref, f32[1024,128]{1,0:T(8,128)S(1)} %get-tuple-element.66.low_ref.refs_6_, f32[1024,128]{1,0:T(8,128)S(1)} %get-tuple-element.67.high_ref.refs_8_, f32[1024,128]{1,0:T(8,128)S(1)} %get-tuple-element.70.bot_ref, ...), custom_call_target="tpu_custom_call" | custom-call | flops 15204352 | bytes 2097152 | tf_op jit(solution)/shard_map/outer_first/pallas_call | solution.py:354
  66.5 0.0 collective-permute-done.6.even_ref
  66.5 1.7 %collective-permute-done.7.odd_ref = f32[256,128]{1,0:T(8,128)S(1)} collective-permute-done((f32[256,128]{1,0:T(8,128)S(1)}, f32[256,128]{1,0:T(8,128)S(1)}, u32[]{:S(2)}, u32[]{:S(2)}) %collective-permute-start.7) | collective-permute-done | bytes 131104 | tf_op jit(solution)/shard_map/ppermute | solution.py:641
  68.1 1.3 %strips.3 = (f32[4,64,128]{2,1,0:T(8,128)S(1)}, f32[4,64,128]{2,1,0:T(8,128)S(1)}) custom-call(f32[256,128]{1,0:T(8,128)S(1)} %collective-permute-done.6.even_ref, f32[256,128]{1,0:T(8,128)S(1)} %collective-permute-done.7.odd_ref, f32[512,128]{1,0:T(8,128)S(1)} %get-tuple-element.76.own_ref, f32[4,48,128]{2,1,0:T(8,128)S(1)} %strip_lines.1.line_ref), custom_call_target="tpu_custom_call" | custom-call | tf_op jit(solution)/shard_map/strips/pallas_call | solution.py:470
  69.5 4.5 %second.5 = (f32[1024,128]{1,0:T(8,128)S(1)}, f32[2048,128]{1,0:T(8,128)S(1)}, f32[1024,128]{1,0:T(8,128)S(1)}) custom-call(f32[1024,128]{1,0:T(8,128)S(1)} %get-tuple-element.71.refs_0_, f32[3072,128]{1,0:T(8,128)S(1)} %get-tuple-element.72.refs_1_, f32[1024,128]{1,0:T(8,128)S(1)} %get-tuple-element.73.refs_2_, ...), custom_call_target="tpu_custom_call" | custom-call | flops 15204352 | bytes 2097152 | tf_op jit(solution)/shard_map/second/pallas_call | solution.py:525
  74.0 2.8 %leave.1 = (f32[16,128,256]{2,1,0:T(8,128)}, f32[512,256]{1,0:T(8,128)S(1)}) custom-call(f32[1024,128]{1,0:T(8,128)S(1)} %get-tuple-element.79.low_ref, f32[2048,128]{1,0:T(8,128)S(1)} %get-tuple-element.80.mid_ref, f32[1024,128]{1,0:T(8,128)S(1)} %get-tuple-element.81.high_ref, bf16[2048,512]{1,0:T(8,128)(2,1)S(1)} %get-tuple-element.82.w_high_ref, ...), custom_call_target="tpu_custom_call" | custom-call | flops 2147483648 | bytes 8388608 | tf_op jit(solution)/shard_map/leave/pallas_call | solution.py:619
  76.8 0.1 reshape.20
  76.9 17.7 %all_to_all.5 = f32[128,4,256]{2,1,0:T(4,128)S(1)} all-to-all(f32[128,4,256]{2,1,0:T(4,128)S(1)} %reshape.20), channel_id=1, replica_groups=mesh['azim'=32,'rad'=4] {'azim','rad'}, dimensions={0} | all-to-all | bytes 1048576 | tf_op jit(solution)/shard_map/all_to_all | solution.py:676
  94.7 0.7 reduce_sum.9
Async XLA Ops:
  2.8 11.8 %copy-start = (f32[16,128,256]{2,1,0:T(8,128)S(1)}, f32[16,128,256]{2,1,0:T(8,128)}, u32[]{:S(2)}) copy-start(f32[16,128,256]{2,1,0:T(8,128)} %x_ref.5) | copy-start | bytes 6291460
  2.8 14.1 %copy-start.1 = (f32[4,29,16,128]{3,2,1,0:T(8,128)S(1)}, f32[4,29,16,128]{3,2,1,0:T(8,128)}, u32[]{:S(2)}) copy-start(f32[4,29,16,128]{3,2,1,0:T(8,128)} %param.7) | copy-start | bytes 2850820
  2.8 29.0 %collective-permute-start = (f32[5,128,256]{2,1,0:T(8,128)}, f32[5,128,256]{2,1,0:T(8,128)S(1)}, u32[]{:S(2)}, u32[]{:S(2)}) collective-permute-start(f32[5,128,256]{2,1,0:T(8,128)} %ship.2), channel_id=1, source_target_pairs={{4,8},{12,16},{20,24},{28,32},{36,40},{44,48},{52,56},{60,64},{68,... | collective-permute-start | bytes 1966088 | tf_op jit(solution)/shard_map/ppermute | solution.py:641
  14.5 3.2 %copy-start.3 = (s32[1024]{0:T(1024)S(1)}, s32[1024]{0:T(1024)}, u32[]{:S(2)}) copy-start(s32[1024]{0:T(1024)} %rows_ref.1) | copy-start | bytes 12292
  14.5 17.3 %collective-permute-start.1 = (f32[5,128,256]{2,1,0:T(8,128)}, f32[5,128,256]{2,1,0:T(8,128)S(1)}, u32[]{:S(2)}, u32[]{:S(2)}) collective-permute-start(f32[5,128,256]{2,1,0:T(8,128)} %ship.3), channel_id=1, source_target_pairs={{0,4},{8,12},{16,20},{24,28},{32,36},{40,44},{48,52},{56,60},{64,6... | collective-permute-start | bytes 1966088 | tf_op jit(solution)/shard_map/ppermute | solution.py:641
  17.7 2.2 %copy-start.2 = (bf16[4096,512]{1,0:T(8,128)(2,1)S(1)}, bf16[4096,512]{1,0:T(8,128)(2,1)}, u32[]{:S(2)}) copy-start(bf16[4096,512]{1,0:T(8,128)(2,1)} %table_ref.1) | copy-start | bytes 12582916
  24.5 3.7 %copy-start.4 = (s32[1024]{0:T(1024)S(1)}, s32[1024]{0:T(1024)}, u32[]{:S(2)}) copy-start(s32[1024]{0:T(1024)} %param.8) | copy-start | bytes 12292
  33.1 5.5 %collective-permute-start.2 = (f32[384,128]{1,0:T(8,128)S(1)}, f32[384,128]{1,0:T(8,128)S(1)}, u32[]{:S(2)}, u32[]{:S(2)}) collective-permute-start(f32[384,128]{1,0:T(8,128)S(1)} %get-tuple-element.59), channel_id=1, source_target_pairs={{0,1},{2,3},{1,0},{3,2},{4,5},{6,7},{5,4},{7,6},{8,9},{10,11},{9,8... | collective-permute-start | bytes 589832 | tf_op jit(solution)/shard_map/ppermute | solution.py:641
  34.1 7.0 %collective-permute-start.3 = (f32[384,128]{1,0:T(8,128)S(1)}, f32[384,128]{1,0:T(8,128)S(1)}, u32[]{:S(2)}, u32[]{:S(2)}) collective-permute-start(f32[384,128]{1,0:T(8,128)S(1)} %get-tuple-element.60), channel_id=1, source_target_pairs={{1,2},{2,1},{5,6},{6,5},{9,10},{10,9},{13,14},{14,13},{17,18},{18,... | collective-permute-start | bytes 589832 | tf_op jit(solution)/shard_map/ppermute | solution.py:641
  45.1 15.9 %collective-permute-start.4 = (f32[1024,128]{1,0:T(8,128)S(1)}, f32[1024,128]{1,0:T(8,128)S(1)}, u32[]{:S(2)}, u32[]{:S(2)}) collective-permute-start(f32[1024,128]{1,0:T(8,128)S(1)} %get-tuple-element.64), channel_id=1, source_target_pairs={{4,8},{12,16},{20,24},{28,32},{36,40},{44,48},{52,56},{60,64},{68,... | collective-permute-start | bytes 1572872 | tf_op jit(solution)/shard_map/ppermute | solution.py:641
  47.9 13.2 %collective-permute-start.5 = (f32[1024,128]{1,0:T(8,128)S(1)}, f32[1024,128]{1,0:T(8,128)S(1)}, u32[]{:S(2)}, u32[]{:S(2)}) collective-permute-start(f32[1024,128]{1,0:T(8,128)S(1)} %get-tuple-element.65), channel_id=1, source_target_pairs={{0,4},{8,12},{16,20},{24,28},{32,36},{40,44},{48,52},{56,60},{64,6... | collective-permute-start | bytes 1572872 | tf_op jit(solution)/shard_map/ppermute | solution.py:641
  61.8 4.7 %collective-permute-start.6 = (f32[256,128]{1,0:T(8,128)S(1)}, f32[256,128]{1,0:T(8,128)S(1)}, u32[]{:S(2)}, u32[]{:S(2)}) collective-permute-start(f32[256,128]{1,0:T(8,128)S(1)} %get-tuple-element.74), channel_id=1, source_target_pairs={{0,1},{2,3},{1,0},{3,2},{4,5},{6,7},{5,4},{7,6},{8,9},{10,11},{9,8... | collective-permute-start | bytes 393224 | tf_op jit(solution)/shard_map/ppermute | solution.py:641
  61.9 6.3 %collective-permute-start.7 = (f32[256,128]{1,0:T(8,128)S(1)}, f32[256,128]{1,0:T(8,128)S(1)}, u32[]{:S(2)}, u32[]{:S(2)}) collective-permute-start(f32[256,128]{1,0:T(8,128)S(1)} %get-tuple-element.75), channel_id=1, source_target_pairs={{1,2},{2,1},{5,6},{6,5},{9,10},{10,9},{13,14},{14,13},{17,18},{18,... | collective-permute-start | bytes 393224 | tf_op jit(solution)/shard_map/ppermute | solution.py:641

commit v9 on v8

--- a/solution.py
+++ b/solution.py
@@ -29,6 +29,9 @@
 
 def cost(rows):
     return pl.CostEstimate(flops=2 * 29 * rows * 128 * 256, bytes_accessed=rows << 18, transcendentals=0)
+
+
+SMALL = pl.CostEstimate(flops=1, bytes_accessed=1, transcendentals=0)
 
 
 def arrays(*shapes):
@@ -215,7 +218,7 @@
         out_specs=whole(2),
         out_shape=arrays((12 * ROWS, 128), (2 * ROWS, 128)),
         compiler_params=params(),
-        cost_estimate=cost(12),
+        cost_estimate=SMALL,
         name="inner_first",
     )(low, mid, high, coef)
 
@@ -546,10 +549,13 @@
             slot = k * 32 + t
             picked_ref[pl.ds(slot, 1)] = wide_ref[pl.ds(rows_ref[slot], 1)]
 
-    @pl.loop(0, 4)
-    def _(k):
-        at = pl.ds(pl.multiple_of(k * 256, 256), 256)
-        out_ref[at] = picked_ref[at].astype(BF16)
+    mode = lax.broadcasted_iota(jnp.int32, (512, 512), 0)
+    place_of = (mode // 4 % 2) * 256 + mode // 8 * 4 + mode % 4
+    order = jnp.where(place_of == lanes((512, 512)), 1.0, 0.0).astype(BF16)
+    for k in range(4):
+        at = slice(256 * k, 256 * k + 256)
+        picked = picked_ref[at].astype(BF16)
+        out_ref[at] = jnp.dot(picked, order, preferred_element_type=F32).astype(BF16)
 
 
 def call_gather(rows, table):
@@ -590,27 +596,55 @@
     )(count, cells, weights)
 
 
-def leave(low_ref, mid_ref, high_ref, w_high_ref, w_low_ref, out_ref, markov_ref, turned_ref, sems):
-    copies = []
-    rows = []
-    for k, ((first, stop), ref) in enumerate(zip(PARTS, (low_ref, mid_ref, high_ref))):
-        for row in range(first, stop):
-            rows.append(ref.at[(row - first) * ROWS : (row - first + 1) * ROWS])
-            turned_ref[row] = rows[-1][...].T
-        at = pl.ds(first, stop - first)
-        copies.append(pltpu.make_async_copy(turned_ref.at[at], out_ref.at[at], sems.at[k]))
-        copies[-1].start()
-    sums = jnp.zeros((256, 512), F32)
+def loads(rows, w_high_ref, w_low_ref, core):
+    half = pl.ds(pl.multiple_of(core * 256, 256), 256)
+    sums = jnp.zeros((256, 256), F32)
     for k in range(8):
         u = jnp.concatenate([rows[2 * k][...], rows[2 * k + 1][...]], axis=1)
         u_high = u.astype(BF16)
         u_low = (u - u_high.astype(F32)).astype(BF16)
-        w_high = w_high_ref[256 * k : 256 * k + 256]
-        w_low = w_low_ref[256 * k : 256 * k + 256]
+        w_high = w_high_ref[256 * k : 256 * k + 256, half]
+        w_low = w_low_ref[256 * k : 256 * k + 256, half]
         sums = sums + jnp.dot(u_high, w_high, preferred_element_type=F32)
         sums = sums + jnp.dot(u_low, w_high, preferred_element_type=F32)
         sums = sums + jnp.dot(u_high, w_low, preferred_element_type=F32)
-    markov_ref[...] = sums.T
+    return sums.T
+
+
+def rows_of(refs):
+    rows = []
+    for (first, stop), ref in zip(PARTS, refs):
+        rows += [ref.at[k * ROWS : (k + 1) * ROWS] for k in range(stop - first)]
+    return rows
+
+
+def other_loads(low_ref, mid_ref, high_ref, w_high_ref, w_low_ref, out_ref):
+    core = 1 - lax.axis_index("rad") % 2
+    out_ref[...] = loads(rows_of((low_ref, mid_ref, high_ref)), w_high_ref, w_low_ref, core)
+
+
+def call_other_loads(low, mid, high, w_high, w_low):
+    return pl.pallas_call(
+        other_loads,
+        in_specs=whole(5),
+        out_specs=whole(1)[0],
+        out_shape=arrays((256, 256))[0],
+        compiler_params=params(),
+        cost_estimate=pl.CostEstimate(flops=1 << 29, bytes_accessed=1 << 20, transcendentals=0),
+        name="other_loads",
+    )(low, mid, high, w_high, w_low)
+
+
+def leave(low_ref, mid_ref, high_ref, w_high_ref, w_low_ref, out_ref, loads_ref, turned_ref, sems):
+    rows = rows_of((low_ref, mid_ref, high_ref))
+    copies = []
+    for k, (first, stop) in enumerate(PARTS):
+        for row in range(first, stop):
+            turned_ref[row] = rows[row][...].T
+        at = pl.ds(first, stop - first)
+        copies.append(pltpu.make_async_copy(turned_ref.at[at], out_ref.at[at], sems.at[k]))
+        copies[-1].start()
+    loads_ref[...] = loads(rows, w_high_ref, w_low_ref, lax.axis_index("rad") % 2)
     for copy in copies:
         copy.wait()
 
@@ -620,10 +654,10 @@
         leave,
         in_specs=whole(5),
         out_specs=[pl.BlockSpec(memory_space=pltpu.HBM)] + whole(1),
-        out_shape=arrays((16, 128, 256), (512, 256)),
+        out_shape=arrays((16, 128, 256), (256, 256)),
         scratch_shapes=[pltpu.VMEM((16, 128, 256), F32), pltpu.SemaphoreType.DMA((3,))],
         compiler_params=params(),
-        cost_estimate=pl.CostEstimate(flops=2 << 30, bytes_accessed=8 << 20, transcendentals=0),
+        cost_estimate=pl.CostEstimate(flops=1 << 30, bytes_accessed=4 << 20, transcendentals=0),
         name="leave",
     )(low, mid, high, w_high, w_low)
 
@@ -671,9 +705,11 @@
             mid = new_mid
         else:
             low, mid, high = call_second(((0, 16),), PARTS, ys, *mends, coef, (low, mid, high))
+    others = swap(call_other_loads(low, mid, high, w_high, w_low), "rad", 0)
     out, term = call_leave(low, mid, high, w_high, w_low)
-    count = n_azim * n_rad
-    parts = lax.all_to_all(term.reshape(count, -1, term.shape[1]), ("azim", "rad"), 0, 0)
+    groups = [[k for k in range(n_azim * n_rad) if k % 2 == core] for core in range(2)]
+    term = (term + others).reshape(len(groups[0]), -1, term.shape[1])
+    parts = lax.all_to_all(term, ("azim", "rad"), 0, 0, axis_index_groups=groups)
     return out, jnp.sum(parts, axis=0)
 
 

time: 95.6 us -> 92.9 us (0.972)
  blocking collectives: 17.7 us -> 15.3 us
  local copies, waits for them, and re-layouts: 2.36 us -> 0.11 us
  starting transfers between devices: 18.4 us -> 20.1 us
    all_to_all x1, blocking collectives: 17.7 us -> 15.3 us  [body(): lax.all_to_all(term, ('azim', 'rad'), 0, 0, axis_index_groups=groups)]
    unnamed x10, local copies, waits for them, and re-layouts: 2.21 us -> 0.03 us
    ppermute x8 -> x9, starting transfers between devices: 18.4 us -> 20.1 us  [swap(): return lax.ppermute(block, axis, swaps(count, odd, axis == 'azim'))]
    pallas_call x0 -> x1, Pallas kernels: none -> 1.06 us  [call_other_loads(): pl.pallas_call(other_loads, in_specs=whole(5), out_specs=whole(1)[0], out...]
    ppermute x8 -> x9, waiting for transfers between devices: 11.6 us -> 10.7 us  [swap(): return lax.ppermute(block, axis, swaps(count, odd, axis == 'azim'))]
  transfers between devices with their start and end apart: 8 -> 9, of which waited for: 3 -> 3; matrix products, arithmetic and copies ran while one was open for 0% -> 0% of each run, Pallas kernels for 28% -> 31%
where the time goes in v9:
time: 92.9 us; the launch traced here: 92.4 us
  Pallas kernels  43.8 us (47%)
  starting transfers between devices  20.1 us (22%)
  blocking collectives  15.3 us (16%)
  waiting for transfers between devices  10.7 us (12%)
  between operations  1.6 us (2%)
    ppermute x9, starting transfers between devices, swap(): return lax.ppermute(block, axis, swaps(count, odd, axis == 'azim'))  20.1 us
    all_to_all x1, blocking collectives, body(): lax.all_to_all(term, ('azim', 'rad'), 0, 0, axis_index_groups=groups)  15.3 us
    ppermute x9, waiting for transfers between devices, swap(): return lax.ppermute(block, axis, swaps(count, odd, axis == 'azim'))  10.7 us
    pallas_call x3, Pallas kernels, call_second(): pl.pallas_call(functools.partial(second, ranges, parts, len(ys), sides),...  9.3 us
    pallas_call x2, Pallas kernels, call_inner_first(): pl.pallas_call(inner_first, in_specs=whole(4), out_specs=whole(2), out_sh...  7.03 us
    pallas_call x1, Pallas kernels, call_gather(): pl.pallas_call(gather, in_specs=[pl.BlockSpec(memory_space=pltpu.SMEM)] +...  5.3 us
    pallas_call x2, Pallas kernels, call_ship(): pl.pallas_call(functools.partial(ship, odd), in_specs=[hbm] * 2, out_spec...  4.24 us
    pallas_call x2, Pallas kernels, call_outer_first(): pl.pallas_call(outer_first, in_specs=whole(7), out_specs=whole(2), out_sh...  4.08 us
  transfers between devices with their start and end apart: 9, of which 3 were waited for; matrix products, arithmetic and copies ran while one was open for 0% of the time, Pallas kernels for 31%

profile of v9, /device:TPU:1, one launch (start us, length us, event | category | flops | bytes accessed | tf_op | source)
XLA Modules:
  0.0 92.4 jit_solution(15581253088005887037)
XLA Ops:
  0.6 2.1 %ship.2 = f32[5,128,256]{2,1,0:T(8,128)} custom-call(f32[16,128,256]{2,1,0:T(8,128)} %x_ref.5, f32[116,16,128]{2,1,0:T(8,128)} %bitcast.3), custom_call_target="tpu_custom_call" | custom-call | tf_op jit(solution)/shard_map/ship/pallas_call | solution.py:160
  2.8 0.0 copy-start
  2.8 0.0 copy-start.1
  2.8 9.6 %collective-permute-start = (f32[5,128,256]{2,1,0:T(8,128)}, f32[5,128,256]{2,1,0:T(8,128)S(1)}, u32[]{:S(2)}, u32[]{:S(2)}) collective-permute-start(f32[5,128,256]{2,1,0:T(8,128)} %ship.2), channel_id=1, source_target_pairs={{4,8},{12,16},{20,24},{28,32},{36,40},{44,48},{52,56},{60,64},{68,... | collective-permute-start | bytes 1966088 | tf_op jit(solution)/shard_map/ppermute | solution.py:675
  12.4 2.1 %ship.3 = f32[5,128,256]{2,1,0:T(8,128)} custom-call(f32[16,128,256]{2,1,0:T(8,128)} %x_ref.5, f32[116,16,128]{2,1,0:T(8,128)} %bitcast.4), custom_call_target="tpu_custom_call" | custom-call | tf_op jit(solution)/shard_map/ship/pallas_call | solution.py:160
  14.5 0.1 collective-permute-start.1
  14.6 0.0 copy-done
  14.6 0.0 copy-start.2
  14.6 1.6 %enter.1 = (f32[1024,128]{1,0:T(8,128)S(1)}, f32[2048,128]{1,0:T(8,128)S(1)}, f32[1024,128]{1,0:T(8,128)S(1)}) custom-call(f32[16,128,256]{2,1,0:T(8,128)S(1)} %copy-done), custom_call_target="tpu_custom_call" | custom-call | tf_op jit(solution)/shard_map/enter/pallas_call | solution.py:180
  16.2 0.0 copy-start.3
  16.2 0.0 copy-done.1
  16.2 0.8 coef_edges.1
  17.0 3.5 %inner_first.2 = (f32[3072,128]{1,0:T(8,128)S(1)}, f32[512,128]{1,0:T(8,128)S(1)}) custom-call(f32[1024,128]{1,0:T(8,128)S(1)} %get-tuple-element.44.low_ref.refs_6_, f32[2048,128]{1,0:T(8,128)S(1)} %get-tuple-element.45.mid_ref.refs_4_, f32[1024,128]{1,0:T(8,128)S(1)} %get-tuple-element.46.high_ref.refs_7_, ...), custom_call_target="tpu_custom_call" | custom-call | flops 1 | bytes 1 | tf_op jit(solution)/shard_map/inner_first/pallas_call | solution.py:215
  21.2 0.0 copy-done.2
  21.2 0.0 copy-done.3
  21.2 0.0 copy-start.4
  21.2 5.3 %gather.1.weights_ref = bf16[1024,512]{1,0:T(8,128)(2,1)S(1)} custom-call(s32[1024]{0:T(1024)S(1)} %copy-done.3, bf16[4096,512]{1,0:T(8,128)(2,1)S(1)} %copy-done.2), custom_call_target="tpu_custom_call" | custom-call | tf_op jit(solution)/shard_map/gather/pallas_call | solution.py:562
  26.5 0.0 copy-done.4
  26.5 3.6 %spread.1 = (bf16[2048,512]{1,0:T(8,128)(2,1)S(1)}, bf16[2048,512]{1,0:T(8,128)(2,1)S(1)}) custom-call(s32[1]{0:T(128)S(6)} %copy.8.count_ref, s32[1,1024]{1,0:T(1,128)S(1)} %bitcast.6, bf16[1024,512]{1,0:T(8,128)(2,1)S(1)} %gather.1.weights_ref), custom_call_target="tpu_custom_call" | custom-call | flops 2147483648 | bytes 6291456 | tf_op jit(solution)/shard_map/spread/pallas_call | solution.py:586
  30.1 0.0 collective-permute-done.odd_ref
  30.1 0.0 collective-permute-done.1.even_ref
  30.1 1.3 %halo_edges.2 = (f32[1024,128]{1,0:T(8,128)S(1)}, f32[1024,128]{1,0:T(8,128)S(1)}, f32[640,128]{1,0:T(8,128)S(1)}, f32[256,128]{1,0:T(8,128)S(1)}, f32[256,128]{...) custom-call(f32[5,128,256]{2,1,0:T(8,128)S(1)} %collective-permute-done.odd_ref, ...), custom_call_target="tpu_custom_call" | custom-call | tf_op jit(solution)/shard_map/halo_edges/pallas_call | solution.py:315
  31.4 1.8 %collective-permute-start.2 = (f32[384,128]{1,0:T(8,128)S(1)}, f32[384,128]{1,0:T(8,128)S(1)}, u32[]{:S(2)}, u32[]{:S(2)}) collective-permute-start(f32[384,128]{1,0:T(8,128)S(1)} %get-tuple-element.59), channel_id=1, source_target_pairs={{0,1},{2,3},{1,0},{3,2},{4,5},{6,7},{5,4},{7,6},{8,9},{10,11},{9,8... | collective-permute-start | bytes 589832 | tf_op jit(solution)/shard_map/ppermute | solution.py:675
  33.3 2.3 %collective-permute-start.3 = (f32[384,128]{1,0:T(8,128)S(1)}, f32[384,128]{1,0:T(8,128)S(1)}, u32[]{:S(2)}, u32[]{:S(2)}) collective-permute-start(f32[384,128]{1,0:T(8,128)S(1)} %get-tuple-element.60), channel_id=1, source_target_pairs={{1,2},{2,1},{5,6},{6,5},{9,10},{10,9},{13,14},{14,13},{17,18},{18,... | collective-permute-start | bytes 589832 | tf_op jit(solution)/shard_map/ppermute | solution.py:675
  35.6 2.0 %outer_first.2 = (f32[1024,128]{1,0:T(8,128)S(1)}, f32[1024,128]{1,0:T(8,128)S(1)}) custom-call(f32[1024,128]{1,0:T(8,128)S(1)} %get-tuple-element.52.top_ref, f32[1024,128]{1,0:T(8,128)S(1)} %get-tuple-element.44.low_ref.refs_6_, f32[1024,128]{1,0:T(8,128)S(1)} %get-tuple-element.46.high_ref.refs_7_, f32[1024,128]{1,0:T(8,128)S(1)} %get-tuple-element.53.bot_ref, ...), custom_call_target="tpu_custom_call" | custom-call | flops 15204352 | bytes 2097152 | tf_op jit(solution)/shard_map/outer_first/pallas_call | solution.py:357
  37.6 0.0 collective-permute-done.2.even_ref
  37.6 2.6 %collective-permute-done.3.odd_ref = f32[384,128]{1,0:T(8,128)S(1)} collective-permute-done((f32[384,128]{1,0:T(8,128)S(1)}, f32[384,128]{1,0:T(8,128)S(1)}, u32[]{:S(2)}, u32[]{:S(2)}) %collective-permute-start.3) | collective-permute-done | bytes 196640 | tf_op jit(solution)/shard_map/ppermute | solution.py:675
  40.3 0.2 strip_lines.1.line_ref
  40.5 1.3 %strips.2 = (f32[4,64,128]{2,1,0:T(8,128)S(1)}, f32[4,64,128]{2,1,0:T(8,128)S(1)}) custom-call(f32[384,128]{1,0:T(8,128)S(1)} %collective-permute-done.2.even_ref, f32[384,128]{1,0:T(8,128)S(1)} %collective-permute-done.3.odd_ref, f32[640,128]{1,0:T(8,128)S(1)} %get-tuple-element.61.own_ref, f32[4,48,128]{2,1,0:T(8,128)S(1)} %strip_lines.1.line_ref), custom_call_target="tpu_custom_call" | custom-call | tf_op jit(solution)/shard_map/strips/pallas_call | solution.py:473
  41.8 2.5 %second.3 = (f32[1024,128]{1,0:T(8,128)S(1)}, f32[1024,128]{1,0:T(8,128)S(1)}, f32[1024,128]{1,0:T(8,128)S(1)}, f32[1024,128]{1,0:T(8,128)S(1)}) custom-call(f32[1024,128]{1,0:T(8,128)S(1)} %get-tuple-element.56.refs_0_, f32[3072,128]{1,0:T(8,128)S(1)} %get-tuple-element.57.refs_1_.refs_0_, f32[1024,128]{1,0:T(8,128)S(1)} %get-tuple-element.58.refs_2_, ...), custom_call_target="tpu_custom_call" | custom-call | flops 15204352 | bytes 2097152 | tf_op jit(solution)/shard_map/second/pallas_call | solution.py:528
  44.3 3.6 %collective-permute-start.4 = (f32[1024,128]{1,0:T(8,128)S(1)}, f32[1024,128]{1,0:T(8,128)S(1)}, u32[]{:S(2)}, u32[]{:S(2)}) collective-permute-start(f32[1024,128]{1,0:T(8,128)S(1)} %get-tuple-element.64), channel_id=1, source_target_pairs={{4,8},{12,16},{20,24},{28,32},{36,40},{44,48},{52,56},{60,64},{68,... | collective-permute-start | bytes 1572872 | tf_op jit(solution)/shard_map/ppermute | solution.py:675
  47.9 0.0 collective-permute-start.5
  47.9 2.3 %second.4.mid_ref.refs_7_ = f32[2048,128]{1,0:T(8,128)S(1)} custom-call(f32[3072,128]{1,0:T(8,128)S(1)} %get-tuple-element.57.refs_1_.refs_0_, f32[4,64,128]{2,1,0:T(8,128)S(1)} %get-tuple-element.62.refs_3_.refs_1_, f32[4,64,128]{2,1,0:T(8,128)S(1)} %get-tuple-element.63.refs_4_.refs_2_, f32[4,29,16,128]{3,2,1,0:T(8,128)S(1)} %get-tuple-element.47.coef_ref.refs_5_.refs_3_, ...), custom_call_target="tpu_custom_call" | custom-call | flops 15204352 | bytes 2097152 | tf_op jit(solution)/shard_map/second/pallas_call | solution.py:528
  50.2 3.5 %inner_first.3 = (f32[3072,128]{1,0:T(8,128)S(1)}, f32[512,128]{1,0:T(8,128)S(1)}) custom-call(f32[1024,128]{1,0:T(8,128)S(1)} %get-tuple-element.66.low_ref.refs_6_, f32[2048,128]{1,0:T(8,128)S(1)} %second.4.mid_ref.refs_7_, f32[1024,128]{1,0:T(8,128)S(1)} %get-tuple-element.67.high_ref.refs_8_, ...), custom_call_target="tpu_custom_call" | custom-call | flops 1 | bytes 1 | tf_op jit(solution)/shard_map/inner_first/pallas_call | solution.py:215
  53.7 6.4 %collective-permute-done.4.odd_ref = f32[1024,128]{1,0:T(8,128)S(1)} collective-permute-done((f32[1024,128]{1,0:T(8,128)S(1)}, f32[1024,128]{1,0:T(8,128)S(1)}, u32[]{:S(2)}, u32[]{:S(2)}) %collective-permute-start.4) | collective-permute-done | bytes 524320 | tf_op jit(solution)/shard_map/ppermute | solution.py:675
  60.1 0.0 collective-permute-done.5.even_ref
  60.1 0.7 halo_edges.3
  60.8 0.1 collective-permute-start.6
  60.9 2.6 %collective-permute-start.7 = (f32[256,128]{1,0:T(8,128)S(1)}, f32[256,128]{1,0:T(8,128)S(1)}, u32[]{:S(2)}, u32[]{:S(2)}) collective-permute-start(f32[256,128]{1,0:T(8,128)S(1)} %get-tuple-element.75), channel_id=1, source_target_pairs={{1,2},{2,1},{5,6},{6,5},{9,10},{10,9},{13,14},{14,13},{17,18},{18,... | collective-permute-start | bytes 393224 | tf_op jit(solution)/shard_map/ppermute | solution.py:675
  63.5 2.0 %outer_first.3 = (f32[1024,128]{1,0:T(8,128)S(1)}, f32[1024,128]{1,0:T(8,128)S(1)}) custom-call(f32[1024,128]{1,0:T(8,128)S(1)} %get-tuple-element.69.top_ref, f32[1024,128]{1,0:T(8,128)S(1)} %get-tuple-element.66.low_ref.refs_6_, f32[1024,128]{1,0:T(8,128)S(1)} %get-tuple-element.67.high_ref.refs_8_, f32[1024,128]{1,0:T(8,128)S(1)} %get-tuple-element.70.bot_ref, ...), custom_call_target="tpu_custom_call" | custom-call | flops 15204352 | bytes 2097152 | tf_op jit(solution)/shard_map/outer_first/pallas_call | solution.py:357
  65.5 0.0 collective-permute-done.6.even_ref
  65.5 1.7 %collective-permute-done.7.odd_ref = f32[256,128]{1,0:T(8,128)S(1)} collective-permute-done((f32[256,128]{1,0:T(8,128)S(1)}, f32[256,128]{1,0:T(8,128)S(1)}, u32[]{:S(2)}, u32[]{:S(2)}) %collective-permute-start.7) | collective-permute-done | bytes 131104 | tf_op jit(solution)/shard_map/ppermute | solution.py:675
  67.2 1.3 %strips.3 = (f32[4,64,128]{2,1,0:T(8,128)S(1)}, f32[4,64,128]{2,1,0:T(8,128)S(1)}) custom-call(f32[256,128]{1,0:T(8,128)S(1)} %collective-permute-done.6.even_ref, f32[256,128]{1,0:T(8,128)S(1)} %collective-permute-done.7.odd_ref, f32[512,128]{1,0:T(8,128)S(1)} %get-tuple-element.76.own_ref, f32[4,48,128]{2,1,0:T(8,128)S(1)} %strip_lines.1.line_ref), custom_call_target="tpu_custom_call" | custom-call | tf_op jit(solution)/shard_map/strips/pallas_call | solution.py:473
  68.5 4.5 %second.5 = (f32[1024,128]{1,0:T(8,128)S(1)}, f32[2048,128]{1,0:T(8,128)S(1)}, f32[1024,128]{1,0:T(8,128)S(1)}) custom-call(f32[1024,128]{1,0:T(8,128)S(1)} %get-tuple-element.71.refs_0_, f32[3072,128]{1,0:T(8,128)S(1)} %get-tuple-element.72.refs_1_, f32[1024,128]{1,0:T(8,128)S(1)} %get-tuple-element.73.refs_2_, ...), custom_call_target="tpu_custom_call" | custom-call | flops 15204352 | bytes 2097152 | tf_op jit(solution)/shard_map/second/pallas_call | solution.py:528
  73.0 1.1 %other_loads.1 = f32[256,256]{1,0:T(8,128)S(1)} custom-call(f32[1024,128]{1,0:T(8,128)S(1)} %get-tuple-element.79.low_ref, f32[2048,128]{1,0:T(8,128)S(1)} %get-tuple-element.80.mid_ref, f32[1024,128]{1,0:T(8,128)S(1)} %get-tuple-element.81.high_ref, bf16[2048,512]{1,0:T(8,128)(2,1)S(1)} %get-tuple-element.82.w_high_ref, ...), custom_call_target="tpu_custom_call" | custom-call | flops 536870912 | bytes 1048576 | tf_op jit(solution)/shard_map/other_loads/pallas_call | solution.py:627
  74.1 0.1 collective-permute-start.8
  74.2 2.1 %leave.1 = (f32[16,128,256]{2,1,0:T(8,128)}, f32[256,256]{1,0:T(8,128)S(1)}) custom-call(f32[1024,128]{1,0:T(8,128)S(1)} %get-tuple-element.79.low_ref, f32[2048,128]{1,0:T(8,128)S(1)} %get-tuple-element.80.mid_ref, f32[1024,128]{1,0:T(8,128)S(1)} %get-tuple-element.81.high_ref, bf16[2048,512]{1,0:T(8,128)(2,1)S(1)} %get-tuple-element.82.w_high_ref, ...), custom_call_target="tpu_custom_call" | custom-call | flops 1073741824 | bytes 4194304 | tf_op jit(solution)/shard_map/leave/pallas_call | solution.py:653
  76.3 0.0 collective-permute-done.8
  76.3 0.1 reshape.20
  76.4 15.3 %all_to_all.5 = f32[64,4,256]{2,1,0:T(4,128)S(1)} all-to-all(f32[64,4,256]{2,1,0:T(4,128)S(1)} %reshape.20), channel_id=1, replica_groups={{0,2,4,6,8,10,12,14,16,18,20,22,24,26,28,30,32,34,36,38,40,42,44,46,48,..., dimensions={0} | all-to-all | bytes 524288 | tf_op jit(solution)/shard_map/all_to_all | solution.py:712
  91.7 0.7 reduce_sum.9
  (1 shorter events, 0.0 us)
Async XLA Ops:
  2.8 11.8 %copy-start = (f32[16,128,256]{2,1,0:T(8,128)S(1)}, f32[16,128,256]{2,1,0:T(8,128)}, u32[]{:S(2)}) copy-start(f32[16,128,256]{2,1,0:T(8,128)} %x_ref.5) | copy-start | bytes 6291460
  2.8 13.4 %copy-start.1 = (f32[4,29,16,128]{3,2,1,0:T(8,128)S(1)}, f32[4,29,16,128]{3,2,1,0:T(8,128)}, u32[]{:S(2)}) copy-start(f32[4,29,16,128]{3,2,1,0:T(8,128)} %param.7) | copy-start | bytes 2850820
  2.8 27.3 %collective-permute-start = (f32[5,128,256]{2,1,0:T(8,128)}, f32[5,128,256]{2,1,0:T(8,128)S(1)}, u32[]{:S(2)}, u32[]{:S(2)}) collective-permute-start(f32[5,128,256]{2,1,0:T(8,128)} %ship.2), channel_id=1, source_target_pairs={{4,8},{12,16},{20,24},{28,32},{36,40},{44,48},{52,56},{60,64},{68,... | collective-permute-start | bytes 1966088 | tf_op jit(solution)/shard_map/ppermute | solution.py:675
  14.5 15.6 %collective-permute-start.1 = (f32[5,128,256]{2,1,0:T(8,128)}, f32[5,128,256]{2,1,0:T(8,128)S(1)}, u32[]{:S(2)}, u32[]{:S(2)}) collective-permute-start(f32[5,128,256]{2,1,0:T(8,128)} %ship.3), channel_id=1, source_target_pairs={{0,4},{8,12},{16,20},{24,28},{32,36},{40,44},{48,52},{56,60},{64,6... | collective-permute-start | bytes 1966088 | tf_op jit(solution)/shard_map/ppermute | solution.py:675
  14.6 6.6 %copy-start.2 = (bf16[4096,512]{1,0:T(8,128)(2,1)S(1)}, bf16[4096,512]{1,0:T(8,128)(2,1)}, u32[]{:S(2)}) copy-start(bf16[4096,512]{1,0:T(8,128)(2,1)} %table_ref.1) | copy-start | bytes 12582916
  16.2 5.0 %copy-start.3 = (s32[1024]{0:T(1024)S(1)}, s32[1024]{0:T(1024)}, u32[]{:S(2)}) copy-start(s32[1024]{0:T(1024)} %rows_ref.1) | copy-start | bytes 12292
  21.2 5.3 %copy-start.4 = (s32[1024]{0:T(1024)S(1)}, s32[1024]{0:T(1024)}, u32[]{:S(2)}) copy-start(s32[1024]{0:T(1024)} %param.8) | copy-start | bytes 12292
  31.4 6.2 %collective-permute-start.2 = (f32[384,128]{1,0:T(8,128)S(1)}, f32[384,128]{1,0:T(8,128)S(1)}, u32[]{:S(2)}, u32[]{:S(2)}) collective-permute-start(f32[384,128]{1,0:T(8,128)S(1)} %get-tuple-element.59), channel_id=1, source_target_pairs={{0,1},{2,3},{1,0},{3,2},{4,5},{6,7},{5,4},{7,6},{8,9},{10,11},{9,8... | collective-permute-start | bytes 589832 | tf_op jit(solution)/shard_map/ppermute | solution.py:675
  33.3 7.0 %collective-permute-start.3 = (f32[384,128]{1,0:T(8,128)S(1)}, f32[384,128]{1,0:T(8,128)S(1)}, u32[]{:S(2)}, u32[]{:S(2)}) collective-permute-start(f32[384,128]{1,0:T(8,128)S(1)} %get-tuple-element.60), channel_id=1, source_target_pairs={{1,2},{2,1},{5,6},{6,5},{9,10},{10,9},{13,14},{14,13},{17,18},{18,... | collective-permute-start | bytes 589832 | tf_op jit(solution)/shard_map/ppermute | solution.py:675
  44.3 15.9 %collective-permute-start.4 = (f32[1024,128]{1,0:T(8,128)S(1)}, f32[1024,128]{1,0:T(8,128)S(1)}, u32[]{:S(2)}, u32[]{:S(2)}) collective-permute-start(f32[1024,128]{1,0:T(8,128)S(1)} %get-tuple-element.64), channel_id=1, source_target_pairs={{4,8},{12,16},{20,24},{28,32},{36,40},{44,48},{52,56},{60,64},{68,... | collective-permute-start | bytes 1572872 | tf_op jit(solution)/shard_map/ppermute | solution.py:675
  47.9 12.3 %collective-permute-start.5 = (f32[1024,128]{1,0:T(8,128)S(1)}, f32[1024,128]{1,0:T(8,128)S(1)}, u32[]{:S(2)}, u32[]{:S(2)}) collective-permute-start(f32[1024,128]{1,0:T(8,128)S(1)} %get-tuple-element.65), channel_id=1, source_target_pairs={{0,4},{8,12},{16,20},{24,28},{32,36},{40,44},{48,52},{56,60},{64,6... | collective-permute-start | bytes 1572872 | tf_op jit(solution)/shard_map/ppermute | solution.py:675
  60.8 4.7 %collective-permute-start.6 = (f32[256,128]{1,0:T(8,128)S(1)}, f32[256,128]{1,0:T(8,128)S(1)}, u32[]{:S(2)}, u32[]{:S(2)}) collective-permute-start(f32[256,128]{1,0:T(8,128)S(1)} %get-tuple-element.74), channel_id=1, source_target_pairs={{0,1},{2,3},{1,0},{3,2},{4,5},{6,7},{5,4},{7,6},{8,9},{10,11},{9,8... | collective-permute-start | bytes 393224 | tf_op jit(solution)/shard_map/ppermute | solution.py:675
  60.9 6.3 %collective-permute-start.7 = (f32[256,128]{1,0:T(8,128)S(1)}, f32[256,128]{1,0:T(8,128)S(1)}, u32[]{:S(2)}, u32[]{:S(2)}) collective-permute-start(f32[256,128]{1,0:T(8,128)S(1)} %get-tuple-element.75), channel_id=1, source_target_pairs={{1,2},{2,1},{5,6},{6,5},{9,10},{10,9},{13,14},{14,13},{17,18},{18,... | collective-permute-start | bytes 393224 | tf_op jit(solution)/shard_map/ppermute | solution.py:675
  74.1 2.2 %collective-permute-start.8 = (f32[256,256]{1,0:T(8,128)S(1)}, f32[256,256]{1,0:T(8,128)S(1)}, u32[]{:S(2)}, u32[]{:S(2)}) collective-permute-start(f32[256,256]{1,0:T(8,128)S(1)} %other_loads.1), channel_id=1, source_target_pairs={{0,1},{2,3},{1,0},{3,2},{4,5},{6,7},{5,4},{7,6},{8,9},{10,11},{9,8... | collective-permute-start | bytes 786440 | tf_op jit(solution)/shard_map/ppermute | solution.py:675

commit v10 on v9

--- a/solution.py
+++ b/solution.py
@@ -365,7 +365,7 @@
     )(top, low, high, bot, coef, ctop, cbot)
 
 
-def strip_lines(even_ref, odd_ref, own_ref, out_ref):
+def strip_lines(odd_ref, even_ref, own_ref, out_ref):
     entry = lanes((32, 128)) % 4
     even_is_right = lanes((32, 128)) * 0 + lax.axis_index("rad") % 2 == 0
     number = lax.broadcasted_iota(jnp.int32, (32, 128), 0)
@@ -402,10 +402,10 @@
         out_shape=arrays((4, 48, 128))[0],
         compiler_params=params(),
         name="strip_lines",
-    )(even, odd, own)
-
-
-def strips(even_ref, odd_ref, own_ref, line_ref, mend_y_ref, mend_u_ref, shift_ref):
+    )(odd, even, own)
+
+
+def strips(odd_ref, even_ref, own_ref, line_ref, mend_y_ref, mend_u_ref, shift_ref):
     entry = lanes((32, 128)) % 4
     even_is_right = lanes((32, 128)) * 0 + lax.axis_index("rad") % 2 == 0
     every = [(var, half) for var in range(4) for half in range(2)]
@@ -478,7 +478,7 @@
         scratch_shapes=[pltpu.VMEM((7, 4, 64, 128), F32)],
         compiler_params=params(),
         name="strips",
-    )(even, odd, own, lines)
+    )(odd, even, own, lines)
 
 
 def second(ranges, parts, n_y, sides, *refs):

time: 92.9 us -> 95.6 us (1.029)
  waiting for transfers between devices: 10.7 us -> 12.6 us
    ppermute x9, waiting for transfers between devices: 10.7 us -> 12.6 us  [swap(): return lax.ppermute(block, axis, swaps(count, odd, axis == 'azim'))]
  transfers between devices with their start and end apart: 9 -> 9, of which waited for: 3 -> 3; matrix products, arithmetic and copies ran while one was open for 0% -> 0% of each run, Pallas kernels for 31% -> 30%
where the time goes in v10:
time: 95.6 us; the launch traced here: 95 us
  Pallas kernels  43.8 us (46%)
  starting transfers between devices  20.4 us (21%)
  blocking collectives  15.9 us (17%)
  waiting for transfers between devices  12.6 us (13%)
  between operations  1.59 us (2%)
    ppermute x9, starting transfers between devices, swap(): return lax.ppermute(block, axis, swaps(count, odd, axis == 'azim'))  20.4 us
    all_to_all x1, blocking collectives, body(): lax.all_to_all(term, ('azim', 'rad'), 0, 0, axis_index_groups=groups)  15.9 us
    ppermute x9, waiting for transfers between devices, swap(): return lax.ppermute(block, axis, swaps(count, odd, axis == 'azim'))  12.6 us
    pallas_call x3, Pallas kernels, call_second(): pl.pallas_call(functools.partial(second, ranges, parts, len(ys), sides),...  9.3 us
    pallas_call x2, Pallas kernels, call_inner_first(): pl.pallas_call(inner_first, in_specs=whole(4), out_specs=whole(2), out_sh...  7.03 us
    pallas_call x1, Pallas kernels, call_gather(): pl.pallas_call(gather, in_specs=[pl.BlockSpec(memory_space=pltpu.SMEM)] +...  5.3 us
    pallas_call x2, Pallas kernels, call_ship(): pl.pallas_call(functools.partial(ship, odd), in_specs=[hbm] * 2, out_spec...  4.24 us
    pallas_call x2, Pallas kernels, call_outer_first(): pl.pallas_call(outer_first, in_specs=whole(7), out_specs=whole(2), out_sh...  4.08 us
  transfers between devices with their start and end apart: 9, of which 3 were waited for; matrix products, arithmetic and copies ran while one was open for 0% of the time, Pallas kernels for 30%

profile of v10, /device:TPU:1, one launch (start us, length us, event | category | flops | bytes accessed | tf_op | source)
XLA Modules:
  0.0 95.0 jit_solution(4445012180859420484)
XLA Ops:
  0.6 2.1 %ship.2 = f32[5,128,256]{2,1,0:T(8,128)} custom-call(f32[16,128,256]{2,1,0:T(8,128)} %x_ref.5, f32[116,16,128]{2,1,0:T(8,128)} %bitcast.3), custom_call_target="tpu_custom_call" | custom-call | tf_op jit(solution)/shard_map/ship/pallas_call | solution.py:160
  2.8 0.0 copy-start
  2.8 0.0 copy-start.1
  2.8 9.6 %collective-permute-start = (f32[5,128,256]{2,1,0:T(8,128)}, f32[5,128,256]{2,1,0:T(8,128)S(1)}, u32[]{:S(2)}, u32[]{:S(2)}) collective-permute-start(f32[5,128,256]{2,1,0:T(8,128)} %ship.2), channel_id=1, source_target_pairs={{4,8},{12,16},{20,24},{28,32},{36,40},{44,48},{52,56},{60,64},{68,... | collective-permute-start | bytes 1966088 | tf_op jit(solution)/shard_map/ppermute | solution.py:675
  12.4 2.1 %ship.3 = f32[5,128,256]{2,1,0:T(8,128)} custom-call(f32[16,128,256]{2,1,0:T(8,128)} %x_ref.5, f32[116,16,128]{2,1,0:T(8,128)} %bitcast.4), custom_call_target="tpu_custom_call" | custom-call | tf_op jit(solution)/shard_map/ship/pallas_call | solution.py:160
  14.5 0.1 collective-permute-start.1
  14.6 0.0 copy-done
  14.6 0.0 copy-start.2
  14.6 1.6 %enter.1 = (f32[1024,128]{1,0:T(8,128)S(1)}, f32[2048,128]{1,0:T(8,128)S(1)}, f32[1024,128]{1,0:T(8,128)S(1)}) custom-call(f32[16,128,256]{2,1,0:T(8,128)S(1)} %copy-done), custom_call_target="tpu_custom_call" | custom-call | tf_op jit(solution)/shard_map/enter/pallas_call | solution.py:180
  16.2 0.0 copy-start.3
  16.2 0.0 copy-done.1
  16.2 0.8 coef_edges.1
  17.0 3.5 %inner_first.2 = (f32[3072,128]{1,0:T(8,128)S(1)}, f32[512,128]{1,0:T(8,128)S(1)}) custom-call(f32[1024,128]{1,0:T(8,128)S(1)} %get-tuple-element.44.low_ref.refs_6_, f32[2048,128]{1,0:T(8,128)S(1)} %get-tuple-element.45.mid_ref.refs_4_, f32[1024,128]{1,0:T(8,128)S(1)} %get-tuple-element.46.high_ref.refs_7_, ...), custom_call_target="tpu_custom_call" | custom-call | flops 1 | bytes 1 | tf_op jit(solution)/shard_map/inner_first/pallas_call | solution.py:215
  21.2 0.0 copy-done.2
  21.2 0.0 copy-done.3
  21.2 0.0 copy-start.4
  21.2 5.3 %gather.1.weights_ref = bf16[1024,512]{1,0:T(8,128)(2,1)S(1)} custom-call(s32[1024]{0:T(1024)S(1)} %copy-done.3, bf16[4096,512]{1,0:T(8,128)(2,1)S(1)} %copy-done.2), custom_call_target="tpu_custom_call" | custom-call | tf_op jit(solution)/shard_map/gather/pallas_call | solution.py:562
  26.5 0.0 copy-done.4
  26.5 3.6 %spread.1 = (bf16[2048,512]{1,0:T(8,128)(2,1)S(1)}, bf16[2048,512]{1,0:T(8,128)(2,1)S(1)}) custom-call(s32[1]{0:T(128)S(6)} %copy.8.count_ref, s32[1,1024]{1,0:T(1,128)S(1)} %bitcast.6, bf16[1024,512]{1,0:T(8,128)(2,1)S(1)} %gather.1.weights_ref), custom_call_target="tpu_custom_call" | custom-call | flops 2147483648 | bytes 6291456 | tf_op jit(solution)/shard_map/spread/pallas_call | solution.py:586
  30.1 0.0 collective-permute-done.odd_ref
  30.1 0.0 collective-permute-done.1.even_ref
  30.1 1.3 %halo_edges.2 = (f32[1024,128]{1,0:T(8,128)S(1)}, f32[1024,128]{1,0:T(8,128)S(1)}, f32[640,128]{1,0:T(8,128)S(1)}, f32[256,128]{1,0:T(8,128)S(1)}, f32[256,128]{...) custom-call(f32[5,128,256]{2,1,0:T(8,128)S(1)} %collective-permute-done.odd_ref, ...), custom_call_target="tpu_custom_call" | custom-call | tf_op jit(solution)/shard_map/halo_edges/pallas_call | solution.py:315
  31.4 3.9 %collective-permute-start.2 = (f32[384,128]{1,0:T(8,128)S(1)}, f32[384,128]{1,0:T(8,128)S(1)}, u32[]{:S(2)}, u32[]{:S(2)}) collective-permute-start(f32[384,128]{1,0:T(8,128)S(1)} %get-tuple-element.59), channel_id=1, source_target_pairs={{1,2},{2,1},{5,6},{6,5},{9,10},{10,9},{13,14},{14,13},{17,18},{18,... | collective-permute-start | bytes 589832 | tf_op jit(solution)/shard_map/ppermute | solution.py:675
  35.3 0.3 collective-permute-start.3
  35.6 2.0 %outer_first.2 = (f32[1024,128]{1,0:T(8,128)S(1)}, f32[1024,128]{1,0:T(8,128)S(1)}) custom-call(f32[1024,128]{1,0:T(8,128)S(1)} %get-tuple-element.52.top_ref, f32[1024,128]{1,0:T(8,128)S(1)} %get-tuple-element.44.low_ref.refs_6_, f32[1024,128]{1,0:T(8,128)S(1)} %get-tuple-element.46.high_ref.refs_7_, f32[1024,128]{1,0:T(8,128)S(1)} %get-tuple-element.53.bot_ref, ...), custom_call_target="tpu_custom_call" | custom-call | flops 15204352 | bytes 2097152 | tf_op jit(solution)/shard_map/outer_first/pallas_call | solution.py:357
  37.6 1.0 %collective-permute-done.2.odd_ref = f32[384,128]{1,0:T(8,128)S(1)} collective-permute-done((f32[384,128]{1,0:T(8,128)S(1)}, f32[384,128]{1,0:T(8,128)S(1)}, u32[]{:S(2)}, u32[]{:S(2)}) %collective-permute-start.2) | collective-permute-done | bytes 196640 | tf_op jit(solution)/shard_map/ppermute | solution.py:675
  38.7 0.0 collective-permute-done.3.even_ref
  38.7 0.2 strip_lines.1.line_ref
  38.9 1.3 %strips.2 = (f32[4,64,128]{2,1,0:T(8,128)S(1)}, f32[4,64,128]{2,1,0:T(8,128)S(1)}) custom-call(f32[384,128]{1,0:T(8,128)S(1)} %collective-permute-done.2.odd_ref, f32[384,128]{1,0:T(8,128)S(1)} %collective-permute-done.3.even_ref, f32[640,128]{1,0:T(8,128)S(1)} %get-tuple-element.61.own_ref, f32[4,48,128]{2,1,0:T(8,128)S(1)} %strip_lines.1.line_ref), custom_call_target="tpu_custom_call" | custom-call | tf_op jit(solution)/shard_map/strips/pallas_call | solution.py:473
  40.2 2.5 %second.3 = (f32[1024,128]{1,0:T(8,128)S(1)}, f32[1024,128]{1,0:T(8,128)S(1)}, f32[1024,128]{1,0:T(8,128)S(1)}, f32[1024,128]{1,0:T(8,128)S(1)}) custom-call(f32[1024,128]{1,0:T(8,128)S(1)} %get-tuple-element.56.refs_0_, f32[3072,128]{1,0:T(8,128)S(1)} %get-tuple-element.57.refs_1_.refs_0_, f32[1024,128]{1,0:T(8,128)S(1)} %get-tuple-element.58.refs_2_, ...), custom_call_target="tpu_custom_call" | custom-call | flops 15204352 | bytes 2097152 | tf_op jit(solution)/shard_map/second/pallas_call | solution.py:528
  42.7 4.2 %collective-permute-start.4 = (f32[1024,128]{1,0:T(8,128)S(1)}, f32[1024,128]{1,0:T(8,128)S(1)}, u32[]{:S(2)}, u32[]{:S(2)}) collective-permute-start(f32[1024,128]{1,0:T(8,128)S(1)} %get-tuple-element.64), channel_id=1, source_target_pairs={{4,8},{12,16},{20,24},{28,32},{36,40},{44,48},{52,56},{60,64},{68,... | collective-permute-start | bytes 1572872 | tf_op jit(solution)/shard_map/ppermute | solution.py:675
  46.9 0.0 collective-permute-start.5
  46.9 2.3 %second.4.mid_ref.refs_7_ = f32[2048,128]{1,0:T(8,128)S(1)} custom-call(f32[3072,128]{1,0:T(8,128)S(1)} %get-tuple-element.57.refs_1_.refs_0_, f32[4,64,128]{2,1,0:T(8,128)S(1)} %get-tuple-element.62.refs_3_.refs_1_, f32[4,64,128]{2,1,0:T(8,128)S(1)} %get-tuple-element.63.refs_4_.refs_2_, f32[4,29,16,128]{3,2,1,0:T(8,128)S(1)} %get-tuple-element.47.coef_ref.refs_5_.refs_3_, ...), custom_call_target="tpu_custom_call" | custom-call | flops 15204352 | bytes 2097152 | tf_op jit(solution)/shard_map/second/pallas_call | solution.py:528
  49.2 3.5 %inner_first.3 = (f32[3072,128]{1,0:T(8,128)S(1)}, f32[512,128]{1,0:T(8,128)S(1)}) custom-call(f32[1024,128]{1,0:T(8,128)S(1)} %get-tuple-element.66.low_ref.refs_6_, f32[2048,128]{1,0:T(8,128)S(1)} %second.4.mid_ref.refs_7_, f32[1024,128]{1,0:T(8,128)S(1)} %get-tuple-element.67.high_ref.refs_8_, ...), custom_call_target="tpu_custom_call" | custom-call | flops 1 | bytes 1 | tf_op jit(solution)/shard_map/inner_first/pallas_call | solution.py:215
  52.7 9.6 %collective-permute-done.4.odd_ref = f32[1024,128]{1,0:T(8,128)S(1)} collective-permute-done((f32[1024,128]{1,0:T(8,128)S(1)}, f32[1024,128]{1,0:T(8,128)S(1)}, u32[]{:S(2)}, u32[]{:S(2)}) %collective-permute-start.4) | collective-permute-done | bytes 524320 | tf_op jit(solution)/shard_map/ppermute | solution.py:675
  62.3 0.0 collective-permute-done.5.even_ref
  62.3 0.7 halo_edges.3
  63.0 1.9 %collective-permute-start.6 = (f32[256,128]{1,0:T(8,128)S(1)}, f32[256,128]{1,0:T(8,128)S(1)}, u32[]{:S(2)}, u32[]{:S(2)}) collective-permute-start(f32[256,128]{1,0:T(8,128)S(1)} %get-tuple-element.74), channel_id=1, source_target_pairs={{1,2},{2,1},{5,6},{6,5},{9,10},{10,9},{13,14},{14,13},{17,18},{18,... | collective-permute-start | bytes 393224 | tf_op jit(solution)/shard_map/ppermute | solution.py:675
  64.9 0.3 collective-permute-start.7
  65.3 2.0 %outer_first.3 = (f32[1024,128]{1,0:T(8,128)S(1)}, f32[1024,128]{1,0:T(8,128)S(1)}) custom-call(f32[1024,128]{1,0:T(8,128)S(1)} %get-tuple-element.69.top_ref, f32[1024,128]{1,0:T(8,128)S(1)} %get-tuple-element.66.low_ref.refs_6_, f32[1024,128]{1,0:T(8,128)S(1)} %get-tuple-element.67.high_ref.refs_8_, f32[1024,128]{1,0:T(8,128)S(1)} %get-tuple-element.70.bot_ref, ...), custom_call_target="tpu_custom_call" | custom-call | flops 15204352 | bytes 2097152 | tf_op jit(solution)/shard_map/outer_first/pallas_call | solution.py:357
  67.3 2.0 %collective-permute-done.6.odd_ref = f32[256,128]{1,0:T(8,128)S(1)} collective-permute-done((f32[256,128]{1,0:T(8,128)S(1)}, f32[256,128]{1,0:T(8,128)S(1)}, u32[]{:S(2)}, u32[]{:S(2)}) %collective-permute-start.6) | collective-permute-done | bytes 131104 | tf_op jit(solution)/shard_map/ppermute | solution.py:675
  69.3 0.0 collective-permute-done.7.even_ref
  69.3 1.3 %strips.3 = (f32[4,64,128]{2,1,0:T(8,128)S(1)}, f32[4,64,128]{2,1,0:T(8,128)S(1)}) custom-call(f32[256,128]{1,0:T(8,128)S(1)} %collective-permute-done.6.odd_ref, f32[256,128]{1,0:T(8,128)S(1)} %collective-permute-done.7.even_ref, f32[512,128]{1,0:T(8,128)S(1)} %get-tuple-element.76.own_ref, f32[4,48,128]{2,1,0:T(8,128)S(1)} %strip_lines.1.line_ref), custom_call_target="tpu_custom_call" | custom-call | tf_op jit(solution)/shard_map/strips/pallas_call | solution.py:473
  70.6 4.5 %second.5 = (f32[1024,128]{1,0:T(8,128)S(1)}, f32[2048,128]{1,0:T(8,128)S(1)}, f32[1024,128]{1,0:T(8,128)S(1)}) custom-call(f32[1024,128]{1,0:T(8,128)S(1)} %get-tuple-element.71.refs_0_, f32[3072,128]{1,0:T(8,128)S(1)} %get-tuple-element.72.refs_1_, f32[1024,128]{1,0:T(8,128)S(1)} %get-tuple-element.73.refs_2_, ...), custom_call_target="tpu_custom_call" | custom-call | flops 15204352 | bytes 2097152 | tf_op jit(solution)/shard_map/second/pallas_call | solution.py:528
  75.1 1.1 %other_loads.1 = f32[256,256]{1,0:T(8,128)S(1)} custom-call(f32[1024,128]{1,0:T(8,128)S(1)} %get-tuple-element.79.low_ref, f32[2048,128]{1,0:T(8,128)S(1)} %get-tuple-element.80.mid_ref, f32[1024,128]{1,0:T(8,128)S(1)} %get-tuple-element.81.high_ref, bf16[2048,512]{1,0:T(8,128)(2,1)S(1)} %get-tuple-element.82.w_high_ref, ...), custom_call_target="tpu_custom_call" | custom-call | flops 536870912 | bytes 1048576 | tf_op jit(solution)/shard_map/other_loads/pallas_call | solution.py:627
  76.2 0.1 collective-permute-start.8
  76.2 2.1 %leave.1 = (f32[16,128,256]{2,1,0:T(8,128)}, f32[256,256]{1,0:T(8,128)S(1)}) custom-call(f32[1024,128]{1,0:T(8,128)S(1)} %get-tuple-element.79.low_ref, f32[2048,128]{1,0:T(8,128)S(1)} %get-tuple-element.80.mid_ref, f32[1024,128]{1,0:T(8,128)S(1)} %get-tuple-element.81.high_ref, bf16[2048,512]{1,0:T(8,128)(2,1)S(1)} %get-tuple-element.82.w_high_ref, ...), custom_call_target="tpu_custom_call" | custom-call | flops 1073741824 | bytes 4194304 | tf_op jit(solution)/shard_map/leave/pallas_call | solution.py:653
  78.4 0.0 collective-permute-done.8
  78.4 0.1 reshape.20
  78.5 15.9 %all_to_all.5 = f32[64,4,256]{2,1,0:T(4,128)S(1)} all-to-all(f32[64,4,256]{2,1,0:T(4,128)S(1)} %reshape.20), channel_id=1, replica_groups={{0,2,4,6,8,10,12,14,16,18,20,22,24,26,28,30,32,34,36,38,40,42,44,46,48,..., dimensions={0} | all-to-all | bytes 524288 | tf_op jit(solution)/shard_map/all_to_all | solution.py:712
  94.4 0.7 reduce_sum.9
  (1 shorter events, 0.0 us)
Async XLA Ops:
  2.8 11.8 %copy-start = (f32[16,128,256]{2,1,0:T(8,128)S(1)}, f32[16,128,256]{2,1,0:T(8,128)}, u32[]{:S(2)}) copy-start(f32[16,128,256]{2,1,0:T(8,128)} %x_ref.5) | copy-start | bytes 6291460
  2.8 13.4 %copy-start.1 = (f32[4,29,16,128]{3,2,1,0:T(8,128)S(1)}, f32[4,29,16,128]{3,2,1,0:T(8,128)}, u32[]{:S(2)}) copy-start(f32[4,29,16,128]{3,2,1,0:T(8,128)} %param.7) | copy-start | bytes 2850820
  2.8 27.3 %collective-permute-start = (f32[5,128,256]{2,1,0:T(8,128)}, f32[5,128,256]{2,1,0:T(8,128)S(1)}, u32[]{:S(2)}, u32[]{:S(2)}) collective-permute-start(f32[5,128,256]{2,1,0:T(8,128)} %ship.2), channel_id=1, source_target_pairs={{4,8},{12,16},{20,24},{28,32},{36,40},{44,48},{52,56},{60,64},{68,... | collective-permute-start | bytes 1966088 | tf_op jit(solution)/shard_map/ppermute | solution.py:675
  14.5 15.6 %collective-permute-start.1 = (f32[5,128,256]{2,1,0:T(8,128)}, f32[5,128,256]{2,1,0:T(8,128)S(1)}, u32[]{:S(2)}, u32[]{:S(2)}) collective-permute-start(f32[5,128,256]{2,1,0:T(8,128)} %ship.3), channel_id=1, source_target_pairs={{0,4},{8,12},{16,20},{24,28},{32,36},{40,44},{48,52},{56,60},{64,6... | collective-permute-start | bytes 1966088 | tf_op jit(solution)/shard_map/ppermute | solution.py:675
  14.6 6.6 %copy-start.2 = (bf16[4096,512]{1,0:T(8,128)(2,1)S(1)}, bf16[4096,512]{1,0:T(8,128)(2,1)}, u32[]{:S(2)}) copy-start(bf16[4096,512]{1,0:T(8,128)(2,1)} %table_ref.1) | copy-start | bytes 12582916
  16.2 5.0 %copy-start.3 = (s32[1024]{0:T(1024)S(1)}, s32[1024]{0:T(1024)}, u32[]{:S(2)}) copy-start(s32[1024]{0:T(1024)} %rows_ref.1) | copy-start | bytes 12292
  21.2 5.3 %copy-start.4 = (s32[1024]{0:T(1024)S(1)}, s32[1024]{0:T(1024)}, u32[]{:S(2)}) copy-start(s32[1024]{0:T(1024)} %param.8) | copy-start | bytes 12292
  31.4 7.2 %collective-permute-start.2 = (f32[384,128]{1,0:T(8,128)S(1)}, f32[384,128]{1,0:T(8,128)S(1)}, u32[]{:S(2)}, u32[]{:S(2)}) collective-permute-start(f32[384,128]{1,0:T(8,128)S(1)} %get-tuple-element.59), channel_id=1, source_target_pairs={{1,2},{2,1},{5,6},{6,5},{9,10},{10,9},{13,14},{14,13},{17,18},{18,... | collective-permute-start | bytes 589832 | tf_op jit(solution)/shard_map/ppermute | solution.py:675
  35.3 3.3 %collective-permute-start.3 = (f32[384,128]{1,0:T(8,128)S(1)}, f32[384,128]{1,0:T(8,128)S(1)}, u32[]{:S(2)}, u32[]{:S(2)}) collective-permute-start(f32[384,128]{1,0:T(8,128)S(1)} %get-tuple-element.60), channel_id=1, source_target_pairs={{0,1},{2,3},{1,0},{3,2},{4,5},{6,7},{5,4},{7,6},{8,9},{10,11},{9,8... | collective-permute-start | bytes 589832 | tf_op jit(solution)/shard_map/ppermute | solution.py:675
  42.7 19.6 %collective-permute-start.4 = (f32[1024,128]{1,0:T(8,128)S(1)}, f32[1024,128]{1,0:T(8,128)S(1)}, u32[]{:S(2)}, u32[]{:S(2)}) collective-permute-start(f32[1024,128]{1,0:T(8,128)S(1)} %get-tuple-element.64), channel_id=1, source_target_pairs={{4,8},{12,16},{20,24},{28,32},{36,40},{44,48},{52,56},{60,64},{68,... | collective-permute-start | bytes 1572872 | tf_op jit(solution)/shard_map/ppermute | solution.py:675
  46.9 15.4 %collective-permute-start.5 = (f32[1024,128]{1,0:T(8,128)S(1)}, f32[1024,128]{1,0:T(8,128)S(1)}, u32[]{:S(2)}, u32[]{:S(2)}) collective-permute-start(f32[1024,128]{1,0:T(8,128)S(1)} %get-tuple-element.65), channel_id=1, source_target_pairs={{0,4},{8,12},{16,20},{24,28},{32,36},{40,44},{48,52},{56,60},{64,6... | collective-permute-start | bytes 1572872 | tf_op jit(solution)/shard_map/ppermute | solution.py:675
  63.0 6.3 %collective-permute-start.6 = (f32[256,128]{1,0:T(8,128)S(1)}, f32[256,128]{1,0:T(8,128)S(1)}, u32[]{:S(2)}, u32[]{:S(2)}) collective-permute-start(f32[256,128]{1,0:T(8,128)S(1)} %get-tuple-element.74), channel_id=1, source_target_pairs={{1,2},{2,1},{5,6},{6,5},{9,10},{10,9},{13,14},{14,13},{17,18},{18,... | collective-permute-start | bytes 393224 | tf_op jit(solution)/shard_map/ppermute | solution.py:675
  64.9 4.4 %collective-permute-start.7 = (f32[256,128]{1,0:T(8,128)S(1)}, f32[256,128]{1,0:T(8,128)S(1)}, u32[]{:S(2)}, u32[]{:S(2)}) collective-permute-start(f32[256,128]{1,0:T(8,128)S(1)} %get-tuple-element.75), channel_id=1, source_target_pairs={{0,1},{2,3},{1,0},{3,2},{4,5},{6,7},{5,4},{7,6},{8,9},{10,11},{9,8... | collective-permute-start | bytes 393224 | tf_op jit(solution)/shard_map/ppermute | solution.py:675
  76.2 2.2 %collective-permute-start.8 = (f32[256,256]{1,0:T(8,128)S(1)}, f32[256,256]{1,0:T(8,128)S(1)}, u32[]{:S(2)}, u32[]{:S(2)}) collective-permute-start(f32[256,256]{1,0:T(8,128)S(1)} %other_loads.1), channel_id=1, source_target_pairs={{0,1},{2,3},{1,0},{3,2},{4,5},{6,7},{5,4},{7,6},{8,9},{10,11},{9,8... | collective-permute-start | bytes 786440 | tf_op jit(solution)/shard_map/ppermute | solution.py:675

commit v11 on v9

--- a/solution.py
+++ b/solution.py
@@ -708,9 +708,10 @@
     others = swap(call_other_loads(low, mid, high, w_high, w_low), "rad", 0)
     out, term = call_leave(low, mid, high, w_high, w_low)
     groups = [[k for k in range(n_azim * n_rad) if k % 2 == core] for core in range(2)]
-    term = (term + others).reshape(len(groups[0]), -1, term.shape[1])
+    columns = term.shape[1]
+    term = (term + others).reshape(len(groups[0]), -1, 128)
     parts = lax.all_to_all(term, ("azim", "rad"), 0, 0, axis_index_groups=groups)
-    return out, jnp.sum(parts, axis=0)
+    return out, jnp.sum(parts, axis=0).reshape(-1, columns)
 
 
 def solution(mesh):

time: 92.9 us -> 92.8 us (level)
  no operation moved by 1% of the time
where the time goes in v11:
time: 92.8 us; the launch traced here: 92.3 us
  Pallas kernels  43.8 us (47%)
  starting transfers between devices  20.1 us (22%)
  blocking collectives  15.3 us (16%)
  waiting for transfers between devices  10.7 us (12%)
  between operations  1.6 us (2%)
    ppermute x9, starting transfers between devices, swap(): return lax.ppermute(block, axis, swaps(count, odd, axis == 'azim'))  20.1 us
    all_to_all x1, blocking collectives, body(): lax.all_to_all(term, ('azim', 'rad'), 0, 0, axis_index_groups=groups)  15.3 us
    ppermute x9, waiting for transfers between devices, swap(): return lax.ppermute(block, axis, swaps(count, odd, axis == 'azim'))  10.7 us
    pallas_call x3, Pallas kernels, call_second(): pl.pallas_call(functools.partial(second, ranges, parts, len(ys), sides),...  9.3 us
    pallas_call x2, Pallas kernels, call_inner_first(): pl.pallas_call(inner_first, in_specs=whole(4), out_specs=whole(2), out_sh...  7.03 us
    pallas_call x1, Pallas kernels, call_gather(): pl.pallas_call(gather, in_specs=[pl.BlockSpec(memory_space=pltpu.SMEM)] +...  5.3 us
    pallas_call x2, Pallas kernels, call_ship(): pl.pallas_call(functools.partial(ship, odd), in_specs=[hbm] * 2, out_spec...  4.24 us
    pallas_call x2, Pallas kernels, call_outer_first(): pl.pallas_call(outer_first, in_specs=whole(7), out_specs=whole(2), out_sh...  4.08 us
  transfers between devices with their start and end apart: 9, of which 3 were waited for; matrix products, arithmetic and copies ran while one was open for 0% of the time, Pallas kernels for 31%

profile of v11, /device:TPU:1, one launch (start us, length us, event | category | flops | bytes accessed | tf_op | source)
XLA Modules:
  0.0 92.3 jit_solution(13647437872740496989)
XLA Ops:
  0.6 2.1 %ship.2 = f32[5,128,256]{2,1,0:T(8,128)} custom-call(f32[16,128,256]{2,1,0:T(8,128)} %x_ref.5, f32[116,16,128]{2,1,0:T(8,128)} %bitcast.3), custom_call_target="tpu_custom_call" | custom-call | tf_op jit(solution)/shard_map/ship/pallas_call | solution.py:160
  2.8 0.0 copy-start
  2.8 0.0 copy-start.1
  2.8 9.6 %collective-permute-start = (f32[5,128,256]{2,1,0:T(8,128)}, f32[5,128,256]{2,1,0:T(8,128)S(1)}, u32[]{:S(2)}, u32[]{:S(2)}) collective-permute-start(f32[5,128,256]{2,1,0:T(8,128)} %ship.2), channel_id=1, source_target_pairs={{4,8},{12,16},{20,24},{28,32},{36,40},{44,48},{52,56},{60,64},{68,... | collective-permute-start | bytes 1966088 | tf_op jit(solution)/shard_map/ppermute | solution.py:675
  12.4 2.1 %ship.3 = f32[5,128,256]{2,1,0:T(8,128)} custom-call(f32[16,128,256]{2,1,0:T(8,128)} %x_ref.5, f32[116,16,128]{2,1,0:T(8,128)} %bitcast.4), custom_call_target="tpu_custom_call" | custom-call | tf_op jit(solution)/shard_map/ship/pallas_call | solution.py:160
  14.5 0.1 collective-permute-start.1
  14.6 0.0 copy-done
  14.6 0.0 copy-start.2
  14.6 1.6 %enter.1 = (f32[1024,128]{1,0:T(8,128)S(1)}, f32[2048,128]{1,0:T(8,128)S(1)}, f32[1024,128]{1,0:T(8,128)S(1)}) custom-call(f32[16,128,256]{2,1,0:T(8,128)S(1)} %copy-done), custom_call_target="tpu_custom_call" | custom-call | tf_op jit(solution)/shard_map/enter/pallas_call | solution.py:180
  16.2 0.0 copy-start.3
  16.2 0.0 copy-done.1
  16.2 0.8 coef_edges.1
  17.0 3.5 %inner_first.2 = (f32[3072,128]{1,0:T(8,128)S(1)}, f32[512,128]{1,0:T(8,128)S(1)}) custom-call(f32[1024,128]{1,0:T(8,128)S(1)} %get-tuple-element.44.low_ref.refs_6_, f32[2048,128]{1,0:T(8,128)S(1)} %get-tuple-element.45.mid_ref.refs_4_, f32[1024,128]{1,0:T(8,128)S(1)} %get-tuple-element.46.high_ref.refs_7_, ...), custom_call_target="tpu_custom_call" | custom-call | flops 1 | bytes 1 | tf_op jit(solution)/shard_map/inner_first/pallas_call | solution.py:215
  21.2 0.0 copy-done.2
  21.2 0.0 copy-done.3
  21.2 0.0 copy-start.4
  21.2 5.3 %gather.1.weights_ref = bf16[1024,512]{1,0:T(8,128)(2,1)S(1)} custom-call(s32[1024]{0:T(1024)S(1)} %copy-done.3, bf16[4096,512]{1,0:T(8,128)(2,1)S(1)} %copy-done.2), custom_call_target="tpu_custom_call" | custom-call | tf_op jit(solution)/shard_map/gather/pallas_call | solution.py:562
  26.5 0.0 copy-done.4
  26.5 3.6 %spread.1 = (bf16[2048,512]{1,0:T(8,128)(2,1)S(1)}, bf16[2048,512]{1,0:T(8,128)(2,1)S(1)}) custom-call(s32[1]{0:T(128)S(6)} %copy.8.count_ref, s32[1,1024]{1,0:T(1,128)S(1)} %bitcast.6, bf16[1024,512]{1,0:T(8,128)(2,1)S(1)} %gather.1.weights_ref), custom_call_target="tpu_custom_call" | custom-call | flops 2147483648 | bytes 6291456 | tf_op jit(solution)/shard_map/spread/pallas_call | solution.py:586
  30.1 0.0 collective-permute-done.odd_ref
  30.1 0.0 collective-permute-done.1.even_ref
  30.1 1.3 %halo_edges.2 = (f32[1024,128]{1,0:T(8,128)S(1)}, f32[1024,128]{1,0:T(8,128)S(1)}, f32[640,128]{1,0:T(8,128)S(1)}, f32[256,128]{1,0:T(8,128)S(1)}, f32[256,128]{...) custom-call(f32[5,128,256]{2,1,0:T(8,128)S(1)} %collective-permute-done.odd_ref, ...), custom_call_target="tpu_custom_call" | custom-call | tf_op jit(solution)/shard_map/halo_edges/pallas_call | solution.py:315
  31.4 1.8 %collective-permute-start.2 = (f32[384,128]{1,0:T(8,128)S(1)}, f32[384,128]{1,0:T(8,128)S(1)}, u32[]{:S(2)}, u32[]{:S(2)}) collective-permute-start(f32[384,128]{1,0:T(8,128)S(1)} %get-tuple-element.59), channel_id=1, source_target_pairs={{0,1},{2,3},{1,0},{3,2},{4,5},{6,7},{5,4},{7,6},{8,9},{10,11},{9,8... | collective-permute-start | bytes 589832 | tf_op jit(solution)/shard_map/ppermute | solution.py:675
  33.3 2.3 %collective-permute-start.3 = (f32[384,128]{1,0:T(8,128)S(1)}, f32[384,128]{1,0:T(8,128)S(1)}, u32[]{:S(2)}, u32[]{:S(2)}) collective-permute-start(f32[384,128]{1,0:T(8,128)S(1)} %get-tuple-element.60), channel_id=1, source_target_pairs={{1,2},{2,1},{5,6},{6,5},{9,10},{10,9},{13,14},{14,13},{17,18},{18,... | collective-permute-start | bytes 589832 | tf_op jit(solution)/shard_map/ppermute | solution.py:675
  35.6 2.0 %outer_first.2 = (f32[1024,128]{1,0:T(8,128)S(1)}, f32[1024,128]{1,0:T(8,128)S(1)}) custom-call(f32[1024,128]{1,0:T(8,128)S(1)} %get-tuple-element.52.top_ref, f32[1024,128]{1,0:T(8,128)S(1)} %get-tuple-element.44.low_ref.refs_6_, f32[1024,128]{1,0:T(8,128)S(1)} %get-tuple-element.46.high_ref.refs_7_, f32[1024,128]{1,0:T(8,128)S(1)} %get-tuple-element.53.bot_ref, ...), custom_call_target="tpu_custom_call" | custom-call | flops 15204352 | bytes 2097152 | tf_op jit(solution)/shard_map/outer_first/pallas_call | solution.py:357
  37.6 0.0 collective-permute-done.2.even_ref
  37.6 2.6 %collective-permute-done.3.odd_ref = f32[384,128]{1,0:T(8,128)S(1)} collective-permute-done((f32[384,128]{1,0:T(8,128)S(1)}, f32[384,128]{1,0:T(8,128)S(1)}, u32[]{:S(2)}, u32[]{:S(2)}) %collective-permute-start.3) | collective-permute-done | bytes 196640 | tf_op jit(solution)/shard_map/ppermute | solution.py:675
  40.3 0.2 strip_lines.1.line_ref
  40.5 1.3 %strips.2 = (f32[4,64,128]{2,1,0:T(8,128)S(1)}, f32[4,64,128]{2,1,0:T(8,128)S(1)}) custom-call(f32[384,128]{1,0:T(8,128)S(1)} %collective-permute-done.2.even_ref, f32[384,128]{1,0:T(8,128)S(1)} %collective-permute-done.3.odd_ref, f32[640,128]{1,0:T(8,128)S(1)} %get-tuple-element.61.own_ref, f32[4,48,128]{2,1,0:T(8,128)S(1)} %strip_lines.1.line_ref), custom_call_target="tpu_custom_call" | custom-call | tf_op jit(solution)/shard_map/strips/pallas_call | solution.py:473
  41.8 2.5 %second.3 = (f32[1024,128]{1,0:T(8,128)S(1)}, f32[1024,128]{1,0:T(8,128)S(1)}, f32[1024,128]{1,0:T(8,128)S(1)}, f32[1024,128]{1,0:T(8,128)S(1)}) custom-call(f32[1024,128]{1,0:T(8,128)S(1)} %get-tuple-element.56.refs_0_, f32[3072,128]{1,0:T(8,128)S(1)} %get-tuple-element.57.refs_1_.refs_0_, f32[1024,128]{1,0:T(8,128)S(1)} %get-tuple-element.58.refs_2_, ...), custom_call_target="tpu_custom_call" | custom-call | flops 15204352 | bytes 2097152 | tf_op jit(solution)/shard_map/second/pallas_call | solution.py:528
  44.3 3.6 %collective-permute-start.4 = (f32[1024,128]{1,0:T(8,128)S(1)}, f32[1024,128]{1,0:T(8,128)S(1)}, u32[]{:S(2)}, u32[]{:S(2)}) collective-permute-start(f32[1024,128]{1,0:T(8,128)S(1)} %get-tuple-element.64), channel_id=1, source_target_pairs={{4,8},{12,16},{20,24},{28,32},{36,40},{44,48},{52,56},{60,64},{68,... | collective-permute-start | bytes 1572872 | tf_op jit(solution)/shard_map/ppermute | solution.py:675
  47.9 0.0 collective-permute-start.5
  47.9 2.3 %second.4.mid_ref.refs_7_ = f32[2048,128]{1,0:T(8,128)S(1)} custom-call(f32[3072,128]{1,0:T(8,128)S(1)} %get-tuple-element.57.refs_1_.refs_0_, f32[4,64,128]{2,1,0:T(8,128)S(1)} %get-tuple-element.62.refs_3_.refs_1_, f32[4,64,128]{2,1,0:T(8,128)S(1)} %get-tuple-element.63.refs_4_.refs_2_, f32[4,29,16,128]{3,2,1,0:T(8,128)S(1)} %get-tuple-element.47.coef_ref.refs_5_.refs_3_, ...), custom_call_target="tpu_custom_call" | custom-call | flops 15204352 | bytes 2097152 | tf_op jit(solution)/shard_map/second/pallas_call | solution.py:528
  50.2 3.5 %inner_first.3 = (f32[3072,128]{1,0:T(8,128)S(1)}, f32[512,128]{1,0:T(8,128)S(1)}) custom-call(f32[1024,128]{1,0:T(8,128)S(1)} %get-tuple-element.66.low_ref.refs_6_, f32[2048,128]{1,0:T(8,128)S(1)} %second.4.mid_ref.refs_7_, f32[1024,128]{1,0:T(8,128)S(1)} %get-tuple-element.67.high_ref.refs_8_, ...), custom_call_target="tpu_custom_call" | custom-call | flops 1 | bytes 1 | tf_op jit(solution)/shard_map/inner_first/pallas_call | solution.py:215
  53.7 6.4 %collective-permute-done.4.odd_ref = f32[1024,128]{1,0:T(8,128)S(1)} collective-permute-done((f32[1024,128]{1,0:T(8,128)S(1)}, f32[1024,128]{1,0:T(8,128)S(1)}, u32[]{:S(2)}, u32[]{:S(2)}) %collective-permute-start.4) | collective-permute-done | bytes 524320 | tf_op jit(solution)/shard_map/ppermute | solution.py:675
  60.1 0.0 collective-permute-done.5.even_ref
  60.1 0.7 halo_edges.3
  60.8 0.1 collective-permute-start.6
  60.9 2.6 %collective-permute-start.7 = (f32[256,128]{1,0:T(8,128)S(1)}, f32[256,128]{1,0:T(8,128)S(1)}, u32[]{:S(2)}, u32[]{:S(2)}) collective-permute-start(f32[256,128]{1,0:T(8,128)S(1)} %get-tuple-element.75), channel_id=1, source_target_pairs={{1,2},{2,1},{5,6},{6,5},{9,10},{10,9},{13,14},{14,13},{17,18},{18,... | collective-permute-start | bytes 393224 | tf_op jit(solution)/shard_map/ppermute | solution.py:675
  63.5 2.0 %outer_first.3 = (f32[1024,128]{1,0:T(8,128)S(1)}, f32[1024,128]{1,0:T(8,128)S(1)}) custom-call(f32[1024,128]{1,0:T(8,128)S(1)} %get-tuple-element.69.top_ref, f32[1024,128]{1,0:T(8,128)S(1)} %get-tuple-element.66.low_ref.refs_6_, f32[1024,128]{1,0:T(8,128)S(1)} %get-tuple-element.67.high_ref.refs_8_, f32[1024,128]{1,0:T(8,128)S(1)} %get-tuple-element.70.bot_ref, ...), custom_call_target="tpu_custom_call" | custom-call | flops 15204352 | bytes 2097152 | tf_op jit(solution)/shard_map/outer_first/pallas_call | solution.py:357
  65.5 0.0 collective-permute-done.6.even_ref
  65.5 1.7 %collective-permute-done.7.odd_ref = f32[256,128]{1,0:T(8,128)S(1)} collective-permute-done((f32[256,128]{1,0:T(8,128)S(1)}, f32[256,128]{1,0:T(8,128)S(1)}, u32[]{:S(2)}, u32[]{:S(2)}) %collective-permute-start.7) | collective-permute-done | bytes 131104 | tf_op jit(solution)/shard_map/ppermute | solution.py:675
  67.2 1.3 %strips.3 = (f32[4,64,128]{2,1,0:T(8,128)S(1)}, f32[4,64,128]{2,1,0:T(8,128)S(1)}) custom-call(f32[256,128]{1,0:T(8,128)S(1)} %collective-permute-done.6.even_ref, f32[256,128]{1,0:T(8,128)S(1)} %collective-permute-done.7.odd_ref, f32[512,128]{1,0:T(8,128)S(1)} %get-tuple-element.76.own_ref, f32[4,48,128]{2,1,0:T(8,128)S(1)} %strip_lines.1.line_ref), custom_call_target="tpu_custom_call" | custom-call | tf_op jit(solution)/shard_map/strips/pallas_call | solution.py:473
  68.5 4.5 %second.5 = (f32[1024,128]{1,0:T(8,128)S(1)}, f32[2048,128]{1,0:T(8,128)S(1)}, f32[1024,128]{1,0:T(8,128)S(1)}) custom-call(f32[1024,128]{1,0:T(8,128)S(1)} %get-tuple-element.71.refs_0_, f32[3072,128]{1,0:T(8,128)S(1)} %get-tuple-element.72.refs_1_, f32[1024,128]{1,0:T(8,128)S(1)} %get-tuple-element.73.refs_2_, ...), custom_call_target="tpu_custom_call" | custom-call | flops 15204352 | bytes 2097152 | tf_op jit(solution)/shard_map/second/pallas_call | solution.py:528
  73.0 1.1 %other_loads.1 = f32[256,256]{1,0:T(8,128)S(1)} custom-call(f32[1024,128]{1,0:T(8,128)S(1)} %get-tuple-element.79.low_ref, f32[2048,128]{1,0:T(8,128)S(1)} %get-tuple-element.80.mid_ref, f32[1024,128]{1,0:T(8,128)S(1)} %get-tuple-element.81.high_ref, bf16[2048,512]{1,0:T(8,128)(2,1)S(1)} %get-tuple-element.82.w_high_ref, ...), custom_call_target="tpu_custom_call" | custom-call | flops 536870912 | bytes 1048576 | tf_op jit(solution)/shard_map/other_loads/pallas_call | solution.py:627
  74.1 0.1 collective-permute-start.8
  74.2 2.1 %leave.1 = (f32[16,128,256]{2,1,0:T(8,128)}, f32[256,256]{1,0:T(8,128)S(1)}) custom-call(f32[1024,128]{1,0:T(8,128)S(1)} %get-tuple-element.79.low_ref, f32[2048,128]{1,0:T(8,128)S(1)} %get-tuple-element.80.mid_ref, f32[1024,128]{1,0:T(8,128)S(1)} %get-tuple-element.81.high_ref, bf16[2048,512]{1,0:T(8,128)(2,1)S(1)} %get-tuple-element.82.w_high_ref, ...), custom_call_target="tpu_custom_call" | custom-call | flops 1073741824 | bytes 4194304 | tf_op jit(solution)/shard_map/leave/pallas_call | solution.py:653
  76.3 0.0 collective-permute-done.8
  76.3 15.3 %all_to_all.5 = f32[64,8,128]{2,1,0:T(8,128)S(1)} all-to-all(f32[64,8,128]{2,1,0:T(8,128)S(1)} %reshape.23), channel_id=1, replica_groups={{0,2,4,6,8,10,12,14,16,18,20,22,24,26,28,30,32,34,36,38,40,42,44,46,48,..., dimensions={0} | all-to-all | bytes 524288 | tf_op jit(solution)/shard_map/all_to_all | solution.py:713
  91.6 0.1 reduce_sum.9
  91.7 0.6 reshape.24
  (2 shorter events, 0.1 us)
Async XLA Ops:
  2.8 11.8 %copy-start = (f32[16,128,256]{2,1,0:T(8,128)S(1)}, f32[16,128,256]{2,1,0:T(8,128)}, u32[]{:S(2)}) copy-start(f32[16,128,256]{2,1,0:T(8,128)} %x_ref.5) | copy-start | bytes 6291460
  2.8 13.4 %copy-start.1 = (f32[4,29,16,128]{3,2,1,0:T(8,128)S(1)}, f32[4,29,16,128]{3,2,1,0:T(8,128)}, u32[]{:S(2)}) copy-start(f32[4,29,16,128]{3,2,1,0:T(8,128)} %param.7) | copy-start | bytes 2850820
  2.8 27.3 %collective-permute-start = (f32[5,128,256]{2,1,0:T(8,128)}, f32[5,128,256]{2,1,0:T(8,128)S(1)}, u32[]{:S(2)}, u32[]{:S(2)}) collective-permute-start(f32[5,128,256]{2,1,0:T(8,128)} %ship.2), channel_id=1, source_target_pairs={{4,8},{12,16},{20,24},{28,32},{36,40},{44,48},{52,56},{60,64},{68,... | collective-permute-start | bytes 1966088 | tf_op jit(solution)/shard_map/ppermute | solution.py:675
  14.5 15.6 %collective-permute-start.1 = (f32[5,128,256]{2,1,0:T(8,128)}, f32[5,128,256]{2,1,0:T(8,128)S(1)}, u32[]{:S(2)}, u32[]{:S(2)}) collective-permute-start(f32[5,128,256]{2,1,0:T(8,128)} %ship.3), channel_id=1, source_target_pairs={{0,4},{8,12},{16,20},{24,28},{32,36},{40,44},{48,52},{56,60},{64,6... | collective-permute-start | bytes 1966088 | tf_op jit(solution)/shard_map/ppermute | solution.py:675
  14.6 6.6 %copy-start.2 = (bf16[4096,512]{1,0:T(8,128)(2,1)S(1)}, bf16[4096,512]{1,0:T(8,128)(2,1)}, u32[]{:S(2)}) copy-start(bf16[4096,512]{1,0:T(8,128)(2,1)} %table_ref.1) | copy-start | bytes 12582916
  16.2 5.0 %copy-start.3 = (s32[1024]{0:T(1024)S(1)}, s32[1024]{0:T(1024)}, u32[]{:S(2)}) copy-start(s32[1024]{0:T(1024)} %rows_ref.1) | copy-start | bytes 12292
  21.2 5.3 %copy-start.4 = (s32[1024]{0:T(1024)S(1)}, s32[1024]{0:T(1024)}, u32[]{:S(2)}) copy-start(s32[1024]{0:T(1024)} %param.8) | copy-start | bytes 12292
  31.4 6.2 %collective-permute-start.2 = (f32[384,128]{1,0:T(8,128)S(1)}, f32[384,128]{1,0:T(8,128)S(1)}, u32[]{:S(2)}, u32[]{:S(2)}) collective-permute-start(f32[384,128]{1,0:T(8,128)S(1)} %get-tuple-element.59), channel_id=1, source_target_pairs={{0,1},{2,3},{1,0},{3,2},{4,5},{6,7},{5,4},{7,6},{8,9},{10,11},{9,8... | collective-permute-start | bytes 589832 | tf_op jit(solution)/shard_map/ppermute | solution.py:675
  33.3 7.0 %collective-permute-start.3 = (f32[384,128]{1,0:T(8,128)S(1)}, f32[384,128]{1,0:T(8,128)S(1)}, u32[]{:S(2)}, u32[]{:S(2)}) collective-permute-start(f32[384,128]{1,0:T(8,128)S(1)} %get-tuple-element.60), channel_id=1, source_target_pairs={{1,2},{2,1},{5,6},{6,5},{9,10},{10,9},{13,14},{14,13},{17,18},{18,... | collective-permute-start | bytes 589832 | tf_op jit(solution)/shard_map/ppermute | solution.py:675
  44.3 15.9 %collective-permute-start.4 = (f32[1024,128]{1,0:T(8,128)S(1)}, f32[1024,128]{1,0:T(8,128)S(1)}, u32[]{:S(2)}, u32[]{:S(2)}) collective-permute-start(f32[1024,128]{1,0:T(8,128)S(1)} %get-tuple-element.64), channel_id=1, source_target_pairs={{4,8},{12,16},{20,24},{28,32},{36,40},{44,48},{52,56},{60,64},{68,... | collective-permute-start | bytes 1572872 | tf_op jit(solution)/shard_map/ppermute | solution.py:675
  47.9 12.3 %collective-permute-start.5 = (f32[1024,128]{1,0:T(8,128)S(1)}, f32[1024,128]{1,0:T(8,128)S(1)}, u32[]{:S(2)}, u32[]{:S(2)}) collective-permute-start(f32[1024,128]{1,0:T(8,128)S(1)} %get-tuple-element.65), channel_id=1, source_target_pairs={{0,4},{8,12},{16,20},{24,28},{32,36},{40,44},{48,52},{56,60},{64,6... | collective-permute-start | bytes 1572872 | tf_op jit(solution)/shard_map/ppermute | solution.py:675
  60.8 4.7 %collective-permute-start.6 = (f32[256,128]{1,0:T(8,128)S(1)}, f32[256,128]{1,0:T(8,128)S(1)}, u32[]{:S(2)}, u32[]{:S(2)}) collective-permute-start(f32[256,128]{1,0:T(8,128)S(1)} %get-tuple-element.74), channel_id=1, source_target_pairs={{0,1},{2,3},{1,0},{3,2},{4,5},{6,7},{5,4},{7,6},{8,9},{10,11},{9,8... | collective-permute-start | bytes 393224 | tf_op jit(solution)/shard_map/ppermute | solution.py:675
  60.9 6.3 %collective-permute-start.7 = (f32[256,128]{1,0:T(8,128)S(1)}, f32[256,128]{1,0:T(8,128)S(1)}, u32[]{:S(2)}, u32[]{:S(2)}) collective-permute-start(f32[256,128]{1,0:T(8,128)S(1)} %get-tuple-element.75), channel_id=1, source_target_pairs={{1,2},{2,1},{5,6},{6,5},{9,10},{10,9},{13,14},{14,13},{17,18},{18,... | collective-permute-start | bytes 393224 | tf_op jit(solution)/shard_map/ppermute | solution.py:675
  74.1 2.2 %collective-permute-start.8 = (f32[256,256]{1,0:T(8,128)S(1)}, f32[256,256]{1,0:T(8,128)S(1)}, u32[]{:S(2)}, u32[]{:S(2)}) collective-permute-start(f32[256,256]{1,0:T(8,128)S(1)} %other_loads.1), channel_id=1, source_target_pairs={{0,1},{2,3},{1,0},{3,2},{4,5},{6,7},{5,4},{7,6},{8,9},{10,11},{9,8... | collective-permute-start | bytes 786440 | tf_op jit(solution)/shard_map/ppermute | solution.py:675
